TPU v7x, 32 devices: a whole 2x2x4 slice. The times are simulated.
32 devices in a mesh: ma: 2 (over y), fr: 4 (over x, core), fc: 4 (over z).
Axes of the slice: x: 2, y: 2, z: 4, core: 2. Of those that a mesh axis runs over, the one named last changes fastest.
Arguments:
- beam_transfer: bfloat16 [2, 256, 64, 512], P(None, ('ma', 'fr'), 'fc'), parts along dimension 1, may hold values from -0.25 to 0.25
- noise_var: float32 [256, 64], P(('ma', 'fr'), 'fc'), parts along dimension 0, may hold values from 0.3 to 30
- spectra: float32 [2, 512], replicated, may hold values from 0.05 to 5
- freq_covariance: float32 [2, 128, 128], replicated, as said below
- start_vectors: float32 [2, 256, 64, 128], P(None, ('ma', 'fr'), 'fc'), parts along dimension 1, may hold values from -6 to 6
Outputs:
- basis: float32 [2, 256, 64, 128], P(None, ('ma', 'fr'), 'fc'), parts along dimension 1
There are 2 independent parts, one for each index of `ma`. A program takes and returns all parts, laid end to end along the dimension named above; an argument that names none is the same for every part. Nothing has to cross between parts.
Inputs may be any that keep to these rules, and one draw needn't show every extreme that they name: freq_covariance[k] is symmetric and positive definite for each k.
All inputs are finite; a program needn't handle non-finite values.
Results may differ from a plain program's by a relative error of at most 0.0071.
Values may be sent and summed in bfloat16 or wider, within the bound.
No kernel may reach another device: no remote copies, remote signals or barrier semaphores. Data moves between devices by JAX's collectives and lax.ppermute only.
A program may use at most 192 MiB of HBM per device.

v0:
```python
import math

import jax
import jax.numpy as jnp
from jax import lax
from jax.sharding import PartitionSpec as P

F = 128
P_SIZE = 64
R = 128
ITERS = 2


def row_operands(row_part, spectra):
    scaled = (row_part.astype(jnp.float32)[None] * spectra[:, None, None, :]).astype(jnp.bfloat16)
    real_rows = jnp.concatenate([scaled[:, 0], scaled[:, 1]], axis=-1)
    imag_rows = jnp.concatenate([scaled[:, 1], -scaled[:, 0]], axis=-1)
    return jnp.stack([real_rows, imag_rows], axis=1)


def apply_tile(pair_tile, vec_bf):
    row_count = pair_tile.shape[1]
    stacked = pair_tile.reshape(2 * row_count, pair_tile.shape[2])
    with_real = jnp.dot(stacked, vec_bf[0], preferred_element_type=jnp.float32)
    with_imag = jnp.dot(stacked, vec_bf[1], preferred_element_type=jnp.float32)
    real_part = with_real[:row_count] - with_imag[row_count:]
    imag_part = with_real[row_count:] + with_imag[:row_count]
    return jnp.stack([real_part, imag_part], axis=0)


def partial_gram(image):
    flat = image.reshape(-1, image.shape[-1])
    return jnp.dot(
        flat.T, flat, precision=lax.Precision.HIGHEST, preferred_element_type=jnp.float32
    )


def orthonormalize(image, gram_matrix):
    lower = jnp.linalg.cholesky(gram_matrix)
    flat = image.reshape(-1, image.shape[-1])
    solved = lax.linalg.triangular_solve(lower, flat, left_side=False, lower=True, transpose_a=True)
    return solved.reshape(image.shape)


def body(beam_transfer, noise_var, spectra, freq_covariance, start_vectors):
    whitened = (beam_transfer.astype(jnp.float32) * lax.rsqrt(noise_var)[None, :, :, None]).astype(
        jnp.bfloat16
    )
    row_beams = lax.all_gather(whitened, "fc", axis=2, tiled=True)
    freq_rows = row_beams.shape[1]
    mode_count = row_beams.shape[2]
    multipoles = row_beams.shape[3]
    row_total = freq_rows * mode_count
    components = spectra.shape[0]
    row_operand = row_operands(row_beams.reshape(2, row_total, multipoles), spectra)
    row_start = lax.axis_index("fr") * freq_rows
    row_cov = lax.dynamic_slice_in_dim(freq_covariance, row_start, freq_rows, 1)
    piece = lax.all_gather(whitened, "fr", axis=1, tiled=True)
    piece_freqs = piece.shape[1]
    piece_modes = piece.shape[2]
    columns = piece.reshape(2, piece_freqs * piece_modes, multipoles)
    col_operand = jnp.concatenate([columns[0], columns[1]], axis=-1)
    products = lax.dot_general(
        row_operand, col_operand, (((3,), (1,)), ((), ())), preferred_element_type=jnp.float32
    )
    weight = jnp.broadcast_to(
        row_cov[:, :, None, :, None], (components, freq_rows, mode_count, piece_freqs, piece_modes)
    )
    weight = weight.reshape(components, row_total, piece_freqs * piece_modes)
    pair_tile = jnp.einsum("kxy,kcxy->cxy", weight, products).astype(jnp.bfloat16)
    vectors = start_vectors
    own_modes = start_vectors.shape[2]
    for iteration in range(ITERS):
        gathered = lax.all_gather(vectors.astype(jnp.bfloat16), "fr", axis=1, tiled=True)
        vec_bf = gathered.reshape(2, -1, R)
        partial_value = apply_tile(pair_tile, vec_bf).reshape(2, freq_rows, mode_count, R)
        summed = lax.psum(partial_value, "fc")
        gram_matrix = lax.psum(partial_gram(summed), "fr")
        own_rows = lax.dynamic_slice_in_dim(summed, lax.axis_index("fc") * own_modes, own_modes, 2)
        vectors = orthonormalize(own_rows, gram_matrix)
    return vectors * math.sqrt(2.0 * F * P_SIZE)


def solution(mesh):
    in_specs = (
        P(None, ("ma", "fr"), "fc", None),
        P(("ma", "fr"), "fc"),
        P(),
        P(),
        P(None, ("ma", "fr"), "fc", None),
    )
    out_specs = P(None, ("ma", "fr"), "fc", None)
    return jax.shard_map(body, mesh=mesh, in_specs=in_specs, out_specs=out_specs, check_vma=False)
```

profile of v0, /device:TPU:0, one launch (start us, length us, event | category | flops | bytes accessed | tf_op | source)
XLA Modules:
  0.0 580.2 jit_solution(9767002180199784841)
XLA Ops:
  6.5 1.8 convert_element_type.41
  8.4 0.0 all-gather.5.cloned.1.call-start
  8.4 0.7 rsqrt.3
  9.1 0.1 copy.13
  9.2 2.5 multiply_convert_fusion.1
  11.7 0.0 all-gather.7.cloned.1.call-start
  11.7 0.7 all-gather.7.cloned.1.call-update
  12.4 0.0 all-reduce.5.cloned.1.call-start
  12.5 0.1 copy.15
  12.6 21.5 %broadcast_in_dim.2 = f32[2,32,64,128,16]{2,1,4,3,0:T(8,128)} broadcast(f32[2,32,128]{1,2,0:T(8,128)S(1)} %copy.15), dimensions={0,1,3} | broadcast | bytes 33587200 | tf_op jit(solution)/shard_map/broadcast_in_dim | solution.py:66
  34.1 56.9 %reshape.67 = f32[2,2048,2048]{1,2,0:T(8,128)} reshape(f32[2,32,64,128,16]{2,1,4,3,0:T(8,128)} %broadcast_in_dim.2) | data formatting | bytes 67108864 | tf_op jit(solution)/shard_map/reshape | solution.py:69
  91.0 33.9 %copy.35 = f32[2048,2048,2]{1,0,2:T(8,128)} copy(f32[2048,2048,2]{0,1,2:T(8,128)} %bitcast.95) | data formatting | bytes 67108864
  124.9 1.4 fusion.17
  126.3 0.0 all-gather.5.cloned.1.call-done
  126.3 6.6 %bitcast_convert_fusion = f32[2,2048,512]{2,1,0:T(8,128)} fusion(bf16[2,32,64,512]{3,2,1,0:T(8,128)(2,1)} %all-gather.5.cloned.1.call-done), kind=kLoop, calls=%fused_computation.11 | loop fusion | flops 2097152 | bytes 12582912 | tf_op jit(solution)/shard_map/convert_element_type | solution.py:15
  132.9 8.3 %multiply_convert_fusion = bf16[2,2,2048,512]{3,2,1,0:T(8,128)(2,1)} fusion(f32[2,512]{1,0:T(2,128)S(1)} %copy-done.6, f32[2,2048,512]{2,1,0:T(8,128)} %bitcast_convert_fusion), kind=kLoop, calls=%fused_computation.3 | loop fusion | flops 8388608 | bytes 16781312 | tf_op jit(solution)/shard_map/convert_element_type | solution.py:15
  141.2 4.8 fusion.14
  146.0 1.4 copy-done.2
  147.4 3.5 slice_bitcast_fusion.1
  150.9 2.8 fusion.15
  153.8 2.8 maximum_bitcast_fusion.7
  156.6 0.8 copy-done.3
  157.4 1.5 copy-done.4
  158.8 6.7 %maximum_bitcast_fusion = (bf16[2,1,2048,1024]{3,2,0,1:T(8,128)(2,1)}, bf16[2,1,2048,1024]{3,2,0,1:T(8,128)(2,1)}) fusion(bf16[2,2048,512]{2,1,0:T(8,128)(2,1)S(1)} %copy-done.5, bf16[2,2048,512]{2,1,0:T(8,128)(2,1)S(1)} %copy-done.4, bf16[2,2048,512]{2,1,0:T(8,128)(2,1)S(1)} %copy-done.3), kind=kLoop, calls=%fused_computation.4 | loop fusion | flops 33554432 | bytes 29360128 | tf_op jit(solution)/shard_map/stack | solution.py:18
  165.5 52.6 %multiply_reduce_fusion = bf16[2048,2048,2]{1,0,2:T(8,128)(2,1)} fusion(f32[2048,2048,2]{1,0,2:T(8,128)} %copy.35, bf16[2,1,2048,1024]{3,2,0,1:T(8,128)(2,1)} %get-tuple-element.16, bf16[2,1,2048,1024]{3,2,0,1:T(8,128)(2,1)} %get-tuple-element.15, bf16[2048,1024,1,1]{1,0,3,2:T(8,128)(2,1)} %maximum_bitcast_fusion.7), kind=kOutput, calls=%fused_computation | convolution fusion | flops 34393292800 | bytes 71303168 | tf_op jit(solution)/shard_map/dot_general | solution.py:63
  218.1 10.1 %fusion.18 = f32[4096,128]{1,0:T(8,128)S(1)} fusion(bf16[4096,2048]{1,0:T(8,128)(2,1)} %bitcast.109, bf16[2048,128]{1,0:T(8,128)(2,1)S(1)} %bitcast.106), kind=kOutput, calls=%fused_computation.50 | convolution fusion | flops 2147483648 | bytes 19398656 | tf_op jit(solution)/shard_map/dot_general | solution.py:24
  228.2 0.4 copy-done.7
  228.7 4.6 fusion.19
  233.3 0.2 slice_subtract_fusion.1
  233.5 1.4 pad_maximum_fusion.1
  235.0 0.0 all-reduce.7.cloned.1.call-start
  235.0 89.3 %all-reduce.5.cloned.1.call-done = f32[2,32,64,128]{3,2,1,0:T(8,128)} async-done(((f32[2,32,64,128]{3,2,1,0:T(8,128)}), f32[2,32,64,128]{3,2,1,0:T(8,128)}) %all-reduce.5.cloned.1.call-update) | async-done | bytes 2097168 | tf_op jit(solution)/shard_map/psum | solution.py:77
  324.4 6.3 %convolution_bitcast_fusion.3 = f32[128,128]{0,1:T(8,128)} fusion(f32[2,32,64,128]{3,2,1,0:T(8,128)} %all-reduce.5.cloned.1.call-done), kind=kOutput, calls=%fused_computation.20 | convolution fusion | flops 805306368 | bytes 2162688 | tf_op jit(solution)/shard_map/dot_general | solution.py:33
  330.7 0.3 all-gather.11.cloned.1.call-start
  331.0 1.1 constant_dynamic-slice_fusion.1
  332.1 28.8 %all-reduce.7.cloned.1.call-done = f32[128,128]{0,1:T(8,128)} async-done(((f32[128,128]{0,1:T(8,128)}), f32[128,128]{0,1:T(8,128)}) %all-reduce.7.cloned.1.call-update) | async-done | bytes 65552 | tf_op jit(solution)/shard_map/psum | solution.py:78
  360.9 0.9 copy.17
  361.8 0.9 fusion.10
  362.7 11.7 %cholesky.44 = f32[128,128]{1,0:T(8,128)S(1)} custom-call(f32[128,128]{1,0:T(8,128)S(1)} %fusion.10), custom_call_target="Cholesky" | custom-call | tf_op jit(solution)/shard_map/jit(cholesky)/cholesky | solution.py:39
  374.4 0.6 compare_reduce_fusion.1
  375.1 0.7 fusion.5
  375.7 9.8 %custom-call.6 = f32[1,128,128]{1,2,0:T(8,128)S(1)} custom-call(f32[1,128,128]{2,1,0:T(8,128)S(1)} %fusion.5), custom_call_target="InvertDiagBlocksLowerTriangular" | custom-call | tf_op jit(solution)/shard_map/triangular_solve/custom-call.0 | solution.py:41
  385.6 0.6 fusion.4
  386.2 0.8 copy.18
  387.1 0.0 all-reduce.9.cloned.1.call-start
  387.1 16.8 %all-gather.11.cloned.1.call-done = bf16[2,128,16,128]{3,2,1,0:T(8,128)(2,1)} async-done(((bf16[2,32,16,128]{3,2,1,0:T(8,128)(2,1)}), bf16[2,128,16,128]{3,2,1,0:T(8,128)(2,1)}) %all-gather.11.cloned.1.call-update) | async-done | bytes 1048592 | tf_op jit(solution)/shard_map/all_gather | solution.py:74
  404.0 1.4 fusion.16
  405.3 8.2 %fusion.20 = f32[4096,128]{1,0:T(8,128)S(1)} fusion(bf16[4096,2048]{1,0:T(8,128)(2,1)} %bitcast.110, bf16[2048,128]{1,0:T(8,128)(2,1)S(1)} %bitcast.108), kind=kOutput, calls=%fused_computation.52 | convolution fusion | flops 2147483648 | bytes 19398656 | tf_op jit(solution)/shard_map/dot_general | solution.py:24
  413.5 8.2 %fusion.21 = f32[4096,128]{1,0:T(8,128)S(1)} fusion(bf16[4096,2048]{1,0:T(8,128)(2,1)} %bitcast.111, bf16[2048,128]{1,0:T(8,128)(2,1)S(1)} %bitcast.107), kind=kOutput, calls=%fused_computation.53 | convolution fusion | flops 2147483648 | bytes 19398656 | tf_op jit(solution)/shard_map/dot_general | solution.py:25
  421.7 0.2 slice_subtract_fusion
  421.9 1.4 pad_maximum_fusion.2
  423.4 0.3 all-reduce.11.cloned.1.call-start
  423.7 86.4 %all-reduce.9.cloned.1.call-done = f32[2,32,64,128]{3,2,1,0:T(8,128)} async-done(((f32[2,32,64,128]{3,2,1,0:T(8,128)}), f32[2,32,64,128]{3,2,1,0:T(8,128)}) %all-reduce.9.cloned.1.call-update) | async-done | bytes 2097168 | tf_op jit(solution)/shard_map/psum | solution.py:77
  510.1 6.3 %convolution_bitcast_fusion.2 = f32[128,128]{0,1:T(8,128)} fusion(f32[2,32,64,128]{3,2,1,0:T(8,128)} %all-reduce.9.cloned.1.call-done), kind=kOutput, calls=%fused_computation.19 | convolution fusion | flops 805306368 | bytes 2162688 | tf_op jit(solution)/shard_map/dot_general | solution.py:33
  516.4 1.1 constant_dynamic-slice_fusion
  517.5 29.1 %all-reduce.11.cloned.1.call-done = f32[128,128]{0,1:T(8,128)} async-done(((f32[128,128]{0,1:T(8,128)}), f32[128,128]{0,1:T(8,128)}) %all-reduce.11.cloned.1.call-update) | async-done | bytes 65552 | tf_op jit(solution)/shard_map/psum | solution.py:78
  546.6 0.9 copy.20
  547.5 0.9 fusion.8
  548.4 11.7 %cholesky.55 = f32[128,128]{1,0:T(8,128)S(1)} custom-call(f32[128,128]{1,0:T(8,128)S(1)} %fusion.8), custom_call_target="Cholesky" | custom-call | tf_op jit(solution)/shard_map/jit(cholesky)/cholesky | solution.py:39
  560.1 0.6 compare_reduce_fusion
  560.8 0.7 fusion.6
  561.4 9.8 %custom-call.7 = f32[1,128,128]{1,2,0:T(8,128)S(1)} custom-call(f32[1,128,128]{2,1,0:T(8,128)S(1)} %fusion.6), custom_call_target="InvertDiagBlocksLowerTriangular" | custom-call | tf_op jit(solution)/shard_map/triangular_solve/custom-call.0 | solution.py:41
  571.3 0.6 fusion.3
  571.9 1.0 copy.21
  (25 shorter events, 0.2 us)
Async XLA Ops:
  6.5 6.0 %copy-start = (f32[2,128,128]{2,1,0:T(8,128)S(1)}, f32[2,128,128]{2,1,0:T(8,128)}, u32[]{:S(2)}) copy-start(f32[2,128,128]{2,1,0:T(8,128)} %param.11) | copy-start | bytes 393220
  6.5 118.3 %all-gather.9.cloned.1.call-start = ((), (), s32[]{:S(2)}) async-start(), calls=%async_computation.2 | async-start | bytes 1310720 | tf_op jit(solution)/shard_map/all_gather | solution.py:74
  8.4 117.9 %all-gather.5.cloned.1.call-start = ((), (), s32[]{:S(2)}) async-start(), calls=%async_computation | async-start | bytes 5242880 | tf_op jit(solution)/shard_map/all_gather | solution.py:49
  11.7 139.2 %all-gather.7.cloned.1.call-start = ((), (), s32[]{:S(2)}) async-start(), calls=%async_computation.1 | async-start | bytes 5242880 | tf_op jit(solution)/shard_map/all_gather | solution.py:58
  12.4 312.0 %all-reduce.5.cloned.1.call-start = ((), (), s32[]{:S(2)}) async-start(), calls=%async_computation.3 | async-start | bytes 4194304 | tf_op jit(solution)/shard_map/psum | solution.py:77
  126.3 6.7 %copy-start.6 = (f32[2,512]{1,0:T(2,128)S(1)}, f32[2,512]{1,0:T(2,128)}, u32[]{:S(2)}) copy-start(f32[2,512]{1,0:T(2,128)} %param.10) | copy-start | bytes 12292
  141.2 6.2 %copy-start.2 = (bf16[2,2,2048,512]{3,2,1,0:T(8,128)(2,1)S(1)}, bf16[2,2,2048,512]{3,2,1,0:T(8,128)(2,1)}, u32[]{:S(2)}) copy-start(bf16[2,2,2048,512]{3,2,1,0:T(8,128)(2,1)} %multiply_convert_fusion) | copy-start | bytes 25165828
  150.9 5.7 copy-start.5
  153.8 3.6 copy-start.3
  153.8 5.0 copy-start.4
  218.1 10.5 %copy-start.7 = (bf16[2048,2048,2]{1,0,2:T(8,128)(2,1)S(1)}, bf16[2048,2048,2]{1,0,2:T(8,128)(2,1)}, u32[]{:S(2)}) copy-start(bf16[2048,2048,2]{1,0,2:T(8,128)(2,1)} %multiply_reduce_fusion) | copy-start | bytes 50331652
  235.0 125.9 %all-reduce.7.cloned.1.call-start = ((), (), s32[]{:S(2)}) async-start(), calls=%async_computation.4 | async-start | bytes 131072 | tf_op jit(solution)/shard_map/psum | solution.py:78
  330.7 73.2 %all-gather.11.cloned.1.call-start = ((), (), s32[]{:S(2)}) async-start(), calls=%async_computation.5 | async-start | bytes 1310720 | tf_op jit(solution)/shard_map/all_gather | solution.py:74
  387.1 123.0 %all-reduce.9.cloned.1.call-start = ((), (), s32[]{:S(2)}) async-start(), calls=%async_computation.6 | async-start | bytes 4194304 | tf_op jit(solution)/shard_map/psum | solution.py:77
  423.4 149.5 %copy-start.1 = (f32[2,128,128]{2,1,0:T(8,128)S(1)}, f32[2,128,128]{2,1,0:T(8,128)}, u32[]{:S(2)}) copy-start(f32[2,128,128]{2,1,0:T(8,128)} %param.11) | copy-start | bytes 393220
  423.4 123.2 %all-reduce.11.cloned.1.call-start = ((), (), s32[]{:S(2)}) async-start(), calls=%async_computation.7 | async-start | bytes 131072 | tf_op jit(solution)/shard_map/psum | solution.py:78
Sparse Core Ops, SparseCore 0:
  8.9 19.4 all-gather.8
  29.9 80.7 all-gather.4
  112.3 32.9 all-gather.6
  235.1 89.2 all-reduce.4
  330.8 30.0 all-reduce.6
  387.2 16.7 all-gather.10
  423.5 86.5 all-reduce.8
  516.5 30.0 all-reduce.10
where the time goes:
time: 591 us; the launch traced here: 580 us
  waiting for transfers between devices  251 us (42%)
  local copies, waits for them, and re-layouts  132 us (22%)
  matrix products  97.6 us (17%)
  other arithmetic  84.2 us (14%)
  between operations  14.2 us (2%)
    psum x2, waiting for transfers between devices, body(): summed = lax.psum(partial_value, 'fc')  176 us
    psum x2, waiting for transfers between devices, body(): gram_matrix = lax.psum(partial_gram(summed), 'fr')  57.9 us
    reshape x1, local copies, waits for them, and re-layouts, body(): weight = weight.reshape(components, row_total, piece_freqs * piece_modes)  56.9 us
    dot_general x1, matrix products, body(): lax.dot_general(row_operand, col_operand, (((3,), (1,)), ((), ())), prefe...  52.6 us
    unnamed x17, local copies, waits for them, and re-layouts  38 us
    another operation x6, other arithmetic, orthonormalize(): lower = jnp.linalg.cholesky(gram_matrix)  24.8 us
    broadcast_in_dim x1, local copies, waits for them, and re-layouts, body(): jnp.broadcast_to(row_cov[:, :, None, :, None], (components, freq_rows, mo...  21.5 us
    another operation x4, other arithmetic, orthonormalize(): lax.linalg.triangular_solve(lower, flat, left_side=False, lower=True, tra...  20.9 us
  transfers between devices with their start and end apart: 8, of which 5 were waited for; matrix products, arithmetic and copies ran while one was open for 25% of the time, Pallas kernels for 0%

commit v1 on v0

v1 whole, which is shorter than its diff:
```python
import functools
import math

import jax
import jax.numpy as jnp
from jax import lax
from jax.experimental import pallas as pl
from jax.experimental.pallas import tpu as pltpu
from jax.sharding import Mesh
from jax.sharding import PartitionSpec as P

ITERS = 2
BF16 = jnp.bfloat16
F32 = jnp.float32
VMEM_BYTES = 56 * 1024 * 1024
HIGH = lax.Precision.HIGHEST


def rolled(value, shift):
    return pltpu.roll(value, shift % value.shape[-1], 1)


def apply_kernel(n_vec, n_chunk, own, *refs):
    vec_refs = refs[:n_vec]
    beam_refs = refs[n_vec : n_vec + n_chunk]
    cov_ref, spec_ref, out_ref, z_ref, y_ref = refs[n_vec + n_chunk :]
    freqs, rows, lanes = vec_refs[0].shape
    half = rows // 2
    components = spec_ref.shape[1]
    lane = lax.broadcasted_iota(jnp.int32, (half, lanes), 1)
    is_real = (lane // own) % 2 == 0
    sign = jnp.where(is_real, -1.0, 1.0).astype(F32)

    for chunk in range(n_chunk):
        beam_ref = beam_refs[chunk]

        def project(freq, carry):
            vec = vec_refs[0][freq]
            for other in vec_refs[1:]:
                vec = vec + other[freq]
            z_ref[pl.ds(freq, rows, stride=freqs), :] = jnp.dot(
                vec.astype(BF16), beam_ref[freq], preferred_element_type=F32
            )
            return carry

        lax.fori_loop(0, freqs, project, 0, unroll=8)

        def mix(row, carry):
            start = pl.multiple_of(row * freqs, freqs)
            z = z_ref[pl.ds(start, freqs), :]
            scaled = [(z * spec_ref[chunk, k][None, :]).astype(BF16) for k in range(components)]
            stacked = jnp.concatenate(scaled, axis=0)
            y_ref[pl.ds(start, freqs), :] = jnp.dot(
                cov_ref[...], stacked, preferred_element_type=F32
            )
            return carry

        lax.fori_loop(0, rows, mix, 0, unroll=4)

        def expand(freq, carry):
            y = y_ref[pl.ds(freq, rows, stride=freqs), :].astype(BF16)
            product = lax.dot_general(
                y, beam_ref[freq], (((1,), (1,)), ((), ())), preferred_element_type=F32
            )
            swapped = jnp.where(
                jnp.concatenate([is_real, is_real], axis=0),
                rolled(product, -own),
                rolled(product, own),
            )
            top = product[:half] + sign * swapped[half:]
            bottom = product[half:] - sign * swapped[:half]
            image = jnp.concatenate([top, bottom], axis=0)
            if chunk:
                image = image + out_ref[freq]
            out_ref[freq] = image
            return carry

        lax.fori_loop(0, freqs, expand, 0, unroll=8)


def apply_covariance(vecs, beams, cov, spec, own):
    freqs, rows, lanes = vecs[0].shape
    depth = beams[0].shape[2]
    flops = 2 * len(beams) * freqs * rows * (2 * lanes * depth + 2 * freqs * depth)
    return pl.pallas_call(
        functools.partial(apply_kernel, len(vecs), len(beams), own),
        out_shape=jax.ShapeDtypeStruct((freqs, rows, lanes), F32),
        in_specs=[pl.BlockSpec(memory_space=pltpu.VMEM)] * (len(vecs) + len(beams) + 2),
        out_specs=pl.BlockSpec(memory_space=pltpu.VMEM),
        scratch_shapes=[
            pltpu.VMEM((rows * freqs, depth), F32),
            pltpu.VMEM((rows * freqs, depth), F32),
        ],
        compiler_params=pltpu.CompilerParams(vmem_limit_bytes=VMEM_BYTES),
        cost_estimate=pl.CostEstimate(
            flops=flops, bytes_accessed=len(beams) * freqs * lanes * depth * 2, transcendentals=0
        ),
    )(*vecs, *beams, cov, spec)


def pack_kernel(own, first_ref, second_ref, out_ref):
    x_count, z_count, groups = out_ref.shape[:3]
    freqs, rows, lanes = first_ref.shape
    per_group = lanes // own
    lane = lax.broadcasted_iota(jnp.int32, (rows, lanes), 1) // own

    def group(index, carry):
        x_index, group_index = index // groups, index % groups
        totals = [jnp.zeros((rows, lanes), F32)] * z_count
        for place in range(per_group):
            freq = index * per_group + place
            image = first_ref[freq] + second_ref[freq]
            for z_index in range(z_count):
                moved = rolled(image, (place - 2 * z_index) * own)
                totals[z_index] = jnp.where(lane == place, moved, totals[z_index])
        for z_index in range(z_count):
            out_ref[x_index, z_index, group_index] = totals[z_index].astype(BF16)
        return carry

    lax.fori_loop(0, x_count * groups, group, 0)


def pack(first, second, x_count, z_count, own):
    freqs, rows, lanes = first.shape
    groups = freqs * own // (x_count * lanes)
    return pl.pallas_call(
        functools.partial(pack_kernel, own),
        out_shape=jax.ShapeDtypeStruct((x_count, z_count, groups, rows, lanes), BF16),
        in_specs=[pl.BlockSpec(memory_space=pltpu.VMEM)] * 2,
        out_specs=pl.BlockSpec(memory_space=pltpu.VMEM),
        compiler_params=pltpu.CompilerParams(vmem_limit_bytes=VMEM_BYTES),
    )(first, second)


def gram_kernel(rows_ref, out_ref):
    senders, images, groups, parts, vectors, lanes = rows_ref.shape
    total = senders * vectors
    for image in range(images):
        gram = jnp.zeros((total, total), F32)
        for group in range(groups):
            for part in range(parts):
                flat = rows_ref[:, image, group, part].reshape(total, lanes)
                gram += lax.dot_general(
                    flat, flat, (((1,), (1,)), ((), ())), preferred_element_type=F32
                )
        out_ref[image] = gram


def grams(rows):
    total = rows.shape[0] * rows.shape[4]
    return pl.pallas_call(
        gram_kernel,
        out_shape=jax.ShapeDtypeStruct((rows.shape[1], total, total), F32),
        in_specs=[pl.BlockSpec(memory_space=pltpu.VMEM)],
        out_specs=pl.BlockSpec(memory_space=pltpu.VMEM),
        compiler_params=pltpu.CompilerParams(vmem_limit_bytes=VMEM_BYTES),
    )(rows)


def finish_kernel(rows_ref, mixing_ref, out_ref):
    senders, groups, parts, vectors, lanes = rows_ref.shape
    total = senders * vectors
    mixing = mixing_ref[...]
    high = mixing.astype(BF16)
    rest = mixing - high.astype(F32)
    middle = rest.astype(BF16)
    low = (rest - middle.astype(F32)).astype(BF16)
    for group in range(groups):
        for part in range(parts):
            flat = rows_ref[:, group, part].reshape(total, lanes)
            turned = flat.astype(F32).T.astype(BF16)
            dot = functools.partial(
                lax.dot_general,
                turned,
                dimension_numbers=(((1,), (1,)), ((), ())),
                preferred_element_type=F32,
            )
            out_ref[part, group] = (dot(low) + dot(middle)) + dot(high)


def finish(rows, mixing):
    senders, groups, parts, vectors, lanes = rows.shape
    return pl.pallas_call(
        finish_kernel,
        out_shape=jax.ShapeDtypeStruct((parts, groups, lanes, senders * vectors), F32),
        in_specs=[pl.BlockSpec(memory_space=pltpu.VMEM)] * 2,
        out_specs=pl.BlockSpec(memory_space=pltpu.VMEM),
        compiler_params=pltpu.CompilerParams(vmem_limit_bytes=VMEM_BYTES),
    )(rows, mixing)


def swap_cores(value):
    return lax.ppermute(value, "core", [(0, 1), (1, 0)])


def line_blocks(block, count):
    place = lax.axis_index("fc")
    found = []
    down = up = merged = block
    joined = False
    for step in range(1, count):
        from_above = [(j, j - 1) for j in range(1, count) if j + step - 1 < count]
        from_below = [(j, j + 1) for j in range(count - 1) if j >= step - 1]
        low_side = [pair[1] for pair in from_above]
        high_side = [pair[1] for pair in from_below]
        distance = jnp.where(place + step < count, step, -step)
        if joined:
            merged = lax.ppermute(merged, "fc", from_above + from_below)
            found.append((merged, distance, low_side + high_side))
            continue
        down = lax.ppermute(down, "fc", from_above)
        up = lax.ppermute(up, "fc", from_below)
        if set(low_side) & set(high_side):
            found.append((down, step, low_side))
            found.append((up, -step, high_side))
        else:
            merged = jnp.where(place + step < count, down, up)
            joined = True
            found.append((merged, distance, low_side + high_side))
    return found


def gather_chunk(block, x_count, z_count):
    cores, freqs, rows, depth = block.shape
    x_place, z_place = lax.axis_index("x"), lax.axis_index("fc")
    whole = jnp.zeros((x_count, cores, freqs, z_count, rows, depth), block.dtype)

    def put(whole, piece, x_at, z_at):
        return lax.dynamic_update_slice(
            whole, piece[None, :, :, None], (x_at, 0, 0, z_at, 0, 0)
        )

    def across(piece, receivers):
        pairs = []
        for x_index in range(x_count):
            for z_index in receivers:
                pairs.append((x_index * z_count + z_index, (1 - x_index) * z_count + z_index))
        return lax.ppermute(piece, ("x", "fc"), pairs)

    everyone = list(range(z_count))
    mirrored = across(block, everyone)
    found = line_blocks(block, z_count)
    whole = put(whole, block, x_place, z_place)
    whole = put(whole, mirrored, 1 - x_place, z_place)
    for piece, distance, receivers in found:
        opposite = across(piece, receivers)
        z_at = z_place + distance
        if len(receivers) < z_count:
            has = functools.reduce(jnp.logical_or, [z_place == z for z in receivers])
            piece = jnp.where(has, piece, block)
            opposite = jnp.where(has, opposite, mirrored)
            z_at = jnp.where(has, z_at, z_place)
        whole = put(whole, piece, x_place, z_at)
        whole = put(whole, opposite, 1 - x_place, z_at)
    return whole.reshape(x_count * cores * freqs, z_count * rows, depth)


def sum_devices(value, z_count):
    value = value + swap_cores(value)
    value = value + lax.ppermute(value, "x", [(0, 1), (1, 0)])
    if z_count & (z_count - 1):
        return lax.psum(value, "fc")
    parts = [lax.ppermute(value, "fc", [(j, j ^ s) for j in range(z_count)]) for s in range(1, z_count)]
    even = z_count == 1
    if even:
        return value
    place = lax.axis_index("fc")
    stacked = jnp.stack([value] + parts)
    ordered = [lax.dynamic_index_in_dim(stacked, place ^ s, 0, False) for s in range(z_count)]
    return functools.reduce(jnp.add, ordered)


def body_split(x_count, z_count, chunks, beam_transfer, noise_var, spectra, freq_covariance, start_vectors):
    parts, freqs, own, multipoles = beam_transfer.shape
    vectors = start_vectors.shape[3]
    cores = 2
    core = lax.axis_index("core")
    all_freqs = x_count * cores * freqs
    mine = vectors // (x_count * z_count)
    depth = multipoles // (cores * chunks)

    whitened = (beam_transfer.astype(F32) * lax.rsqrt(noise_var)[None, :, :, None]).astype(BF16)
    rows = whitened.transpose(1, 0, 2, 3).reshape(freqs, parts * own, cores, chunks, depth)
    rows = rows.transpose(2, 3, 0, 1, 4)
    kept = lax.dynamic_index_in_dim(rows, core, 0, False)
    given = swap_cores(lax.dynamic_index_in_dim(rows, 1 - core, 0, False))
    beams = []
    for chunk in range(chunks):
        first = jnp.where(core == 0, kept[chunk], given[chunk])
        second = jnp.where(core == 0, given[chunk], kept[chunk])
        beams.append(gather_chunk(jnp.stack([first, second]), x_count, z_count))

    spec = spectra.reshape(-1, cores, chunks, depth).transpose(1, 2, 0, 3)
    spec = lax.dynamic_index_in_dim(spec, core, 0, False)
    cov = freq_covariance.transpose(1, 0, 2).reshape(all_freqs, -1).astype(BF16)

    start = start_vectors.astype(BF16).reshape(parts, freqs, own, x_count * z_count, mine)
    start = start.transpose(3, 1, 0, 4, 2)
    start = lax.all_to_all(start, ("x", "fc"), 0, 0, tiled=True)
    other = swap_cores(start)
    both = jnp.stack([jnp.where(core == 0, start, other), jnp.where(core == 0, other, start)])
    both = both.reshape(cores, x_count, z_count, freqs, parts, mine, own)
    both = both.transpose(1, 0, 3, 4, 5, 2, 6)
    real, imag = both[:, :, :, 0], both[:, :, :, 1]
    top = jnp.stack([real, imag], axis=5)
    bottom = jnp.stack([imag, -real], axis=5)
    operand = jnp.stack([top, bottom], axis=3).reshape(all_freqs, parts * mine, z_count * parts * own)

    partials = [
        apply_covariance([operand], [beams[c]], cov, spec[c : c + 1], own) for c in range(chunks)
    ]
    first_own = functools.reduce(jnp.add, partials)
    first_other = swap_cores(first_own)
    second_own = apply_covariance([first_own, first_other], beams, cov, spec, own)

    def of_core(value, which):
        split = value.reshape(x_count, cores, freqs, *value.shape[1:])
        return lax.dynamic_index_in_dim(split, which, 1, False).reshape(-1, *value.shape[1:])

    first_packed = pack(of_core(first_own, core), of_core(first_other, core), x_count, z_count, own)
    second_other = swap_cores(of_core(second_own, 1 - core))
    second_packed = pack(of_core(second_own, core), second_other, x_count, z_count, own)
    packed = jnp.stack([first_packed, second_packed], axis=2)
    packed = packed.reshape(x_count * z_count, *packed.shape[2:])
    received = lax.all_to_all(packed, ("x", "fc"), 0, 0, tiled=True)
    groups, lanes = received.shape[2], received.shape[4]
    received = received.reshape(-1, ITERS, groups, parts, mine, lanes)

    gram_pair = sum_devices(grams(received), z_count)
    lower = jnp.linalg.cholesky(gram_pair[0])
    eye = jnp.eye(vectors, dtype=F32)
    solve = functools.partial(lax.linalg.triangular_solve, left_side=True, lower=True)
    inverse = solve(lower, eye)
    dot = functools.partial(jnp.dot, precision=HIGH, preferred_element_type=F32)
    gram_second = dot(dot(inverse, gram_pair[1]), inverse.T)
    lower = jnp.linalg.cholesky(gram_second)
    mixing = solve(lower, inverse) * math.sqrt(2.0 * all_freqs * z_count * own)
    basis = finish(received[:, 1], mixing)
    return basis.reshape(parts, freqs, own, vectors)


def row_operands(row_part, spectra):
    scaled = (row_part.astype(F32)[None] * spectra[:, None, None, :]).astype(BF16)
    real_rows = jnp.concatenate([scaled[:, 0], scaled[:, 1]], axis=-1)
    imag_rows = jnp.concatenate([scaled[:, 1], -scaled[:, 0]], axis=-1)
    return jnp.stack([real_rows, imag_rows], axis=1)


def apply_tile(pair_tile, vec_bf):
    row_count = pair_tile.shape[1]
    stacked = pair_tile.reshape(2 * row_count, pair_tile.shape[2])
    with_real = jnp.dot(stacked, vec_bf[0], preferred_element_type=F32)
    with_imag = jnp.dot(stacked, vec_bf[1], preferred_element_type=F32)
    real_part = with_real[:row_count] - with_imag[row_count:]
    imag_part = with_real[row_count:] + with_imag[:row_count]
    return jnp.stack([real_part, imag_part], axis=0)


def partial_gram(image):
    flat = image.reshape(-1, image.shape[-1])
    return jnp.dot(flat.T, flat, precision=HIGH, preferred_element_type=F32)


def orthonormalize(image, gram_matrix):
    lower = jnp.linalg.cholesky(gram_matrix)
    flat = image.reshape(-1, image.shape[-1])
    solved = lax.linalg.triangular_solve(lower, flat, left_side=False, lower=True, transpose_a=True)
    return solved.reshape(image.shape)


def body_general(beam_transfer, noise_var, spectra, freq_covariance, start_vectors):
    row_axes = ("x", "core")
    whitened = (beam_transfer.astype(F32) * lax.rsqrt(noise_var)[None, :, :, None]).astype(BF16)
    row_beams = lax.all_gather(whitened, "fc", axis=2, tiled=True)
    _, freq_rows, mode_count, multipoles = row_beams.shape
    row_total = freq_rows * mode_count
    components = spectra.shape[0]
    vectors_count = start_vectors.shape[3]
    row_operand = row_operands(row_beams.reshape(2, row_total, multipoles), spectra)
    row_start = lax.axis_index(row_axes) * freq_rows
    row_cov = lax.dynamic_slice_in_dim(freq_covariance, row_start, freq_rows, 1)
    piece = lax.all_gather(whitened, row_axes, axis=1, tiled=True)
    _, piece_freqs, piece_modes, _ = piece.shape
    columns = piece.reshape(2, piece_freqs * piece_modes, multipoles)
    col_operand = jnp.concatenate([columns[0], columns[1]], axis=-1)
    products = lax.dot_general(
        row_operand, col_operand, (((3,), (1,)), ((), ())), preferred_element_type=F32
    )
    weight = jnp.broadcast_to(
        row_cov[:, :, None, :, None], (components, freq_rows, mode_count, piece_freqs, piece_modes)
    )
    weight = weight.reshape(components, row_total, piece_freqs * piece_modes)
    pair_tile = jnp.einsum("kxy,kcxy->cxy", weight, products).astype(BF16)
    vectors = start_vectors
    own_modes = start_vectors.shape[2]
    for _ in range(ITERS):
        gathered = lax.all_gather(vectors.astype(BF16), row_axes, axis=1, tiled=True)
        vec_bf = gathered.reshape(2, -1, vectors_count)
        partial_value = apply_tile(pair_tile, vec_bf).reshape(2, freq_rows, mode_count, vectors_count)
        summed = lax.psum(partial_value, "fc")
        gram_matrix = lax.psum(partial_gram(summed), row_axes)
        own_rows = lax.dynamic_slice_in_dim(summed, lax.axis_index("fc") * own_modes, own_modes, 2)
        vectors = orthonormalize(own_rows, gram_matrix)
    return vectors * math.sqrt(2.0 * piece_freqs * mode_count)


def body(x_count, z_count, *args):
    beam_transfer, start_vectors = args[0], args[4]
    parts, freqs, own, multipoles = beam_transfer.shape
    vectors = start_vectors.shape[3]
    lanes = parts * own * z_count
    chunks = multipoles // (2 * 128)
    fits = (
        x_count == 2
        and vectors % (16 * x_count * z_count) == 0
        and lanes == 128
        and own % 16 == 0
        and chunks * 256 == multipoles
        and (freqs * own) % lanes == 0
    )
    if fits:
        return body_split(x_count, z_count, chunks, *args)
    return body_general(*args)


def solution(mesh):
    sizes = dict(mesh.shape)
    x_count = sizes["fr"] // 2
    shape = (sizes["ma"], x_count, 2, sizes["fc"])
    devices = mesh.devices.reshape(shape)
    split = Mesh(devices, ("ma", "x", "core", "fc"))
    rows = ("ma", "x", "core")
    in_specs = (
        P(None, rows, "fc", None),
        P(rows, "fc"),
        P(),
        P(),
        P(None, rows, "fc", None),
    )
    return jax.shard_map(
        functools.partial(body, x_count, sizes["fc"]),
        mesh=split,
        in_specs=in_specs,
        out_specs=P(None, rows, "fc", None),
        check_vma=False,
    )
```

time: 591 us -> 364 us (0.62); the launches traced: 580 us -> 362 us
  waiting for transfers between devices: 251 us -> 75.9 us
  matrix products: 97.6 us -> 1.73 us
  local copies, waits for them, and re-layouts: 132 us -> 54.8 us
  Pallas kernels: 0 us -> 69.3 us
  starting transfers between devices: 0.76 us -> 64.1 us
  blocking collectives: 0 us -> 19.3 us
  between operations: 14.2 us -> 0.84 us
  other arithmetic: 84.2 us -> 76 us
    psum x4 -> x0, waiting for transfers between devices: 234 us -> none  [the longest x2 176 us: body(): summed = lax.psum(partial_value, 'fc')]
    dot_general x7 -> x2, matrix products: 96.3 us -> 0.53 us  [body_split(): gram_second = dot(dot(inverse, gram_pair[1]), inverse.T)]
    pallas_call x0 -> x7, Pallas kernels: none -> 69.3 us  [the longest x3 58.1 us: apply_covariance(): pl.pallas_call(functools.partial(apply_kernel, len(vecs), len(beams), own...]
    ppermute x0 -> x29, waiting for transfers between devices: none -> 67.2 us  [the longest x10 40.8 us: across(): return lax.ppermute(piece, ('x', 'fc'), pairs)]
    ppermute x0 -> x29, starting transfers between devices: none -> 57.3 us  [the longest x10 17.4 us: across(): return lax.ppermute(piece, ('x', 'fc'), pairs)]
    reshape x1 -> x3, local copies, waits for them, and re-layouts: 56.9 us -> 9.95 us  [the longest x2 9.66 us: body_split(): jnp.stack([top, bottom], axis=3)]
    unnamed x17 -> x31, local copies, waits for them, and re-layouts: 38 us -> 5.78 us
    broadcast_in_dim x1 -> x0, local copies, waits for them, and re-layouts: 21.5 us -> none  [body(): jnp.broadcast_to(row_cov[:, :, None, :, None], (components, freq_rows, mo...]
  transfers between devices with their start and end apart: 8 -> 30, of which waited for: 5 -> 13; matrix products, arithmetic and copies ran while one was open for 25% -> 19% of each run, Pallas kernels for 0% -> 1%
where the time goes in v1:
time: 364 us; the launch traced here: 362 us
  other arithmetic  76 us (21%)
  waiting for transfers between devices  75.9 us (21%)
  Pallas kernels  69.3 us (19%)
  starting transfers between devices  64.1 us (18%)
  local copies, waits for them, and re-layouts  54.8 us (15%)
  blocking collectives  19.3 us (5%)
    pallas_call x3, Pallas kernels, apply_covariance(): pl.pallas_call(functools.partial(apply_kernel, len(vecs), len(beams), own...  58.1 us
    ppermute x10, waiting for transfers between devices, across(): return lax.ppermute(piece, ('x', 'fc'), pairs)  40.8 us
    all_to_all x1, blocking collectives, body_split(): received = lax.all_to_all(packed, ('x', 'fc'), 0, 0, tiled=True)  19.3 us
    ppermute x10, starting transfers between devices, across(): return lax.ppermute(piece, ('x', 'fc'), pairs)  17.4 us
    ppermute x4, starting transfers between devices, line_blocks(): down = lax.ppermute(down, 'fc', from_above)  17.4 us
    ppermute x4, starting transfers between devices, line_blocks(): up = lax.ppermute(up, 'fc', from_below)  13.7 us
    broadcast_in_dim x6, other arithmetic, put(): piece[None, :, :, None]  13.2 us
    dynamic_update_slice x19, local copies, waits for them, and re-layouts, put(): lax.dynamic_update_slice(whole, piece[None, :, :, None], (x_at, 0, 0, z_a...  12.6 us
  transfers between devices with their start and end apart: 30, of which 13 were waited for; matrix products, arithmetic and copies ran while one was open for 19% of the time, Pallas kernels for 1%

profile of v1, /device:TPU:0, one launch (start us, length us, event | category | flops | bytes accessed | tf_op | source)
XLA Modules:
  0.0 361.9 jit_solution(11588711659697218706)
XLA Ops:
  0.8 1.5 fusion
  2.7 1.9 dynamic-slice_bitcast_fusion
  5.8 1.7 reshape.122
  7.5 6.8 %all-to-all-start = ((bf16[8,2,8192]{2,1,0:T(2,128)(2,1)}), bf16[8,2,8192]{2,1,0:T(2,128)(2,1)S(1)}, u32[]{:S(2)}, u32[]{:S(2)}) async-start(bf16[8,2,8192]{2,1,0:T(2,128)(2,1)} %reshape.122), calls=%async_computation | async-start | bytes 524288 | tf_op jit(solution)/shard_map/all_to_all | solution.py:299
  16.0 8.7 %all-to-all-done = bf16[8,2,8192]{2,1,0:T(2,128)(2,1)S(1)} async-done(((bf16[8,2,8192]{2,1,0:T(2,128)(2,1)}), bf16[8,2,8192]{2,1,0:T(2,128)(2,1)S(1)}, u32[]{:S(2)}, u32[]{:S(2)}) %all-to-all-start) | async-done | bytes 262176 | tf_op jit(solution)/shard_map/all_to_all | solution.py:299
  26.4 3.9 %broadcast_select_fusion.15 = (bf16[1,32,32,128]{3,0,2,1:T(2,128)(2,1)S(1)}, bf16[1,32,32,128]{3,0,2,1:T(2,128)(2,1)S(1)}, bf16[1,32,32,128]{3,0,2,1:T(2,128)(2,1)S(1)}, bf16[1,32,32,128]{3,0,2,1:T(2,128)(2,1)S(1)}) fusion(pred[]{:T(512)S(6)} %eq.12, bf16[1,2,32,32,128]{4,1,0,3,2:T(2,128)(2,1)} %get-tuple-element.18, bf16[2,32,32,128]{3,0,2,1:T(2,128)(2,1)} %copy-done.8), kind=kLoop, calls=%fused_computation.24 | loop fusion | flops 524288 | bytes 2097153 | tf_op jit(solution)/shard_map/jit(_where)/select_n | solution.py:289
  30.3 2.0 pad_maximum_fusion.1
  32.2 1.3 collective-permute-start.3
  33.5 5.4 %collective-permute-start.5 = (bf16[2,32,32,128]{3,0,2,1:T(2,128)(2,1)}, bf16[2,32,32,128]{3,0,2,1:T(2,128)(2,1)}, u32[]{:S(2)}, u32[]{:S(2)}) collective-permute-start(bf16[2,32,32,128]{3,0,2,1:T(2,128)(2,1)} %pad_maximum_fusion.1), channel_id=1, source_target_pairs={{0,1},{1,2},{2,3},{4,5},{5,6},{6,7},{8,9},{9,10},{10,11},{12,13},{... | collective-permute-start | bytes 1572872 | tf_op jit(solution)/shard_map/ppermute | solution.py:212
  39.5 1.2 fusion.34
  40.7 1.2 pad_maximum_fusion.2
  41.9 13.5 %collective-permute-start.13 = (bf16[2,32,32,128]{3,0,2,1:T(2,128)(2,1)S(1)}, bf16[2,32,32,128]{3,0,2,1:T(2,128)(2,1)}, u32[]{:S(2)}, u32[]{:S(2)}) collective-permute-start(bf16[2,32,32,128]{3,0,2,1:T(2,128)(2,1)S(1)} %pad_maximum_fusion.2), channel_id=1, source_target_pairs={{1,0},{2,1},{3,2},{5,4},{6,5},{7,6},{9,8},{10,9},{11,10},{13,12},{... | collective-permute-start | bytes 1572872 | tf_op jit(solution)/shard_map/ppermute | solution.py:211
  56.6 1.2 fusion.35
  57.8 3.1 broadcast.40.clone
  61.8 5.4 %collective-permute-start.15 = (bf16[2,32,32,128]{3,0,2,1:T(2,128)(2,1)S(1)}, bf16[2,32,32,128]{3,0,2,1:T(2,128)(2,1)}, u32[]{:S(2)}, u32[]{:S(2)}) collective-permute-start(bf16[2,32,32,128]{3,0,2,1:T(2,128)(2,1)S(1)} %pad_maximum_fusion.2), channel_id=1, source_target_pairs={{0,1},{1,2},{2,3},{4,5},{5,6},{6,7},{8,9},{9,10},{10,11},{12,13},{... | collective-permute-start | bytes 1572872 | tf_op jit(solution)/shard_map/ppermute | solution.py:212
  69.0 1.3 collective-permute-start.7
  70.3 1.5 collective-permute-start.8
  72.6 1.3 collective-permute-start.17
  73.9 3.2 collective-permute-done.15
  77.0 1.5 collective-permute-start.18
  79.5 8.9 %copy.123 = bf16[2,2,32,2,16,4,2,16]{2,1,0,7,6,5,4,3:T(2,128)(2,1)} copy(bf16[2,2,32,2,16,4,2,16]{2,7,6,5,4,1,0,3:T(8,128)(2,1)S(1)} %pad_maximum_fusion) | data formatting | bytes 2097152 | tf_op jit(solution)/shard_map/stack | solution.py:307
  88.4 8.0 %reshape.102 = bf16[128,32,128]{0,2,1:T(8,128)(2,1)S(1)} reshape(bf16[2,2,32,2,16,4,2,16]{2,1,0,7,6,5,4,3:T(2,128)(2,1)} %copy.123) | data formatting | bytes 2097152 | tf_op jit(solution)/shard_map/reshape | solution.py:307
  96.4 1.7 copy.139.refs_0_
  98.1 1.5 collective-permute-start.12
  100.7 1.3 collective-permute-start.10
  102.0 2.0 copy_dynamic-update-slice_fusion.18
  104.0 1.1 broadcast_select_fusion.4
  105.1 1.7 collective-permute-start.20
  106.8 3.7 %collective-permute-done.12 = bf16[2,32,32,128]{3,0,2,1:T(2,128)(2,1)S(1)} collective-permute-done((bf16[2,32,32,128]{3,0,2,1:T(2,128)(2,1)}, bf16[2,32,32,128]{3,0,2,1:T(2,128)(2,1)S(1)}, u32[]{:S(2)}, u32[]{:S(2)}) %collective-permute-start.12) | collective-permute-done | bytes 524320 | tf_op jit(solution)/shard_map/ppermute | solution.py:238
  111.5 3.7 %collective-permute-start.4 = (bf16[2,32,32,128]{3,0,2,1:T(2,128)(2,1)}, bf16[2,32,32,128]{3,0,2,1:T(2,128)(2,1)S(1)}, u32[]{:S(2)}, u32[]{:S(2)}) collective-permute-start(bf16[2,32,32,128]{3,0,2,1:T(2,128)(2,1)} %collective-permute-done.3), channel_id=1, source_target_pairs={{0,8},{1,9},{2,10},{8,0},{9,1},{10,2},{4,12},{5,13},{6,14},{12,4},... | collective-permute-start | bytes 1572872 | tf_op jit(solution)/shard_map/ppermute | solution.py:238
  115.9 2.4 collective-permute-start.14
  118.3 2.0 collective-permute-done.10
  121.0 3.6 fusion.9
  124.6 4.1 %collective-permute-done.20 = bf16[2,32,32,128]{3,0,2,1:T(2,128)(2,1)S(1)} collective-permute-done((bf16[2,32,32,128]{3,0,2,1:T(2,128)(2,1)S(1)}, bf16[2,32,32,128]{3,0,2,1:T(2,128)(2,1)S(1)}, u32[]{:S(2)}, u32[]{:S(2)}) %collective-permute-start.20) | collective-permute-done | bytes 524320 | tf_op jit(solution)/shard_map/ppermute | solution.py:208
  128.6 2.4 collective-permute-start.11
  131.0 3.6 fusion.11
  135.7 1.6 collective-permute-start.9
  137.7 13.5 %collective-permute-done.11 = bf16[2,32,32,128]{3,0,2,1:T(2,128)(2,1)S(1)} collective-permute-done((bf16[2,32,32,128]{3,0,2,1:T(2,128)(2,1)S(1)}, bf16[2,32,32,128]{3,0,2,1:T(2,128)(2,1)S(1)}, u32[]{:S(2)}, u32[]{:S(2)}) %collective-permute-start.11) | collective-permute-done | bytes 524320 | tf_op jit(solution)/shard_map/ppermute | solution.py:238
  151.2 3.4 collective-permute-start.21
  154.6 2.4 fusion.10
  157.6 4.8 %collective-permute-done.9 = bf16[2,32,32,128]{3,0,2,1:T(2,128)(2,1)S(1)} collective-permute-done((bf16[2,32,32,128]{3,0,2,1:T(2,128)(2,1)S(1)}, bf16[2,32,32,128]{3,0,2,1:T(2,128)(2,1)S(1)}, u32[]{:S(2)}, u32[]{:S(2)}) %collective-permute-start.9) | collective-permute-done | bytes 524320 | tf_op jit(solution)/shard_map/ppermute | solution.py:238
  162.6 18.8 %collective-permute-done.21 = bf16[2,32,32,128]{3,0,2,1:T(2,128)(2,1)S(1)} collective-permute-done((bf16[2,32,32,128]{3,0,2,1:T(2,128)(2,1)S(1)}, bf16[2,32,32,128]{3,0,2,1:T(2,128)(2,1)S(1)}, u32[]{:S(2)}, u32[]{:S(2)}) %collective-permute-start.21) | collective-permute-done | bytes 524320 | tf_op jit(solution)/shard_map/ppermute | solution.py:238
  181.4 1.4 fusion.12
  189.6 16.0 %shard_map.56 = f32[128,32,128]{2,1,0:T(8,128)} custom-call(bf16[128,32,128]{2,1,0:T(8,128)(2,1)} %copy.139.refs_0_, bf16[128,128,128]{2,1,0:T(8,128)(2,1)} %bitcast.42.refs_1_.refs_3_, bf16[128,256]{1,0:T(8,128)(2,1)} %copy_bitcast_fusion.2.refs_2_.refs_4_, f32[1,2,128]{2,1,0:T(2,128)} %get-tuple-element.35.refs_3_), custom_call_target="tpu_custom_call" | custom-call | flops 536870912 | bytes 4194304 | tf_op jit(solution)/shard_map/pallas_call | solution.py:85
  205.6 14.7 %shard_map.55 = f32[128,32,128]{2,1,0:T(8,128)} custom-call(bf16[128,32,128]{2,1,0:T(8,128)(2,1)} %copy.139.refs_0_, bf16[128,128,128]{2,1,0:T(8,128)(2,1)} %bitcast.159, bf16[128,256]{1,0:T(8,128)(2,1)} %copy_bitcast_fusion.2.refs_2_.refs_4_, f32[1,2,128]{2,1,0:T(2,128)} %get-tuple-element.36.refs_3_), custom_call_target="tpu_custom_call" | custom-call | flops 536870912 | bytes 4194304 | tf_op jit(solution)/shard_map/pallas_call | solution.py:85
  220.3 2.1 add.151.refs_0_
  222.5 4.1 %collective-permute-done.22.refs_1_ = f32[128,32,128]{2,1,0:T(8,128)S(1)} collective-permute-done((f32[128,32,128]{2,1,0:T(8,128)S(1)}, f32[128,32,128]{2,1,0:T(8,128)S(1)}, u32[]{:S(2)}, u32[]{:S(2)}) %collective-permute-start.22) | collective-permute-done | bytes 2097184 | tf_op jit(solution)/shard_map/ppermute | solution.py:193
  226.6 1.3 copy-done.6
  227.9 27.3 %shard_map.58 = f32[128,32,128]{2,1,0:T(8,128)} custom-call(f32[128,32,128]{2,1,0:T(8,128)} %copy-done.3, f32[128,32,128]{2,1,0:T(8,128)} %copy-done.6, bf16[128,128,128]{2,1,0:T(8,128)(2,1)} %bitcast.160, bf16[128,128,128]{2,1,0:T(8,128)(2,1)} %bitcast.42.refs_1_.refs_3_, bf16[128,256]{1,0:T(8,128)(2,1)} %copy_bitcast_fusion.2.refs_2_.refs_4_, ...), custom_call_target="tpu_custom_call" | custom-call | flops 1073741824 | bytes 8388608 | tf_op jit(solution)/shard_map/pallas_call | solution.py:85
  255.3 2.9 constant_dynamic-slice_fusion
  260.4 3.3 shard_map.57
  264.7 3.3 shard_map.59
  269.1 19.3 %all_to_all.10 = bf16[8,2,4,32,128]{4,3,2,1,0:T(8,128)(2,1)} all-to-all(bf16[8,2,4,32,128]{4,3,2,1,0:T(8,128)(2,1)S(1)} %pad_maximum_fusion.3), channel_id=1, replica_groups=mesh['ma'=2,'x'=2,'core'=2,'fc'=4] {'x','fc'}, dimensions={0} | all-to-all | bytes 1048576 | tf_op jit(solution)/shard_map/all_to_all | solution.py:325
  288.4 2.2 shard_map.60
  291.7 1.3 collective-permute-done.24
  294.7 3.9 %collective-permute-done.25 = f32[2,128,128]{1,2,0:T(8,128)S(1)} collective-permute-done((f32[2,128,128]{1,2,0:T(8,128)S(1)}, f32[2,128,128]{1,2,0:T(8,128)S(1)}, u32[]{:S(2)}, u32[]{:S(2)}) %collective-permute-start.25) | collective-permute-done | bytes 131104 | tf_op jit(solution)/shard_map/ppermute | solution.py:260
  298.8 4.3 %collective-permute-start.28 = (f32[2,128,128]{1,2,0:T(8,128)S(1)}, f32[2,128,128]{1,2,0:T(8,128)S(1)}, u32[]{:S(2)}, u32[]{:S(2)}) collective-permute-start(f32[2,128,128]{1,2,0:T(8,128)S(1)} %add.153), channel_id=1, source_target_pairs={{0,3},{1,2},{2,1},{3,0},{4,7},{5,6},{6,5},{7,4},{8,11},{9,10},{10,... | collective-permute-start | bytes 393224 | tf_op jit(solution)/shard_map/ppermute | solution.py:263
  303.8 1.6 collective-permute-done.26
  305.4 6.1 %collective-permute-done.27 = f32[2,128,128]{1,2,0:T(8,128)S(1)} collective-permute-done((f32[2,128,128]{1,2,0:T(8,128)S(1)}, f32[2,128,128]{1,2,0:T(8,128)S(1)}, u32[]{:S(2)}, u32[]{:S(2)}) %collective-permute-start.27) | collective-permute-done | bytes 131104 | tf_op jit(solution)/shard_map/ppermute | solution.py:263
  311.7 11.7 %cholesky.44 = f32[128,128]{1,0:T(8,128)S(1)} custom-call(f32[128,128]{1,0:T(8,128)S(1)} %fusion.16), custom_call_target="Cholesky" | custom-call | tf_op jit(solution)/shard_map/jit(cholesky)/cholesky | solution.py:330
  324.8 9.8 %custom-call.6 = f32[1,128,128]{1,2,0:T(8,128)S(1)} custom-call(f32[1,128,128]{2,1,0:T(8,128)S(1)} %fusion.13), custom_call_target="InvertDiagBlocksLowerTriangular" | custom-call | tf_op jit(solution)/shard_map/triangular_solve/custom-call.0 | solution.py:333
  335.5 11.7 %cholesky.55 = f32[128,128]{1,0:T(8,128)S(1)} custom-call(f32[128,128]{1,0:T(8,128)S(1)} %fusion.18), custom_call_target="Cholesky" | custom-call | tf_op jit(solution)/shard_map/jit(cholesky)/cholesky | solution.py:336
  348.6 9.8 %custom-call.7 = f32[1,128,128]{1,2,0:T(8,128)S(1)} custom-call(f32[1,128,128]{2,1,0:T(8,128)S(1)} %fusion.14), custom_call_target="InvertDiagBlocksLowerTriangular" | custom-call | tf_op jit(solution)/shard_map/triangular_solve/custom-call.0 | solution.py:337
  359.3 2.4 shard_map.61
  (119 shorter events, 37.1 us)
Async XLA Ops:
  0.8 4.3 %copy-start.10 = (f32[2,32,16,128]{3,2,1,0:T(8,128)S(1)}, f32[2,32,16,128]{3,2,1,0:T(8,128)}, u32[]{:S(2)}) copy-start(f32[2,32,16,128]{3,2,1,0:T(8,128)} %param.12) | copy-start | bytes 1572868
  2.7 11.6 %copy-start.13 = (f32[2,512]{1,0:T(2,128)S(1)}, f32[2,512]{1,0:T(2,128)}, u32[]{:S(2)}) copy-start(f32[2,512]{1,0:T(2,128)} %param.10) | copy-start | bytes 12292
  2.7 12.7 %copy-start.12 = (f32[2,128,128]{2,1,0:T(8,128)S(1)}, f32[2,128,128]{2,1,0:T(8,128)}, u32[]{:S(2)}) copy-start(f32[2,128,128]{2,1,0:T(8,128)} %param.11) | copy-start | bytes 393220
  4.6 21.0 %collective-permute-start.1 = (bf16[2,32,32,128]{3,0,2,1:T(2,128)(2,1)}, bf16[2,32,32,128]{3,0,2,1:T(2,128)(2,1)S(1)}, u32[]{:S(2)}, u32[]{:S(2)}) collective-permute-start(bf16[2,32,32,128]{3,0,2,1:T(2,128)(2,1)} %get-tuple-element.17), channel_id=1, source_target_pairs={{0,4},{4,0},{1,5},{5,1},{2,6},{6,2},{3,7},{7,3},{8,12},{12,8},{9,1... | collective-permute-start | bytes 1572872 | tf_op jit(solution)/shard_map/ppermute | solution.py:193
  7.5 17.2 %all-to-all-start = ((bf16[8,2,8192]{2,1,0:T(2,128)(2,1)}), bf16[8,2,8192]{2,1,0:T(2,128)(2,1)S(1)}, u32[]{:S(2)}, u32[]{:S(2)}) async-start(bf16[8,2,8192]{2,1,0:T(2,128)(2,1)} %reshape.122), calls=%async_computation | async-start | bytes 524288 | tf_op jit(solution)/shard_map/all_to_all | solution.py:299
  25.5 36.3 %collective-permute-start = (bf16[8,32,2,16,16]{1,4,3,2,0:T(8,128)(2,1)S(1)}, bf16[8,32,2,16,16]{1,4,3,2,0:T(8,128)(2,1)S(1)}, u32[]{:S(2)}, u32[]{:S(2)}) collective-permute-start(bf16[8,32,2,16,16]{1,4,3,2,0:T(8,128)(2,1)S(1)} %copy.119), channel_id=1, source_target_pairs={{0,4},{4,0},{1,5},{5,1},{2,6},{6,2},{3,7},{7,3},{8,12},{12,8},{9,1... | collective-permute-start | bytes 786440 | tf_op jit(solution)/shard_map/ppermute | solution.py:193
  25.6 0.8 copy-start.8
  32.2 36.7 %collective-permute-start.3 = (bf16[2,32,32,128]{3,0,2,1:T(2,128)(2,1)}, bf16[2,32,32,128]{3,0,2,1:T(2,128)(2,1)}, u32[]{:S(2)}, u32[]{:S(2)}) collective-permute-start(bf16[2,32,32,128]{3,0,2,1:T(2,128)(2,1)} %pad_maximum_fusion.1), channel_id=1, source_target_pairs={{1,0},{2,1},{3,2},{5,4},{6,5},{7,6},{9,8},{10,9},{11,10},{13,12},{... | collective-permute-start | bytes 1572872 | tf_op jit(solution)/shard_map/ppermute | solution.py:211
  33.5 36.8 %collective-permute-start.5 = (bf16[2,32,32,128]{3,0,2,1:T(2,128)(2,1)}, bf16[2,32,32,128]{3,0,2,1:T(2,128)(2,1)}, u32[]{:S(2)}, u32[]{:S(2)}) collective-permute-start(bf16[2,32,32,128]{3,0,2,1:T(2,128)(2,1)} %pad_maximum_fusion.1), channel_id=1, source_target_pairs={{0,1},{1,2},{2,3},{4,5},{5,6},{6,7},{8,9},{9,10},{10,11},{12,13},{... | collective-permute-start | bytes 1572872 | tf_op jit(solution)/shard_map/ppermute | solution.py:212
  38.9 63.1 %collective-permute-start.2 = (bf16[2,32,32,128]{3,0,2,1:T(2,128)(2,1)}, bf16[2,32,32,128]{3,0,2,1:T(2,128)(2,1)}, u32[]{:S(2)}, u32[]{:S(2)}) collective-permute-start(bf16[2,32,32,128]{3,0,2,1:T(2,128)(2,1)} %pad_maximum_fusion.1), channel_id=1, source_target_pairs={{0,8},{1,9},{2,10},{3,11},{8,0},{9,1},{10,2},{11,3},{4,12},{5,13},... | collective-permute-start | bytes 1572872 | tf_op jit(solution)/shard_map/ppermute | solution.py:238
  41.9 19.9 %copy-start.11 = (bf16[2,32,32,128]{3,0,2,1:T(2,128)(2,1)}, bf16[2,32,32,128]{3,0,2,1:T(2,128)(2,1)S(1)}, u32[]{:S(2)}) copy-start(bf16[2,32,32,128]{3,0,2,1:T(2,128)(2,1)S(1)} %pad_maximum_fusion.2) | copy-start | bytes 1572868
  41.9 30.7 %collective-permute-start.13 = (bf16[2,32,32,128]{3,0,2,1:T(2,128)(2,1)S(1)}, bf16[2,32,32,128]{3,0,2,1:T(2,128)(2,1)}, u32[]{:S(2)}, u32[]{:S(2)}) collective-permute-start(bf16[2,32,32,128]{3,0,2,1:T(2,128)(2,1)S(1)} %pad_maximum_fusion.2), channel_id=1, source_target_pairs={{1,0},{2,1},{3,2},{5,4},{6,5},{7,6},{9,8},{10,9},{11,10},{13,12},{... | collective-permute-start | bytes 1572872 | tf_op jit(solution)/shard_map/ppermute | solution.py:211
  56.6 10.8 %copy-start = (bf16[2,2,32,4,32,128]{5,4,3,2,1,0:T(8,128)(2,1)}, bf16[2,2,32,4,32,128]{5,4,3,2,1,0:T(8,128)(2,1)S(1)}, u32[]{:S(2)}) copy-start(bf16[2,2,32,4,32,128]{5,4,3,2,1,0:T(8,128)(2,1)S(1)} %copy_dynamic-update-slice_fusion.19) | copy-start | bytes 12582916
  61.8 15.3 %collective-permute-start.15 = (bf16[2,32,32,128]{3,0,2,1:T(2,128)(2,1)S(1)}, bf16[2,32,32,128]{3,0,2,1:T(2,128)(2,1)}, u32[]{:S(2)}, u32[]{:S(2)}) collective-permute-start(bf16[2,32,32,128]{3,0,2,1:T(2,128)(2,1)S(1)} %pad_maximum_fusion.2), channel_id=1, source_target_pairs={{0,1},{1,2},{2,3},{4,5},{5,6},{6,7},{8,9},{9,10},{10,11},{12,13},{... | collective-permute-start | bytes 1572872 | tf_op jit(solution)/shard_map/ppermute | solution.py:212
  69.0 29.1 %collective-permute-start.7 = (bf16[2,32,32,128]{3,0,2,1:T(2,128)(2,1)}, bf16[2,32,32,128]{3,0,2,1:T(2,128)(2,1)}, u32[]{:S(2)}, u32[]{:S(2)}) collective-permute-start(bf16[2,32,32,128]{3,0,2,1:T(2,128)(2,1)} %collective-permute-done.3), channel_id=1, source_target_pairs={{1,0},{2,1},{5,4},{6,5},{9,8},{10,9},{13,12},{14,13},{17,16},{18,1... | collective-permute-start | bytes 1572872 | tf_op jit(solution)/shard_map/ppermute | solution.py:211
  70.3 29.3 %collective-permute-start.8 = (bf16[2,32,32,128]{3,0,2,1:T(2,128)(2,1)}, bf16[2,32,32,128]{3,0,2,1:T(2,128)(2,1)}, u32[]{:S(2)}, u32[]{:S(2)}) collective-permute-start(bf16[2,32,32,128]{3,0,2,1:T(2,128)(2,1)} %collective-permute-done.5), channel_id=1, source_target_pairs={{1,2},{2,3},{5,6},{6,7},{9,10},{10,11},{13,14},{14,15},{17,18},{18... | collective-permute-start | bytes 1572872 | tf_op jit(solution)/shard_map/ppermute | solution.py:212
  72.6 31.4 %collective-permute-start.17 = (bf16[2,32,32,128]{3,0,2,1:T(2,128)(2,1)}, bf16[2,32,32,128]{3,0,2,1:T(2,128)(2,1)}, u32[]{:S(2)}, u32[]{:S(2)}) collective-permute-start(bf16[2,32,32,128]{3,0,2,1:T(2,128)(2,1)} %collective-permute-done.13), channel_id=1, source_target_pairs={{1,0},{2,1},{5,4},{6,5},{9,8},{10,9},{13,12},{14,13},{17,16},{18,1... | collective-permute-start | bytes 1572872 | tf_op jit(solution)/shard_map/ppermute | solution.py:211
  77.0 27.0 %collective-permute-start.18 = (bf16[2,32,32,128]{3,0,2,1:T(2,128)(2,1)}, bf16[2,32,32,128]{3,0,2,1:T(2,128)(2,1)}, u32[]{:S(2)}, u32[]{:S(2)}) collective-permute-start(bf16[2,32,32,128]{3,0,2,1:T(2,128)(2,1)} %collective-permute-done.15), channel_id=1, source_target_pairs={{1,2},{2,3},{5,6},{6,7},{9,10},{10,11},{13,14},{14,15},{17,18},{18... | collective-permute-start | bytes 1572872 | tf_op jit(solution)/shard_map/ppermute | solution.py:212
  98.1 12.5 %collective-permute-start.12 = (bf16[2,32,32,128]{3,0,2,1:T(2,128)(2,1)}, bf16[2,32,32,128]{3,0,2,1:T(2,128)(2,1)S(1)}, u32[]{:S(2)}, u32[]{:S(2)}) collective-permute-start(bf16[2,32,32,128]{3,0,2,1:T(2,128)(2,1)} %copy-done.11), channel_id=1, source_target_pairs={{0,8},{1,9},{2,10},{3,11},{8,0},{9,1},{10,2},{11,3},{4,12},{5,13},... | collective-permute-start | bytes 1572872 | tf_op jit(solution)/shard_map/ppermute | solution.py:238
  100.7 19.6 %collective-permute-start.10 = (bf16[2,32,32,128]{3,0,2,1:T(2,128)(2,1)S(1)}, bf16[2,32,32,128]{3,0,2,1:T(2,128)(2,1)S(1)}, u32[]{:S(2)}, u32[]{:S(2)}) collective-permute-start(bf16[2,32,32,128]{3,0,2,1:T(2,128)(2,1)S(1)} %bitcast.177), channel_id=1, source_target_pairs={{1,0},{2,3},{5,4},{6,7},{9,8},{10,11},{13,12},{14,15},{17,16},{18,... | collective-permute-start | bytes 1572872 | tf_op jit(solution)/shard_map/ppermute | solution.py:208
  105.1 23.5 %collective-permute-start.20 = (bf16[2,32,32,128]{3,0,2,1:T(2,128)(2,1)S(1)}, bf16[2,32,32,128]{3,0,2,1:T(2,128)(2,1)S(1)}, u32[]{:S(2)}, u32[]{:S(2)}) collective-permute-start(bf16[2,32,32,128]{3,0,2,1:T(2,128)(2,1)S(1)} %bitcast.174), channel_id=1, source_target_pairs={{1,0},{2,3},{5,4},{6,7},{9,8},{10,11},{13,12},{14,15},{17,16},{18,... | collective-permute-start | bytes 1572872 | tf_op jit(solution)/shard_map/ppermute | solution.py:208
  111.5 23.1 %copy-start.1 = (bf16[2,2,32,4,32,128]{5,4,3,2,1,0:T(8,128)(2,1)S(1)}, bf16[2,2,32,4,32,128]{5,4,3,2,1,0:T(8,128)(2,1)}, u32[]{:S(2)}) copy-start(bf16[2,2,32,4,32,128]{5,4,3,2,1,0:T(8,128)(2,1)} %copy_dynamic-update-slice_fusion.18) | copy-start | bytes 12582916
  111.5 24.2 %collective-permute-start.4 = (bf16[2,32,32,128]{3,0,2,1:T(2,128)(2,1)}, bf16[2,32,32,128]{3,0,2,1:T(2,128)(2,1)S(1)}, u32[]{:S(2)}, u32[]{:S(2)}) collective-permute-start(bf16[2,32,32,128]{3,0,2,1:T(2,128)(2,1)} %collective-permute-done.3), channel_id=1, source_target_pairs={{0,8},{1,9},{2,10},{8,0},{9,1},{10,2},{4,12},{5,13},{6,14},{12,4},... | collective-permute-start | bytes 1572872 | tf_op jit(solution)/shard_map/ppermute | solution.py:238
  115.2 22.1 %collective-permute-start.6 = (bf16[2,32,32,128]{3,0,2,1:T(2,128)(2,1)}, bf16[2,32,32,128]{3,0,2,1:T(2,128)(2,1)S(1)}, u32[]{:S(2)}, u32[]{:S(2)}) collective-permute-start(bf16[2,32,32,128]{3,0,2,1:T(2,128)(2,1)} %collective-permute-done.5), channel_id=1, source_target_pairs={{1,9},{2,10},{3,11},{9,1},{10,2},{11,3},{5,13},{6,14},{7,15},{13,5... | collective-permute-start | bytes 1572872 | tf_op jit(solution)/shard_map/ppermute | solution.py:238
  115.9 46.7 %collective-permute-start.14 = (bf16[2,32,32,128]{3,0,2,1:T(2,128)(2,1)}, bf16[2,32,32,128]{3,0,2,1:T(2,128)(2,1)S(1)}, u32[]{:S(2)}, u32[]{:S(2)}) collective-permute-start(bf16[2,32,32,128]{3,0,2,1:T(2,128)(2,1)} %collective-permute-done.13), channel_id=1, source_target_pairs={{0,8},{1,9},{2,10},{8,0},{9,1},{10,2},{4,12},{5,13},{6,14},{12,4},... | collective-permute-start | bytes 1572872 | tf_op jit(solution)/shard_map/ppermute | solution.py:238
  120.3 42.3 %collective-permute-start.16 = (bf16[2,32,32,128]{3,0,2,1:T(2,128)(2,1)}, bf16[2,32,32,128]{3,0,2,1:T(2,128)(2,1)S(1)}, u32[]{:S(2)}, u32[]{:S(2)}) collective-permute-start(bf16[2,32,32,128]{3,0,2,1:T(2,128)(2,1)} %collective-permute-done.15), channel_id=1, source_target_pairs={{1,9},{2,10},{3,11},{9,1},{10,2},{11,3},{5,13},{6,14},{7,15},{13,5... | collective-permute-start | bytes 1572872 | tf_op jit(solution)/shard_map/ppermute | solution.py:238
  128.6 22.5 %collective-permute-start.11 = (bf16[2,32,32,128]{3,0,2,1:T(2,128)(2,1)S(1)}, bf16[2,32,32,128]{3,0,2,1:T(2,128)(2,1)S(1)}, u32[]{:S(2)}, u32[]{:S(2)}) collective-permute-start(bf16[2,32,32,128]{3,0,2,1:T(2,128)(2,1)S(1)} %collective-permute-done.10), channel_id=1, source_target_pairs={{0,8},{3,11},{8,0},{11,3},{4,12},{7,15},{12,4},{15,7},{16,24},{19,... | collective-permute-start | bytes 1572872 | tf_op jit(solution)/shard_map/ppermute | solution.py:238
  135.7 26.7 %collective-permute-start.9 = (bf16[2,32,32,128]{3,0,2,1:T(2,128)(2,1)S(1)}, bf16[2,32,32,128]{3,0,2,1:T(2,128)(2,1)S(1)}, u32[]{:S(2)}, u32[]{:S(2)}) collective-permute-start(bf16[2,32,32,128]{3,0,2,1:T(2,128)(2,1)S(1)} %bitcast.178), channel_id=1, source_target_pairs={{0,8},{1,9},{2,10},{3,11},{8,0},{9,1},{10,2},{11,3},{4,12},{5,13},... | collective-permute-start | bytes 1572872 | tf_op jit(solution)/shard_map/ppermute | solution.py:238
  137.3 49.2 %collective-permute-start.19 = (bf16[2,32,32,128]{3,0,2,1:T(2,128)(2,1)S(1)}, bf16[2,32,32,128]{3,0,2,1:T(2,128)(2,1)S(1)}, u32[]{:S(2)}, u32[]{:S(2)}) collective-permute-start(bf16[2,32,32,128]{3,0,2,1:T(2,128)(2,1)S(1)} %bitcast.175), channel_id=1, source_target_pairs={{0,8},{1,9},{2,10},{3,11},{8,0},{9,1},{10,2},{11,3},{4,12},{5,13},... | collective-permute-start | bytes 1572872 | tf_op jit(solution)/shard_map/ppermute | solution.py:238
  151.2 30.2 %collective-permute-start.21 = (bf16[2,32,32,128]{3,0,2,1:T(2,128)(2,1)S(1)}, bf16[2,32,32,128]{3,0,2,1:T(2,128)(2,1)S(1)}, u32[]{:S(2)}, u32[]{:S(2)}) collective-permute-start(bf16[2,32,32,128]{3,0,2,1:T(2,128)(2,1)S(1)} %collective-permute-done.20), channel_id=1, source_target_pairs={{0,8},{3,11},{8,0},{11,3},{4,12},{7,15},{12,4},{15,7},{16,24},{19,... | collective-permute-start | bytes 1572872 | tf_op jit(solution)/shard_map/ppermute | solution.py:238
  189.5 16.0 %copy-start.2 = (bf16[2,2,32,4,32,128]{5,4,3,2,1,0:T(8,128)(2,1)}, bf16[2,2,32,4,32,128]{5,4,3,2,1,0:T(8,128)(2,1)S(1)}, u32[]{:S(2)}) copy-start(bf16[2,2,32,4,32,128]{5,4,3,2,1,0:T(8,128)(2,1)S(1)} %copy_dynamic-update-slice_fusion.10) | copy-start | bytes 12582916
  205.6 14.7 %copy-start.5 = (f32[128,32,128]{2,1,0:T(8,128)S(1)}, f32[128,32,128]{2,1,0:T(8,128)}, u32[]{:S(2)}) copy-start(f32[128,32,128]{2,1,0:T(8,128)} %shard_map.56) | copy-start | bytes 6291460
  222.4 4.2 %copy-start.3 = (f32[128,32,128]{2,1,0:T(8,128)}, f32[128,32,128]{2,1,0:T(8,128)S(1)}, u32[]{:S(2)}) copy-start(f32[128,32,128]{2,1,0:T(8,128)S(1)} %add.151.refs_0_) | copy-start | bytes 6291460
  222.4 4.2 %collective-permute-start.22 = (f32[128,32,128]{2,1,0:T(8,128)S(1)}, f32[128,32,128]{2,1,0:T(8,128)S(1)}, u32[]{:S(2)}, u32[]{:S(2)}) collective-permute-start(f32[128,32,128]{2,1,0:T(8,128)S(1)} %add.151.refs_0_), channel_id=1, source_target_pairs={{0,4},{4,0},{1,5},{5,1},{2,6},{6,2},{3,7},{7,3},{8,12},{12,8},{9,1... | collective-permute-start | bytes 6291464 | tf_op jit(solution)/shard_map/ppermute | solution.py:193
  226.6 1.3 copy-start.6
  255.3 3.0 copy-start.4
  255.3 4.1 %copy-start.7 = (f32[128,32,128]{2,1,0:T(8,128)S(1)}, f32[128,32,128]{2,1,0:T(8,128)}, u32[]{:S(2)}) copy-start(f32[128,32,128]{2,1,0:T(8,128)} %copy-done.6) | copy-start | bytes 6291460
  258.1 5.5 %collective-permute-start.23 = (f32[64,32,128]{2,1,0:T(8,128)S(1)}, f32[64,32,128]{2,1,0:T(8,128)S(1)}, u32[]{:S(2)}, u32[]{:S(2)}) collective-permute-start(f32[64,32,128]{2,1,0:T(8,128)S(1)} %bitcast.182), channel_id=1, source_target_pairs={{0,4},{4,0},{1,5},{5,1},{2,6},{6,2},{3,7},{7,3},{8,12},{12,8},{9,1... | collective-permute-start | bytes 3145736 | tf_op jit(solution)/shard_map/ppermute | solution.py:193
  263.7 1.0 copy-start.9
  291.6 1.4 collective-permute-start.24
  293.0 5.6 %collective-permute-start.25 = (f32[2,128,128]{1,2,0:T(8,128)S(1)}, f32[2,128,128]{1,2,0:T(8,128)S(1)}, u32[]{:S(2)}, u32[]{:S(2)}) collective-permute-start(f32[2,128,128]{1,2,0:T(8,128)S(1)} %add.152), channel_id=1, source_target_pairs={{0,8},{8,0},{1,9},{9,1},{2,10},{10,2},{3,11},{11,3},{4,12},{12,4},... | collective-permute-start | bytes 393224 | tf_op jit(solution)/shard_map/ppermute | solution.py:260
  298.6 6.8 %collective-permute-start.26 = (f32[2,128,128]{1,2,0:T(8,128)S(1)}, f32[2,128,128]{1,2,0:T(8,128)S(1)}, u32[]{:S(2)}, u32[]{:S(2)}) collective-permute-start(f32[2,128,128]{1,2,0:T(8,128)S(1)} %add.153), channel_id=1, source_target_pairs={{0,1},{1,0},{2,3},{3,2},{4,5},{5,4},{6,7},{7,6},{8,9},{9,8},{10,11... | collective-permute-start | bytes 393224 | tf_op jit(solution)/shard_map/ppermute | solution.py:263
  298.7 12.8 %collective-permute-start.27 = (f32[2,128,128]{1,2,0:T(8,128)S(1)}, f32[2,128,128]{1,2,0:T(8,128)S(1)}, u32[]{:S(2)}, u32[]{:S(2)}) collective-permute-start(f32[2,128,128]{1,2,0:T(8,128)S(1)} %add.153), channel_id=1, source_target_pairs={{0,2},{1,3},{2,0},{3,1},{4,6},{5,7},{6,4},{7,5},{8,10},{9,11},{10,... | collective-permute-start | bytes 393224 | tf_op jit(solution)/shard_map/ppermute | solution.py:263
  298.8 12.7 %collective-permute-start.28 = (f32[2,128,128]{1,2,0:T(8,128)S(1)}, f32[2,128,128]{1,2,0:T(8,128)S(1)}, u32[]{:S(2)}, u32[]{:S(2)}) collective-permute-start(f32[2,128,128]{1,2,0:T(8,128)S(1)} %add.153), channel_id=1, source_target_pairs={{0,3},{1,2},{2,1},{3,0},{4,7},{5,6},{6,5},{7,4},{8,11},{9,10},{10,... | collective-permute-start | bytes 393224 | tf_op jit(solution)/shard_map/ppermute | solution.py:263

commit v2 on v1

--- a/solution.py
+++ b/solution.py
@@ -23,7 +23,7 @@
 def apply_kernel(n_vec, n_chunk, own, *refs):
     vec_refs = refs[:n_vec]
     beam_refs = refs[n_vec : n_vec + n_chunk]
-    cov_ref, spec_ref, out_ref, z_ref, y_ref = refs[n_vec + n_chunk :]
+    cov_ref, spec_ref, *added, out_ref, z_ref, y_ref = refs[n_vec + n_chunk :]
     freqs, rows, lanes = vec_refs[0].shape
     half = rows // 2
     components = spec_ref.shape[1]
@@ -43,7 +43,7 @@
             )
             return carry
 
-        lax.fori_loop(0, freqs, project, 0, unroll=8)
+        lax.fori_loop(0, freqs, project, 0, unroll=32)
 
         def mix(row, carry):
             start = pl.multiple_of(row * freqs, freqs)
@@ -55,7 +55,7 @@
             )
             return carry
 
-        lax.fori_loop(0, rows, mix, 0, unroll=4)
+        lax.fori_loop(0, rows, mix, 0, unroll=16)
 
         def expand(freq, carry):
             y = y_ref[pl.ds(freq, rows, stride=freqs), :].astype(BF16)
@@ -72,20 +72,22 @@
             image = jnp.concatenate([top, bottom], axis=0)
             if chunk:
                 image = image + out_ref[freq]
+            elif added:
+                image = image + added[0][freq]
             out_ref[freq] = image
             return carry
 
-        lax.fori_loop(0, freqs, expand, 0, unroll=8)
-
-
-def apply_covariance(vecs, beams, cov, spec, own):
+        lax.fori_loop(0, freqs, expand, 0, unroll=32)
+
+
+def apply_covariance(vecs, beams, cov, spec, own, added=()):
     freqs, rows, lanes = vecs[0].shape
     depth = beams[0].shape[2]
     flops = 2 * len(beams) * freqs * rows * (2 * lanes * depth + 2 * freqs * depth)
     return pl.pallas_call(
         functools.partial(apply_kernel, len(vecs), len(beams), own),
         out_shape=jax.ShapeDtypeStruct((freqs, rows, lanes), F32),
-        in_specs=[pl.BlockSpec(memory_space=pltpu.VMEM)] * (len(vecs) + len(beams) + 2),
+        in_specs=[pl.BlockSpec(memory_space=pltpu.VMEM)] * (len(vecs) + len(beams) + 2 + len(added)),
         out_specs=pl.BlockSpec(memory_space=pltpu.VMEM),
         scratch_shapes=[
             pltpu.VMEM((rows * freqs, depth), F32),
@@ -95,7 +97,7 @@
         cost_estimate=pl.CostEstimate(
             flops=flops, bytes_accessed=len(beams) * freqs * lanes * depth * 2, transcendentals=0
         ),
-    )(*vecs, *beams, cov, spec)
+    )(*vecs, *beams, cov, spec, *added)
 
 
 def pack_kernel(own, first_ref, second_ref, out_ref):
@@ -157,10 +159,55 @@
     )(rows)
 
 
-def finish_kernel(rows_ref, mixing_ref, out_ref):
+def inverse_factor(work_ref, matrix):
+    order = matrix.shape[0]
+    step = 8
+    row = lax.broadcasted_iota(jnp.int32, (step, order), 0)
+    lane = lax.broadcasted_iota(jnp.int32, (step, order), 1)
+    at = lax.broadcasted_iota(jnp.int32, (order, order), 0)
+    work_ref[:, :order] = matrix
+    work_ref[:, order:] = jnp.where(at == lax.broadcasted_iota(jnp.int32, (order, order), 1), 1.0, 0.0)
+    for begin in range(0, order, step):
+        block = slice(begin, begin + step)
+        left, right = work_ref[block, :order], work_ref[block, order:]
+        columns = [
+            jnp.broadcast_to(left[:, begin + k : begin + k + 1], (step, order)) for k in range(step)
+        ]
+        for k in range(step):
+            root = lax.rsqrt(columns[k][k : k + 1])
+            factor = columns[k] * root
+
+            def eliminate(value):
+                pivot = value[k : k + 1] * root
+                return jnp.where(row == k, pivot, jnp.where(row > k, value - factor * pivot, value))
+
+            left, right = eliminate(left), eliminate(right)
+            columns = columns[: k + 1] + [eliminate(c) for c in columns[k + 1 :]]
+        work_ref[block, order:] = right
+        after = begin + step
+        if after < order:
+            kept = jnp.where(lane >= after, left, 0.0)
+            change = lax.dot_general(
+                kept,
+                jnp.concatenate([kept, right], axis=1),
+                (((0,), (0,)), ((), ())),
+                precision=HIGH,
+                preferred_element_type=F32,
+            )
+            work_ref[after:, :] = work_ref[after:, :] - change[after:]
+    return work_ref[:, order:]
+
+
+def finish_kernel(scale, rows_ref, gram_ref, out_ref, work_ref):
     senders, groups, parts, vectors, lanes = rows_ref.shape
     total = senders * vectors
-    mixing = mixing_ref[...]
+    exact = functools.partial(lax.dot_general, precision=HIGH, preferred_element_type=F32)
+    across = (((1,), (1,)), ((), ()))
+    plain = (((1,), (0,)), ((), ()))
+    first = inverse_factor(work_ref, gram_ref[0])
+    gram_second = exact(exact(first, gram_ref[1], plain), first, across)
+    second = inverse_factor(work_ref, gram_second)
+    mixing = exact(second, first, plain) * scale
     high = mixing.astype(BF16)
     rest = mixing - high.astype(F32)
     middle = rest.astype(BF16)
@@ -170,89 +217,132 @@
             flat = rows_ref[:, group, part].reshape(total, lanes)
             turned = flat.astype(F32).T.astype(BF16)
             dot = functools.partial(
-                lax.dot_general,
-                turned,
-                dimension_numbers=(((1,), (1,)), ((), ())),
-                preferred_element_type=F32,
+                lax.dot_general, turned, dimension_numbers=across, preferred_element_type=F32
             )
             out_ref[part, group] = (dot(low) + dot(middle)) + dot(high)
 
 
-def finish(rows, mixing):
+def finish(rows, gram_pair, scale):
     senders, groups, parts, vectors, lanes = rows.shape
+    total = senders * vectors
     return pl.pallas_call(
-        finish_kernel,
-        out_shape=jax.ShapeDtypeStruct((parts, groups, lanes, senders * vectors), F32),
+        functools.partial(finish_kernel, scale),
+        out_shape=jax.ShapeDtypeStruct((parts, groups, lanes, total), F32),
         in_specs=[pl.BlockSpec(memory_space=pltpu.VMEM)] * 2,
         out_specs=pl.BlockSpec(memory_space=pltpu.VMEM),
+        scratch_shapes=[pltpu.VMEM((total, 2 * total), F32)],
         compiler_params=pltpu.CompilerParams(vmem_limit_bytes=VMEM_BYTES),
-    )(rows, mixing)
+    )(rows, gram_pair)
+
+
+def turn_kernel(start_ref, out_ref):
+    parts, freqs, own, vectors = start_ref.shape
+    receivers, groups, mine, lanes = out_ref.shape
+    per_group = lanes // (parts * own)
+
+    def group(index, carry):
+        tiles = [
+            start_ref[part, index * per_group + place]
+            for place in range(per_group)
+            for part in range(parts)
+        ]
+        turned = jnp.concatenate(tiles, axis=0).T
+        out_ref[:, index] = turned.reshape(receivers, mine, lanes).astype(BF16)
+        return carry
+
+    lax.fori_loop(0, groups, group, 0)
+
+
+def turn(start, receivers, lanes):
+    parts, freqs, own, vectors = start.shape
+    groups = parts * freqs * own // lanes
+    return pl.pallas_call(
+        turn_kernel,
+        out_shape=jax.ShapeDtypeStruct((receivers, groups, vectors // receivers, lanes), BF16),
+        in_specs=[pl.BlockSpec(memory_space=pltpu.VMEM)],
+        out_specs=pl.BlockSpec(memory_space=pltpu.VMEM),
+        compiler_params=pltpu.CompilerParams(vmem_limit_bytes=VMEM_BYTES),
+    )(start)
+
+
+def operand_kernel(own, rows_ref, out_ref):
+    cores, x_count, z_count, groups, mine, lanes = rows_ref.shape
+    parts = lanes // (z_count * own)
+    width = parts * own
+    lane = lax.broadcasted_iota(jnp.int32, (mine, lanes), 1)
+    is_real = (lane // own) % 2 == 0
+
+    def group(index, carry):
+        x_index = index // (cores * groups)
+        core, at = (index // groups) % cores, index % groups
+        tiles = [rows_ref[core, x_index, z, at].astype(F32) for z in range(z_count)]
+        for place in range(z_count):
+            top = tiles[0]
+            for z in range(z_count):
+                top = jnp.where(lane // width == z, rolled(tiles[z], (z - place) * width), top)
+            bottom = jnp.where(is_real, rolled(top, -own), -rolled(top, own))
+            out_ref[index * z_count + place] = jnp.concatenate([top, bottom], axis=0).astype(BF16)
+        return carry
+
+    lax.fori_loop(0, x_count * cores * groups, group, 0, unroll=2)
+
+
+def start_operand(rows, own):
+    cores, x_count, z_count, groups, mine, lanes = rows.shape
+    freqs = x_count * cores * groups * z_count
+    return pl.pallas_call(
+        functools.partial(operand_kernel, own),
+        out_shape=jax.ShapeDtypeStruct((freqs, 2 * mine, lanes), BF16),
+        in_specs=[pl.BlockSpec(memory_space=pltpu.VMEM)],
+        out_specs=pl.BlockSpec(memory_space=pltpu.VMEM),
+        compiler_params=pltpu.CompilerParams(vmem_limit_bytes=VMEM_BYTES),
+    )(rows)
 
 
 def swap_cores(value):
     return lax.ppermute(value, "core", [(0, 1), (1, 0)])
 
 
-def line_blocks(block, count):
-    place = lax.axis_index("fc")
-    found = []
-    down = up = merged = block
-    joined = False
-    for step in range(1, count):
-        from_above = [(j, j - 1) for j in range(1, count) if j + step - 1 < count]
-        from_below = [(j, j + 1) for j in range(count - 1) if j >= step - 1]
-        low_side = [pair[1] for pair in from_above]
-        high_side = [pair[1] for pair in from_below]
-        distance = jnp.where(place + step < count, step, -step)
-        if joined:
-            merged = lax.ppermute(merged, "fc", from_above + from_below)
-            found.append((merged, distance, low_side + high_side))
-            continue
-        down = lax.ppermute(down, "fc", from_above)
-        up = lax.ppermute(up, "fc", from_below)
-        if set(low_side) & set(high_side):
-            found.append((down, step, low_side))
-            found.append((up, -step, high_side))
-        else:
-            merged = jnp.where(place + step < count, down, up)
-            joined = True
-            found.append((merged, distance, low_side + high_side))
-    return found
-
-
-def gather_chunk(block, x_count, z_count):
-    cores, freqs, rows, depth = block.shape
+def gather_ring(sets, x_count, z_count):
+    count = x_count * z_count
+    ring = [k if k < z_count else z_count + count - 1 - k for k in range(count)]
+    pairs = {
+        1: [(ring[k], ring[(k + 1) % count]) for k in range(count)],
+        -1: [(ring[(k + 1) % count], ring[k]) for k in range(count)],
+    }
     x_place, z_place = lax.axis_index("x"), lax.axis_index("fc")
-    whole = jnp.zeros((x_count, cores, freqs, z_count, rows, depth), block.dtype)
-
-    def put(whole, piece, x_at, z_at):
-        return lax.dynamic_update_slice(
-            whole, piece[None, :, :, None], (x_at, 0, 0, z_at, 0, 0)
+    place = jnp.where(x_place == 0, z_place, count - 1 - z_place)
+    freqs, rows, depth = sets[0][0].shape
+    cores = len(sets[0])
+    wholes = [jnp.zeros((x_count, cores, freqs, z_count, rows, depth), BF16) for _ in sets]
+
+    def put(chunk, core, piece, at):
+        x_at = at // z_count
+        z_at = jnp.where(x_at == 0, at, count - 1 - at)
+        wholes[chunk] = lax.dynamic_update_slice(
+            wholes[chunk], piece[None, None, :, None], (x_at, core, 0, z_at, 0, 0)
         )
 
-    def across(piece, receivers):
-        pairs = []
-        for x_index in range(x_count):
-            for z_index in receivers:
-                pairs.append((x_index * z_count + z_index, (1 - x_index) * z_count + z_index))
-        return lax.ppermute(piece, ("x", "fc"), pairs)
-
-    everyone = list(range(z_count))
-    mirrored = across(block, everyone)
-    found = line_blocks(block, z_count)
-    whole = put(whole, block, x_place, z_place)
-    whole = put(whole, mirrored, 1 - x_place, z_place)
-    for piece, distance, receivers in found:
-        opposite = across(piece, receivers)
-        z_at = z_place + distance
-        if len(receivers) < z_count:
-            has = functools.reduce(jnp.logical_or, [z_place == z for z in receivers])
-            piece = jnp.where(has, piece, block)
-            opposite = jnp.where(has, opposite, mirrored)
-            z_at = jnp.where(has, z_at, z_place)
-        whole = put(whole, piece, x_place, z_at)
-        whole = put(whole, opposite, 1 - x_place, z_at)
-    return whole.reshape(x_count * cores * freqs, z_count * rows, depth)
+    moving = {
+        (chunk, core, way): sets[chunk][core]
+        for chunk in range(len(sets))
+        for core in range(cores)
+        for way in (1, -1)
+    }
+    arrived = []
+    for hop in range(1, count // 2 + 1):
+        for (chunk, core, way), piece in moving.items():
+            if 2 * hop == count and (way == 1) != (core == 0):
+                continue
+            piece = lax.ppermute(piece, ("x", "fc"), pairs[way])
+            moving[chunk, core, way] = piece
+            arrived.append((chunk, core, piece, (place - way * hop) % count))
+    for chunk, pieces in enumerate(sets):
+        for core, piece in enumerate(pieces):
+            put(chunk, core, piece, place)
+    for item in arrived:
+        put(*item)
+    return [w.reshape(x_count * cores * freqs, z_count * rows, depth) for w in wholes]
 
 
 def sum_devices(value, z_count):
@@ -284,32 +374,31 @@
     rows = rows.transpose(2, 3, 0, 1, 4)
     kept = lax.dynamic_index_in_dim(rows, core, 0, False)
     given = swap_cores(lax.dynamic_index_in_dim(rows, 1 - core, 0, False))
-    beams = []
-    for chunk in range(chunks):
-        first = jnp.where(core == 0, kept[chunk], given[chunk])
-        second = jnp.where(core == 0, given[chunk], kept[chunk])
-        beams.append(gather_chunk(jnp.stack([first, second]), x_count, z_count))
+    sets = [
+        [
+            jnp.where(core == 0, kept[chunk], given[chunk]),
+            jnp.where(core == 0, given[chunk], kept[chunk]),
+        ]
+        for chunk in range(chunks)
+    ]
+    beams = gather_ring(sets, x_count, z_count)
 
     spec = spectra.reshape(-1, cores, chunks, depth).transpose(1, 2, 0, 3)
     spec = lax.dynamic_index_in_dim(spec, core, 0, False)
     cov = freq_covariance.transpose(1, 0, 2).reshape(all_freqs, -1).astype(BF16)
 
-    start = start_vectors.astype(BF16).reshape(parts, freqs, own, x_count * z_count, mine)
-    start = start.transpose(3, 1, 0, 4, 2)
+    start = turn(start_vectors, x_count * z_count, z_count * parts * own)
     start = lax.all_to_all(start, ("x", "fc"), 0, 0, tiled=True)
     other = swap_cores(start)
     both = jnp.stack([jnp.where(core == 0, start, other), jnp.where(core == 0, other, start)])
-    both = both.reshape(cores, x_count, z_count, freqs, parts, mine, own)
-    both = both.transpose(1, 0, 3, 4, 5, 2, 6)
-    real, imag = both[:, :, :, 0], both[:, :, :, 1]
-    top = jnp.stack([real, imag], axis=5)
-    bottom = jnp.stack([imag, -real], axis=5)
-    operand = jnp.stack([top, bottom], axis=3).reshape(all_freqs, parts * mine, z_count * parts * own)
-
-    partials = [
-        apply_covariance([operand], [beams[c]], cov, spec[c : c + 1], own) for c in range(chunks)
-    ]
-    first_own = functools.reduce(jnp.add, partials)
+    operand = start_operand(both.reshape(cores, x_count, z_count, *both.shape[2:]), own)
+
+    added = ()
+    for chunk in range(chunks):
+        first_own = apply_covariance(
+            [operand], [beams[chunk]], cov, spec[chunk : chunk + 1], own, added
+        )
+        added = (first_own,)
     first_other = swap_cores(first_own)
     second_own = apply_covariance([first_own, first_other], beams, cov, spec, own)
 
@@ -327,15 +416,7 @@
     received = received.reshape(-1, ITERS, groups, parts, mine, lanes)
 
     gram_pair = sum_devices(grams(received), z_count)
-    lower = jnp.linalg.cholesky(gram_pair[0])
-    eye = jnp.eye(vectors, dtype=F32)
-    solve = functools.partial(lax.linalg.triangular_solve, left_side=True, lower=True)
-    inverse = solve(lower, eye)
-    dot = functools.partial(jnp.dot, precision=HIGH, preferred_element_type=F32)
-    gram_second = dot(dot(inverse, gram_pair[1]), inverse.T)
-    lower = jnp.linalg.cholesky(gram_second)
-    mixing = solve(lower, inverse) * math.sqrt(2.0 * all_freqs * z_count * own)
-    basis = finish(received[:, 1], mixing)
+    basis = finish(received[:, 1], gram_pair, math.sqrt(2.0 * all_freqs * z_count * own))
     return basis.reshape(parts, freqs, own, vectors)
 
 

time: 364 us -> 230 us (0.63)
  other arithmetic: 76 us -> 7.1 us
  starting transfers between devices: 64.1 us -> 32.2 us
  local copies, waits for them, and re-layouts: 54.8 us -> 31.8 us
  waiting for transfers between devices: 75.9 us -> 64.8 us
  Pallas kernels: 69.3 us -> 73.5 us
    another operation x14 -> x1, other arithmetic: 50.4 us -> 0.84 us  [body_split(): jnp.stack([jnp.where(core == 0, start, other), jnp.where(core == 0, other...]
    ppermute x20 -> x28, starting transfers between devices: 51.5 us -> 19.7 us  [gather_ring(): piece = lax.ppermute(piece, ('x', 'fc'), pairs[way])]
    pallas_call x1 -> x3, Pallas kernels: 2.44 us -> 26.9 us  [the longest x1 19.3 us: finish(): pl.pallas_call(functools.partial(finish_kernel, scale), out_shape=jax.Sha...]
    pallas_call x3, Pallas kernels: 58.1 us -> 37.9 us  [apply_covariance(): pl.pallas_call(functools.partial(apply_kernel, len(vecs), len(beams), own...]
    broadcast_in_dim x6 -> x0, other arithmetic: 13.2 us -> none  [put(): piece[None, :, :, None]]
    another operation x4 -> x2, local copies, waits for them, and re-layouts: 13.6 us -> 2.07 us  [the longest x1 8.91 us: body_split(): jnp.stack([top, bottom], axis=3)]
    ppermute x20 -> x28, waiting for transfers between devices: 50.1 us -> 39.8 us  [gather_ring(): piece = lax.ppermute(piece, ('x', 'fc'), pairs[way])]
    reshape x2 -> x0, local copies, waits for them, and re-layouts: 9.66 us -> none  [body_split(): jnp.stack([top, bottom], axis=3)]
  transfers between devices with their start and end apart: 30 -> 38, of which waited for: 13 -> 26; matrix products, arithmetic and copies ran while one was open for 19% -> 10% of each run, Pallas kernels for 1% -> 9%
where the time goes in v2:
time: 230 us; the launch traced here: 229 us
  Pallas kernels  73.5 us (32%)
  waiting for transfers between devices  64.8 us (28%)
  starting transfers between devices  32.2 us (14%)
  local copies, waits for them, and re-layouts  31.8 us (14%)
  blocking collectives  19.3 us (8%)
  other arithmetic  7.1 us (3%)
    ppermute x28, waiting for transfers between devices, gather_ring(): piece = lax.ppermute(piece, ('x', 'fc'), pairs[way])  39.8 us
    pallas_call x3, Pallas kernels, apply_covariance(): pl.pallas_call(functools.partial(apply_kernel, len(vecs), len(beams), own...  37.9 us
    ppermute x28, starting transfers between devices, gather_ring(): piece = lax.ppermute(piece, ('x', 'fc'), pairs[way])  19.7 us
    all_to_all x1, blocking collectives, body_split(): received = lax.all_to_all(packed, ('x', 'fc'), 0, 0, tiled=True)  19.3 us
    pallas_call x1, Pallas kernels, finish(): pl.pallas_call(functools.partial(finish_kernel, scale), out_shape=jax.Sha...  19.3 us
    dynamic_update_slice x28, local copies, waits for them, and re-layouts, put(): lax.dynamic_update_slice(wholes[chunk], piece[None, None, :, None], (x_at...  11.5 us
    ppermute x3, waiting for transfers between devices, sum_devices(): lax.ppermute(value, 'fc', [(j, j ^ s) for j in range(z_count)])  7.64 us
    all_to_all x1, waiting for transfers between devices, body_split(): start = lax.all_to_all(start, ('x', 'fc'), 0, 0, tiled=True)  7.44 us
  transfers between devices with their start and end apart: 38, of which 26 were waited for; matrix products, arithmetic and copies ran while one was open for 10% of the time, Pallas kernels for 9%

profile of v2, /device:TPU:0, one launch (start us, length us, event | category | flops | bytes accessed | tf_op | source)
XLA Modules:
  0.0 229.0 jit_solution(8216046057945742044)
XLA Ops:
  0.8 1.5 fusion
  2.7 0.9 dynamic-slice_bitcast_fusion
  4.1 2.6 %shard_map.55 = bf16[8,8,16,128]{3,2,1,0:T(8,128)(2,1)} custom-call(f32[2,32,16,128]{3,2,1,0:T(8,128)} %start_ref.1), custom_call_target="tpu_custom_call" | custom-call | tf_op jit(solution)/shard_map/pallas_call | solution.py:259
  6.7 6.8 %all-to-all-start = ((bf16[8,8,16,128]{3,2,1,0:T(8,128)(2,1)}), bf16[8,8,16,128]{3,2,1,0:T(8,128)(2,1)S(1)}, u32[]{:S(2)}, u32[]{:S(2)}) async-start(bf16[8,8,16,128]{3,2,1,0:T(8,128)(2,1)} %shard_map.55), calls=%async_computation | async-start | bytes 524288 | tf_op jit(solution)/shard_map/all_to_all | solution.py:391
  15.3 1.2 fusion.12
  16.5 7.4 %all-to-all-done = bf16[8,8,16,128]{3,2,1,0:T(8,128)(2,1)S(1)} async-done(((bf16[8,8,16,128]{3,2,1,0:T(8,128)(2,1)}), bf16[8,8,16,128]{3,2,1,0:T(8,128)(2,1)S(1)}, u32[]{:S(2)}, u32[]{:S(2)}) %all-to-all-start) | async-done | bytes 262176 | tf_op jit(solution)/shard_map/all_to_all | solution.py:391
  25.5 2.0 collective-permute-start.17
  27.5 2.0 collective-permute-start.19
  29.7 1.0 broadcast.49.clone.1
  30.8 1.0 broadcast.49.clone
  32.2 2.0 copy-done.1
  34.3 0.8 pad_maximum_fusion.rows_ref
  35.1 5.0 %shard_map.56.refs_0_ = bf16[128,32,128]{2,1,0:T(8,128)(2,1)} custom-call(bf16[2,2,4,8,16,128]{5,4,3,2,1,0:T(8,128)(2,1)} %pad_maximum_fusion.rows_ref), custom_call_target="tpu_custom_call" | custom-call | tf_op jit(solution)/shard_map/pallas_call | solution.py:293
  40.1 2.0 collective-permute-start.3
  42.3 2.1 collective-permute-start.5
  44.6 1.5 collective-permute-done.2
  47.4 2.0 collective-permute-done.3
  49.9 0.8 bitcast_dynamic-update-slice_fusion.26
  50.7 1.0 collective-permute-done.4
  53.0 2.0 collective-permute-done.5
  55.5 0.8 bitcast_dynamic-update-slice_fusion.24
  56.3 1.0 collective-permute-done.20
  57.9 2.7 %collective-permute-done.21 = bf16[32,32,128]{2,1,0:T(8,128)(2,1)S(1)} collective-permute-done((bf16[32,32,128]{2,1,0:T(8,128)(2,1)S(1)}, bf16[32,32,128]{2,1,0:T(8,128)(2,1)S(1)}, u32[]{:S(2)}, u32[]{:S(2)}) %collective-permute-start.21) | collective-permute-done | bytes 262176 | tf_op jit(solution)/shard_map/ppermute | solution.py:337
  61.1 1.8 collective-permute-done.22
  63.5 2.7 %collective-permute-done.23 = bf16[32,32,128]{2,1,0:T(8,128)(2,1)S(1)} collective-permute-done((bf16[32,32,128]{2,1,0:T(8,128)(2,1)S(1)}, bf16[32,32,128]{2,1,0:T(8,128)(2,1)S(1)}, u32[]{:S(2)}, u32[]{:S(2)}) %collective-permute-start.23) | collective-permute-done | bytes 262176 | tf_op jit(solution)/shard_map/ppermute | solution.py:337
  66.8 1.8 collective-permute-done.6
  69.9 2.0 collective-permute-done.7
  73.1 1.0 collective-permute-done.8
  74.7 0.8 bitcast_dynamic-update-slice_fusion.21
  75.5 2.0 collective-permute-done.9
  78.7 1.0 collective-permute-done.24
  80.4 2.7 %collective-permute-done.25 = bf16[32,32,128]{2,1,0:T(8,128)(2,1)S(1)} collective-permute-done((bf16[32,32,128]{2,1,0:T(8,128)(2,1)S(1)}, bf16[32,32,128]{2,1,0:T(8,128)(2,1)S(1)}, u32[]{:S(2)}, u32[]{:S(2)}) %collective-permute-start.25) | collective-permute-done | bytes 262176 | tf_op jit(solution)/shard_map/ppermute | solution.py:337
  83.6 1.8 collective-permute-done.26
  86.0 2.7 %collective-permute-done.27 = bf16[32,32,128]{2,1,0:T(8,128)(2,1)S(1)} collective-permute-done((bf16[32,32,128]{2,1,0:T(8,128)(2,1)S(1)}, bf16[32,32,128]{2,1,0:T(8,128)(2,1)S(1)}, u32[]{:S(2)}, u32[]{:S(2)}) %collective-permute-start.27) | collective-permute-done | bytes 262176 | tf_op jit(solution)/shard_map/ppermute | solution.py:337
  89.2 1.8 collective-permute-done.10
  91.6 0.8 bitcast_dynamic-update-slice_fusion.19
  92.3 2.0 collective-permute-done.11
  94.8 5.1 %collective-permute-done.13 = bf16[32,32,128]{2,1,0:T(8,128)(2,1)S(1)} collective-permute-done((bf16[32,32,128]{2,1,0:T(8,128)(2,1)S(1)}, bf16[32,32,128]{2,1,0:T(8,128)(2,1)S(1)}, u32[]{:S(2)}, u32[]{:S(2)}) %collective-permute-start.13) | collective-permute-done | bytes 262176 | tf_op jit(solution)/shard_map/ppermute | solution.py:337
  99.9 2.0 collective-permute-start.15
  104.4 1.2 collective-permute-done.29
  105.6 2.0 copy-done
  107.6 9.8 %shard_map.57.refs_4_ = f32[128,32,128]{2,1,0:T(8,128)} custom-call(bf16[128,32,128]{2,1,0:T(8,128)(2,1)} %shard_map.56.refs_0_, bf16[128,128,128]{2,1,0:T(8,128)(2,1)} %bitcast.228, bf16[128,256]{1,0:T(8,128)(2,1)} %copy_bitcast_fusion.refs_2_.refs_4_, f32[1,2,128]{2,1,0:T(2,128)} %get-tuple-element.23.refs_3_), custom_call_target="tpu_custom_call" | custom-call | flops 536870912 | bytes 4194304 | tf_op jit(solution)/shard_map/pallas_call | solution.py:87
  117.3 0.8 bitcast_dynamic-update-slice_fusion.15
  118.9 10.4 %shard_map.58.refs_0_ = f32[128,32,128]{2,1,0:T(8,128)} custom-call(bf16[128,32,128]{2,1,0:T(8,128)(2,1)} %shard_map.56.refs_0_, bf16[128,128,128]{2,1,0:T(8,128)(2,1)} %bitcast.230, bf16[128,256]{1,0:T(8,128)(2,1)} %copy_bitcast_fusion.refs_2_.refs_4_, f32[1,2,128]{2,1,0:T(2,128)} %get-tuple-element.24.refs_3_, f32[128,32,128]{2,1,0:T(8,128)} %shard_map.57.refs_4_), custom_call_target="tpu_custom_call" | custom-call | flops 536870912 | bytes 4194304 | tf_op jit(solution)/shard_map/pallas_call | solution.py:87
  129.3 4.4 %collective-permute-done.30.refs_1_ = f32[128,32,128]{2,1,0:T(8,128)S(1)} collective-permute-done((f32[128,32,128]{2,1,0:T(8,128)}, f32[128,32,128]{2,1,0:T(8,128)S(1)}, u32[]{:S(2)}, u32[]{:S(2)}) %collective-permute-start.30) | collective-permute-done | bytes 2097184 | tf_op jit(solution)/shard_map/ppermute | solution.py:303
  133.7 1.4 copy-done.3
  135.1 17.7 %shard_map.60 = f32[128,32,128]{2,1,0:T(8,128)} custom-call(f32[128,32,128]{2,1,0:T(8,128)} %shard_map.58.refs_0_, f32[128,32,128]{2,1,0:T(8,128)} %copy-done.3, bf16[128,128,128]{2,1,0:T(8,128)(2,1)} %bitcast.229, bf16[128,128,128]{2,1,0:T(8,128)(2,1)} %bitcast.231, bf16[128,256]{1,0:T(8,128)(2,1)} %copy_bitcast_fusion.refs_2_.refs_4_, ...), custom_call_target="tpu_custom_call" | custom-call | flops 1073741824 | bytes 8388608 | tf_op jit(solution)/shard_map/pallas_call | solution.py:87
  152.8 2.9 %constant_dynamic-slice_fusion = (f32[2,1,32,32,128]{4,3,2,1,0:T(8,128)S(1)}, f32[2,1,32,32,128]{4,3,2,1,0:T(8,128)}) fusion(f32[2,2,32,32,128]{4,3,2,1,0:T(8,128)} %bitcast.233, s32[]{:T(128)S(6)} %select_n.381, s32[]{:T(128)S(6)} %select_n.380), kind=kLoop, calls=%fused_computation.57 | loop fusion | bytes 4194312 | tf_op jit(solution)/shard_map/jit(dynamic_index_in_dim)/dynamic_slice | solution.py:407
  155.8 1.1 constant_dynamic-slice_fusion.3
  156.9 1.1 constant_dynamic-slice_fusion.2
  158.0 3.3 %shard_map.59 = bf16[2,4,4,32,128]{4,3,2,1,0:T(8,128)(2,1)} custom-call(f32[64,32,128]{2,1,0:T(8,128)} %bitcast.237, f32[64,32,128]{2,1,0:T(8,128)} %bitcast.238), custom_call_target="tpu_custom_call" | custom-call | tf_op jit(solution)/shard_map/pallas_call | solution.py:128
  161.3 1.0 copy-done.5
  162.2 3.3 %shard_map.61 = bf16[2,4,4,32,128]{4,3,2,1,0:T(8,128)(2,1)} custom-call(f32[64,32,128]{2,1,0:T(8,128)} %bitcast.236, f32[64,32,128]{2,1,0:T(8,128)} %copy-done.5), custom_call_target="tpu_custom_call" | custom-call | tf_op jit(solution)/shard_map/pallas_call | solution.py:128
  165.5 1.1 pad_maximum_fusion.1
  166.6 19.3 %all_to_all.10 = bf16[8,2,4,32,128]{4,3,2,1,0:T(8,128)(2,1)} all-to-all(bf16[8,2,4,32,128]{4,3,2,1,0:T(8,128)(2,1)S(1)} %pad_maximum_fusion.1), channel_id=1, replica_groups=mesh['ma'=2,'x'=2,'core'=2,'fc'=4] {'x','fc'}, dimensions={0} | all-to-all | bytes 1048576 | tf_op jit(solution)/shard_map/all_to_all | solution.py:414
  185.9 2.2 shard_map.62
  188.1 1.6 collective-permute-done.32
  189.7 0.9 add.237
  191.2 1.1 copy.282
  192.3 3.9 %collective-permute-done.33 = f32[2,128,128]{2,1,0:T(8,128)S(1)} collective-permute-done((f32[2,128,128]{2,1,0:T(8,128)S(1)}, f32[2,128,128]{2,1,0:T(8,128)S(1)}, u32[]{:S(2)}, u32[]{:S(2)}) %collective-permute-start.33) | collective-permute-done | bytes 131104 | tf_op jit(solution)/shard_map/ppermute | solution.py:350
  196.8 3.9 %collective-permute-start.36 = (f32[2,128,128]{2,1,0:T(8,128)S(1)}, f32[2,128,128]{2,1,0:T(8,128)S(1)}, u32[]{:S(2)}, u32[]{:S(2)}) collective-permute-start(f32[2,128,128]{2,1,0:T(8,128)S(1)} %add.238), channel_id=1, source_target_pairs={{0,3},{1,2},{2,1},{3,0},{4,7},{5,6},{6,5},{7,4},{8,11},{9,10},{10,... | collective-permute-start | bytes 393224 | tf_op jit(solution)/shard_map/ppermute | solution.py:353
  201.4 1.4 collective-permute-done.34
  202.8 6.3 %collective-permute-done.35 = f32[2,128,128]{2,1,0:T(8,128)S(1)} collective-permute-done((f32[2,128,128]{2,1,0:T(8,128)S(1)}, f32[2,128,128]{2,1,0:T(8,128)S(1)}, u32[]{:S(2)}, u32[]{:S(2)}) %collective-permute-start.35) | collective-permute-done | bytes 131104 | tf_op jit(solution)/shard_map/ppermute | solution.py:353
  209.8 19.3 %shard_map.63 = f32[2,4,128,128]{3,2,1,0:T(8,128)} custom-call(bf16[8,4,2,16,128]{4,3,2,1,0:T(8,128)(2,1)} %slice_bitcast_fusion.rows_ref, f32[2,128,128]{2,1,0:T(8,128)} %add_bitcast_fusion.gram_ref), custom_call_target="tpu_custom_call" | custom-call | tf_op jit(solution)/shard_map/pallas_call | solution.py:228
  (98 shorter events, 25.4 us)
Async XLA Ops:
  2.2 11.2 %copy-start.6 = (f32[2,128,128]{2,1,0:T(8,128)S(1)}, f32[2,128,128]{2,1,0:T(8,128)}, u32[]{:S(2)}) copy-start(f32[2,128,128]{2,1,0:T(8,128)} %param.8) | copy-start | bytes 393220
  2.3 11.9 %copy-start.7 = (f32[2,512]{1,0:T(2,128)S(1)}, f32[2,512]{1,0:T(2,128)}, u32[]{:S(2)}) copy-start(f32[2,512]{1,0:T(2,128)} %param.7) | copy-start | bytes 12292
  3.6 20.3 %collective-permute-start.1 = (bf16[2,32,32,128]{3,0,2,1:T(2,128)(2,1)S(1)}, bf16[2,32,32,128]{3,0,2,1:T(2,128)(2,1)S(1)}, u32[]{:S(2)}, u32[]{:S(2)}) collective-permute-start(bf16[2,32,32,128]{3,0,2,1:T(2,128)(2,1)S(1)} %get-tuple-element.13), channel_id=1, source_target_pairs={{0,4},{4,0},{1,5},{5,1},{2,6},{6,2},{3,7},{7,3},{8,12},{12,8},{9,1... | collective-permute-start | bytes 1572872 | tf_op jit(solution)/shard_map/ppermute | solution.py:303
  6.7 17.2 %all-to-all-start = ((bf16[8,8,16,128]{3,2,1,0:T(8,128)(2,1)}), bf16[8,8,16,128]{3,2,1,0:T(8,128)(2,1)S(1)}, u32[]{:S(2)}, u32[]{:S(2)}) async-start(bf16[8,8,16,128]{3,2,1,0:T(8,128)(2,1)} %shard_map.55), calls=%async_computation | async-start | bytes 524288 | tf_op jit(solution)/shard_map/all_to_all | solution.py:391
  23.9 10.3 %collective-permute-start = (bf16[8,8,16,128]{3,2,1,0:T(8,128)(2,1)S(1)}, bf16[8,8,16,128]{3,2,1,0:T(8,128)(2,1)S(1)}, u32[]{:S(2)}, u32[]{:S(2)}) collective-permute-start(bf16[8,8,16,128]{3,2,1,0:T(8,128)(2,1)S(1)} %all-to-all-done), channel_id=1, source_target_pairs={{0,4},{4,0},{1,5},{5,1},{2,6},{6,2},{3,7},{7,3},{8,12},{12,8},{9,1... | collective-permute-start | bytes 786440 | tf_op jit(solution)/shard_map/ppermute | solution.py:303
  25.5 14.6 %collective-permute-start.16 = (bf16[32,32,128]{2,1,0:T(8,128)(2,1)}, bf16[32,32,128]{2,1,0:T(8,128)(2,1)S(1)}, u32[]{:S(2)}, u32[]{:S(2)}) collective-permute-start(bf16[32,32,128]{2,1,0:T(8,128)(2,1)} %bitcast_select_fusion.1), channel_id=1, source_target_pairs={{0,1},{1,2},{2,3},{3,11},{11,10},{10,9},{9,8},{8,0},{4,5},{5,6},{6... | collective-permute-start | bytes 786440 | tf_op jit(solution)/shard_map/ppermute | solution.py:337
  25.5 16.7 %collective-permute-start.17 = (bf16[32,32,128]{2,1,0:T(8,128)(2,1)}, bf16[32,32,128]{2,1,0:T(8,128)(2,1)S(1)}, u32[]{:S(2)}, u32[]{:S(2)}) collective-permute-start(bf16[32,32,128]{2,1,0:T(8,128)(2,1)} %bitcast_select_fusion.1), channel_id=1, source_target_pairs={{1,0},{2,1},{3,2},{11,3},{10,11},{9,10},{8,9},{0,8},{5,4},{6,5},{7... | collective-permute-start | bytes 786440 | tf_op jit(solution)/shard_map/ppermute | solution.py:337
  27.5 14.8 %collective-permute-start.18 = (bf16[32,32,128]{2,1,0:T(8,128)(2,1)S(1)}, bf16[32,32,128]{2,1,0:T(8,128)(2,1)S(1)}, u32[]{:S(2)}, u32[]{:S(2)}) collective-permute-start(bf16[32,32,128]{2,1,0:T(8,128)(2,1)S(1)} %get-tuple-element.5), channel_id=1, source_target_pairs={{0,1},{1,2},{2,3},{3,11},{11,10},{10,9},{9,8},{8,0},{4,5},{5,6},{6... | collective-permute-start | bytes 786440 | tf_op jit(solution)/shard_map/ppermute | solution.py:337
  27.5 16.9 %collective-permute-start.19 = (bf16[32,32,128]{2,1,0:T(8,128)(2,1)S(1)}, bf16[32,32,128]{2,1,0:T(8,128)(2,1)S(1)}, u32[]{:S(2)}, u32[]{:S(2)}) collective-permute-start(bf16[32,32,128]{2,1,0:T(8,128)(2,1)S(1)} %get-tuple-element.5), channel_id=1, source_target_pairs={{1,0},{2,1},{3,2},{11,3},{10,11},{9,10},{8,9},{0,8},{5,4},{6,5},{7... | collective-permute-start | bytes 786440 | tf_op jit(solution)/shard_map/ppermute | solution.py:337
  32.2 2.0 copy-start.1
  34.2 11.8 %collective-permute-start.2 = (bf16[32,32,128]{2,1,0:T(8,128)(2,1)S(1)}, bf16[32,32,128]{2,1,0:T(8,128)(2,1)S(1)}, u32[]{:S(2)}, u32[]{:S(2)}) collective-permute-start(bf16[32,32,128]{2,1,0:T(8,128)(2,1)S(1)} %bitcast_select_fusion.5), channel_id=1, source_target_pairs={{0,1},{1,2},{2,3},{3,11},{11,10},{10,9},{9,8},{8,0},{4,5},{5,6},{6... | collective-permute-start | bytes 786440 | tf_op jit(solution)/shard_map/ppermute | solution.py:337
  40.1 9.2 %collective-permute-start.3 = (bf16[32,32,128]{2,1,0:T(8,128)(2,1)S(1)}, bf16[32,32,128]{2,1,0:T(8,128)(2,1)S(1)}, u32[]{:S(2)}, u32[]{:S(2)}) collective-permute-start(bf16[32,32,128]{2,1,0:T(8,128)(2,1)S(1)} %bitcast_select_fusion.5), channel_id=1, source_target_pairs={{1,0},{2,1},{3,2},{11,3},{10,11},{9,10},{8,9},{0,8},{5,4},{6,5},{7... | collective-permute-start | bytes 786440 | tf_op jit(solution)/shard_map/ppermute | solution.py:337
  42.2 9.5 %collective-permute-start.4 = (bf16[32,32,128]{2,1,0:T(8,128)(2,1)S(1)}, bf16[32,32,128]{2,1,0:T(8,128)(2,1)S(1)}, u32[]{:S(2)}, u32[]{:S(2)}) collective-permute-start(bf16[32,32,128]{2,1,0:T(8,128)(2,1)S(1)} %get-tuple-element.8), channel_id=1, source_target_pairs={{0,1},{1,2},{2,3},{3,11},{11,10},{10,9},{9,8},{8,0},{4,5},{5,6},{6... | collective-permute-start | bytes 786440 | tf_op jit(solution)/shard_map/ppermute | solution.py:337
  42.3 12.7 %collective-permute-start.5 = (bf16[32,32,128]{2,1,0:T(8,128)(2,1)S(1)}, bf16[32,32,128]{2,1,0:T(8,128)(2,1)S(1)}, u32[]{:S(2)}, u32[]{:S(2)}) collective-permute-start(bf16[32,32,128]{2,1,0:T(8,128)(2,1)S(1)} %get-tuple-element.8), channel_id=1, source_target_pairs={{1,0},{2,1},{3,2},{11,3},{10,11},{9,10},{8,9},{0,8},{5,4},{6,5},{7... | collective-permute-start | bytes 786440 | tf_op jit(solution)/shard_map/ppermute | solution.py:337
  44.4 12.8 %collective-permute-start.20 = (bf16[32,32,128]{2,1,0:T(8,128)(2,1)S(1)}, bf16[32,32,128]{2,1,0:T(8,128)(2,1)S(1)}, u32[]{:S(2)}, u32[]{:S(2)}) collective-permute-start(bf16[32,32,128]{2,1,0:T(8,128)(2,1)S(1)} %collective-permute-done.16), channel_id=1, source_target_pairs={{0,1},{1,2},{2,3},{3,11},{11,10},{10,9},{9,8},{8,0},{4,5},{5,6},{6... | collective-permute-start | bytes 786440 | tf_op jit(solution)/shard_map/ppermute | solution.py:337
  46.0 14.6 %collective-permute-start.21 = (bf16[32,32,128]{2,1,0:T(8,128)(2,1)S(1)}, bf16[32,32,128]{2,1,0:T(8,128)(2,1)S(1)}, u32[]{:S(2)}, u32[]{:S(2)}) collective-permute-start(bf16[32,32,128]{2,1,0:T(8,128)(2,1)S(1)} %collective-permute-done.17), channel_id=1, source_target_pairs={{1,0},{2,1},{3,2},{11,3},{10,11},{9,10},{8,9},{0,8},{5,4},{6,5},{7... | collective-permute-start | bytes 786440 | tf_op jit(solution)/shard_map/ppermute | solution.py:337
  49.4 13.5 %collective-permute-start.22 = (bf16[32,32,128]{2,1,0:T(8,128)(2,1)S(1)}, bf16[32,32,128]{2,1,0:T(8,128)(2,1)S(1)}, u32[]{:S(2)}, u32[]{:S(2)}) collective-permute-start(bf16[32,32,128]{2,1,0:T(8,128)(2,1)S(1)} %collective-permute-done.18), channel_id=1, source_target_pairs={{0,1},{1,2},{2,3},{3,11},{11,10},{10,9},{9,8},{8,0},{4,5},{5,6},{6... | collective-permute-start | bytes 786440 | tf_op jit(solution)/shard_map/ppermute | solution.py:337
  51.7 14.6 %collective-permute-start.23 = (bf16[32,32,128]{2,1,0:T(8,128)(2,1)S(1)}, bf16[32,32,128]{2,1,0:T(8,128)(2,1)S(1)}, u32[]{:S(2)}, u32[]{:S(2)}) collective-permute-start(bf16[32,32,128]{2,1,0:T(8,128)(2,1)S(1)} %collective-permute-done.19), channel_id=1, source_target_pairs={{1,0},{2,1},{3,2},{11,3},{10,11},{9,10},{8,9},{0,8},{5,4},{6,5},{7... | collective-permute-start | bytes 786440 | tf_op jit(solution)/shard_map/ppermute | solution.py:337
  55.0 13.5 %collective-permute-start.6 = (bf16[32,32,128]{2,1,0:T(8,128)(2,1)S(1)}, bf16[32,32,128]{2,1,0:T(8,128)(2,1)S(1)}, u32[]{:S(2)}, u32[]{:S(2)}) collective-permute-start(bf16[32,32,128]{2,1,0:T(8,128)(2,1)S(1)} %collective-permute-done.2), channel_id=1, source_target_pairs={{0,1},{1,2},{2,3},{3,11},{11,10},{10,9},{9,8},{8,0},{4,5},{5,6},{6... | collective-permute-start | bytes 786440 | tf_op jit(solution)/shard_map/ppermute | solution.py:337
  57.3 14.6 %collective-permute-start.7 = (bf16[32,32,128]{2,1,0:T(8,128)(2,1)S(1)}, bf16[32,32,128]{2,1,0:T(8,128)(2,1)S(1)}, u32[]{:S(2)}, u32[]{:S(2)}) collective-permute-start(bf16[32,32,128]{2,1,0:T(8,128)(2,1)S(1)} %collective-permute-done.3), channel_id=1, source_target_pairs={{1,0},{2,1},{3,2},{11,3},{10,11},{9,10},{8,9},{0,8},{5,4},{6,5},{7... | collective-permute-start | bytes 786440 | tf_op jit(solution)/shard_map/ppermute | solution.py:337
  60.6 13.5 %collective-permute-start.8 = (bf16[32,32,128]{2,1,0:T(8,128)(2,1)S(1)}, bf16[32,32,128]{2,1,0:T(8,128)(2,1)S(1)}, u32[]{:S(2)}, u32[]{:S(2)}) collective-permute-start(bf16[32,32,128]{2,1,0:T(8,128)(2,1)S(1)} %collective-permute-done.4), channel_id=1, source_target_pairs={{0,1},{1,2},{2,3},{3,11},{11,10},{10,9},{9,8},{8,0},{4,5},{5,6},{6... | collective-permute-start | bytes 786440 | tf_op jit(solution)/shard_map/ppermute | solution.py:337
  62.9 14.6 %collective-permute-start.9 = (bf16[32,32,128]{2,1,0:T(8,128)(2,1)S(1)}, bf16[32,32,128]{2,1,0:T(8,128)(2,1)S(1)}, u32[]{:S(2)}, u32[]{:S(2)}) collective-permute-start(bf16[32,32,128]{2,1,0:T(8,128)(2,1)S(1)} %collective-permute-done.5), channel_id=1, source_target_pairs={{1,0},{2,1},{3,2},{11,3},{10,11},{9,10},{8,9},{0,8},{5,4},{6,5},{7... | collective-permute-start | bytes 786440 | tf_op jit(solution)/shard_map/ppermute | solution.py:337
  66.2 13.5 %collective-permute-start.24 = (bf16[32,32,128]{2,1,0:T(8,128)(2,1)S(1)}, bf16[32,32,128]{2,1,0:T(8,128)(2,1)S(1)}, u32[]{:S(2)}, u32[]{:S(2)}) collective-permute-start(bf16[32,32,128]{2,1,0:T(8,128)(2,1)S(1)} %collective-permute-done.20), channel_id=1, source_target_pairs={{0,1},{1,2},{2,3},{3,11},{11,10},{10,9},{9,8},{8,0},{4,5},{5,6},{6... | collective-permute-start | bytes 786440 | tf_op jit(solution)/shard_map/ppermute | solution.py:337
  68.5 14.6 %collective-permute-start.25 = (bf16[32,32,128]{2,1,0:T(8,128)(2,1)S(1)}, bf16[32,32,128]{2,1,0:T(8,128)(2,1)S(1)}, u32[]{:S(2)}, u32[]{:S(2)}) collective-permute-start(bf16[32,32,128]{2,1,0:T(8,128)(2,1)S(1)} %collective-permute-done.21), channel_id=1, source_target_pairs={{1,0},{2,1},{3,2},{11,3},{10,11},{9,10},{8,9},{0,8},{5,4},{6,5},{7... | collective-permute-start | bytes 786440 | tf_op jit(solution)/shard_map/ppermute | solution.py:337
  71.9 13.5 %collective-permute-start.26 = (bf16[32,32,128]{2,1,0:T(8,128)(2,1)S(1)}, bf16[32,32,128]{2,1,0:T(8,128)(2,1)S(1)}, u32[]{:S(2)}, u32[]{:S(2)}) collective-permute-start(bf16[32,32,128]{2,1,0:T(8,128)(2,1)S(1)} %collective-permute-done.22), channel_id=1, source_target_pairs={{0,1},{1,2},{2,3},{3,11},{11,10},{10,9},{9,8},{8,0},{4,5},{5,6},{6... | collective-permute-start | bytes 786440 | tf_op jit(solution)/shard_map/ppermute | solution.py:337
  74.1 14.6 %collective-permute-start.27 = (bf16[32,32,128]{2,1,0:T(8,128)(2,1)S(1)}, bf16[32,32,128]{2,1,0:T(8,128)(2,1)S(1)}, u32[]{:S(2)}, u32[]{:S(2)}) collective-permute-start(bf16[32,32,128]{2,1,0:T(8,128)(2,1)S(1)} %collective-permute-done.23), channel_id=1, source_target_pairs={{1,0},{2,1},{3,2},{11,3},{10,11},{9,10},{8,9},{0,8},{5,4},{6,5},{7... | collective-permute-start | bytes 786440 | tf_op jit(solution)/shard_map/ppermute | solution.py:337
  77.5 13.5 %collective-permute-start.10 = (bf16[32,32,128]{2,1,0:T(8,128)(2,1)S(1)}, bf16[32,32,128]{2,1,0:T(8,128)(2,1)S(1)}, u32[]{:S(2)}, u32[]{:S(2)}) collective-permute-start(bf16[32,32,128]{2,1,0:T(8,128)(2,1)S(1)} %collective-permute-done.6), channel_id=1, source_target_pairs={{0,1},{1,2},{2,3},{3,11},{11,10},{10,9},{9,8},{8,0},{4,5},{5,6},{6... | collective-permute-start | bytes 786440 | tf_op jit(solution)/shard_map/ppermute | solution.py:337
  79.8 14.6 %collective-permute-start.11 = (bf16[32,32,128]{2,1,0:T(8,128)(2,1)S(1)}, bf16[32,32,128]{2,1,0:T(8,128)(2,1)S(1)}, u32[]{:S(2)}, u32[]{:S(2)}) collective-permute-start(bf16[32,32,128]{2,1,0:T(8,128)(2,1)S(1)} %collective-permute-done.7), channel_id=1, source_target_pairs={{1,0},{2,1},{3,2},{11,3},{10,11},{9,10},{8,9},{0,8},{5,4},{6,5},{7... | collective-permute-start | bytes 786440 | tf_op jit(solution)/shard_map/ppermute | solution.py:337
  83.1 19.7 %collective-permute-start.12 = (bf16[32,32,128]{2,1,0:T(8,128)(2,1)S(1)}, bf16[32,32,128]{2,1,0:T(8,128)(2,1)S(1)}, u32[]{:S(2)}, u32[]{:S(2)}) collective-permute-start(bf16[32,32,128]{2,1,0:T(8,128)(2,1)S(1)} %collective-permute-done.8), channel_id=1, source_target_pairs={{0,1},{1,2},{2,3},{3,11},{11,10},{10,9},{9,8},{8,0},{4,5},{5,6},{6... | collective-permute-start | bytes 786440 | tf_op jit(solution)/shard_map/ppermute | solution.py:337
  85.4 14.6 %collective-permute-start.13 = (bf16[32,32,128]{2,1,0:T(8,128)(2,1)S(1)}, bf16[32,32,128]{2,1,0:T(8,128)(2,1)S(1)}, u32[]{:S(2)}, u32[]{:S(2)}) collective-permute-start(bf16[32,32,128]{2,1,0:T(8,128)(2,1)S(1)} %collective-permute-done.9), channel_id=1, source_target_pairs={{1,0},{2,1},{3,2},{11,3},{10,11},{9,10},{8,9},{0,8},{5,4},{6,5},{7... | collective-permute-start | bytes 786440 | tf_op jit(solution)/shard_map/ppermute | solution.py:337
  88.7 15.6 %collective-permute-start.28 = (bf16[32,32,128]{2,1,0:T(8,128)(2,1)S(1)}, bf16[32,32,128]{2,1,0:T(8,128)(2,1)S(1)}, u32[]{:S(2)}, u32[]{:S(2)}) collective-permute-start(bf16[32,32,128]{2,1,0:T(8,128)(2,1)S(1)} %collective-permute-done.24), channel_id=1, source_target_pairs={{0,1},{1,2},{2,3},{3,11},{11,10},{10,9},{9,8},{8,0},{4,5},{5,6},{6... | collective-permute-start | bytes 786440 | tf_op jit(solution)/shard_map/ppermute | solution.py:337
  91.0 14.6 %collective-permute-start.29 = (bf16[32,32,128]{2,1,0:T(8,128)(2,1)S(1)}, bf16[32,32,128]{2,1,0:T(8,128)(2,1)S(1)}, u32[]{:S(2)}, u32[]{:S(2)}) collective-permute-start(bf16[32,32,128]{2,1,0:T(8,128)(2,1)S(1)} %collective-permute-done.27), channel_id=1, source_target_pairs={{1,0},{2,1},{3,2},{11,3},{10,11},{9,10},{8,9},{0,8},{5,4},{6,5},{7... | collective-permute-start | bytes 786440 | tf_op jit(solution)/shard_map/ppermute | solution.py:337
  94.3 23.0 %collective-permute-start.14 = (bf16[32,32,128]{2,1,0:T(8,128)(2,1)S(1)}, bf16[32,32,128]{2,1,0:T(8,128)(2,1)S(1)}, u32[]{:S(2)}, u32[]{:S(2)}) collective-permute-start(bf16[32,32,128]{2,1,0:T(8,128)(2,1)S(1)} %collective-permute-done.10), channel_id=1, source_target_pairs={{0,1},{1,2},{2,3},{3,11},{11,10},{10,9},{9,8},{8,0},{4,5},{5,6},{6... | collective-permute-start | bytes 786440 | tf_op jit(solution)/shard_map/ppermute | solution.py:337
  99.9 18.2 %collective-permute-start.15 = (bf16[32,32,128]{2,1,0:T(8,128)(2,1)S(1)}, bf16[32,32,128]{2,1,0:T(8,128)(2,1)S(1)}, u32[]{:S(2)}, u32[]{:S(2)}) collective-permute-start(bf16[32,32,128]{2,1,0:T(8,128)(2,1)S(1)} %collective-permute-done.13), channel_id=1, source_target_pairs={{1,0},{2,1},{3,2},{11,3},{10,11},{9,10},{8,9},{0,8},{5,4},{6,5},{7... | collective-permute-start | bytes 786440 | tf_op jit(solution)/shard_map/ppermute | solution.py:337
  105.6 2.0 copy-start
  129.3 4.4 %collective-permute-start.30 = (f32[128,32,128]{2,1,0:T(8,128)}, f32[128,32,128]{2,1,0:T(8,128)S(1)}, u32[]{:S(2)}, u32[]{:S(2)}) collective-permute-start(f32[128,32,128]{2,1,0:T(8,128)} %shard_map.58.refs_0_), channel_id=1, source_target_pairs={{0,4},{4,0},{1,5},{5,1},{2,6},{6,2},{3,7},{7,3},{8,12},{12,8},{9,1... | collective-permute-start | bytes 6291464 | tf_op jit(solution)/shard_map/ppermute | solution.py:303
  133.7 1.4 copy-start.3
  152.8 3.0 %copy-start.2 = (f32[128,32,128]{2,1,0:T(8,128)S(1)}, f32[128,32,128]{2,1,0:T(8,128)}, u32[]{:S(2)}) copy-start(f32[128,32,128]{2,1,0:T(8,128)} %shard_map.58.refs_0_) | copy-start | bytes 6291460
  152.8 4.1 %copy-start.4 = (f32[128,32,128]{2,1,0:T(8,128)S(1)}, f32[128,32,128]{2,1,0:T(8,128)}, u32[]{:S(2)}) copy-start(f32[128,32,128]{2,1,0:T(8,128)} %copy-done.3) | copy-start | bytes 6291460
  155.7 5.5 %collective-permute-start.31 = (f32[64,32,128]{2,1,0:T(8,128)S(1)}, f32[64,32,128]{2,1,0:T(8,128)S(1)}, u32[]{:S(2)}, u32[]{:S(2)}) collective-permute-start(f32[64,32,128]{2,1,0:T(8,128)S(1)} %bitcast.240), channel_id=1, source_target_pairs={{0,4},{4,0},{1,5},{5,1},{2,6},{6,2},{3,7},{7,3},{8,12},{12,8},{9,1... | collective-permute-start | bytes 3145736 | tf_op jit(solution)/shard_map/ppermute | solution.py:303
  161.3 1.0 copy-start.5
  188.1 1.6 collective-permute-start.32
  190.6 5.6 %collective-permute-start.33 = (f32[2,128,128]{2,1,0:T(8,128)S(1)}, f32[2,128,128]{2,1,0:T(8,128)S(1)}, u32[]{:S(2)}, u32[]{:S(2)}) collective-permute-start(f32[2,128,128]{2,1,0:T(8,128)S(1)} %add.237), channel_id=1, source_target_pairs={{0,8},{8,0},{1,9},{9,1},{2,10},{10,2},{3,11},{11,3},{4,12},{12,4},... | collective-permute-start | bytes 393224 | tf_op jit(solution)/shard_map/ppermute | solution.py:350
  196.2 6.6 %collective-permute-start.34 = (f32[2,128,128]{2,1,0:T(8,128)S(1)}, f32[2,128,128]{2,1,0:T(8,128)S(1)}, u32[]{:S(2)}, u32[]{:S(2)}) collective-permute-start(f32[2,128,128]{2,1,0:T(8,128)S(1)} %add.238), channel_id=1, source_target_pairs={{0,1},{1,0},{2,3},{3,2},{4,5},{5,4},{6,7},{7,6},{8,9},{9,8},{10,11... | collective-permute-start | bytes 393224 | tf_op jit(solution)/shard_map/ppermute | solution.py:353
  196.3 12.7 %collective-permute-start.35 = (f32[2,128,128]{2,1,0:T(8,128)S(1)}, f32[2,128,128]{2,1,0:T(8,128)S(1)}, u32[]{:S(2)}, u32[]{:S(2)}) collective-permute-start(f32[2,128,128]{2,1,0:T(8,128)S(1)} %add.238), channel_id=1, source_target_pairs={{0,2},{1,3},{2,0},{3,1},{4,6},{5,7},{6,4},{7,5},{8,10},{9,11},{10,... | collective-permute-start | bytes 393224 | tf_op jit(solution)/shard_map/ppermute | solution.py:353
  196.8 12.3 %collective-permute-start.36 = (f32[2,128,128]{2,1,0:T(8,128)S(1)}, f32[2,128,128]{2,1,0:T(8,128)S(1)}, u32[]{:S(2)}, u32[]{:S(2)}) collective-permute-start(f32[2,128,128]{2,1,0:T(8,128)S(1)} %add.238), channel_id=1, source_target_pairs={{0,3},{1,2},{2,1},{3,0},{4,7},{5,6},{6,5},{7,4},{8,11},{9,10},{10,... | collective-permute-start | bytes 393224 | tf_op jit(solution)/shard_map/ppermute | solution.py:353

commit v3 on v2

v3 whole, which is shorter than its diff:
```python
import functools
import math

import jax
import jax.numpy as jnp
from jax import lax
from jax.experimental import pallas as pl
from jax.experimental.pallas import tpu as pltpu
from jax.sharding import Mesh
from jax.sharding import PartitionSpec as P

ITERS = 2
BF16 = jnp.bfloat16
F32 = jnp.float32
VMEM_BYTES = 56 * 1024 * 1024
HIGH = lax.Precision.HIGHEST


def rolled(value, shift):
    return pltpu.roll(value, shift % value.shape[-1], 1)


def apply_kernel(n_vec, z_count, own, offsets, *refs):
    place_ref, *refs = refs
    vec_refs = (refs[:n_vec], refs[n_vec : 2 * n_vec])
    piece_refs = refs[2 * n_vec : 2 * n_vec + len(offsets)]
    cov_ref, spec_ref, mine_ref, theirs_ref, beam_ref, vec_ref, *tiles, sems = refs[2 * n_vec + len(offsets) :]
    z_refs, y_refs = tiles[: len(tiles) // 2], tiles[len(tiles) // 2 :]
    out_refs = (mine_ref, theirs_ref)
    count, rows, lanes = mine_ref.shape
    freqs = 2 * count
    half = rows // 2
    components = spec_ref.shape[0]
    size, width, depth = piece_refs[0].shape
    chips = count // size * z_count
    step = depth // len(z_refs)
    lane = lax.broadcasted_iota(jnp.int32, (half, lanes), 1)
    is_real = (lane // own) % 2 == 0
    sign = jnp.where(is_real, -1.0, 1.0).astype(F32)

    copies = []
    for index, (core, offset) in enumerate(offsets):
        at = lax.rem(place_ref[0] + (offset % chips), chips)
        x_at = at // z_count
        z_at = jnp.where(x_at == 0, at, chips - 1 - at)
        target = beam_ref.at[
            pl.ds(core * count + x_at * size, size), pl.ds(pl.multiple_of(z_at * width, width), width)
        ]
        copies.append(pltpu.make_async_copy(piece_refs[index], target, sems.at[index]))
    for copy in copies:
        copy.start()

    def gather(side, place, carry):
        vec = vec_refs[side][0][place]
        for other in vec_refs[side][1:]:
            vec = vec + other[place]
        vec_ref[side * count + place] = vec.astype(BF16)
        return carry

    for side in range(2):
        lax.fori_loop(0, count, functools.partial(gather, side), 0, unroll=8)
    for copy in copies:
        copy.wait()

    def project(freq, carry):
        z = jnp.dot(vec_ref[freq], beam_ref[freq], preferred_element_type=F32)
        for tile, z_ref in enumerate(z_refs):
            z_ref[pl.ds(freq, rows, stride=freqs), :] = z[:, tile * step : (tile + 1) * step]
        return carry

    lax.fori_loop(0, freqs, project, 0, unroll=32)

    def mix(row, carry):
        start = pl.multiple_of(row * freqs, freqs)
        z = jnp.concatenate([z_ref[pl.ds(start, freqs), :] for z_ref in z_refs], axis=1)
        scaled = [(z * spec_ref[k][None, :]).astype(BF16) for k in range(components)]
        y = jnp.dot(cov_ref[...], jnp.concatenate(scaled, axis=0), preferred_element_type=F32)
        for tile, y_ref in enumerate(y_refs):
            y_ref[pl.ds(start, freqs), :] = y[:, tile * step : (tile + 1) * step]
        return carry

    lax.fori_loop(0, rows, mix, 0, unroll=8)

    def expand(side, place, carry):
        freq = side * count + place
        y = [y_ref[pl.ds(freq, rows, stride=freqs), :].astype(BF16) for y_ref in y_refs]
        product = lax.dot_general(
            jnp.concatenate(y, axis=1),
            beam_ref[freq],
            (((1,), (1,)), ((), ())),
            preferred_element_type=F32,
        )
        swapped = jnp.where(
            jnp.concatenate([is_real, is_real], axis=0),
            rolled(product, -own),
            rolled(product, own),
        )
        top = product[:half] + sign * swapped[half:]
        bottom = product[half:] - sign * swapped[:half]
        out_refs[side][place] = jnp.concatenate([top, bottom], axis=0)
        return carry

    for side in range(2):
        lax.fori_loop(0, count, functools.partial(expand, side), 0, unroll=32)


def apply_covariance(place, vecs, beams, cov, spec, own, z_count):
    count, rows, lanes = vecs[0][0].shape
    freqs = 2 * count
    depth = spec.shape[1]
    step = min(depth, 128)
    flops = 2 * freqs * rows * (2 * lanes * depth + 2 * freqs * depth)
    vmem = pl.BlockSpec(memory_space=pltpu.VMEM)
    n_vec = len(vecs[0])
    offsets = tuple((core, offset) for _, core, offset in beams)
    tile = pltpu.VMEM((rows * freqs, step), F32)
    return pl.pallas_call(
        functools.partial(apply_kernel, n_vec, z_count, own, offsets),
        out_shape=[jax.ShapeDtypeStruct((count, rows, lanes), F32)] * 2,
        in_specs=[pl.BlockSpec(memory_space=pltpu.SMEM)]
        + [vmem] * (2 * n_vec)
        + [pl.BlockSpec(memory_space=pl.ANY)] * len(beams)
        + [vmem] * 2,
        out_specs=[vmem] * 2,
        scratch_shapes=[
            pltpu.VMEM((freqs, lanes, depth), BF16),
            pltpu.VMEM((freqs, rows, lanes), BF16),
            *[tile] * (2 * depth // step),
            pltpu.SemaphoreType.DMA((len(beams),)),
        ],
        compiler_params=pltpu.CompilerParams(vmem_limit_bytes=VMEM_BYTES),
        cost_estimate=pl.CostEstimate(
            flops=flops, bytes_accessed=freqs * lanes * depth * 2, transcendentals=0
        ),
    )(place, *vecs[0], *vecs[1], *[piece for piece, _, _ in beams], cov, spec)


def pack_kernel(own, *refs):
    out_ref = refs[-1]
    x_count, z_count, images, groups = out_ref.shape[:4]
    freqs, rows, lanes = refs[0].shape
    per_group = lanes // own
    lane = lax.broadcasted_iota(jnp.int32, (rows, lanes), 1) // own

    def group(step, index, carry):
        x_index, group_index = index // groups, index % groups
        totals = [jnp.zeros((rows, lanes), F32)] * z_count
        for place in range(per_group):
            freq = index * per_group + place
            image = refs[2 * step][freq] + refs[2 * step + 1][freq]
            for z_index in range(z_count):
                moved = rolled(image, (place - 2 * z_index) * own)
                totals[z_index] = jnp.where(lane == place, moved, totals[z_index])
        for z_index in range(z_count):
            out_ref[x_index, z_index, step, group_index] = totals[z_index].astype(BF16)
        return carry

    for step in range(images):
        lax.fori_loop(0, x_count * groups, functools.partial(group, step), 0)


def pack(pairs, x_count, z_count, own):
    freqs, rows, lanes = pairs[0][0].shape
    groups = freqs * own // (x_count * lanes)
    flat = [part for pair in pairs for part in pair]
    return pl.pallas_call(
        functools.partial(pack_kernel, own),
        out_shape=jax.ShapeDtypeStruct((x_count, z_count, len(pairs), groups, rows, lanes), BF16),
        in_specs=[pl.BlockSpec(memory_space=pltpu.VMEM)] * len(flat),
        out_specs=pl.BlockSpec(memory_space=pltpu.VMEM),
        compiler_params=pltpu.CompilerParams(vmem_limit_bytes=VMEM_BYTES),
    )(*flat)


def gram_kernel(core_ref, rows_ref, keep_ref, send_ref):
    senders, images, groups, parts, vectors, lanes = rows_ref.shape
    total = senders * vectors
    found = []
    for image in range(images):
        gram = jnp.zeros((total, total), F32)
        for group in range(groups):
            for part in range(parts):
                flat = rows_ref[:, image, group, part].reshape(total, lanes)
                gram += lax.dot_general(
                    flat, flat, (((1,), (1,)), ((), ())), preferred_element_type=F32
                )
        found.append(gram)
    is_first = core_ref[0] == 0
    keep_ref[...] = jnp.where(is_first, found[0], found[1])
    send_ref[...] = jnp.where(is_first, found[1], found[0])


def grams(core, rows):
    total = rows.shape[0] * rows.shape[4]
    return pl.pallas_call(
        gram_kernel,
        out_shape=[jax.ShapeDtypeStruct((total, total), F32)] * 2,
        in_specs=[pl.BlockSpec(memory_space=pltpu.SMEM), pl.BlockSpec(memory_space=pltpu.VMEM)],
        out_specs=[pl.BlockSpec(memory_space=pltpu.VMEM)] * 2,
        compiler_params=pltpu.CompilerParams(vmem_limit_bytes=VMEM_BYTES),
    )(core, rows)


def inverse_factor(work_ref, matrix):
    order = matrix.shape[0]
    step = 8
    row = lax.broadcasted_iota(jnp.int32, (step, order), 0)
    lane = lax.broadcasted_iota(jnp.int32, (step, order), 1)
    at = lax.broadcasted_iota(jnp.int32, (order, order), 0)
    work_ref[:, :order] = matrix
    work_ref[:, order:] = jnp.where(at == lax.broadcasted_iota(jnp.int32, (order, order), 1), 1.0, 0.0)
    for begin in range(0, order, step):
        block = slice(begin, begin + step)
        left, right = work_ref[block, :order], work_ref[block, order:]
        columns = [
            jnp.broadcast_to(left[:, begin + k : begin + k + 1], (step, order)) for k in range(step)
        ]
        for k in range(step):
            root = lax.rsqrt(columns[k][k : k + 1])
            factor = columns[k] * root

            def eliminate(value):
                pivot = value[k : k + 1] * root
                return jnp.where(row == k, pivot, jnp.where(row > k, value - factor * pivot, value))

            left, right = eliminate(left), eliminate(right)
            columns = columns[: k + 1] + [eliminate(c) for c in columns[k + 1 :]]
        work_ref[block, order:] = right
        after = begin + step
        if after < order:
            kept = jnp.where(lane >= after, left, 0.0)
            change = lax.dot_general(
                kept,
                jnp.concatenate([kept, right], axis=1),
                (((0,), (0,)), ((), ())),
                precision=HIGH,
                preferred_element_type=F32,
            )
            work_ref[after:, :] = work_ref[after:, :] - change[after:]
    return work_ref[:, order:]


def finish_kernel(scale, core_ref, rows_ref, kept_ref, given_ref, out_ref, work_ref):
    senders, groups, parts, vectors, lanes = rows_ref.shape
    total = senders * vectors
    exact = functools.partial(lax.dot_general, precision=HIGH, preferred_element_type=F32)
    across = (((1,), (1,)), ((), ()))
    plain = (((1,), (0,)), ((), ()))
    is_first = core_ref[0] == 0
    first = inverse_factor(work_ref, jnp.where(is_first, kept_ref[...], given_ref[...]))
    gram_second = jnp.where(is_first, given_ref[...], kept_ref[...])
    gram_second = exact(exact(first, gram_second, plain), first, across)
    second = inverse_factor(work_ref, gram_second)
    mixing = exact(second, first, plain) * scale
    high = mixing.astype(BF16)
    rest = mixing - high.astype(F32)
    middle = rest.astype(BF16)
    low = (rest - middle.astype(F32)).astype(BF16)
    for group in range(groups):
        for part in range(parts):
            flat = rows_ref[:, group, part].reshape(total, lanes)
            turned = flat.astype(F32).T.astype(BF16)
            dot = functools.partial(
                lax.dot_general, turned, dimension_numbers=across, preferred_element_type=F32
            )
            out_ref[part, group] = (dot(low) + dot(middle)) + dot(high)


def finish(core, rows, kept, given, scale):
    senders, groups, parts, vectors, lanes = rows.shape
    total = senders * vectors
    return pl.pallas_call(
        functools.partial(finish_kernel, scale),
        out_shape=jax.ShapeDtypeStruct((parts, groups, lanes, total), F32),
        in_specs=[pl.BlockSpec(memory_space=pltpu.SMEM)] + [pl.BlockSpec(memory_space=pltpu.VMEM)] * 3,
        out_specs=pl.BlockSpec(memory_space=pltpu.VMEM),
        scratch_shapes=[pltpu.VMEM((total, 2 * total), F32)],
        compiler_params=pltpu.CompilerParams(vmem_limit_bytes=VMEM_BYTES),
    )(core, rows, kept, given)


def turn_kernel(start_ref, out_ref):
    parts, freqs, own, vectors = start_ref.shape
    receivers, groups, mine, lanes = out_ref.shape
    per_group = lanes // (parts * own)

    def group(index, carry):
        tiles = [
            start_ref[part, index * per_group + place]
            for place in range(per_group)
            for part in range(parts)
        ]
        turned = jnp.concatenate(tiles, axis=0).T
        out_ref[:, index] = turned.reshape(receivers, mine, lanes).astype(BF16)
        return carry

    lax.fori_loop(0, groups, group, 0)


def turn(start, receivers, lanes):
    parts, freqs, own, vectors = start.shape
    groups = parts * freqs * own // lanes
    return pl.pallas_call(
        turn_kernel,
        out_shape=jax.ShapeDtypeStruct((receivers, groups, vectors // receivers, lanes), BF16),
        in_specs=[pl.BlockSpec(memory_space=pltpu.VMEM)],
        out_specs=pl.BlockSpec(memory_space=pltpu.VMEM),
        compiler_params=pltpu.CompilerParams(vmem_limit_bytes=VMEM_BYTES),
    )(start)


def operand_kernel(own, *refs):
    x_count, z_count, groups, mine, lanes = refs[0].shape
    parts = lanes // (z_count * own)
    width = parts * own
    lane = lax.broadcasted_iota(jnp.int32, (mine, lanes), 1)
    is_real = (lane // own) % 2 == 0

    def group(side, index, carry):
        x_index, at = index // groups, index % groups
        tiles = [refs[side][x_index, z, at].astype(F32) for z in range(z_count)]
        for place in range(z_count):
            top = tiles[0]
            for z in range(z_count):
                top = jnp.where(lane // width == z, rolled(tiles[z], (z - place) * width), top)
            bottom = jnp.where(is_real, rolled(top, -own), -rolled(top, own))
            image = jnp.concatenate([top, bottom], axis=0).astype(BF16)
            refs[2 + side][index * z_count + place] = image
        return carry

    for side in range(2):
        lax.fori_loop(0, x_count * groups, functools.partial(group, side), 0, unroll=2)


def start_operand(sides, own):
    x_count, z_count, groups, mine, lanes = sides[0].shape
    freqs = x_count * groups * z_count
    return pl.pallas_call(
        functools.partial(operand_kernel, own),
        out_shape=[jax.ShapeDtypeStruct((freqs, 2 * mine, lanes), BF16)] * 2,
        in_specs=[pl.BlockSpec(memory_space=pltpu.VMEM)] * 2,
        out_specs=[pl.BlockSpec(memory_space=pltpu.VMEM)] * 2,
        compiler_params=pltpu.CompilerParams(vmem_limit_bytes=VMEM_BYTES),
    )(*sides)


def swap_cores(value):
    return lax.ppermute(value, "core", [(0, 1), (1, 0)])


def after(value, event):
    return lax.optimization_barrier((value, event))


def gather_ring(blocks, late, x_count, z_count):
    count = x_count * z_count
    ring = [k if k < z_count else z_count + count - 1 - k for k in range(count)]
    pairs = {
        1: [(ring[k], ring[(k + 1) % count]) for k in range(count)],
        -1: [(ring[(k + 1) % count], ring[k]) for k in range(count)],
    }
    x_place, z_place = lax.axis_index("x"), lax.axis_index("fc")
    place = jnp.where(x_place == 0, z_place, count - 1 - z_place).astype(jnp.int32).reshape(1)
    moving = {(core, way): block for core, block in enumerate(blocks) for way in (1, -1)}
    found = [(block, core, 0) for core, block in enumerate(blocks)]
    for hop in range(1, count // 2 + 1):
        for core, way in moving:
            if 2 * hop == count and (way == 1) != (core == 0):
                continue
            moving[core, way] = lax.ppermute(moving[core, way], ("x", "fc"), pairs[way])
            if hop == 1 and core == 0 and way == 1:
                late, moving[core, way] = after(late, moving[core, way])
            found.append((moving[core, way], core, -way * hop))
    return place, found, late


def sum_devices(keep, send, z_count):
    value = keep + swap_cores(send)
    value = value + lax.ppermute(value, "x", [(0, 1), (1, 0)])
    if z_count & (z_count - 1):
        value = lax.psum(value, "fc")
    else:
        terms = [value] + [
            lax.ppermute(value, "fc", [(j, j ^ s) for j in range(z_count)]) for s in range(1, z_count)
        ]
        while len(terms) > 1:
            terms = [terms[i] + terms[i + 1] for i in range(0, len(terms), 2)]
        value = terms[0]
    return value, swap_cores(value)


def body_split(x_count, z_count, beam_transfer, noise_var, spectra, freq_covariance, start_vectors):
    parts, freqs, own, multipoles = beam_transfer.shape
    vectors = start_vectors.shape[3]
    cores = 2
    core = lax.axis_index("core")
    all_freqs = x_count * cores * freqs
    mine_vectors = vectors // (x_count * z_count)
    depth = multipoles // cores

    whitened = (beam_transfer.astype(F32) * lax.rsqrt(noise_var)[None, :, :, None]).astype(BF16)
    rows = whitened.transpose(1, 0, 2, 3).reshape(freqs, parts * own, cores, depth)
    rows = rows.transpose(2, 0, 1, 3)
    kept = lax.dynamic_index_in_dim(rows, core, 0, False)
    given = swap_cores(lax.dynamic_index_in_dim(rows, 1 - core, 0, False))
    start = turn(start_vectors, x_count * z_count, z_count * parts * own)
    place, beams, start = gather_ring([kept, given], start, x_count, z_count)

    spec = spectra.reshape(-1, cores, depth)
    spec = lax.dynamic_index_in_dim(spec, core, 1, False)
    cov = freq_covariance.reshape(-1, x_count, cores, freqs, x_count, cores, freqs).astype(BF16)
    cov = jnp.where(core == 0, cov, jnp.flip(cov, (2, 5)))
    cov = cov.transpose(2, 1, 3, 0, 5, 4, 6).reshape(all_freqs, -1)

    start = lax.all_to_all(start, ("x", "fc"), 0, 0, tiled=True)
    start = start.reshape(x_count, z_count, *start.shape[1:])
    operand = start_operand([start, swap_cores(start)], own)

    mine, theirs = apply_covariance(
        place, [[operand[0]], [operand[1]]], beams, cov, spec, own, z_count
    )
    got_mine, got_theirs = swap_cores(theirs), swap_cores(mine)
    second_mine, second_theirs = apply_covariance(
        place, [[mine, got_mine], [theirs, got_theirs]], beams, cov, spec, own, z_count
    )
    packed = pack(
        [(mine, got_mine), (second_mine, swap_cores(second_theirs))], x_count, z_count, own
    )
    packed = packed.reshape(x_count * z_count, *packed.shape[2:])
    received = lax.all_to_all(packed, ("x", "fc"), 0, 0, tiled=True)
    groups, lanes = received.shape[2], received.shape[4]
    received = received.reshape(-1, ITERS, groups, parts, mine_vectors, lanes)

    core_index = core.astype(jnp.int32).reshape(1)
    kept_gram, given_gram = sum_devices(*grams(core_index, received), z_count)
    scale = math.sqrt(2.0 * all_freqs * z_count * own)
    basis = finish(core_index, received[:, 1], kept_gram, given_gram, scale)
    return basis.reshape(parts, freqs, own, vectors)


def row_operands(row_part, spectra):
    scaled = (row_part.astype(F32)[None] * spectra[:, None, None, :]).astype(BF16)
    real_rows = jnp.concatenate([scaled[:, 0], scaled[:, 1]], axis=-1)
    imag_rows = jnp.concatenate([scaled[:, 1], -scaled[:, 0]], axis=-1)
    return jnp.stack([real_rows, imag_rows], axis=1)


def apply_tile(pair_tile, vec_bf):
    row_count = pair_tile.shape[1]
    stacked = pair_tile.reshape(2 * row_count, pair_tile.shape[2])
    with_real = jnp.dot(stacked, vec_bf[0], preferred_element_type=F32)
    with_imag = jnp.dot(stacked, vec_bf[1], preferred_element_type=F32)
    real_part = with_real[:row_count] - with_imag[row_count:]
    imag_part = with_real[row_count:] + with_imag[:row_count]
    return jnp.stack([real_part, imag_part], axis=0)


def partial_gram(image):
    flat = image.reshape(-1, image.shape[-1])
    return jnp.dot(flat.T, flat, precision=HIGH, preferred_element_type=F32)


def orthonormalize(image, gram_matrix):
    lower = jnp.linalg.cholesky(gram_matrix)
    flat = image.reshape(-1, image.shape[-1])
    solved = lax.linalg.triangular_solve(lower, flat, left_side=False, lower=True, transpose_a=True)
    return solved.reshape(image.shape)


def body_general(beam_transfer, noise_var, spectra, freq_covariance, start_vectors):
    row_axes = ("x", "core")
    whitened = (beam_transfer.astype(F32) * lax.rsqrt(noise_var)[None, :, :, None]).astype(BF16)
    row_beams = lax.all_gather(whitened, "fc", axis=2, tiled=True)
    _, freq_rows, mode_count, multipoles = row_beams.shape
    row_total = freq_rows * mode_count
    components = spectra.shape[0]
    vectors_count = start_vectors.shape[3]
    row_operand = row_operands(row_beams.reshape(2, row_total, multipoles), spectra)
    row_start = lax.axis_index(row_axes) * freq_rows
    row_cov = lax.dynamic_slice_in_dim(freq_covariance, row_start, freq_rows, 1)
    piece = lax.all_gather(whitened, row_axes, axis=1, tiled=True)
    _, piece_freqs, piece_modes, _ = piece.shape
    columns = piece.reshape(2, piece_freqs * piece_modes, multipoles)
    col_operand = jnp.concatenate([columns[0], columns[1]], axis=-1)
    products = lax.dot_general(
        row_operand, col_operand, (((3,), (1,)), ((), ())), preferred_element_type=F32
    )
    weight = jnp.broadcast_to(
        row_cov[:, :, None, :, None], (components, freq_rows, mode_count, piece_freqs, piece_modes)
    )
    weight = weight.reshape(components, row_total, piece_freqs * piece_modes)
    pair_tile = jnp.einsum("kxy,kcxy->cxy", weight, products).astype(BF16)
    vectors = start_vectors
    own_modes = start_vectors.shape[2]
    for _ in range(ITERS):
        gathered = lax.all_gather(vectors.astype(BF16), row_axes, axis=1, tiled=True)
        vec_bf = gathered.reshape(2, -1, vectors_count)
        partial_value = apply_tile(pair_tile, vec_bf).reshape(2, freq_rows, mode_count, vectors_count)
        summed = lax.psum(partial_value, "fc")
        gram_matrix = lax.psum(partial_gram(summed), row_axes)
        own_rows = lax.dynamic_slice_in_dim(summed, lax.axis_index("fc") * own_modes, own_modes, 2)
        vectors = orthonormalize(own_rows, gram_matrix)
    return vectors * math.sqrt(2.0 * piece_freqs * mode_count)


def body(x_count, z_count, *args):
    beam_transfer, start_vectors = args[0], args[4]
    parts, freqs, own, multipoles = beam_transfer.shape
    vectors = start_vectors.shape[3]
    lanes = parts * own * z_count
    fits = (
        x_count == 2
        and vectors % (16 * x_count * z_count) == 0
        and lanes == 128
        and own % 16 == 0
        and multipoles % 256 == 0
        and (freqs * own) % lanes == 0
    )
    if fits:
        return body_split(x_count, z_count, *args)
    return body_general(*args)


def solution(mesh):
    sizes = dict(mesh.shape)
    x_count = sizes["fr"] // 2
    shape = (sizes["ma"], x_count, 2, sizes["fc"])
    devices = mesh.devices.reshape(shape)
    split = Mesh(devices, ("ma", "x", "core", "fc"))
    rows = ("ma", "x", "core")
    in_specs = (
        P(None, rows, "fc", None),
        P(rows, "fc"),
        P(),
        P(),
        P(None, rows, "fc", None),
    )
    return jax.shard_map(
        functools.partial(body, x_count, sizes["fc"]),
        mesh=split,
        in_specs=in_specs,
        out_specs=P(None, rows, "fc", None),
        check_vma=False,
    )
```

time: 230 us -> 200 us (0.87)
  local copies, waits for them, and re-layouts: 31.8 us -> 12.7 us
  Pallas kernels: 73.5 us -> 63.6 us
  other arithmetic: 7.1 us -> 2.63 us
  blocking collectives: 19.3 us -> 22 us
    dynamic_update_slice x28 -> x0, local copies, waits for them, and re-layouts: 11.5 us -> none  [put(): lax.dynamic_update_slice(wholes[chunk], piece[None, None, :, None], (x_at...]
    pallas_call x5 -> x4, Pallas kernels: 45.1 us -> 36.8 us  [the longest x2 29.8 us: apply_covariance(): pl.pallas_call(functools.partial(apply_kernel, n_vec, z_count, own, offse...]
    ppermute x28 -> x14, waiting for transfers between devices: 39.8 us -> 47.1 us  [gather_ring(): moving[core, way] = lax.ppermute(moving[core, way], ('x', 'fc'), pairs[way])]
    all_to_all x1, waiting for transfers between devices: 7.44 us -> 2.41 us  [body_split(): start = lax.all_to_all(start, ('x', 'fc'), 0, 0, tiled=True)]
    dynamic_slice x3 -> x0, local copies, waits for them, and re-layouts: 4.98 us -> none  [of_core(): lax.dynamic_index_in_dim(split, which, 1, False)]
    ppermute x3, waiting for transfers between devices: 7.64 us -> 3.07 us  [sum_devices(): lax.ppermute(value, 'fc', [(j, j ^ s) for j in range(z_count)])]
    unnamed x16 -> x32, local copies, waits for them, and re-layouts: 6.39 us -> 3.61 us
    all_to_all x1, blocking collectives: 19.3 us -> 22 us  [body_split(): received = lax.all_to_all(packed, ('x', 'fc'), 0, 0, tiled=True)]
  transfers between devices with their start and end apart: 38 -> 26, of which waited for: 26 -> 15; matrix products, arithmetic and copies ran while one was open for 10% -> 2% of each run, Pallas kernels for 9% -> 4%
where the time goes in v3:
time: 200 us
  waiting for transfers between devices  64.3 us (32%)
  Pallas kernels  63.6 us (32%)
  starting transfers between devices  34.1 us (17%)
  blocking collectives  22 us (11%)
  local copies, waits for them, and re-layouts  12.7 us (6%)
  other arithmetic  2.63 us (1%)
    ppermute x14, waiting for transfers between devices, gather_ring(): moving[core, way] = lax.ppermute(moving[core, way], ('x', 'fc'), pairs[way])  47.1 us
    pallas_call x2, Pallas kernels, apply_covariance(): pl.pallas_call(functools.partial(apply_kernel, n_vec, z_count, own, offse...  29.8 us
    all_to_all x1, blocking collectives, body_split(): received = lax.all_to_all(packed, ('x', 'fc'), 0, 0, tiled=True)  22 us
    ppermute x14, starting transfers between devices, gather_ring(): moving[core, way] = lax.ppermute(moving[core, way], ('x', 'fc'), pairs[way])  21 us
    pallas_call x1, Pallas kernels, finish(): pl.pallas_call(functools.partial(finish_kernel, scale), out_shape=jax.Sha...  19.3 us
    ppermute x7, waiting for transfers between devices, swap_cores(): return lax.ppermute(value, 'core', [(0, 1), (1, 0)])  8.59 us
    all_to_all x1, starting transfers between devices, body_split(): start = lax.all_to_all(start, ('x', 'fc'), 0, 0, tiled=True)  6.08 us
    pallas_call x1, Pallas kernels, pack(): pl.pallas_call(functools.partial(pack_kernel, own), out_shape=jax.ShapeDt...  5.07 us
  transfers between devices with their start and end apart: 26, of which 15 were waited for; matrix products, arithmetic and copies ran while one was open for 2% of the time, Pallas kernels for 4%

profile of v3, /device:TPU:0, one launch (start us, length us, event | category | flops | bytes accessed | tf_op | source)
XLA Modules:
  0.0 199.5 jit_solution(16487806324331998365)
XLA Ops:
  0.0 0.7 rsqrt.3
  0.7 0.1 copy.26
  0.8 1.5 fusion
  2.3 0.3 reshape.36
  2.6 3.7 %constant_dynamic-slice_fusion = (bf16[32,32,1,256]{3,2,1,0:T(2,128)(2,1)S(1)}, bf16[32,32,1,256]{3,2,1,0:T(2,128)(2,1)S(1)}) fusion(bf16[32,32,2,256]{3,2,1,0:T(2,128)(2,1)S(1)} %reshape.36, s32[]{:T(128)S(6)} %select_n.23, s32[]{:T(128)S(6)} %select_n.22), kind=kLoop, calls=%fused_computation.9 | loop fusion | bytes 2097160 | tf_op jit(solution)/shard_map/dynamic-slice.1
  6.4 0.1 copy.38
  6.5 0.5 collective-permute-start.2
  7.0 0.1 copy.39
  7.2 2.6 %collective-permute-start = (bf16[32,32,256]{2,1,0:T(8,128)(2,1)S(1)}, bf16[32,32,256]{2,1,0:T(8,128)(2,1)S(1)}, u32[]{:S(2)}, u32[]{:S(2)}) collective-permute-start(bf16[32,32,256]{2,1,0:T(8,128)(2,1)S(1)} %bitcast.26), channel_id=1, source_target_pairs={{0,1},{1,2},{2,3},{3,11},{11,10},{10,9},{9,8},{8,0},{4,5},{5,6},{6... | collective-permute-start | bytes 1572872 | tf_op jit(solution)/shard_map/ppermute | solution.py:370
  9.8 1.6 collective-permute-start.5
  11.4 1.6 collective-permute-start.3
  13.0 2.6 %shard_map.55 = bf16[8,8,16,128]{3,2,1,0:T(8,128)(2,1)} custom-call(f32[2,32,16,128]{3,2,1,0:T(8,128)} %start_ref.1), custom_call_target="tpu_custom_call" | custom-call | tf_op jit(solution)/shard_map/pallas_call | solution.py:303
  15.5 6.8 %collective-permute-done.refs_5_.refs_7_ = bf16[32,32,256]{2,1,0:T(8,128)(2,1)S(1)} collective-permute-done((bf16[32,32,256]{2,1,0:T(8,128)(2,1)S(1)}, bf16[32,32,256]{2,1,0:T(8,128)(2,1)S(1)}, u32[]{:S(2)}, u32[]{:S(2)}) %collective-permute-start) | collective-permute-done | bytes 524320 | tf_op jit(solution)/shard_map/ppermute | solution.py:370
  22.3 1.8 collective-permute-start.6
  24.1 1.6 collective-permute-start.4
  25.7 0.5 collective-permute-start.9
  26.2 9.6 %collective-permute-done.3.refs_6_.refs_8_ = bf16[32,32,256]{2,1,0:T(8,128)(2,1)S(1)} collective-permute-done((bf16[32,32,256]{2,1,0:T(8,128)(2,1)S(1)}, bf16[32,32,256]{2,1,0:T(8,128)(2,1)S(1)}, u32[]{:S(2)}, u32[]{:S(2)}) %collective-permute-start.3) | collective-permute-done | bytes 524320 | tf_op jit(solution)/shard_map/ppermute | solution.py:370
  35.8 1.6 collective-permute-start.7
  37.4 1.5 collective-permute-start.10
  39.0 9.5 %collective-permute-done.4.refs_7_.refs_9_ = bf16[32,32,256]{2,1,0:T(8,128)(2,1)} collective-permute-done((bf16[32,32,256]{2,1,0:T(8,128)(2,1)S(1)}, bf16[32,32,256]{2,1,0:T(8,128)(2,1)}, u32[]{:S(2)}, u32[]{:S(2)}) %collective-permute-start.4) | collective-permute-done | bytes 524320 | tf_op jit(solution)/shard_map/ppermute | solution.py:370
  48.4 1.9 collective-permute-start.8
  50.3 0.2 collective-permute-start.13
  50.5 6.1 %all-to-all-start = ((bf16[8,8,16,128]{3,2,1,0:T(8,128)(2,1)}), bf16[8,8,16,128]{3,2,1,0:T(8,128)(2,1)}, u32[]{:S(2)}, u32[]{:S(2)}) async-start(bf16[8,8,16,128]{3,2,1,0:T(8,128)(2,1)} %shard_map.55), calls=%async_computation | async-start | bytes 524288 | tf_op jit(solution)/shard_map/all_to_all | solution.py:415
  56.6 1.8 collective-permute-done.7.refs_10_.refs_12_
  58.4 1.6 collective-permute-start.11
  60.0 1.5 collective-permute-start.14
  61.5 9.7 %collective-permute-done.8.refs_11_.refs_13_ = bf16[32,32,256]{2,1,0:T(8,128)(2,1)} collective-permute-done((bf16[32,32,256]{2,1,0:T(8,128)(2,1)}, bf16[32,32,256]{2,1,0:T(8,128)(2,1)}, u32[]{:S(2)}, u32[]{:S(2)}) %collective-permute-start.8) | collective-permute-done | bytes 524320 | tf_op jit(solution)/shard_map/ppermute | solution.py:370
  71.3 3.0 %collective-permute-start.12 = (bf16[32,32,256]{2,1,0:T(8,128)(2,1)}, bf16[32,32,256]{2,1,0:T(8,128)(2,1)}, u32[]{:S(2)}, u32[]{:S(2)}) collective-permute-start(bf16[32,32,256]{2,1,0:T(8,128)(2,1)} %collective-permute-done.8.refs_11_.refs_13_), channel_id=1, source_target_pairs={{0,1},{1,2},{2,3},{3,11},{11,10},{10,9},{9,8},{8,0},{4,5},{5,6},{6... | collective-permute-start | bytes 1572872 | tf_op jit(solution)/shard_map/ppermute | solution.py:370
  74.3 0.9 convert_element_type.15
  75.2 1.1 copy.29
  76.3 2.4 %all-to-all-done = bf16[8,8,16,128]{3,2,1,0:T(8,128)(2,1)} async-done(((bf16[8,8,16,128]{3,2,1,0:T(8,128)(2,1)}), bf16[8,8,16,128]{3,2,1,0:T(8,128)(2,1)}, u32[]{:S(2)}, u32[]{:S(2)}) %all-to-all-start) | async-done | bytes 262176 | tf_op jit(solution)/shard_map/all_to_all | solution.py:415
  78.8 0.3 fusion.1
  79.1 0.8 reshape.38.refs_19_.refs_21_
  79.9 0.6 dynamic-slice_bitcast_fusion.refs_20_.refs_22_
  80.5 0.7 copy-done.12
  81.2 4.8 %shard_map.56 = (bf16[64,32,128]{2,1,0:T(8,128)(2,1)}, bf16[64,32,128]{2,1,0:T(8,128)(2,1)}) custom-call(bf16[2,4,8,16,128]{4,3,2,1,0:T(8,128)(2,1)} %bitcast.3.refs_0_, bf16[2,4,8,16,128]{4,3,2,1,0:T(8,128)(2,1)} %copy-done.12), custom_call_target="tpu_custom_call" | custom-call | tf_op jit(solution)/shard_map/pallas_call | solution.py:338
  86.0 9.7 %collective-permute-done.12.refs_15_.refs_17_ = bf16[32,32,256]{2,1,0:T(8,128)(2,1)} collective-permute-done((bf16[32,32,256]{2,1,0:T(8,128)(2,1)}, bf16[32,32,256]{2,1,0:T(8,128)(2,1)}, u32[]{:S(2)}, u32[]{:S(2)}) %collective-permute-start.12) | collective-permute-done | bytes 524320 | tf_op jit(solution)/shard_map/ppermute | solution.py:370
  95.7 14.4 %shard_map.57 = (f32[64,32,128]{2,1,0:T(8,128)}, f32[64,32,128]{2,1,0:T(8,128)}) custom-call(s32[1]{0:T(128)} %bitcast.1.refs_0_, bf16[64,32,128]{2,1,0:T(8,128)(2,1)} %get-tuple-element.16.refs_1_, bf16[64,32,128]{2,1,0:T(8,128)(2,1)} %get-tuple-element.17.refs_2_, bf16[32,32,256]{2,1,0:T(8,128)(2,1)} %bitcast.28, bf16[32,32,256]{2,1,0:T(8,128)(2,1)} %copy-done.4, ...), custom_call_target="tpu_custom_call" | custom-call | flops 1073741824 | bytes 8388608 | tf_op jit(solution)/shard_map/pallas_call | solution.py:117
  110.1 0.1 collective-permute-start.16
  110.2 0.5 collective-permute-start.17
  110.7 2.4 %collective-permute-done.16.refs_2_.refs_1_ = f32[64,32,128]{2,1,0:T(8,128)S(1)} collective-permute-done((f32[64,32,128]{2,1,0:T(8,128)}, f32[64,32,128]{2,1,0:T(8,128)S(1)}, u32[]{:S(2)}, u32[]{:S(2)}) %collective-permute-start.16) | collective-permute-done | bytes 1048608 | tf_op jit(solution)/shard_map/ppermute | solution.py:348
  113.0 1.5 collective-permute-done.17.refs_4_
  114.5 1.0 copy-done.10
  115.6 15.4 %shard_map.58 = (f32[64,32,128]{2,1,0:T(8,128)}, f32[64,32,128]{2,1,0:T(8,128)}) custom-call(s32[1]{0:T(128)} %bitcast.1.refs_0_, f32[64,32,128]{2,1,0:T(8,128)} %get-tuple-element.19.refs_1_.refs_0_, f32[64,32,128]{2,1,0:T(8,128)} %copy-done.3, f32[64,32,128]{2,1,0:T(8,128)} %get-tuple-element.20.refs_3_, f32[64,32,128]{2,1,0:T(8,128)} %copy-done.10, ...), custom_call_target="tpu_custom_call" | custom-call | flops 1073741824 | bytes 8388608 | tf_op jit(solution)/shard_map/pallas_call | solution.py:117
  130.9 0.2 collective-permute-start.18
  131.1 2.7 %collective-permute-done.18.refs_3_ = f32[64,32,128]{2,1,0:T(8,128)S(1)} collective-permute-done((f32[64,32,128]{2,1,0:T(8,128)}, f32[64,32,128]{2,1,0:T(8,128)S(1)}, u32[]{:S(2)}, u32[]{:S(2)}) %collective-permute-start.18) | collective-permute-done | bytes 1048608 | tf_op jit(solution)/shard_map/ppermute | solution.py:348
  133.9 1.0 copy-done.9
  134.8 5.1 %shard_map.59 = bf16[2,4,2,4,32,128]{5,4,3,2,1,0:T(8,128)(2,1)} custom-call(f32[64,32,128]{2,1,0:T(8,128)} %get-tuple-element.19.refs_1_.refs_0_, f32[64,32,128]{2,1,0:T(8,128)} %copy-done.3, f32[64,32,128]{2,1,0:T(8,128)} %get-tuple-element.21.refs_2_, f32[64,32,128]{2,1,0:T(8,128)} %copy-done.9), custom_call_target="tpu_custom_call" | custom-call | tf_op jit(solution)/shard_map/pallas_call | solution.py:166
  139.9 22.0 %all_to_all.10 = bf16[8,2,4,32,128]{4,3,2,1,0:T(8,128)(2,1)} all-to-all(bf16[8,2,4,32,128]{4,3,2,1,0:T(8,128)(2,1)} %bitcast.30), channel_id=1, replica_groups=mesh['ma'=2,'x'=2,'core'=2,'fc'=4] {'x','fc'}, dimensions={0} | all-to-all | bytes 1048576 | tf_op jit(solution)/shard_map/all_to_all | solution.py:430
  161.9 2.2 %shard_map.60 = (f32[128,128]{1,0:T(8,128)}, f32[128,128]{1,0:T(8,128)}) custom-call(s32[1]{0:T(128)} %bitcast.core_ref, bf16[8,2,4,2,16,128]{5,4,3,2,1,0:T(8,128)(2,1)} %bitcast.25), custom_call_target="tpu_custom_call" | custom-call | tf_op jit(solution)/shard_map/pallas_call | solution.py:195
  164.1 1.5 collective-permute-done.19
  165.6 0.9 add.27
  166.4 1.2 collective-permute-start.20
  167.6 3.1 %collective-permute-done.20 = f32[128,128]{1,0:T(8,128)S(1)} collective-permute-done((f32[128,128]{1,0:T(8,128)S(1)}, f32[128,128]{1,0:T(8,128)S(1)}, u32[]{:S(2)}, u32[]{:S(2)}) %collective-permute-start.20) | collective-permute-done | bytes 65568 | tf_op jit(solution)/shard_map/ppermute | solution.py:379
  170.7 0.1 collective-permute-start.23
  170.8 1.3 collective-permute-start.22
  172.1 3.1 %collective-permute-start.21 = (f32[128,128]{1,0:T(8,128)S(1)}, f32[128,128]{1,0:T(8,128)S(1)}, u32[]{:S(2)}, u32[]{:S(2)}) collective-permute-start(f32[128,128]{1,0:T(8,128)S(1)} %add.28), channel_id=1, source_target_pairs={{0,1},{1,0},{2,3},{3,2},{4,5},{5,4},{6,7},{7,6},{8,9},{9,8},{10,11... | collective-permute-start | bytes 196616 | tf_op jit(solution)/shard_map/ppermute | solution.py:384
  175.2 2.0 collective-permute-done.23
  177.2 1.1 collective-permute-done.22
  178.3 0.1 collective-permute-start.24
  178.4 0.7 slice_bitcast_fusion.rows_ref
  179.1 0.5 collective-permute-done.24.given_ref
  179.6 0.6 copy-done.14
  180.2 19.3 %shard_map.61 = f32[2,4,128,128]{3,2,1,0:T(8,128)} custom-call(s32[1]{0:T(128)} %bitcast.core_ref, bf16[8,4,2,16,128]{4,3,2,1,0:T(8,128)(2,1)} %slice_bitcast_fusion.rows_ref, f32[128,128]{1,0:T(8,128)} %copy-done.11, f32[128,128]{1,0:T(8,128)} %copy-done.14), custom_call_target="tpu_custom_call" | custom-call | tf_op jit(solution)/shard_map/pallas_call | solution.py:272
  (45 shorter events, 0.2 us)
Async XLA Ops:
  0.0 79.9 %copy-start = (f32[2,512]{1,0:T(2,128)S(1)}, f32[2,512]{1,0:T(2,128)}, u32[]{:S(2)}) copy-start(f32[2,512]{1,0:T(2,128)} %param.7) | copy-start | bytes 12292
  6.5 3.3 %collective-permute-start.2 = (bf16[32,32,256]{2,1,0:T(8,128)(2,1)S(1)}, bf16[32,32,256]{2,1,0:T(8,128)(2,1)S(1)}, u32[]{:S(2)}, u32[]{:S(2)}) collective-permute-start(bf16[32,32,256]{2,1,0:T(8,128)(2,1)S(1)} %bitcast.32), channel_id=1, source_target_pairs={{0,4},{4,0},{1,5},{5,1},{2,6},{6,2},{3,7},{7,3},{8,12},{12,8},{9,1... | collective-permute-start | bytes 1572872 | tf_op jit(solution)/shard_map/ppermute | solution.py:348
  7.1 69.2 %copy-start.2 = (bf16[32,32,1,256]{3,1,2,0:T(8,128)(2,1)}, bf16[32,32,1,256]{3,1,2,0:T(8,128)(2,1)S(1)}, u32[]{:S(2)}) copy-start(bf16[32,32,1,256]{3,1,2,0:T(8,128)(2,1)S(1)} %copy.39) | copy-start | bytes 1572868
  7.2 67.1 %copy-start.13 = (f32[2,128,128]{2,1,0:T(8,128)S(1)}, f32[2,128,128]{2,1,0:T(8,128)}, u32[]{:S(2)}) copy-start(f32[2,128,128]{2,1,0:T(8,128)} %param.8) | copy-start | bytes 393220
  7.2 15.1 %collective-permute-start = (bf16[32,32,256]{2,1,0:T(8,128)(2,1)S(1)}, bf16[32,32,256]{2,1,0:T(8,128)(2,1)S(1)}, u32[]{:S(2)}, u32[]{:S(2)}) collective-permute-start(bf16[32,32,256]{2,1,0:T(8,128)(2,1)S(1)} %bitcast.26), channel_id=1, source_target_pairs={{0,1},{1,2},{2,3},{3,11},{11,10},{10,9},{9,8},{8,0},{4,5},{5,6},{6... | collective-permute-start | bytes 1572872 | tf_op jit(solution)/shard_map/ppermute | solution.py:370
  9.8 66.5 %copy-start.4 = (bf16[32,32,256]{2,1,0:T(8,128)(2,1)}, bf16[32,32,256]{2,1,0:T(8,128)(2,1)S(1)}, u32[]{:S(2)}) copy-start(bf16[32,32,256]{2,1,0:T(8,128)(2,1)S(1)} %collective-permute-done.2.refs_4_.refs_6_) | copy-start | bytes 1572868
  9.8 15.9 %collective-permute-start.5 = (bf16[32,32,256]{2,1,0:T(8,128)(2,1)S(1)}, bf16[32,32,256]{2,1,0:T(8,128)(2,1)S(1)}, u32[]{:S(2)}, u32[]{:S(2)}) collective-permute-start(bf16[32,32,256]{2,1,0:T(8,128)(2,1)S(1)} %collective-permute-done.2.refs_4_.refs_6_), channel_id=1, source_target_pairs={{1,0},{2,1},{3,2},{11,3},{10,11},{9,10},{8,9},{0,8},{5,4},{6,5},{7... | collective-permute-start | bytes 1572872 | tf_op jit(solution)/shard_map/ppermute | solution.py:370
  11.4 24.4 %collective-permute-start.3 = (bf16[32,32,256]{2,1,0:T(8,128)(2,1)S(1)}, bf16[32,32,256]{2,1,0:T(8,128)(2,1)S(1)}, u32[]{:S(2)}, u32[]{:S(2)}) collective-permute-start(bf16[32,32,256]{2,1,0:T(8,128)(2,1)S(1)} %bitcast.27), channel_id=1, source_target_pairs={{1,0},{2,1},{3,2},{11,3},{10,11},{9,10},{8,9},{0,8},{5,4},{6,5},{7... | collective-permute-start | bytes 1572872 | tf_op jit(solution)/shard_map/ppermute | solution.py:370
  22.3 56.7 %copy-start.5 = (bf16[32,32,256]{2,1,0:T(8,128)(2,1)}, bf16[32,32,256]{2,1,0:T(8,128)(2,1)S(1)}, u32[]{:S(2)}) copy-start(bf16[32,32,256]{2,1,0:T(8,128)(2,1)S(1)} %collective-permute-done.refs_5_.refs_7_) | copy-start | bytes 1572868
  22.3 15.1 %collective-permute-start.6 = (bf16[32,32,256]{2,1,0:T(8,128)(2,1)S(1)}, bf16[32,32,256]{2,1,0:T(8,128)(2,1)S(1)}, u32[]{:S(2)}, u32[]{:S(2)}) collective-permute-start(bf16[32,32,256]{2,1,0:T(8,128)(2,1)S(1)} %collective-permute-done.refs_5_.refs_7_), channel_id=1, source_target_pairs={{0,1},{1,2},{2,3},{3,11},{11,10},{10,9},{9,8},{8,0},{4,5},{5,6},{6... | collective-permute-start | bytes 1572872 | tf_op jit(solution)/shard_map/ppermute | solution.py:370
  24.1 24.3 %collective-permute-start.4 = (bf16[32,32,256]{2,1,0:T(8,128)(2,1)S(1)}, bf16[32,32,256]{2,1,0:T(8,128)(2,1)}, u32[]{:S(2)}, u32[]{:S(2)}) collective-permute-start(bf16[32,32,256]{2,1,0:T(8,128)(2,1)S(1)} %collective-permute-done.2.refs_4_.refs_6_), channel_id=1, source_target_pairs={{0,1},{1,2},{2,3},{3,11},{11,10},{10,9},{9,8},{8,0},{4,5},{5,6},{6... | collective-permute-start | bytes 1572872 | tf_op jit(solution)/shard_map/ppermute | solution.py:370
  25.7 53.3 %copy-start.6 = (bf16[32,32,256]{2,1,0:T(8,128)(2,1)}, bf16[32,32,256]{2,1,0:T(8,128)(2,1)S(1)}, u32[]{:S(2)}) copy-start(bf16[32,32,256]{2,1,0:T(8,128)(2,1)S(1)} %collective-permute-done.5.refs_8_.refs_10_) | copy-start | bytes 1572868
  25.7 24.6 %collective-permute-start.9 = (bf16[32,32,256]{2,1,0:T(8,128)(2,1)S(1)}, bf16[32,32,256]{2,1,0:T(8,128)(2,1)}, u32[]{:S(2)}, u32[]{:S(2)}) collective-permute-start(bf16[32,32,256]{2,1,0:T(8,128)(2,1)S(1)} %collective-permute-done.5.refs_8_.refs_10_), channel_id=1, source_target_pairs={{1,0},{2,1},{3,2},{11,3},{10,11},{9,10},{8,9},{0,8},{5,4},{6,5},{7... | collective-permute-start | bytes 1572872 | tf_op jit(solution)/shard_map/ppermute | solution.py:370
  35.8 43.3 %copy-start.7 = (bf16[32,32,256]{2,1,0:T(8,128)(2,1)}, bf16[32,32,256]{2,1,0:T(8,128)(2,1)S(1)}, u32[]{:S(2)}) copy-start(bf16[32,32,256]{2,1,0:T(8,128)(2,1)S(1)} %collective-permute-done.3.refs_6_.refs_8_) | copy-start | bytes 1572868
  35.8 22.6 %collective-permute-start.7 = (bf16[32,32,256]{2,1,0:T(8,128)(2,1)S(1)}, bf16[32,32,256]{2,1,0:T(8,128)(2,1)}, u32[]{:S(2)}, u32[]{:S(2)}) collective-permute-start(bf16[32,32,256]{2,1,0:T(8,128)(2,1)S(1)} %collective-permute-done.3.refs_6_.refs_8_), channel_id=1, source_target_pairs={{1,0},{2,1},{3,2},{11,3},{10,11},{9,10},{8,9},{0,8},{5,4},{6,5},{7... | collective-permute-start | bytes 1572872 | tf_op jit(solution)/shard_map/ppermute | solution.py:370
  37.4 58.3 %copy-start.8 = (bf16[32,32,256]{2,1,0:T(8,128)(2,1)}, bf16[32,32,256]{2,1,0:T(8,128)(2,1)S(1)}, u32[]{:S(2)}) copy-start(bf16[32,32,256]{2,1,0:T(8,128)(2,1)S(1)} %collective-permute-done.6.refs_9_.refs_11_) | copy-start | bytes 1572868
  37.4 22.6 %collective-permute-start.10 = (bf16[32,32,256]{2,1,0:T(8,128)(2,1)S(1)}, bf16[32,32,256]{2,1,0:T(8,128)(2,1)}, u32[]{:S(2)}, u32[]{:S(2)}) collective-permute-start(bf16[32,32,256]{2,1,0:T(8,128)(2,1)S(1)} %collective-permute-done.6.refs_9_.refs_11_), channel_id=1, source_target_pairs={{0,1},{1,2},{2,3},{3,11},{11,10},{10,9},{9,8},{8,0},{4,5},{5,6},{6... | collective-permute-start | bytes 1572872 | tf_op jit(solution)/shard_map/ppermute | solution.py:370
  48.4 22.8 %collective-permute-start.8 = (bf16[32,32,256]{2,1,0:T(8,128)(2,1)}, bf16[32,32,256]{2,1,0:T(8,128)(2,1)}, u32[]{:S(2)}, u32[]{:S(2)}) collective-permute-start(bf16[32,32,256]{2,1,0:T(8,128)(2,1)} %collective-permute-done.4.refs_7_.refs_9_), channel_id=1, source_target_pairs={{0,1},{1,2},{2,3},{3,11},{11,10},{10,9},{9,8},{8,0},{4,5},{5,6},{6... | collective-permute-start | bytes 1572872 | tf_op jit(solution)/shard_map/ppermute | solution.py:370
  50.3 24.0 %collective-permute-start.13 = (bf16[32,32,256]{2,1,0:T(8,128)(2,1)}, bf16[32,32,256]{2,1,0:T(8,128)(2,1)}, u32[]{:S(2)}, u32[]{:S(2)}) collective-permute-start(bf16[32,32,256]{2,1,0:T(8,128)(2,1)} %collective-permute-done.9.refs_12_.refs_14_), channel_id=1, source_target_pairs={{1,0},{2,1},{3,2},{11,3},{10,11},{9,10},{8,9},{0,8},{5,4},{6,5},{7... | collective-permute-start | bytes 1572872 | tf_op jit(solution)/shard_map/ppermute | solution.py:370
  50.5 28.3 %all-to-all-start = ((bf16[8,8,16,128]{3,2,1,0:T(8,128)(2,1)}), bf16[8,8,16,128]{3,2,1,0:T(8,128)(2,1)}, u32[]{:S(2)}, u32[]{:S(2)}) async-start(bf16[8,8,16,128]{3,2,1,0:T(8,128)(2,1)} %shard_map.55), calls=%async_computation | async-start | bytes 524288 | tf_op jit(solution)/shard_map/all_to_all | solution.py:415
  58.4 27.6 %collective-permute-start.11 = (bf16[32,32,256]{2,1,0:T(8,128)(2,1)}, bf16[32,32,256]{2,1,0:T(8,128)(2,1)}, u32[]{:S(2)}, u32[]{:S(2)}) collective-permute-start(bf16[32,32,256]{2,1,0:T(8,128)(2,1)} %collective-permute-done.7.refs_10_.refs_12_), channel_id=1, source_target_pairs={{1,0},{2,1},{3,2},{11,3},{10,11},{9,10},{8,9},{0,8},{5,4},{6,5},{7... | collective-permute-start | bytes 1572872 | tf_op jit(solution)/shard_map/ppermute | solution.py:370
  60.0 26.0 %collective-permute-start.14 = (bf16[32,32,256]{2,1,0:T(8,128)(2,1)}, bf16[32,32,256]{2,1,0:T(8,128)(2,1)}, u32[]{:S(2)}, u32[]{:S(2)}) collective-permute-start(bf16[32,32,256]{2,1,0:T(8,128)(2,1)} %collective-permute-done.10.refs_13_.refs_15_), channel_id=1, source_target_pairs={{0,1},{1,2},{2,3},{3,11},{11,10},{10,9},{9,8},{8,0},{4,5},{5,6},{6... | collective-permute-start | bytes 1572872 | tf_op jit(solution)/shard_map/ppermute | solution.py:370
  71.3 24.4 %collective-permute-start.12 = (bf16[32,32,256]{2,1,0:T(8,128)(2,1)}, bf16[32,32,256]{2,1,0:T(8,128)(2,1)}, u32[]{:S(2)}, u32[]{:S(2)}) collective-permute-start(bf16[32,32,256]{2,1,0:T(8,128)(2,1)} %collective-permute-done.8.refs_11_.refs_13_), channel_id=1, source_target_pairs={{0,1},{1,2},{2,3},{3,11},{11,10},{10,9},{9,8},{8,0},{4,5},{5,6},{6... | collective-permute-start | bytes 1572872 | tf_op jit(solution)/shard_map/ppermute | solution.py:370
  74.3 21.4 %collective-permute-start.15 = (bf16[32,32,256]{2,1,0:T(8,128)(2,1)}, bf16[32,32,256]{2,1,0:T(8,128)(2,1)}, u32[]{:S(2)}, u32[]{:S(2)}) collective-permute-start(bf16[32,32,256]{2,1,0:T(8,128)(2,1)} %collective-permute-done.13.refs_16_.refs_18_), channel_id=1, source_target_pairs={{1,0},{2,1},{3,2},{11,3},{10,11},{9,10},{8,9},{0,8},{5,4},{6,5},{7... | collective-permute-start | bytes 1572872 | tf_op jit(solution)/shard_map/ppermute | solution.py:370
  78.8 1.7 collective-permute-start.1
  80.5 0.7 copy-start.12
  110.1 2.9 %collective-permute-start.16 = (f32[64,32,128]{2,1,0:T(8,128)}, f32[64,32,128]{2,1,0:T(8,128)S(1)}, u32[]{:S(2)}, u32[]{:S(2)}) collective-permute-start(f32[64,32,128]{2,1,0:T(8,128)} %get-tuple-element.20.refs_3_), channel_id=1, source_target_pairs={{0,4},{4,0},{1,5},{5,1},{2,6},{6,2},{3,7},{7,3},{8,12},{12,8},{9,1... | collective-permute-start | bytes 3145736 | tf_op jit(solution)/shard_map/ppermute | solution.py:348
  110.2 4.4 %collective-permute-start.17 = (f32[64,32,128]{2,1,0:T(8,128)}, f32[64,32,128]{2,1,0:T(8,128)S(1)}, u32[]{:S(2)}, u32[]{:S(2)}) collective-permute-start(f32[64,32,128]{2,1,0:T(8,128)} %get-tuple-element.19.refs_1_.refs_0_), channel_id=1, source_target_pairs={{0,4},{4,0},{1,5},{5,1},{2,6},{6,2},{3,7},{7,3},{8,12},{12,8},{9,1... | collective-permute-start | bytes 3145736 | tf_op jit(solution)/shard_map/ppermute | solution.py:348
  113.0 1.5 copy-start.3
  114.5 1.0 copy-start.10
  130.9 2.9 %collective-permute-start.18 = (f32[64,32,128]{2,1,0:T(8,128)}, f32[64,32,128]{2,1,0:T(8,128)S(1)}, u32[]{:S(2)}, u32[]{:S(2)}) collective-permute-start(f32[64,32,128]{2,1,0:T(8,128)} %get-tuple-element.22), channel_id=1, source_target_pairs={{0,4},{4,0},{1,5},{5,1},{2,6},{6,2},{3,7},{7,3},{8,12},{12,8},{9,1... | collective-permute-start | bytes 3145736 | tf_op jit(solution)/shard_map/ppermute | solution.py:348
  133.9 1.0 copy-start.9
  161.9 13.3 %copy-start.1 = (bf16[8,2,4,32,128]{4,3,2,1,0:T(8,128)(2,1)S(1)}, bf16[8,2,4,32,128]{4,3,2,1,0:T(8,128)(2,1)}, u32[]{:S(2)}) copy-start(bf16[8,2,4,32,128]{4,3,2,1,0:T(8,128)(2,1)} %all_to_all.10) | copy-start | bytes 1572868
  164.1 1.5 collective-permute-start.19
  166.4 4.3 %collective-permute-start.20 = (f32[128,128]{1,0:T(8,128)S(1)}, f32[128,128]{1,0:T(8,128)S(1)}, u32[]{:S(2)}, u32[]{:S(2)}) collective-permute-start(f32[128,128]{1,0:T(8,128)S(1)} %add.27), channel_id=1, source_target_pairs={{0,8},{8,0},{1,9},{9,1},{2,10},{10,2},{3,11},{11,3},{4,12},{12,4},... | collective-permute-start | bytes 196616 | tf_op jit(solution)/shard_map/ppermute | solution.py:379
  170.7 6.5 %collective-permute-start.23 = (f32[128,128]{1,0:T(8,128)S(1)}, f32[128,128]{1,0:T(8,128)S(1)}, u32[]{:S(2)}, u32[]{:S(2)}) collective-permute-start(f32[128,128]{1,0:T(8,128)S(1)} %add.28), channel_id=1, source_target_pairs={{0,3},{1,2},{2,1},{3,0},{4,7},{5,6},{6,5},{7,4},{8,11},{9,10},{10,... | collective-permute-start | bytes 196616 | tf_op jit(solution)/shard_map/ppermute | solution.py:384
  170.8 7.5 %collective-permute-start.22 = (f32[128,128]{1,0:T(8,128)S(1)}, f32[128,128]{1,0:T(8,128)S(1)}, u32[]{:S(2)}, u32[]{:S(2)}) collective-permute-start(f32[128,128]{1,0:T(8,128)S(1)} %add.28), channel_id=1, source_target_pairs={{0,2},{1,3},{2,0},{3,1},{4,6},{5,7},{6,4},{7,5},{8,10},{9,11},{10,... | collective-permute-start | bytes 196616 | tf_op jit(solution)/shard_map/ppermute | solution.py:384
  172.1 6.2 %collective-permute-start.21 = (f32[128,128]{1,0:T(8,128)S(1)}, f32[128,128]{1,0:T(8,128)S(1)}, u32[]{:S(2)}, u32[]{:S(2)}) collective-permute-start(f32[128,128]{1,0:T(8,128)S(1)} %add.28), channel_id=1, source_target_pairs={{0,1},{1,0},{2,3},{3,2},{4,5},{5,4},{6,7},{7,6},{8,9},{9,8},{10,11... | collective-permute-start | bytes 196616 | tf_op jit(solution)/shard_map/ppermute | solution.py:384
  178.3 1.3 copy-start.11
  178.3 1.3 collective-permute-start.24
  179.6 0.6 copy-start.14

commit v4 on v3

--- a/solution.py
+++ b/solution.py
@@ -135,75 +135,81 @@
     )(place, *vecs[0], *vecs[1], *[piece for piece, _, _ in beams], cov, spec)
 
 
-def pack_kernel(own, *refs):
-    out_ref = refs[-1]
-    x_count, z_count, images, groups = out_ref.shape[:4]
-    freqs, rows, lanes = refs[0].shape
+def pack_kernel(own, first_ref, second_ref, out_ref):
+    x_count, z_count, groups = out_ref.shape[:3]
+    freqs, rows, lanes = first_ref.shape
     per_group = lanes // own
     lane = lax.broadcasted_iota(jnp.int32, (rows, lanes), 1) // own
 
-    def group(step, index, carry):
+    def group(index, carry):
         x_index, group_index = index // groups, index % groups
         totals = [jnp.zeros((rows, lanes), F32)] * z_count
         for place in range(per_group):
             freq = index * per_group + place
-            image = refs[2 * step][freq] + refs[2 * step + 1][freq]
+            image = first_ref[freq] + second_ref[freq]
             for z_index in range(z_count):
                 moved = rolled(image, (place - 2 * z_index) * own)
                 totals[z_index] = jnp.where(lane == place, moved, totals[z_index])
         for z_index in range(z_count):
-            out_ref[x_index, z_index, step, group_index] = totals[z_index].astype(BF16)
-        return carry
-
-    for step in range(images):
-        lax.fori_loop(0, x_count * groups, functools.partial(group, step), 0)
-
-
-def pack(pairs, x_count, z_count, own):
-    freqs, rows, lanes = pairs[0][0].shape
+            out_ref[x_index, z_index, group_index] = totals[z_index].astype(BF16)
+        return carry
+
+    lax.fori_loop(0, x_count * groups, group, 0, unroll=2)
+
+
+def pack(first, second, x_count, z_count, own):
+    freqs, rows, lanes = first.shape
     groups = freqs * own // (x_count * lanes)
-    flat = [part for pair in pairs for part in pair]
     return pl.pallas_call(
         functools.partial(pack_kernel, own),
-        out_shape=jax.ShapeDtypeStruct((x_count, z_count, len(pairs), groups, rows, lanes), BF16),
-        in_specs=[pl.BlockSpec(memory_space=pltpu.VMEM)] * len(flat),
+        out_shape=jax.ShapeDtypeStruct((x_count, z_count, groups, rows, lanes), BF16),
+        in_specs=[pl.BlockSpec(memory_space=pltpu.VMEM)] * 2,
         out_specs=pl.BlockSpec(memory_space=pltpu.VMEM),
         compiler_params=pltpu.CompilerParams(vmem_limit_bytes=VMEM_BYTES),
-    )(*flat)
-
-
-def gram_kernel(core_ref, rows_ref, keep_ref, send_ref):
-    senders, images, groups, parts, vectors, lanes = rows_ref.shape
+    )(first, second)
+
+
+def gram_kernel(core_ref, rows_ref, start_ref, keep_ref, send_ref):
+    senders, groups, parts, vectors, lanes = rows_ref.shape
     total = senders * vectors
-    found = []
-    for image in range(images):
-        gram = jnp.zeros((total, total), F32)
-        for group in range(groups):
-            for part in range(parts):
-                flat = rows_ref[:, image, group, part].reshape(total, lanes)
-                gram += lax.dot_general(
-                    flat, flat, (((1,), (1,)), ((), ())), preferred_element_type=F32
-                )
-        found.append(gram)
+    own = start_ref.shape[2]
+    per_group = lanes // own
+    first = jnp.zeros((total, total), F32)
+    second = jnp.zeros((total, total), F32)
+    for group in range(groups):
+        for part in range(parts):
+            flat = rows_ref[:, group, part].reshape(total, lanes)
+            start = start_ref[part, group * per_group : (group + 1) * per_group].reshape(lanes, total)
+            first += jnp.dot(flat, start.astype(BF16), preferred_element_type=F32)
+            second += lax.dot_general(
+                flat, flat, (((1,), (1,)), ((), ())), preferred_element_type=F32
+            )
     is_first = core_ref[0] == 0
-    keep_ref[...] = jnp.where(is_first, found[0], found[1])
-    send_ref[...] = jnp.where(is_first, found[1], found[0])
-
-
-def grams(core, rows):
-    total = rows.shape[0] * rows.shape[4]
+    keep_ref[...] = jnp.where(is_first, first, second)
+    send_ref[...] = jnp.where(is_first, second, first)
+
+
+def grams(core, rows, start):
+    total = rows.shape[0] * rows.shape[3]
     return pl.pallas_call(
         gram_kernel,
         out_shape=[jax.ShapeDtypeStruct((total, total), F32)] * 2,
-        in_specs=[pl.BlockSpec(memory_space=pltpu.SMEM), pl.BlockSpec(memory_space=pltpu.VMEM)],
+        in_specs=[pl.BlockSpec(memory_space=pltpu.SMEM)] + [pl.BlockSpec(memory_space=pltpu.VMEM)] * 2,
         out_specs=[pl.BlockSpec(memory_space=pltpu.VMEM)] * 2,
         compiler_params=pltpu.CompilerParams(vmem_limit_bytes=VMEM_BYTES),
-    )(core, rows)
+    )(core, rows, start)
+
+
+def triple(value):
+    high = value.astype(BF16)
+    rest = value - high.astype(F32)
+    middle = rest.astype(BF16)
+    return high, middle, (rest - middle.astype(F32)).astype(BF16)
 
 
 def inverse_factor(work_ref, matrix):
     order = matrix.shape[0]
-    step = 8
+    step = 16
     row = lax.broadcasted_iota(jnp.int32, (step, order), 0)
     lane = lax.broadcasted_iota(jnp.int32, (step, order), 1)
     at = lax.broadcasted_iota(jnp.int32, (order, order), 0)
@@ -226,17 +232,15 @@
             left, right = eliminate(left), eliminate(right)
             columns = columns[: k + 1] + [eliminate(c) for c in columns[k + 1 :]]
         work_ref[block, order:] = right
-        after = begin + step
-        if after < order:
-            kept = jnp.where(lane >= after, left, 0.0)
-            change = lax.dot_general(
-                kept,
-                jnp.concatenate([kept, right], axis=1),
-                (((0,), (0,)), ((), ())),
-                precision=HIGH,
-                preferred_element_type=F32,
-            )
-            work_ref[after:, :] = work_ref[after:, :] - change[after:]
+        end = begin + step
+        if end < order:
+            kept = jnp.where(lane >= end, left, 0.0)
+            high, middle, low = triple(kept)
+            first = jnp.concatenate([high, high, middle, high, low, middle], axis=0).astype(F32).T
+            high, middle, low = triple(jnp.concatenate([kept, right], axis=1))
+            second = jnp.concatenate([high, middle, high, low, high, middle], axis=0)
+            change = jnp.dot(first[end:].astype(BF16), second, preferred_element_type=F32)
+            work_ref[end:, :] = work_ref[end:, :] - change
     return work_ref[:, order:]
 
 
@@ -247,15 +251,13 @@
     across = (((1,), (1,)), ((), ()))
     plain = (((1,), (0,)), ((), ()))
     is_first = core_ref[0] == 0
-    first = inverse_factor(work_ref, jnp.where(is_first, kept_ref[...], given_ref[...]))
+    gram_first = jnp.where(is_first, kept_ref[...], given_ref[...])
+    first = inverse_factor(work_ref, 0.5 * (gram_first + gram_first.T))
     gram_second = jnp.where(is_first, given_ref[...], kept_ref[...])
     gram_second = exact(exact(first, gram_second, plain), first, across)
     second = inverse_factor(work_ref, gram_second)
     mixing = exact(second, first, plain) * scale
-    high = mixing.astype(BF16)
-    rest = mixing - high.astype(F32)
-    middle = rest.astype(BF16)
-    low = (rest - middle.astype(F32)).astype(BF16)
+    high, middle, low = triple(mixing)
     for group in range(groups):
         for part in range(parts):
             flat = rows_ref[:, group, part].reshape(total, lanes)
@@ -277,6 +279,32 @@
         scratch_shapes=[pltpu.VMEM((total, 2 * total), F32)],
         compiler_params=pltpu.CompilerParams(vmem_limit_bytes=VMEM_BYTES),
     )(core, rows, kept, given)
+
+
+def whiten_kernel(core_ref, beam_ref, noise_ref, keep_ref, send_ref):
+    parts, freqs, own, multipoles = beam_ref.shape
+    half = multipoles // 2
+    level = lax.rsqrt(noise_ref[...])
+    is_first = core_ref[0] == 0
+    for freq in range(freqs):
+        column = jnp.broadcast_to(level[:, freq : freq + 1], (own, half))
+        for part in range(parts):
+            low = (beam_ref[part, freq, :, :half].astype(F32) * column).astype(BF16)
+            high = (beam_ref[part, freq, :, half:].astype(F32) * column).astype(BF16)
+            rows = slice(part * own, (part + 1) * own)
+            keep_ref[freq, rows] = jnp.where(is_first, low, high)
+            send_ref[freq, rows] = jnp.where(is_first, high, low)
+
+
+def whiten(core, beam, noise):
+    parts, freqs, own, multipoles = beam.shape
+    return pl.pallas_call(
+        whiten_kernel,
+        out_shape=[jax.ShapeDtypeStruct((freqs, parts * own, multipoles // 2), BF16)] * 2,
+        in_specs=[pl.BlockSpec(memory_space=pltpu.SMEM)] + [pl.BlockSpec(memory_space=pltpu.VMEM)] * 2,
+        out_specs=[pl.BlockSpec(memory_space=pltpu.VMEM)] * 2,
+        compiler_params=pltpu.CompilerParams(vmem_limit_bytes=VMEM_BYTES),
+    )(core, beam, noise.T)
 
 
 def turn_kernel(start_ref, out_ref):
@@ -398,11 +426,9 @@
     mine_vectors = vectors // (x_count * z_count)
     depth = multipoles // cores
 
-    whitened = (beam_transfer.astype(F32) * lax.rsqrt(noise_var)[None, :, :, None]).astype(BF16)
-    rows = whitened.transpose(1, 0, 2, 3).reshape(freqs, parts * own, cores, depth)
-    rows = rows.transpose(2, 0, 1, 3)
-    kept = lax.dynamic_index_in_dim(rows, core, 0, False)
-    given = swap_cores(lax.dynamic_index_in_dim(rows, 1 - core, 0, False))
+    core_index = core.astype(jnp.int32).reshape(1)
+    kept, given = whiten(core_index, beam_transfer, noise_var)
+    given = swap_cores(given)
     start = turn(start_vectors, x_count * z_count, z_count * parts * own)
     place, beams, start = gather_ring([kept, given], start, x_count, z_count)
 
@@ -423,18 +449,15 @@
     second_mine, second_theirs = apply_covariance(
         place, [[mine, got_mine], [theirs, got_theirs]], beams, cov, spec, own, z_count
     )
-    packed = pack(
-        [(mine, got_mine), (second_mine, swap_cores(second_theirs))], x_count, z_count, own
-    )
+    packed = pack(second_mine, swap_cores(second_theirs), x_count, z_count, own)
     packed = packed.reshape(x_count * z_count, *packed.shape[2:])
     received = lax.all_to_all(packed, ("x", "fc"), 0, 0, tiled=True)
-    groups, lanes = received.shape[2], received.shape[4]
-    received = received.reshape(-1, ITERS, groups, parts, mine_vectors, lanes)
-
-    core_index = core.astype(jnp.int32).reshape(1)
-    kept_gram, given_gram = sum_devices(*grams(core_index, received), z_count)
+    groups, lanes = received.shape[1], received.shape[3]
+    received = received.reshape(-1, groups, parts, mine_vectors, lanes)
+
+    kept_gram, given_gram = sum_devices(*grams(core_index, received, start_vectors), z_count)
     scale = math.sqrt(2.0 * all_freqs * z_count * own)
-    basis = finish(core_index, received[:, 1], kept_gram, given_gram, scale)
+    basis = finish(core_index, received, kept_gram, given_gram, scale)
     return basis.reshape(parts, freqs, own, vectors)
 
 

time: 200 us -> 180 us (0.900)
  Pallas kernels: 63.6 us -> 55.5 us
  local copies, waits for them, and re-layouts: 12.7 us -> 6.79 us
  blocking collectives: 22 us -> 16.5 us
    pallas_call x1, Pallas kernels: 19.3 us -> 10.6 us  [finish(): pl.pallas_call(functools.partial(finish_kernel, scale), out_shape=jax.Sha...]
    all_to_all x1, blocking collectives: 22 us -> 16.5 us  [body_split(): received = lax.all_to_all(packed, ('x', 'fc'), 0, 0, tiled=True)]
    another operation x1 -> x0, local copies, waits for them, and re-layouts: 3.72 us -> none
    pallas_call x0 -> x1, Pallas kernels: none -> 2.52 us  [whiten(): pl.pallas_call(whiten_kernel, out_shape=[jax.ShapeDtypeStruct((freqs, par...]
    pallas_call x1, Pallas kernels: 5.07 us -> 3.01 us  [pack(): pl.pallas_call(functools.partial(pack_kernel, own), out_shape=jax.ShapeDt...]
  transfers between devices with their start and end apart: 26 -> 26, of which waited for: 15 -> 16; matrix products, arithmetic and copies ran while one was open for 2% -> 2% of each run, Pallas kernels for 4% -> 4%
where the time goes in v4:
time: 180 us; the launch traced here: 179 us
  waiting for transfers between devices  64.5 us (36%)
  Pallas kernels  55.5 us (31%)
  starting transfers between devices  34.5 us (19%)
  blocking collectives  16.5 us (9%)
  local copies, waits for them, and re-layouts  6.79 us (4%)
    ppermute x14, waiting for transfers between devices, gather_ring(): moving[core, way] = lax.ppermute(moving[core, way], ('x', 'fc'), pairs[way])  46.4 us
    pallas_call x2, Pallas kernels, apply_covariance(): pl.pallas_call(functools.partial(apply_kernel, n_vec, z_count, own, offse...  29.9 us
    ppermute x14, starting transfers between devices, gather_ring(): moving[core, way] = lax.ppermute(moving[core, way], ('x', 'fc'), pairs[way])  21.8 us
    all_to_all x1, blocking collectives, body_split(): received = lax.all_to_all(packed, ('x', 'fc'), 0, 0, tiled=True)  16.5 us
    pallas_call x1, Pallas kernels, finish(): pl.pallas_call(functools.partial(finish_kernel, scale), out_shape=jax.Sha...  10.6 us
    ppermute x7, waiting for transfers between devices, swap_cores(): return lax.ppermute(value, 'core', [(0, 1), (1, 0)])  9.37 us
    all_to_all x1, starting transfers between devices, body_split(): start = lax.all_to_all(start, ('x', 'fc'), 0, 0, tiled=True)  6.09 us
    pallas_call x1, Pallas kernels, start_operand(): pl.pallas_call(functools.partial(operand_kernel, own), out_shape=[jax.Sha...  4.77 us
  transfers between devices with their start and end apart: 26, of which 16 were waited for; matrix products, arithmetic and copies ran while one was open for 2% of the time, Pallas kernels for 4%

profile of v4, /device:TPU:0, one launch (start us, length us, event | category | flops | bytes accessed | tf_op | source)
XLA Modules:
  0.0 179.1 jit_solution(10794887734557691690)
XLA Ops:
  0.0 2.5 %shard_map.56 = (bf16[32,32,256]{2,1,0:T(8,128)(2,1)}, bf16[32,32,256]{2,1,0:T(8,128)(2,1)}) custom-call(s32[1]{0:T(128)} %bitcast.core_ref, bf16[2,32,16,512]{3,2,1,0:T(8,128)(2,1)} %beam_ref.1, f32[16,32]{1,0:T(8,128)} %bitcast.16), custom_call_target="tpu_custom_call" | custom-call | tf_op jit(solution)/shard_map/pallas_call | solution.py:301
  2.5 0.5 collective-permute-start.2
  3.0 2.6 %collective-permute-start = (bf16[32,32,256]{2,1,0:T(8,128)(2,1)}, bf16[32,32,256]{2,1,0:T(8,128)(2,1)S(1)}, u32[]{:S(2)}, u32[]{:S(2)}) collective-permute-start(bf16[32,32,256]{2,1,0:T(8,128)(2,1)} %get-tuple-element.17.refs_3_.refs_5_), channel_id=1, source_target_pairs={{0,1},{1,2},{2,3},{3,11},{11,10},{10,9},{9,8},{8,0},{4,5},{5,6},{6... | collective-permute-start | bytes 1572872 | tf_op jit(solution)/shard_map/ppermute | solution.py:398
  5.5 0.0 collective-permute-done.2.refs_4_.refs_6_
  5.6 2.0 %collective-permute-start.5 = (bf16[32,32,256]{2,1,0:T(8,128)(2,1)S(1)}, bf16[32,32,256]{2,1,0:T(8,128)(2,1)S(1)}, u32[]{:S(2)}, u32[]{:S(2)}) collective-permute-start(bf16[32,32,256]{2,1,0:T(8,128)(2,1)S(1)} %collective-permute-done.2.refs_4_.refs_6_), channel_id=1, source_target_pairs={{1,0},{2,1},{3,2},{11,3},{10,11},{9,10},{8,9},{0,8},{5,4},{6,5},{7... | collective-permute-start | bytes 1572872 | tf_op jit(solution)/shard_map/ppermute | solution.py:398
  7.6 1.6 collective-permute-start.3
  9.2 2.6 %shard_map.55 = bf16[8,8,16,128]{3,2,1,0:T(8,128)(2,1)} custom-call(f32[2,32,16,128]{3,2,1,0:T(8,128)} %start_ref.3), custom_call_target="tpu_custom_call" | custom-call | tf_op jit(solution)/shard_map/pallas_call | solution.py:331
  11.7 6.6 %collective-permute-done.refs_5_.refs_7_ = bf16[32,32,256]{2,1,0:T(8,128)(2,1)S(1)} collective-permute-done((bf16[32,32,256]{2,1,0:T(8,128)(2,1)}, bf16[32,32,256]{2,1,0:T(8,128)(2,1)S(1)}, u32[]{:S(2)}, u32[]{:S(2)}) %collective-permute-start) | collective-permute-done | bytes 524320 | tf_op jit(solution)/shard_map/ppermute | solution.py:398
  18.3 1.8 %collective-permute-start.4 = (bf16[32,32,256]{2,1,0:T(8,128)(2,1)S(1)}, bf16[32,32,256]{2,1,0:T(8,128)(2,1)S(1)}, u32[]{:S(2)}, u32[]{:S(2)}) collective-permute-start(bf16[32,32,256]{2,1,0:T(8,128)(2,1)S(1)} %collective-permute-done.2.refs_4_.refs_6_), channel_id=1, source_target_pairs={{0,1},{1,2},{2,3},{3,11},{11,10},{10,9},{9,8},{8,0},{4,5},{5,6},{6... | collective-permute-start | bytes 1572872 | tf_op jit(solution)/shard_map/ppermute | solution.py:398
  20.1 1.6 collective-permute-start.6
  21.7 0.0 collective-permute-done.5.refs_8_.refs_10_
  21.7 0.7 collective-permute-start.9
  22.4 9.3 %collective-permute-done.3.refs_6_.refs_8_ = bf16[32,32,256]{2,1,0:T(8,128)(2,1)S(1)} collective-permute-done((bf16[32,32,256]{2,1,0:T(8,128)(2,1)}, bf16[32,32,256]{2,1,0:T(8,128)(2,1)S(1)}, u32[]{:S(2)}, u32[]{:S(2)}) %collective-permute-start.3) | collective-permute-done | bytes 524320 | tf_op jit(solution)/shard_map/ppermute | solution.py:398
  31.6 2.0 %collective-permute-start.7 = (bf16[32,32,256]{2,1,0:T(8,128)(2,1)S(1)}, bf16[32,32,256]{2,1,0:T(8,128)(2,1)}, u32[]{:S(2)}, u32[]{:S(2)}) collective-permute-start(bf16[32,32,256]{2,1,0:T(8,128)(2,1)S(1)} %collective-permute-done.3.refs_6_.refs_8_), channel_id=1, source_target_pairs={{1,0},{2,1},{3,2},{11,3},{10,11},{9,10},{8,9},{0,8},{5,4},{6,5},{7... | collective-permute-start | bytes 1572872 | tf_op jit(solution)/shard_map/ppermute | solution.py:398
  33.6 0.0 collective-permute-done.4.refs_7_.refs_9_
  33.6 1.3 collective-permute-start.8
  34.9 9.4 %collective-permute-done.6.refs_9_.refs_11_ = bf16[32,32,256]{2,1,0:T(8,128)(2,1)S(1)} collective-permute-done((bf16[32,32,256]{2,1,0:T(8,128)(2,1)S(1)}, bf16[32,32,256]{2,1,0:T(8,128)(2,1)S(1)}, u32[]{:S(2)}, u32[]{:S(2)}) %collective-permute-start.6) | collective-permute-done | bytes 524320 | tf_op jit(solution)/shard_map/ppermute | solution.py:398
  44.3 1.9 %collective-permute-start.10 = (bf16[32,32,256]{2,1,0:T(8,128)(2,1)S(1)}, bf16[32,32,256]{2,1,0:T(8,128)(2,1)}, u32[]{:S(2)}, u32[]{:S(2)}) collective-permute-start(bf16[32,32,256]{2,1,0:T(8,128)(2,1)S(1)} %collective-permute-done.6.refs_9_.refs_11_), channel_id=1, source_target_pairs={{0,1},{1,2},{2,3},{3,11},{11,10},{10,9},{9,8},{8,0},{4,5},{5,6},{6... | collective-permute-start | bytes 1572872 | tf_op jit(solution)/shard_map/ppermute | solution.py:398
  46.2 0.0 collective-permute-done.9.refs_12_.refs_14_
  46.2 0.2 collective-permute-start.13
  46.3 6.1 %all-to-all-start = ((bf16[8,8,16,128]{3,2,1,0:T(8,128)(2,1)}), bf16[8,8,16,128]{3,2,1,0:T(8,128)(2,1)}, u32[]{:S(2)}, u32[]{:S(2)}) async-start(bf16[8,8,16,128]{3,2,1,0:T(8,128)(2,1)} %shard_map.55), calls=%async_computation | async-start | bytes 524288 | tf_op jit(solution)/shard_map/all_to_all | solution.py:441
  52.4 1.8 collective-permute-done.7.refs_10_.refs_12_
  54.2 2.0 %collective-permute-start.11 = (bf16[32,32,256]{2,1,0:T(8,128)(2,1)}, bf16[32,32,256]{2,1,0:T(8,128)(2,1)S(1)}, u32[]{:S(2)}, u32[]{:S(2)}) collective-permute-start(bf16[32,32,256]{2,1,0:T(8,128)(2,1)} %collective-permute-done.7.refs_10_.refs_12_), channel_id=1, source_target_pairs={{1,0},{2,1},{3,2},{11,3},{10,11},{9,10},{8,9},{0,8},{5,4},{6,5},{7... | collective-permute-start | bytes 1572872 | tf_op jit(solution)/shard_map/ppermute | solution.py:398
  56.2 1.3 collective-permute-start.12
  57.5 9.7 %collective-permute-done.10.refs_13_.refs_15_ = bf16[32,32,256]{2,1,0:T(8,128)(2,1)} collective-permute-done((bf16[32,32,256]{2,1,0:T(8,128)(2,1)S(1)}, bf16[32,32,256]{2,1,0:T(8,128)(2,1)}, u32[]{:S(2)}, u32[]{:S(2)}) %collective-permute-start.10) | collective-permute-done | bytes 524320 | tf_op jit(solution)/shard_map/ppermute | solution.py:398
  67.2 2.9 %collective-permute-start.14 = (bf16[32,32,256]{2,1,0:T(8,128)(2,1)}, bf16[32,32,256]{2,1,0:T(8,128)(2,1)}, u32[]{:S(2)}, u32[]{:S(2)}) collective-permute-start(bf16[32,32,256]{2,1,0:T(8,128)(2,1)} %collective-permute-done.10.refs_13_.refs_15_), channel_id=1, source_target_pairs={{0,1},{1,2},{2,3},{3,11},{11,10},{10,9},{9,8},{8,0},{4,5},{5,6},{6... | collective-permute-start | bytes 1572872 | tf_op jit(solution)/shard_map/ppermute | solution.py:398
  70.1 0.0 collective-permute-done.13.refs_16_.refs_18_
  70.1 0.0 collective-permute-start.15
  70.2 0.9 convert_element_type.7
  71.1 1.1 copy.7
  72.2 2.5 %all-to-all-done = bf16[8,8,16,128]{3,2,1,0:T(8,128)(2,1)} async-done(((bf16[8,8,16,128]{3,2,1,0:T(8,128)(2,1)}), bf16[8,8,16,128]{3,2,1,0:T(8,128)(2,1)}, u32[]{:S(2)}, u32[]{:S(2)}) %all-to-all-start) | async-done | bytes 262176 | tf_op jit(solution)/shard_map/all_to_all | solution.py:441
  74.7 0.3 fusion
  75.0 0.8 reshape.29.refs_19_.refs_21_
  75.8 0.6 dynamic-slice_bitcast_fusion.refs_20_.refs_22_
  76.4 0.1 collective-permute-done.1.refs_1_
  76.5 0.7 copy-done.12
  77.2 4.8 %shard_map.57 = (bf16[64,32,128]{2,1,0:T(8,128)(2,1)}, bf16[64,32,128]{2,1,0:T(8,128)(2,1)}) custom-call(bf16[2,4,8,16,128]{4,3,2,1,0:T(8,128)(2,1)} %bitcast.3.refs_0_, bf16[2,4,8,16,128]{4,3,2,1,0:T(8,128)(2,1)} %copy-done.12), custom_call_target="tpu_custom_call" | custom-call | tf_op jit(solution)/shard_map/pallas_call | solution.py:366
  82.0 9.7 %collective-permute-done.14.refs_17_.refs_19_ = bf16[32,32,256]{2,1,0:T(8,128)(2,1)} collective-permute-done((bf16[32,32,256]{2,1,0:T(8,128)(2,1)}, bf16[32,32,256]{2,1,0:T(8,128)(2,1)}, u32[]{:S(2)}, u32[]{:S(2)}) %collective-permute-start.14) | collective-permute-done | bytes 524320 | tf_op jit(solution)/shard_map/ppermute | solution.py:398
  91.7 14.5 %shard_map.58 = (f32[64,32,128]{2,1,0:T(8,128)}, f32[64,32,128]{2,1,0:T(8,128)}) custom-call(s32[1]{0:T(128)} %bitcast.1.refs_0_, bf16[64,32,128]{2,1,0:T(8,128)(2,1)} %get-tuple-element.19.refs_1_, bf16[64,32,128]{2,1,0:T(8,128)(2,1)} %get-tuple-element.20.refs_2_, bf16[32,32,256]{2,1,0:T(8,128)(2,1)} %get-tuple-element.17.refs_3_.refs_5_, ...), custom_call_target="tpu_custom_call" | custom-call | flops 1073741824 | bytes 8388608 | tf_op jit(solution)/shard_map/pallas_call | solution.py:117
  106.1 0.1 collective-permute-start.17
  106.2 0.5 collective-permute-start.16
  106.7 2.4 %collective-permute-done.17.refs_4_ = f32[64,32,128]{2,1,0:T(8,128)S(1)} collective-permute-done((f32[64,32,128]{2,1,0:T(8,128)}, f32[64,32,128]{2,1,0:T(8,128)S(1)}, u32[]{:S(2)}, u32[]{:S(2)}) %collective-permute-start.17) | collective-permute-done | bytes 1048608 | tf_op jit(solution)/shard_map/ppermute | solution.py:376
  109.1 1.5 collective-permute-done.16.refs_2_
  110.6 1.0 copy-done.10
  111.6 15.5 %shard_map.59 = (f32[64,32,128]{2,1,0:T(8,128)}, f32[64,32,128]{2,1,0:T(8,128)}) custom-call(s32[1]{0:T(128)} %bitcast.1.refs_0_, f32[64,32,128]{2,1,0:T(8,128)} %get-tuple-element.23.refs_1_, f32[64,32,128]{2,1,0:T(8,128)} %copy-done.10, f32[64,32,128]{2,1,0:T(8,128)} %get-tuple-element.24.refs_3_, f32[64,32,128]{2,1,0:T(8,128)} %copy-done.9, ...), custom_call_target="tpu_custom_call" | custom-call | flops 1073741824 | bytes 8388608 | tf_op jit(solution)/shard_map/pallas_call | solution.py:117
  127.0 0.2 collective-permute-start.18
  127.2 2.8 %collective-permute-done.18.second_ref = f32[64,32,128]{2,1,0:T(8,128)S(1)} collective-permute-done((f32[64,32,128]{2,1,0:T(8,128)}, f32[64,32,128]{2,1,0:T(8,128)S(1)}, u32[]{:S(2)}, u32[]{:S(2)}) %collective-permute-start.18) | collective-permute-done | bytes 1048608 | tf_op jit(solution)/shard_map/ppermute | solution.py:376
  130.0 1.0 copy-done.8
  131.0 3.0 %shard_map.60 = bf16[2,4,4,32,128]{4,3,2,1,0:T(8,128)(2,1)} custom-call(f32[64,32,128]{2,1,0:T(8,128)} %get-tuple-element.25.first_ref, f32[64,32,128]{2,1,0:T(8,128)} %copy-done.8), custom_call_target="tpu_custom_call" | custom-call | tf_op jit(solution)/shard_map/pallas_call | solution.py:163
  134.0 16.5 %all_to_all.10 = bf16[8,4,32,128]{3,2,1,0:T(8,128)(2,1)} all-to-all(bf16[8,4,32,128]{3,2,1,0:T(8,128)(2,1)} %bitcast.15), channel_id=1, replica_groups=mesh['ma'=2,'x'=2,'core'=2,'fc'=4] {'x','fc'}, dimensions={0} | all-to-all | bytes 524288 | tf_op jit(solution)/shard_map/all_to_all | solution.py:454
  150.5 2.1 %shard_map.61 = (f32[128,128]{1,0:T(8,128)}, f32[128,128]{1,0:T(8,128)}) custom-call(s32[1]{0:T(128)} %bitcast.core_ref, bf16[8,4,2,16,128]{4,3,2,1,0:T(8,128)(2,1)} %bitcast.13, f32[2,32,16,128]{3,2,1,0:T(8,128)} %start_ref.3), custom_call_target="tpu_custom_call" | custom-call | tf_op jit(solution)/shard_map/pallas_call | solution.py:194
  152.6 1.5 collective-permute-done.19
  154.1 0.9 add.20
  155.0 0.9 collective-permute-start.20
  155.8 3.4 %collective-permute-done.20 = f32[128,128]{1,0:T(8,128)S(1)} collective-permute-done((f32[128,128]{1,0:T(8,128)S(1)}, f32[128,128]{1,0:T(8,128)S(1)}, u32[]{:S(2)}, u32[]{:S(2)}) %collective-permute-start.20) | collective-permute-done | bytes 65568 | tf_op jit(solution)/shard_map/ppermute | solution.py:407
  159.2 0.1 collective-permute-start.23
  159.3 0.8 collective-permute-start.22
  160.1 3.6 %collective-permute-start.21 = (f32[128,128]{1,0:T(8,128)S(1)}, f32[128,128]{1,0:T(8,128)S(1)}, u32[]{:S(2)}, u32[]{:S(2)}) collective-permute-start(f32[128,128]{1,0:T(8,128)S(1)} %add.21), channel_id=1, source_target_pairs={{0,1},{1,0},{2,3},{3,2},{4,5},{5,4},{6,7},{7,6},{8,9},{9,8},{10,11... | collective-permute-start | bytes 196616 | tf_op jit(solution)/shard_map/ppermute | solution.py:412
  163.7 2.0 %collective-permute-done.23 = f32[128,128]{1,0:T(8,128)S(1)} collective-permute-done((f32[128,128]{1,0:T(8,128)S(1)}, f32[128,128]{1,0:T(8,128)S(1)}, u32[]{:S(2)}, u32[]{:S(2)}) %collective-permute-start.23) | collective-permute-done | bytes 65568 | tf_op jit(solution)/shard_map/ppermute | solution.py:412
  165.7 0.9 collective-permute-done.22
  166.6 0.1 collective-permute-start.24
  166.7 1.2 collective-permute-done.24.given_ref
  167.9 0.6 copy-done.14
  168.5 10.6 %shard_map.62 = f32[2,4,128,128]{3,2,1,0:T(8,128)} custom-call(s32[1]{0:T(128)} %bitcast.core_ref, bf16[8,4,2,16,128]{4,3,2,1,0:T(8,128)(2,1)} %bitcast.14, f32[128,128]{1,0:T(8,128)} %copy-done.11, f32[128,128]{1,0:T(8,128)} %copy-done.14), custom_call_target="tpu_custom_call" | custom-call | tf_op jit(solution)/shard_map/pallas_call | solution.py:274
  (36 shorter events, 0.1 us)
Async XLA Ops:
  0.0 75.8 %copy-start = (f32[2,512]{1,0:T(2,128)S(1)}, f32[2,512]{1,0:T(2,128)}, u32[]{:S(2)}) copy-start(f32[2,512]{1,0:T(2,128)} %param.7) | copy-start | bytes 12292
  2.5 3.0 %collective-permute-start.2 = (bf16[32,32,256]{2,1,0:T(8,128)(2,1)}, bf16[32,32,256]{2,1,0:T(8,128)(2,1)S(1)}, u32[]{:S(2)}, u32[]{:S(2)}) collective-permute-start(bf16[32,32,256]{2,1,0:T(8,128)(2,1)} %get-tuple-element.21), channel_id=1, source_target_pairs={{0,4},{4,0},{1,5},{5,1},{2,6},{6,2},{3,7},{7,3},{8,12},{12,8},{9,1... | collective-permute-start | bytes 1572872 | tf_op jit(solution)/shard_map/ppermute | solution.py:376
  3.0 15.3 %collective-permute-start = (bf16[32,32,256]{2,1,0:T(8,128)(2,1)}, bf16[32,32,256]{2,1,0:T(8,128)(2,1)S(1)}, u32[]{:S(2)}, u32[]{:S(2)}) collective-permute-start(bf16[32,32,256]{2,1,0:T(8,128)(2,1)} %get-tuple-element.17.refs_3_.refs_5_), channel_id=1, source_target_pairs={{0,1},{1,2},{2,3},{3,11},{11,10},{10,9},{9,8},{8,0},{4,5},{5,6},{6... | collective-permute-start | bytes 1572872 | tf_op jit(solution)/shard_map/ppermute | solution.py:398
  5.5 40.8 %copy-start.1 = (bf16[32,32,256]{2,1,0:T(8,128)(2,1)}, bf16[32,32,256]{2,1,0:T(8,128)(2,1)S(1)}, u32[]{:S(2)}) copy-start(bf16[32,32,256]{2,1,0:T(8,128)(2,1)S(1)} %collective-permute-done.2.refs_4_.refs_6_) | copy-start | bytes 1572868
  5.6 16.1 %collective-permute-start.5 = (bf16[32,32,256]{2,1,0:T(8,128)(2,1)S(1)}, bf16[32,32,256]{2,1,0:T(8,128)(2,1)S(1)}, u32[]{:S(2)}, u32[]{:S(2)}) collective-permute-start(bf16[32,32,256]{2,1,0:T(8,128)(2,1)S(1)} %collective-permute-done.2.refs_4_.refs_6_), channel_id=1, source_target_pairs={{1,0},{2,1},{3,2},{11,3},{10,11},{9,10},{8,9},{0,8},{5,4},{6,5},{7... | collective-permute-start | bytes 1572872 | tf_op jit(solution)/shard_map/ppermute | solution.py:398
  7.6 24.0 %collective-permute-start.3 = (bf16[32,32,256]{2,1,0:T(8,128)(2,1)}, bf16[32,32,256]{2,1,0:T(8,128)(2,1)S(1)}, u32[]{:S(2)}, u32[]{:S(2)}) collective-permute-start(bf16[32,32,256]{2,1,0:T(8,128)(2,1)} %get-tuple-element.17.refs_3_.refs_5_), channel_id=1, source_target_pairs={{1,0},{2,1},{3,2},{11,3},{10,11},{9,10},{8,9},{0,8},{5,4},{6,5},{7... | collective-permute-start | bytes 1572872 | tf_op jit(solution)/shard_map/ppermute | solution.py:398
  11.7 58.4 %copy-start.13 = (f32[2,128,128]{2,1,0:T(8,128)S(1)}, f32[2,128,128]{2,1,0:T(8,128)}, u32[]{:S(2)}) copy-start(f32[2,128,128]{2,1,0:T(8,128)} %param.8) | copy-start | bytes 393220
  18.3 52.8 %copy-start.2 = (bf16[32,32,256]{2,1,0:T(8,128)(2,1)}, bf16[32,32,256]{2,1,0:T(8,128)(2,1)S(1)}, u32[]{:S(2)}) copy-start(bf16[32,32,256]{2,1,0:T(8,128)(2,1)S(1)} %collective-permute-done.refs_5_.refs_7_) | copy-start | bytes 1572868
  18.3 15.3 %collective-permute-start.4 = (bf16[32,32,256]{2,1,0:T(8,128)(2,1)S(1)}, bf16[32,32,256]{2,1,0:T(8,128)(2,1)S(1)}, u32[]{:S(2)}, u32[]{:S(2)}) collective-permute-start(bf16[32,32,256]{2,1,0:T(8,128)(2,1)S(1)} %collective-permute-done.2.refs_4_.refs_6_), channel_id=1, source_target_pairs={{0,1},{1,2},{2,3},{3,11},{11,10},{10,9},{9,8},{8,0},{4,5},{5,6},{6... | collective-permute-start | bytes 1572872 | tf_op jit(solution)/shard_map/ppermute | solution.py:398
  20.1 24.2 %collective-permute-start.6 = (bf16[32,32,256]{2,1,0:T(8,128)(2,1)S(1)}, bf16[32,32,256]{2,1,0:T(8,128)(2,1)S(1)}, u32[]{:S(2)}, u32[]{:S(2)}) collective-permute-start(bf16[32,32,256]{2,1,0:T(8,128)(2,1)S(1)} %collective-permute-done.refs_5_.refs_7_), channel_id=1, source_target_pairs={{0,1},{1,2},{2,3},{3,11},{11,10},{10,9},{9,8},{8,0},{4,5},{5,6},{6... | collective-permute-start | bytes 1572872 | tf_op jit(solution)/shard_map/ppermute | solution.py:398
  21.7 49.4 %copy-start.3 = (bf16[32,32,256]{2,1,0:T(8,128)(2,1)}, bf16[32,32,256]{2,1,0:T(8,128)(2,1)S(1)}, u32[]{:S(2)}) copy-start(bf16[32,32,256]{2,1,0:T(8,128)(2,1)S(1)} %collective-permute-done.5.refs_8_.refs_10_) | copy-start | bytes 1572868
  21.7 24.5 %collective-permute-start.9 = (bf16[32,32,256]{2,1,0:T(8,128)(2,1)S(1)}, bf16[32,32,256]{2,1,0:T(8,128)(2,1)}, u32[]{:S(2)}, u32[]{:S(2)}) collective-permute-start(bf16[32,32,256]{2,1,0:T(8,128)(2,1)S(1)} %collective-permute-done.5.refs_8_.refs_10_), channel_id=1, source_target_pairs={{1,0},{2,1},{3,2},{11,3},{10,11},{9,10},{8,9},{0,8},{5,4},{6,5},{7... | collective-permute-start | bytes 1572872 | tf_op jit(solution)/shard_map/ppermute | solution.py:398
  31.6 60.1 %copy-start.4 = (bf16[32,32,256]{2,1,0:T(8,128)(2,1)}, bf16[32,32,256]{2,1,0:T(8,128)(2,1)S(1)}, u32[]{:S(2)}) copy-start(bf16[32,32,256]{2,1,0:T(8,128)(2,1)S(1)} %collective-permute-done.3.refs_6_.refs_8_) | copy-start | bytes 1572868
  31.6 22.6 %collective-permute-start.7 = (bf16[32,32,256]{2,1,0:T(8,128)(2,1)S(1)}, bf16[32,32,256]{2,1,0:T(8,128)(2,1)}, u32[]{:S(2)}, u32[]{:S(2)}) collective-permute-start(bf16[32,32,256]{2,1,0:T(8,128)(2,1)S(1)} %collective-permute-done.3.refs_6_.refs_8_), channel_id=1, source_target_pairs={{1,0},{2,1},{3,2},{11,3},{10,11},{9,10},{8,9},{0,8},{5,4},{6,5},{7... | collective-permute-start | bytes 1572872 | tf_op jit(solution)/shard_map/ppermute | solution.py:398
  33.6 58.1 %copy-start.5 = (bf16[32,32,256]{2,1,0:T(8,128)(2,1)}, bf16[32,32,256]{2,1,0:T(8,128)(2,1)S(1)}, u32[]{:S(2)}) copy-start(bf16[32,32,256]{2,1,0:T(8,128)(2,1)S(1)} %collective-permute-done.4.refs_7_.refs_9_) | copy-start | bytes 1572868
  33.6 22.6 %collective-permute-start.8 = (bf16[32,32,256]{2,1,0:T(8,128)(2,1)S(1)}, bf16[32,32,256]{2,1,0:T(8,128)(2,1)}, u32[]{:S(2)}, u32[]{:S(2)}) collective-permute-start(bf16[32,32,256]{2,1,0:T(8,128)(2,1)S(1)} %collective-permute-done.4.refs_7_.refs_9_), channel_id=1, source_target_pairs={{0,1},{1,2},{2,3},{3,11},{11,10},{10,9},{9,8},{8,0},{4,5},{5,6},{6... | collective-permute-start | bytes 1572872 | tf_op jit(solution)/shard_map/ppermute | solution.py:398
  44.3 47.4 %copy-start.6 = (bf16[32,32,256]{2,1,0:T(8,128)(2,1)}, bf16[32,32,256]{2,1,0:T(8,128)(2,1)S(1)}, u32[]{:S(2)}) copy-start(bf16[32,32,256]{2,1,0:T(8,128)(2,1)S(1)} %collective-permute-done.6.refs_9_.refs_11_) | copy-start | bytes 1572868
  44.3 22.9 %collective-permute-start.10 = (bf16[32,32,256]{2,1,0:T(8,128)(2,1)S(1)}, bf16[32,32,256]{2,1,0:T(8,128)(2,1)}, u32[]{:S(2)}, u32[]{:S(2)}) collective-permute-start(bf16[32,32,256]{2,1,0:T(8,128)(2,1)S(1)} %collective-permute-done.6.refs_9_.refs_11_), channel_id=1, source_target_pairs={{0,1},{1,2},{2,3},{3,11},{11,10},{10,9},{9,8},{8,0},{4,5},{5,6},{6... | collective-permute-start | bytes 1572872 | tf_op jit(solution)/shard_map/ppermute | solution.py:398
  46.2 24.0 %collective-permute-start.13 = (bf16[32,32,256]{2,1,0:T(8,128)(2,1)}, bf16[32,32,256]{2,1,0:T(8,128)(2,1)}, u32[]{:S(2)}, u32[]{:S(2)}) collective-permute-start(bf16[32,32,256]{2,1,0:T(8,128)(2,1)} %collective-permute-done.9.refs_12_.refs_14_), channel_id=1, source_target_pairs={{1,0},{2,1},{3,2},{11,3},{10,11},{9,10},{8,9},{0,8},{5,4},{6,5},{7... | collective-permute-start | bytes 1572872 | tf_op jit(solution)/shard_map/ppermute | solution.py:398
  46.3 28.4 %all-to-all-start = ((bf16[8,8,16,128]{3,2,1,0:T(8,128)(2,1)}), bf16[8,8,16,128]{3,2,1,0:T(8,128)(2,1)}, u32[]{:S(2)}, u32[]{:S(2)}) async-start(bf16[8,8,16,128]{3,2,1,0:T(8,128)(2,1)} %shard_map.55), calls=%async_computation | async-start | bytes 524288 | tf_op jit(solution)/shard_map/all_to_all | solution.py:441
  54.2 27.8 %collective-permute-start.11 = (bf16[32,32,256]{2,1,0:T(8,128)(2,1)}, bf16[32,32,256]{2,1,0:T(8,128)(2,1)S(1)}, u32[]{:S(2)}, u32[]{:S(2)}) collective-permute-start(bf16[32,32,256]{2,1,0:T(8,128)(2,1)} %collective-permute-done.7.refs_10_.refs_12_), channel_id=1, source_target_pairs={{1,0},{2,1},{3,2},{11,3},{10,11},{9,10},{8,9},{0,8},{5,4},{6,5},{7... | collective-permute-start | bytes 1572872 | tf_op jit(solution)/shard_map/ppermute | solution.py:398
  56.2 25.8 %collective-permute-start.12 = (bf16[32,32,256]{2,1,0:T(8,128)(2,1)}, bf16[32,32,256]{2,1,0:T(8,128)(2,1)}, u32[]{:S(2)}, u32[]{:S(2)}) collective-permute-start(bf16[32,32,256]{2,1,0:T(8,128)(2,1)} %collective-permute-done.8.refs_11_.refs_13_), channel_id=1, source_target_pairs={{0,1},{1,2},{2,3},{3,11},{11,10},{10,9},{9,8},{8,0},{4,5},{5,6},{6... | collective-permute-start | bytes 1572872 | tf_op jit(solution)/shard_map/ppermute | solution.py:398
  67.2 24.4 %collective-permute-start.14 = (bf16[32,32,256]{2,1,0:T(8,128)(2,1)}, bf16[32,32,256]{2,1,0:T(8,128)(2,1)}, u32[]{:S(2)}, u32[]{:S(2)}) collective-permute-start(bf16[32,32,256]{2,1,0:T(8,128)(2,1)} %collective-permute-done.10.refs_13_.refs_15_), channel_id=1, source_target_pairs={{0,1},{1,2},{2,3},{3,11},{11,10},{10,9},{9,8},{8,0},{4,5},{5,6},{6... | collective-permute-start | bytes 1572872 | tf_op jit(solution)/shard_map/ppermute | solution.py:398
  70.1 21.5 %collective-permute-start.15 = (bf16[32,32,256]{2,1,0:T(8,128)(2,1)}, bf16[32,32,256]{2,1,0:T(8,128)(2,1)}, u32[]{:S(2)}, u32[]{:S(2)}) collective-permute-start(bf16[32,32,256]{2,1,0:T(8,128)(2,1)} %collective-permute-done.13.refs_16_.refs_18_), channel_id=1, source_target_pairs={{1,0},{2,1},{3,2},{11,3},{10,11},{9,10},{8,9},{0,8},{5,4},{6,5},{7... | collective-permute-start | bytes 1572872 | tf_op jit(solution)/shard_map/ppermute | solution.py:398
  74.7 1.7 collective-permute-start.1
  76.5 0.7 copy-start.12
  82.0 9.7 %copy-start.7 = (bf16[32,32,256]{2,1,0:T(8,128)(2,1)}, bf16[32,32,256]{2,1,0:T(8,128)(2,1)S(1)}, u32[]{:S(2)}) copy-start(bf16[32,32,256]{2,1,0:T(8,128)(2,1)S(1)} %collective-permute-done.11.refs_14_.refs_16_) | copy-start | bytes 1572868
  106.1 2.9 %collective-permute-start.17 = (f32[64,32,128]{2,1,0:T(8,128)}, f32[64,32,128]{2,1,0:T(8,128)S(1)}, u32[]{:S(2)}, u32[]{:S(2)}) collective-permute-start(f32[64,32,128]{2,1,0:T(8,128)} %get-tuple-element.23.refs_1_), channel_id=1, source_target_pairs={{0,4},{4,0},{1,5},{5,1},{2,6},{6,2},{3,7},{7,3},{8,12},{12,8},{9,1... | collective-permute-start | bytes 3145736 | tf_op jit(solution)/shard_map/ppermute | solution.py:376
  106.2 4.4 %collective-permute-start.16 = (f32[64,32,128]{2,1,0:T(8,128)}, f32[64,32,128]{2,1,0:T(8,128)S(1)}, u32[]{:S(2)}, u32[]{:S(2)}) collective-permute-start(f32[64,32,128]{2,1,0:T(8,128)} %get-tuple-element.24.refs_3_), channel_id=1, source_target_pairs={{0,4},{4,0},{1,5},{5,1},{2,6},{6,2},{3,7},{7,3},{8,12},{12,8},{9,1... | collective-permute-start | bytes 3145736 | tf_op jit(solution)/shard_map/ppermute | solution.py:376
  109.1 1.5 copy-start.9
  110.6 1.0 copy-start.10
  127.0 2.9 %collective-permute-start.18 = (f32[64,32,128]{2,1,0:T(8,128)}, f32[64,32,128]{2,1,0:T(8,128)S(1)}, u32[]{:S(2)}, u32[]{:S(2)}) collective-permute-start(f32[64,32,128]{2,1,0:T(8,128)} %get-tuple-element.26), channel_id=1, source_target_pairs={{0,4},{4,0},{1,5},{5,1},{2,6},{6,2},{3,7},{7,3},{8,12},{12,8},{9,1... | collective-permute-start | bytes 3145736 | tf_op jit(solution)/shard_map/ppermute | solution.py:376
  130.0 1.0 copy-start.8
  152.6 1.5 collective-permute-start.19
  155.0 4.3 %collective-permute-start.20 = (f32[128,128]{1,0:T(8,128)S(1)}, f32[128,128]{1,0:T(8,128)S(1)}, u32[]{:S(2)}, u32[]{:S(2)}) collective-permute-start(f32[128,128]{1,0:T(8,128)S(1)} %add.20), channel_id=1, source_target_pairs={{0,8},{8,0},{1,9},{9,1},{2,10},{10,2},{3,11},{11,3},{4,12},{12,4},... | collective-permute-start | bytes 196616 | tf_op jit(solution)/shard_map/ppermute | solution.py:407
  159.2 6.5 %collective-permute-start.23 = (f32[128,128]{1,0:T(8,128)S(1)}, f32[128,128]{1,0:T(8,128)S(1)}, u32[]{:S(2)}, u32[]{:S(2)}) collective-permute-start(f32[128,128]{1,0:T(8,128)S(1)} %add.21), channel_id=1, source_target_pairs={{0,3},{1,2},{2,1},{3,0},{4,7},{5,6},{6,5},{7,4},{8,11},{9,10},{10,... | collective-permute-start | bytes 196616 | tf_op jit(solution)/shard_map/ppermute | solution.py:412
  159.3 7.3 %collective-permute-start.22 = (f32[128,128]{1,0:T(8,128)S(1)}, f32[128,128]{1,0:T(8,128)S(1)}, u32[]{:S(2)}, u32[]{:S(2)}) collective-permute-start(f32[128,128]{1,0:T(8,128)S(1)} %add.21), channel_id=1, source_target_pairs={{0,2},{1,3},{2,0},{3,1},{4,6},{5,7},{6,4},{7,5},{8,10},{9,11},{10,... | collective-permute-start | bytes 196616 | tf_op jit(solution)/shard_map/ppermute | solution.py:412
  160.1 6.5 %collective-permute-start.21 = (f32[128,128]{1,0:T(8,128)S(1)}, f32[128,128]{1,0:T(8,128)S(1)}, u32[]{:S(2)}, u32[]{:S(2)}) collective-permute-start(f32[128,128]{1,0:T(8,128)S(1)} %add.21), channel_id=1, source_target_pairs={{0,1},{1,0},{2,3},{3,2},{4,5},{5,4},{6,7},{7,6},{8,9},{9,8},{10,11... | collective-permute-start | bytes 196616 | tf_op jit(solution)/shard_map/ppermute | solution.py:412
  166.6 1.3 copy-start.11
  166.6 1.3 collective-permute-start.24
  167.9 0.6 copy-start.14

commit v5 on v4

--- a/solution.py
+++ b/solution.py
@@ -12,7 +12,9 @@
 ITERS = 2
 BF16 = jnp.bfloat16
 F32 = jnp.float32
-VMEM_BYTES = 56 * 1024 * 1024
+MIB = 1024 * 1024
+APPLY_BYTES = 30 * MIB
+SMALL_BYTES = 8 * MIB
 HIGH = lax.Precision.HIGHEST
 
 
@@ -20,31 +22,34 @@
     return pltpu.roll(value, shift % value.shape[-1], 1)
 
 
-def apply_kernel(n_vec, z_count, own, offsets, *refs):
+def apply_kernel(n_vec, z_count, own, offsets, keep, send, *refs):
     place_ref, *refs = refs
     vec_refs = (refs[:n_vec], refs[n_vec : 2 * n_vec])
     piece_refs = refs[2 * n_vec : 2 * n_vec + len(offsets)]
-    cov_ref, spec_ref, mine_ref, theirs_ref, beam_ref, vec_ref, *tiles, sems = refs[2 * n_vec + len(offsets) :]
-    z_refs, y_refs = tiles[: len(tiles) // 2], tiles[len(tiles) // 2 :]
-    out_refs = (mine_ref, theirs_ref)
-    count, rows, lanes = mine_ref.shape
+    cov_ref, spec_ref, *refs = refs[2 * n_vec + len(offsets) :]
+    *refs, beam_ref, vec_ref, z_ref, y_ref, sems = refs
+    n_out = len(keep) + len(send)
+    added, out_refs = refs[: len(refs) - n_out], refs[len(refs) - n_out :]
+    count, rows, lanes = out_refs[0].shape
     freqs = 2 * count
     half = rows // 2
     components = spec_ref.shape[0]
-    size, width, depth = piece_refs[0].shape
+    size, width, part_depth = piece_refs[0].shape
     chips = count // size * z_count
-    step = depth // len(z_refs)
+    tiles, _, step = z_ref.shape
     lane = lax.broadcasted_iota(jnp.int32, (half, lanes), 1)
     is_real = (lane // own) % 2 == 0
     sign = jnp.where(is_real, -1.0, 1.0).astype(F32)
 
     copies = []
-    for index, (core, offset) in enumerate(offsets):
+    for index, (core, offset, part) in enumerate(offsets):
         at = lax.rem(place_ref[0] + (offset % chips), chips)
         x_at = at // z_count
         z_at = jnp.where(x_at == 0, at, chips - 1 - at)
         target = beam_ref.at[
-            pl.ds(core * count + x_at * size, size), pl.ds(pl.multiple_of(z_at * width, width), width)
+            pl.ds(core * count + x_at * size, size),
+            pl.ds(pl.multiple_of(z_at * width, width), width),
+            pl.ds(part * part_depth, part_depth),
         ]
         copies.append(pltpu.make_async_copy(piece_refs[index], target, sems.at[index]))
     for copy in copies:
@@ -64,26 +69,28 @@
 
     def project(freq, carry):
         z = jnp.dot(vec_ref[freq], beam_ref[freq], preferred_element_type=F32)
-        for tile, z_ref in enumerate(z_refs):
-            z_ref[pl.ds(freq, rows, stride=freqs), :] = z[:, tile * step : (tile + 1) * step]
-        return carry
-
-    lax.fori_loop(0, freqs, project, 0, unroll=32)
+        for tile in range(tiles):
+            z_ref[tile, pl.ds(freq, rows, stride=freqs), :] = z[:, tile * step : (tile + 1) * step]
+        return carry
+
+    lax.fori_loop(0, freqs, project, 0, unroll=64)
 
     def mix(row, carry):
         start = pl.multiple_of(row * freqs, freqs)
-        z = jnp.concatenate([z_ref[pl.ds(start, freqs), :] for z_ref in z_refs], axis=1)
+        z = jnp.concatenate([z_ref[tile, pl.ds(start, freqs), :] for tile in range(tiles)], axis=1)
         scaled = [(z * spec_ref[k][None, :]).astype(BF16) for k in range(components)]
         y = jnp.dot(cov_ref[...], jnp.concatenate(scaled, axis=0), preferred_element_type=F32)
-        for tile, y_ref in enumerate(y_refs):
-            y_ref[pl.ds(start, freqs), :] = y[:, tile * step : (tile + 1) * step]
-        return carry
-
-    lax.fori_loop(0, rows, mix, 0, unroll=8)
+        for tile in range(tiles):
+            y_ref[tile, pl.ds(start, freqs), :] = y[:, tile * step : (tile + 1) * step]
+        return carry
+
+    lax.fori_loop(0, rows, mix, 0, unroll=32)
 
     def expand(side, place, carry):
         freq = side * count + place
-        y = [y_ref[pl.ds(freq, rows, stride=freqs), :].astype(BF16) for y_ref in y_refs]
+        y = [
+            y_ref[tile, pl.ds(freq, rows, stride=freqs), :].astype(BF16) for tile in range(tiles)
+        ]
         product = lax.dot_general(
             jnp.concatenate(y, axis=1),
             beam_ref[freq],
@@ -97,14 +104,20 @@
         )
         top = product[:half] + sign * swapped[half:]
         bottom = product[half:] - sign * swapped[:half]
-        out_refs[side][place] = jnp.concatenate([top, bottom], axis=0)
+        image = jnp.concatenate([top, bottom], axis=0)
+        if added:
+            image = image + added[side][place]
+        if side in keep:
+            out_refs[keep.index(side)][place] = image
+        if side in send:
+            out_refs[len(keep) + send.index(side)][place] = image.astype(BF16)
         return carry
 
     for side in range(2):
-        lax.fori_loop(0, count, functools.partial(expand, side), 0, unroll=32)
-
-
-def apply_covariance(place, vecs, beams, cov, spec, own, z_count):
+        lax.fori_loop(0, count, functools.partial(expand, side), 0, unroll=64)
+
+
+def apply_covariance(place, vecs, beams, cov, spec, own, z_count, keep, send, added=()):
     count, rows, lanes = vecs[0][0].shape
     freqs = 2 * count
     depth = spec.shape[1]
@@ -112,27 +125,29 @@
     flops = 2 * freqs * rows * (2 * lanes * depth + 2 * freqs * depth)
     vmem = pl.BlockSpec(memory_space=pltpu.VMEM)
     n_vec = len(vecs[0])
-    offsets = tuple((core, offset) for _, core, offset in beams)
-    tile = pltpu.VMEM((rows * freqs, step), F32)
-    return pl.pallas_call(
-        functools.partial(apply_kernel, n_vec, z_count, own, offsets),
-        out_shape=[jax.ShapeDtypeStruct((count, rows, lanes), F32)] * 2,
+    offsets = tuple(beam[1:] for beam in beams)
+    tiles = pltpu.VMEM((depth // step, rows * freqs, step), F32)
+    return pl.pallas_call(
+        functools.partial(apply_kernel, n_vec, z_count, own, offsets, keep, send),
+        out_shape=[jax.ShapeDtypeStruct((count, rows, lanes), F32)] * len(keep)
+        + [jax.ShapeDtypeStruct((count, rows, lanes), BF16)] * len(send),
         in_specs=[pl.BlockSpec(memory_space=pltpu.SMEM)]
         + [vmem] * (2 * n_vec)
         + [pl.BlockSpec(memory_space=pl.ANY)] * len(beams)
-        + [vmem] * 2,
-        out_specs=[vmem] * 2,
+        + [vmem] * (2 + len(added)),
+        out_specs=[vmem] * (len(keep) + len(send)),
         scratch_shapes=[
             pltpu.VMEM((freqs, lanes, depth), BF16),
             pltpu.VMEM((freqs, rows, lanes), BF16),
-            *[tile] * (2 * depth // step),
+            tiles,
+            tiles,
             pltpu.SemaphoreType.DMA((len(beams),)),
         ],
-        compiler_params=pltpu.CompilerParams(vmem_limit_bytes=VMEM_BYTES),
+        compiler_params=pltpu.CompilerParams(vmem_limit_bytes=APPLY_BYTES),
         cost_estimate=pl.CostEstimate(
             flops=flops, bytes_accessed=freqs * lanes * depth * 2, transcendentals=0
         ),
-    )(place, *vecs[0], *vecs[1], *[piece for piece, _, _ in beams], cov, spec)
+    )(place, *vecs[0], *vecs[1], *[beam[0] for beam in beams], cov, spec, *added)
 
 
 def pack_kernel(own, first_ref, second_ref, out_ref):
@@ -165,7 +180,7 @@
         out_shape=jax.ShapeDtypeStruct((x_count, z_count, groups, rows, lanes), BF16),
         in_specs=[pl.BlockSpec(memory_space=pltpu.VMEM)] * 2,
         out_specs=pl.BlockSpec(memory_space=pltpu.VMEM),
-        compiler_params=pltpu.CompilerParams(vmem_limit_bytes=VMEM_BYTES),
+        compiler_params=pltpu.CompilerParams(vmem_limit_bytes=SMALL_BYTES),
     )(first, second)
 
 
@@ -196,7 +211,7 @@
         out_shape=[jax.ShapeDtypeStruct((total, total), F32)] * 2,
         in_specs=[pl.BlockSpec(memory_space=pltpu.SMEM)] + [pl.BlockSpec(memory_space=pltpu.VMEM)] * 2,
         out_specs=[pl.BlockSpec(memory_space=pltpu.VMEM)] * 2,
-        compiler_params=pltpu.CompilerParams(vmem_limit_bytes=VMEM_BYTES),
+        compiler_params=pltpu.CompilerParams(vmem_limit_bytes=SMALL_BYTES),
     )(core, rows, start)
 
 
@@ -277,7 +292,7 @@
         in_specs=[pl.BlockSpec(memory_space=pltpu.SMEM)] + [pl.BlockSpec(memory_space=pltpu.VMEM)] * 3,
         out_specs=pl.BlockSpec(memory_space=pltpu.VMEM),
         scratch_shapes=[pltpu.VMEM((total, 2 * total), F32)],
-        compiler_params=pltpu.CompilerParams(vmem_limit_bytes=VMEM_BYTES),
+        compiler_params=pltpu.CompilerParams(vmem_limit_bytes=SMALL_BYTES),
     )(core, rows, kept, given)
 
 
@@ -303,7 +318,7 @@
         out_shape=[jax.ShapeDtypeStruct((freqs, parts * own, multipoles // 2), BF16)] * 2,
         in_specs=[pl.BlockSpec(memory_space=pltpu.SMEM)] + [pl.BlockSpec(memory_space=pltpu.VMEM)] * 2,
         out_specs=[pl.BlockSpec(memory_space=pltpu.VMEM)] * 2,
-        compiler_params=pltpu.CompilerParams(vmem_limit_bytes=VMEM_BYTES),
+        compiler_params=pltpu.CompilerParams(vmem_limit_bytes=SMALL_BYTES),
     )(core, beam, noise.T)
 
 
@@ -333,7 +348,7 @@
         out_shape=jax.ShapeDtypeStruct((receivers, groups, vectors // receivers, lanes), BF16),
         in_specs=[pl.BlockSpec(memory_space=pltpu.VMEM)],
         out_specs=pl.BlockSpec(memory_space=pltpu.VMEM),
-        compiler_params=pltpu.CompilerParams(vmem_limit_bytes=VMEM_BYTES),
+        compiler_params=pltpu.CompilerParams(vmem_limit_bytes=SMALL_BYTES),
     )(start)
 
 
@@ -368,7 +383,7 @@
         out_shape=[jax.ShapeDtypeStruct((freqs, 2 * mine, lanes), BF16)] * 2,
         in_specs=[pl.BlockSpec(memory_space=pltpu.VMEM)] * 2,
         out_specs=[pl.BlockSpec(memory_space=pltpu.VMEM)] * 2,
-        compiler_params=pltpu.CompilerParams(vmem_limit_bytes=VMEM_BYTES),
+        compiler_params=pltpu.CompilerParams(vmem_limit_bytes=SMALL_BYTES),
     )(*sides)
 
 
@@ -390,7 +405,7 @@
     x_place, z_place = lax.axis_index("x"), lax.axis_index("fc")
     place = jnp.where(x_place == 0, z_place, count - 1 - z_place).astype(jnp.int32).reshape(1)
     moving = {(core, way): block for core, block in enumerate(blocks) for way in (1, -1)}
-    found = [(block, core, 0) for core, block in enumerate(blocks)]
+    found = [(block, core, 0, 0) for core, block in enumerate(blocks)]
     for hop in range(1, count // 2 + 1):
         for core, way in moving:
             if 2 * hop == count and (way == 1) != (core == 0):
@@ -398,7 +413,7 @@
             moving[core, way] = lax.ppermute(moving[core, way], ("x", "fc"), pairs[way])
             if hop == 1 and core == 0 and way == 1:
                 late, moving[core, way] = after(late, moving[core, way])
-            found.append((moving[core, way], core, -way * hop))
+            found.append((moving[core, way], core, -way * hop, 0))
     return place, found, late
 
 
@@ -442,14 +457,15 @@
     start = start.reshape(x_count, z_count, *start.shape[1:])
     operand = start_operand([start, swap_cores(start)], own)
 
-    mine, theirs = apply_covariance(
-        place, [[operand[0]], [operand[1]]], beams, cov, spec, own, z_count
-    )
-    got_mine, got_theirs = swap_cores(theirs), swap_cores(mine)
-    second_mine, second_theirs = apply_covariance(
-        place, [[mine, got_mine], [theirs, got_theirs]], beams, cov, spec, own, z_count
-    )
-    packed = pack(second_mine, swap_cores(second_theirs), x_count, z_count, own)
+    apply = functools.partial(apply_covariance, place)
+    mine, theirs, mine_sent, theirs_sent = apply(
+        [[operand[0]], [operand[1]]], beams, cov, spec, own, z_count, (0, 1), (0, 1)
+    )
+    got_mine, got_theirs = swap_cores(theirs_sent), swap_cores(mine_sent)
+    second_mine, second_sent = apply(
+        [[mine, got_mine], [theirs, got_theirs]], beams, cov, spec, own, z_count, (0,), (1,)
+    )
+    packed = pack(second_mine, swap_cores(second_sent), x_count, z_count, own)
     packed = packed.reshape(x_count * z_count, *packed.shape[2:])
     received = lax.all_to_all(packed, ("x", "fc"), 0, 0, tiled=True)
     groups, lanes = received.shape[1], received.shape[3]

time: 180 us -> 159 us (0.88)
  Pallas kernels: 55.5 us -> 37.6 us
  waiting for transfers between devices: 64.5 us -> 61.6 us
    pallas_call x2, Pallas kernels: 29.9 us -> 21.2 us  [apply_covariance(): pl.pallas_call(functools.partial(apply_kernel, n_vec, z_count, own, offse...]
    ppermute x7, waiting for transfers between devices: 9.37 us -> 6.4 us  [swap_cores(): return lax.ppermute(value, 'core', [(0, 1), (1, 0)])]
    pallas_call x1, Pallas kernels: 3.01 us -> 0.78 us  [pack(): pl.pallas_call(functools.partial(pack_kernel, own), out_shape=jax.ShapeDt...]
    pallas_call x1, Pallas kernels: 2.52 us -> 0.31 us  [whiten(): pl.pallas_call(whiten_kernel, out_shape=[jax.ShapeDtypeStruct((freqs, par...]
  transfers between devices with their start and end apart: 26 -> 26, of which waited for: 16 -> 15; matrix products, arithmetic and copies ran while one was open for 2% -> 4% of each run, Pallas kernels for 4% -> 3%
where the time goes in v5:
time: 159 us; the launch traced here: 158 us
  waiting for transfers between devices  61.6 us (39%)
  Pallas kernels  37.6 us (24%)
  starting transfers between devices  34 us (21%)
  blocking collectives  16.2 us (10%)
  local copies, waits for them, and re-layouts  5.83 us (4%)
  other arithmetic  2.95 us (2%)
    ppermute x14, waiting for transfers between devices, gather_ring(): moving[core, way] = lax.ppermute(moving[core, way], ('x', 'fc'), pairs[way])  47.9 us
    ppermute x14, starting transfers between devices, gather_ring(): moving[core, way] = lax.ppermute(moving[core, way], ('x', 'fc'), pairs[way])  21.4 us
    pallas_call x2, Pallas kernels, apply_covariance(): pl.pallas_call(functools.partial(apply_kernel, n_vec, z_count, own, offse...  21.2 us
    all_to_all x1, blocking collectives, body_split(): received = lax.all_to_all(packed, ('x', 'fc'), 0, 0, tiled=True)  16.2 us
    pallas_call x1, Pallas kernels, finish(): pl.pallas_call(functools.partial(finish_kernel, scale), out_shape=jax.Sha...  9.6 us
    ppermute x7, waiting for transfers between devices, swap_cores(): return lax.ppermute(value, 'core', [(0, 1), (1, 0)])  6.4 us
    all_to_all x1, starting transfers between devices, body_split(): start = lax.all_to_all(start, ('x', 'fc'), 0, 0, tiled=True)  6.09 us
    ppermute x3, starting transfers between devices, sum_devices(): lax.ppermute(value, 'fc', [(j, j ^ s) for j in range(z_count)])  4.45 us
  transfers between devices with their start and end apart: 26, of which 15 were waited for; matrix products, arithmetic and copies ran while one was open for 4% of the time, Pallas kernels for 3%

profile of v5, /device:TPU:0, one launch (start us, length us, event | category | flops | bytes accessed | tf_op | source)
XLA Modules:
  0.0 158.5 jit_solution(15537607372345420989)
XLA Ops:
  0.0 0.7 copy-done.3
  0.7 1.2 copy-done.2
  1.9 0.3 shard_map.56
  2.3 0.5 collective-permute-start.2
  2.8 2.6 %collective-permute-start = (bf16[32,32,256]{2,1,0:T(8,128)(2,1)S(1)}, bf16[32,32,256]{2,1,0:T(8,128)(2,1)S(1)}, u32[]{:S(2)}, u32[]{:S(2)}) collective-permute-start(bf16[32,32,256]{2,1,0:T(8,128)(2,1)S(1)} %get-tuple-element.19.refs_3_.refs_5_), channel_id=1, source_target_pairs={{0,1},{1,2},{2,3},{3,11},{11,10},{10,9},{9,8},{8,0},{4,5},{5,6},{6... | collective-permute-start | bytes 1572872 | tf_op jit(solution)/shard_map/ppermute | solution.py:413
  5.4 0.0 collective-permute-done.2.refs_4_.refs_6_
  5.4 1.8 %collective-permute-start.5 = (bf16[32,32,256]{2,1,0:T(8,128)(2,1)S(1)}, bf16[32,32,256]{2,1,0:T(8,128)(2,1)S(1)}, u32[]{:S(2)}, u32[]{:S(2)}) collective-permute-start(bf16[32,32,256]{2,1,0:T(8,128)(2,1)S(1)} %collective-permute-done.2.refs_4_.refs_6_), channel_id=1, source_target_pairs={{1,0},{2,1},{3,2},{11,3},{10,11},{9,10},{8,9},{0,8},{5,4},{6,5},{7... | collective-permute-start | bytes 1572872 | tf_op jit(solution)/shard_map/ppermute | solution.py:413
  7.2 1.6 collective-permute-start.3
  8.8 1.5 shard_map.55
  10.3 7.6 %collective-permute-done.refs_5_.refs_7_ = bf16[32,32,256]{2,1,0:T(8,128)(2,1)S(1)} collective-permute-done((bf16[32,32,256]{2,1,0:T(8,128)(2,1)S(1)}, bf16[32,32,256]{2,1,0:T(8,128)(2,1)S(1)}, u32[]{:S(2)}, u32[]{:S(2)}) %collective-permute-start) | collective-permute-done | bytes 524320 | tf_op jit(solution)/shard_map/ppermute | solution.py:413
  17.9 1.8 %collective-permute-start.4 = (bf16[32,32,256]{2,1,0:T(8,128)(2,1)S(1)}, bf16[32,32,256]{2,1,0:T(8,128)(2,1)}, u32[]{:S(2)}, u32[]{:S(2)}) collective-permute-start(bf16[32,32,256]{2,1,0:T(8,128)(2,1)S(1)} %collective-permute-done.2.refs_4_.refs_6_), channel_id=1, source_target_pairs={{0,1},{1,2},{2,3},{3,11},{11,10},{10,9},{9,8},{8,0},{4,5},{5,6},{6... | collective-permute-start | bytes 1572872 | tf_op jit(solution)/shard_map/ppermute | solution.py:413
  19.7 1.6 collective-permute-start.6
  21.3 0.0 collective-permute-done.5.refs_8_.refs_10_
  21.3 0.7 collective-permute-start.9
  21.9 9.5 %collective-permute-done.3.refs_6_.refs_8_ = bf16[32,32,256]{2,1,0:T(8,128)(2,1)S(1)} collective-permute-done((bf16[32,32,256]{2,1,0:T(8,128)(2,1)S(1)}, bf16[32,32,256]{2,1,0:T(8,128)(2,1)S(1)}, u32[]{:S(2)}, u32[]{:S(2)}) %collective-permute-start.3) | collective-permute-done | bytes 524320 | tf_op jit(solution)/shard_map/ppermute | solution.py:413
  31.4 1.8 %collective-permute-start.7 = (bf16[32,32,256]{2,1,0:T(8,128)(2,1)S(1)}, bf16[32,32,256]{2,1,0:T(8,128)(2,1)}, u32[]{:S(2)}, u32[]{:S(2)}) collective-permute-start(bf16[32,32,256]{2,1,0:T(8,128)(2,1)S(1)} %collective-permute-done.3.refs_6_.refs_8_), channel_id=1, source_target_pairs={{1,0},{2,1},{3,2},{11,3},{10,11},{9,10},{8,9},{0,8},{5,4},{6,5},{7... | collective-permute-start | bytes 1572872 | tf_op jit(solution)/shard_map/ppermute | solution.py:413
  33.2 0.0 collective-permute-done.4.refs_7_.refs_9_
  33.2 1.4 collective-permute-start.8
  34.6 9.4 %collective-permute-done.6.refs_9_.refs_11_ = bf16[32,32,256]{2,1,0:T(8,128)(2,1)} collective-permute-done((bf16[32,32,256]{2,1,0:T(8,128)(2,1)S(1)}, bf16[32,32,256]{2,1,0:T(8,128)(2,1)}, u32[]{:S(2)}, u32[]{:S(2)}) %collective-permute-start.6) | collective-permute-done | bytes 524320 | tf_op jit(solution)/shard_map/ppermute | solution.py:413
  44.0 1.9 %collective-permute-start.10 = (bf16[32,32,256]{2,1,0:T(8,128)(2,1)}, bf16[32,32,256]{2,1,0:T(8,128)(2,1)}, u32[]{:S(2)}, u32[]{:S(2)}) collective-permute-start(bf16[32,32,256]{2,1,0:T(8,128)(2,1)} %collective-permute-done.6.refs_9_.refs_11_), channel_id=1, source_target_pairs={{0,1},{1,2},{2,3},{3,11},{11,10},{10,9},{9,8},{8,0},{4,5},{5,6},{6... | collective-permute-start | bytes 1572872 | tf_op jit(solution)/shard_map/ppermute | solution.py:413
  45.9 0.2 collective-permute-start.13
  46.0 6.1 %all-to-all-start = ((bf16[8,8,16,128]{3,2,1,0:T(8,128)(2,1)}), bf16[8,8,16,128]{3,2,1,0:T(8,128)(2,1)S(1)}, u32[]{:S(2)}, u32[]{:S(2)}) async-start(bf16[8,8,16,128]{3,2,1,0:T(8,128)(2,1)} %shard_map.55), calls=%async_computation | async-start | bytes 524288 | tf_op jit(solution)/shard_map/all_to_all | solution.py:456
  52.1 1.9 %collective-permute-done.7.refs_10_.refs_12_ = bf16[32,32,256]{2,1,0:T(8,128)(2,1)} collective-permute-done((bf16[32,32,256]{2,1,0:T(8,128)(2,1)S(1)}, bf16[32,32,256]{2,1,0:T(8,128)(2,1)}, u32[]{:S(2)}, u32[]{:S(2)}) %collective-permute-start.7) | collective-permute-done | bytes 524320 | tf_op jit(solution)/shard_map/ppermute | solution.py:413
  54.0 1.8 %collective-permute-start.11 = (bf16[32,32,256]{2,1,0:T(8,128)(2,1)}, bf16[32,32,256]{2,1,0:T(8,128)(2,1)}, u32[]{:S(2)}, u32[]{:S(2)}) collective-permute-start(bf16[32,32,256]{2,1,0:T(8,128)(2,1)} %collective-permute-done.7.refs_10_.refs_12_), channel_id=1, source_target_pairs={{1,0},{2,1},{3,2},{11,3},{10,11},{9,10},{8,9},{0,8},{5,4},{6,5},{7... | collective-permute-start | bytes 1572872 | tf_op jit(solution)/shard_map/ppermute | solution.py:413
  55.8 1.3 collective-permute-start.12
  57.1 9.7 %collective-permute-done.10.refs_13_.refs_15_ = bf16[32,32,256]{2,1,0:T(8,128)(2,1)} collective-permute-done((bf16[32,32,256]{2,1,0:T(8,128)(2,1)}, bf16[32,32,256]{2,1,0:T(8,128)(2,1)}, u32[]{:S(2)}, u32[]{:S(2)}) %collective-permute-start.10) | collective-permute-done | bytes 524320 | tf_op jit(solution)/shard_map/ppermute | solution.py:413
  66.8 3.0 %collective-permute-start.14 = (bf16[32,32,256]{2,1,0:T(8,128)(2,1)}, bf16[32,32,256]{2,1,0:T(8,128)(2,1)}, u32[]{:S(2)}, u32[]{:S(2)}) collective-permute-start(bf16[32,32,256]{2,1,0:T(8,128)(2,1)} %collective-permute-done.10.refs_13_.refs_15_), channel_id=1, source_target_pairs={{0,1},{1,2},{2,3},{3,11},{11,10},{10,9},{9,8},{8,0},{4,5},{5,6},{6... | collective-permute-start | bytes 1572872 | tf_op jit(solution)/shard_map/ppermute | solution.py:413
  69.8 0.0 collective-permute-done.13.refs_16_.refs_18_
  69.9 0.9 convert_element_type.6
  70.8 0.9 convert_element_type.7
  71.6 1.8 %copy.7 = bf16[2,2,2,32,2,2,32]{6,4,5,0,3,1,2:T(2,128)(2,1)} copy(bf16[2,2,2,32,2,2,32]{6,5,4,3,2,1,0:T(2,128)(2,1)} %convert_element_type.7) | data formatting | bytes 131072 | tf_op jit(solution)/shard_map/convert_element_type | solution.py:452
  73.5 0.7 all-to-all-done
  74.2 0.0 collective-permute-start.1
  74.2 2.0 %fusion = bf16[2,2,32,2,2,2,32]{6,5,4,3,2,1,0:T(2,128)(2,1)} fusion(bf16[2,2,2,32,2,2,32]{6,4,5,0,3,1,2:T(2,128)(2,1)} %copy.7, pred[]{:T(512)S(6)} %eq.7), kind=kLoop, calls=%fused_computation.1 | loop fusion | flops 32768 | bytes 131073 | tf_op jit(solution)/shard_map/transpose | solution.py:454
  76.2 1.2 reshape.29.refs_19_.refs_21_
  77.4 0.0 collective-permute-done.1.refs_1_
  77.5 3.9 %shard_map.57 = (bf16[64,32,128]{2,1,0:T(8,128)(2,1)S(1)}, bf16[64,32,128]{2,1,0:T(8,128)(2,1)S(1)}) custom-call(bf16[2,4,8,16,128]{4,3,2,1,0:T(8,128)(2,1)S(1)} %bitcast.17, bf16[2,4,8,16,128]{4,3,2,1,0:T(8,128)(2,1)} %collective-permute-done.1.refs_1_), custom_call_target="tpu_custom_call" | custom-call | tf_op jit(solution)/shard_map/pallas_call | solution.py:381
  81.3 0.0 collective-permute-done.11.refs_14_.refs_16_
  81.4 9.8 %collective-permute-done.14.refs_17_.refs_19_ = bf16[32,32,256]{2,1,0:T(8,128)(2,1)} collective-permute-done((bf16[32,32,256]{2,1,0:T(8,128)(2,1)}, bf16[32,32,256]{2,1,0:T(8,128)(2,1)}, u32[]{:S(2)}, u32[]{:S(2)}) %collective-permute-start.14) | collective-permute-done | bytes 524320 | tf_op jit(solution)/shard_map/ppermute | solution.py:413
  91.2 0.0 collective-permute-done.15.refs_18_.refs_20_
  91.2 10.6 %shard_map.58 = (f32[64,32,128]{2,1,0:T(8,128)S(1)}, f32[64,32,128]{2,1,0:T(8,128)S(1)}, bf16[64,32,128]{2,1,0:T(8,128)(2,1)S(1)}, bf16[64,32,128]{2,1,0:T(8,128)(2,1)S(1)}) custom-call(s32[1]{0:T(128)} %bitcast.1.refs_0_, bf16[64,32,128]{2,1,0:T(8,128)(2,1)S(1)} %get-tuple-element.21.refs_1_, bf16[64,32,128]{2,1,0:T(8,128)(2,1)S(1)} %get-tuple-element.22.refs_2_, ...), custom_call_target="tpu_custom_call" | custom-call | flops 1073741824 | bytes 8388608 | tf_op jit(solution)/shard_map/pallas_call | solution.py:130
  101.8 0.1 collective-permute-start.16
  101.9 0.5 collective-permute-start.17
  102.4 1.4 collective-permute-done.16.refs_2_
  103.8 0.7 collective-permute-done.17.refs_4_
  104.5 10.6 %shard_map.59 = (f32[64,32,128]{2,1,0:T(8,128)S(1)}, bf16[64,32,128]{2,1,0:T(8,128)(2,1)S(1)}) custom-call(s32[1]{0:T(128)} %bitcast.1.refs_0_, f32[64,32,128]{2,1,0:T(8,128)S(1)} %get-tuple-element.25.refs_1_, bf16[64,32,128]{2,1,0:T(8,128)(2,1)S(1)} %collective-permute-done.16.refs_2_, f32[64,32,128]{2,1,0:T(8,128)S(1)} %get-tuple-element.27.refs_3_, ...), custom_call_target="tpu_custom_call" | custom-call | flops 1073741824 | bytes 8388608 | tf_op jit(solution)/shard_map/pallas_call | solution.py:130
  115.1 0.2 collective-permute-start.18
  115.3 1.8 %collective-permute-done.18.second_ref = bf16[64,32,128]{2,1,0:T(8,128)(2,1)S(1)} collective-permute-done((bf16[64,32,128]{2,1,0:T(8,128)(2,1)S(1)}, bf16[64,32,128]{2,1,0:T(8,128)(2,1)S(1)}, u32[]{:S(2)}, u32[]{:S(2)}) %collective-permute-start.18) | collective-permute-done | bytes 524320 | tf_op jit(solution)/shard_map/ppermute | solution.py:391
  117.1 0.8 shard_map.60
  117.9 16.2 %all_to_all.10 = bf16[8,4,32,128]{3,2,1,0:T(8,128)(2,1)S(1)} all-to-all(bf16[8,4,32,128]{3,2,1,0:T(8,128)(2,1)S(1)} %bitcast.15), channel_id=1, replica_groups=mesh['ma'=2,'x'=2,'core'=2,'fc'=4] {'x','fc'}, dimensions={0} | all-to-all | bytes 524288 | tf_op jit(solution)/shard_map/all_to_all | solution.py:470
  134.1 0.4 shard_map.61
  134.5 0.1 collective-permute-start.19
  134.6 1.2 collective-permute-done.19
  135.8 0.6 collective-permute-start.20
  136.5 3.7 %collective-permute-done.20 = f32[128,128]{1,0:T(8,128)S(1)} collective-permute-done((f32[128,128]{1,0:T(8,128)S(1)}, f32[128,128]{1,0:T(8,128)S(1)}, u32[]{:S(2)}, u32[]{:S(2)}) %collective-permute-start.20) | collective-permute-done | bytes 65568 | tf_op jit(solution)/shard_map/ppermute | solution.py:422
  140.2 0.1 collective-permute-start.23
  140.3 0.8 collective-permute-start.22
  141.1 3.6 %collective-permute-start.21 = (f32[128,128]{1,0:T(8,128)S(1)}, f32[128,128]{1,0:T(8,128)S(1)}, u32[]{:S(2)}, u32[]{:S(2)}) collective-permute-start(f32[128,128]{1,0:T(8,128)S(1)} %add.21), channel_id=1, source_target_pairs={{0,1},{1,0},{2,3},{3,2},{4,5},{5,4},{6,7},{7,6},{8,9},{9,8},{10,11... | collective-permute-start | bytes 196616 | tf_op jit(solution)/shard_map/ppermute | solution.py:427
  144.6 2.0 %collective-permute-done.23 = f32[128,128]{1,0:T(8,128)S(1)} collective-permute-done((f32[128,128]{1,0:T(8,128)S(1)}, f32[128,128]{1,0:T(8,128)S(1)}, u32[]{:S(2)}, u32[]{:S(2)}) %collective-permute-start.23) | collective-permute-done | bytes 65568 | tf_op jit(solution)/shard_map/ppermute | solution.py:427
  146.6 0.9 collective-permute-done.22
  147.5 0.0 collective-permute-done.21
  147.5 0.1 collective-permute-start.24
  147.6 1.2 collective-permute-done.24.given_ref
  148.9 9.6 %shard_map.62 = f32[2,4,128,128]{3,2,1,0:T(8,128)} custom-call(s32[1]{0:T(128)} %bitcast.core_ref, bf16[8,4,2,16,128]{4,3,2,1,0:T(8,128)(2,1)S(1)} %bitcast.14, f32[128,128]{1,0:T(8,128)S(1)} %add_add_fusion.kept_ref, f32[128,128]{1,0:T(8,128)S(1)} %collective-permute-done.24.given_ref), custom_call_target="tpu_custom_call" | custom-call | tf_op jit(solution)/shard_map/pallas_call | solution.py:289
  (14 shorter events, 0.1 us)
Async XLA Ops:
  0.0 77.4 %copy-start = (f32[2,512]{1,0:T(2,128)S(1)}, f32[2,512]{1,0:T(2,128)}, u32[]{:S(2)}) copy-start(f32[2,512]{1,0:T(2,128)} %param.7) | copy-start | bytes 12292
  0.0 0.7 copy-start.3
  0.7 1.2 copy-start.2
  1.9 6.8 %copy-start.1 = (f32[2,32,16,128]{3,2,1,0:T(8,128)S(1)}, f32[2,32,16,128]{3,2,1,0:T(8,128)}, u32[]{:S(2)}) copy-start(f32[2,32,16,128]{3,2,1,0:T(8,128)} %start_ref.3) | copy-start | bytes 1572868
  2.3 3.2 %collective-permute-start.2 = (bf16[32,32,256]{2,1,0:T(8,128)(2,1)S(1)}, bf16[32,32,256]{2,1,0:T(8,128)(2,1)S(1)}, u32[]{:S(2)}, u32[]{:S(2)}) collective-permute-start(bf16[32,32,256]{2,1,0:T(8,128)(2,1)S(1)} %get-tuple-element.23), channel_id=1, source_target_pairs={{0,4},{4,0},{1,5},{5,1},{2,6},{6,2},{3,7},{7,3},{8,12},{12,8},{9,1... | collective-permute-start | bytes 1572872 | tf_op jit(solution)/shard_map/ppermute | solution.py:391
  2.8 15.1 %collective-permute-start = (bf16[32,32,256]{2,1,0:T(8,128)(2,1)S(1)}, bf16[32,32,256]{2,1,0:T(8,128)(2,1)S(1)}, u32[]{:S(2)}, u32[]{:S(2)}) collective-permute-start(bf16[32,32,256]{2,1,0:T(8,128)(2,1)S(1)} %get-tuple-element.19.refs_3_.refs_5_), channel_id=1, source_target_pairs={{0,1},{1,2},{2,3},{3,11},{11,10},{10,9},{9,8},{8,0},{4,5},{5,6},{6... | collective-permute-start | bytes 1572872 | tf_op jit(solution)/shard_map/ppermute | solution.py:413
  5.4 15.9 %collective-permute-start.5 = (bf16[32,32,256]{2,1,0:T(8,128)(2,1)S(1)}, bf16[32,32,256]{2,1,0:T(8,128)(2,1)S(1)}, u32[]{:S(2)}, u32[]{:S(2)}) collective-permute-start(bf16[32,32,256]{2,1,0:T(8,128)(2,1)S(1)} %collective-permute-done.2.refs_4_.refs_6_), channel_id=1, source_target_pairs={{1,0},{2,1},{3,2},{11,3},{10,11},{9,10},{8,9},{0,8},{5,4},{6,5},{7... | collective-permute-start | bytes 1572872 | tf_op jit(solution)/shard_map/ppermute | solution.py:413
  7.2 24.2 %collective-permute-start.3 = (bf16[32,32,256]{2,1,0:T(8,128)(2,1)S(1)}, bf16[32,32,256]{2,1,0:T(8,128)(2,1)S(1)}, u32[]{:S(2)}, u32[]{:S(2)}) collective-permute-start(bf16[32,32,256]{2,1,0:T(8,128)(2,1)S(1)} %get-tuple-element.19.refs_3_.refs_5_), channel_id=1, source_target_pairs={{1,0},{2,1},{3,2},{11,3},{10,11},{9,10},{8,9},{0,8},{5,4},{6,5},{7... | collective-permute-start | bytes 1572872 | tf_op jit(solution)/shard_map/ppermute | solution.py:413
  17.9 15.3 %collective-permute-start.4 = (bf16[32,32,256]{2,1,0:T(8,128)(2,1)S(1)}, bf16[32,32,256]{2,1,0:T(8,128)(2,1)}, u32[]{:S(2)}, u32[]{:S(2)}) collective-permute-start(bf16[32,32,256]{2,1,0:T(8,128)(2,1)S(1)} %collective-permute-done.2.refs_4_.refs_6_), channel_id=1, source_target_pairs={{0,1},{1,2},{2,3},{3,11},{11,10},{10,9},{9,8},{8,0},{4,5},{5,6},{6... | collective-permute-start | bytes 1572872 | tf_op jit(solution)/shard_map/ppermute | solution.py:413
  19.7 24.3 %collective-permute-start.6 = (bf16[32,32,256]{2,1,0:T(8,128)(2,1)S(1)}, bf16[32,32,256]{2,1,0:T(8,128)(2,1)}, u32[]{:S(2)}, u32[]{:S(2)}) collective-permute-start(bf16[32,32,256]{2,1,0:T(8,128)(2,1)S(1)} %collective-permute-done.refs_5_.refs_7_), channel_id=1, source_target_pairs={{0,1},{1,2},{2,3},{3,11},{11,10},{10,9},{9,8},{8,0},{4,5},{5,6},{6... | collective-permute-start | bytes 1572872 | tf_op jit(solution)/shard_map/ppermute | solution.py:413
  21.3 24.6 %collective-permute-start.9 = (bf16[32,32,256]{2,1,0:T(8,128)(2,1)S(1)}, bf16[32,32,256]{2,1,0:T(8,128)(2,1)}, u32[]{:S(2)}, u32[]{:S(2)}) collective-permute-start(bf16[32,32,256]{2,1,0:T(8,128)(2,1)S(1)} %collective-permute-done.5.refs_8_.refs_10_), channel_id=1, source_target_pairs={{1,0},{2,1},{3,2},{11,3},{10,11},{9,10},{8,9},{0,8},{5,4},{6,5},{7... | collective-permute-start | bytes 1572872 | tf_op jit(solution)/shard_map/ppermute | solution.py:413
  31.4 22.6 %collective-permute-start.7 = (bf16[32,32,256]{2,1,0:T(8,128)(2,1)S(1)}, bf16[32,32,256]{2,1,0:T(8,128)(2,1)}, u32[]{:S(2)}, u32[]{:S(2)}) collective-permute-start(bf16[32,32,256]{2,1,0:T(8,128)(2,1)S(1)} %collective-permute-done.3.refs_6_.refs_8_), channel_id=1, source_target_pairs={{1,0},{2,1},{3,2},{11,3},{10,11},{9,10},{8,9},{0,8},{5,4},{6,5},{7... | collective-permute-start | bytes 1572872 | tf_op jit(solution)/shard_map/ppermute | solution.py:413
  33.2 22.6 %collective-permute-start.8 = (bf16[32,32,256]{2,1,0:T(8,128)(2,1)}, bf16[32,32,256]{2,1,0:T(8,128)(2,1)}, u32[]{:S(2)}, u32[]{:S(2)}) collective-permute-start(bf16[32,32,256]{2,1,0:T(8,128)(2,1)} %collective-permute-done.4.refs_7_.refs_9_), channel_id=1, source_target_pairs={{0,1},{1,2},{2,3},{3,11},{11,10},{10,9},{9,8},{8,0},{4,5},{5,6},{6... | collective-permute-start | bytes 1572872 | tf_op jit(solution)/shard_map/ppermute | solution.py:413
  44.0 22.8 %collective-permute-start.10 = (bf16[32,32,256]{2,1,0:T(8,128)(2,1)}, bf16[32,32,256]{2,1,0:T(8,128)(2,1)}, u32[]{:S(2)}, u32[]{:S(2)}) collective-permute-start(bf16[32,32,256]{2,1,0:T(8,128)(2,1)} %collective-permute-done.6.refs_9_.refs_11_), channel_id=1, source_target_pairs={{0,1},{1,2},{2,3},{3,11},{11,10},{10,9},{9,8},{8,0},{4,5},{5,6},{6... | collective-permute-start | bytes 1572872 | tf_op jit(solution)/shard_map/ppermute | solution.py:413
  45.9 24.0 %collective-permute-start.13 = (bf16[32,32,256]{2,1,0:T(8,128)(2,1)}, bf16[32,32,256]{2,1,0:T(8,128)(2,1)}, u32[]{:S(2)}, u32[]{:S(2)}) collective-permute-start(bf16[32,32,256]{2,1,0:T(8,128)(2,1)} %collective-permute-done.9.refs_12_.refs_14_), channel_id=1, source_target_pairs={{1,0},{2,1},{3,2},{11,3},{10,11},{9,10},{8,9},{0,8},{5,4},{6,5},{7... | collective-permute-start | bytes 1572872 | tf_op jit(solution)/shard_map/ppermute | solution.py:413
  46.0 28.2 %all-to-all-start = ((bf16[8,8,16,128]{3,2,1,0:T(8,128)(2,1)}), bf16[8,8,16,128]{3,2,1,0:T(8,128)(2,1)S(1)}, u32[]{:S(2)}, u32[]{:S(2)}) async-start(bf16[8,8,16,128]{3,2,1,0:T(8,128)(2,1)} %shard_map.55), calls=%async_computation | async-start | bytes 524288 | tf_op jit(solution)/shard_map/all_to_all | solution.py:456
  54.0 27.4 %collective-permute-start.11 = (bf16[32,32,256]{2,1,0:T(8,128)(2,1)}, bf16[32,32,256]{2,1,0:T(8,128)(2,1)}, u32[]{:S(2)}, u32[]{:S(2)}) collective-permute-start(bf16[32,32,256]{2,1,0:T(8,128)(2,1)} %collective-permute-done.7.refs_10_.refs_12_), channel_id=1, source_target_pairs={{1,0},{2,1},{3,2},{11,3},{10,11},{9,10},{8,9},{0,8},{5,4},{6,5},{7... | collective-permute-start | bytes 1572872 | tf_op jit(solution)/shard_map/ppermute | solution.py:413
  55.8 25.6 %collective-permute-start.12 = (bf16[32,32,256]{2,1,0:T(8,128)(2,1)}, bf16[32,32,256]{2,1,0:T(8,128)(2,1)}, u32[]{:S(2)}, u32[]{:S(2)}) collective-permute-start(bf16[32,32,256]{2,1,0:T(8,128)(2,1)} %collective-permute-done.8.refs_11_.refs_13_), channel_id=1, source_target_pairs={{0,1},{1,2},{2,3},{3,11},{11,10},{10,9},{9,8},{8,0},{4,5},{5,6},{6... | collective-permute-start | bytes 1572872 | tf_op jit(solution)/shard_map/ppermute | solution.py:413
  66.8 24.4 %collective-permute-start.14 = (bf16[32,32,256]{2,1,0:T(8,128)(2,1)}, bf16[32,32,256]{2,1,0:T(8,128)(2,1)}, u32[]{:S(2)}, u32[]{:S(2)}) collective-permute-start(bf16[32,32,256]{2,1,0:T(8,128)(2,1)} %collective-permute-done.10.refs_13_.refs_15_), channel_id=1, source_target_pairs={{0,1},{1,2},{2,3},{3,11},{11,10},{10,9},{9,8},{8,0},{4,5},{5,6},{6... | collective-permute-start | bytes 1572872 | tf_op jit(solution)/shard_map/ppermute | solution.py:413
  69.8 21.4 %collective-permute-start.15 = (bf16[32,32,256]{2,1,0:T(8,128)(2,1)}, bf16[32,32,256]{2,1,0:T(8,128)(2,1)}, u32[]{:S(2)}, u32[]{:S(2)}) collective-permute-start(bf16[32,32,256]{2,1,0:T(8,128)(2,1)} %collective-permute-done.13.refs_16_.refs_18_), channel_id=1, source_target_pairs={{1,0},{2,1},{3,2},{11,3},{10,11},{9,10},{8,9},{0,8},{5,4},{6,5},{7... | collective-permute-start | bytes 1572872 | tf_op jit(solution)/shard_map/ppermute | solution.py:413
  74.2 3.2 %collective-permute-start.1 = (bf16[2,4,8,16,128]{4,3,2,1,0:T(8,128)(2,1)S(1)}, bf16[2,4,8,16,128]{4,3,2,1,0:T(8,128)(2,1)}, u32[]{:S(2)}, u32[]{:S(2)}) collective-permute-start(bf16[2,4,8,16,128]{4,3,2,1,0:T(8,128)(2,1)S(1)} %bitcast.16), channel_id=1, source_target_pairs={{0,4},{4,0},{1,5},{5,1},{2,6},{6,2},{3,7},{7,3},{8,12},{12,8},{9,1... | collective-permute-start | bytes 786440 | tf_op jit(solution)/shard_map/ppermute | solution.py:391
  101.8 2.0 %collective-permute-start.16 = (bf16[64,32,128]{2,1,0:T(8,128)(2,1)S(1)}, bf16[64,32,128]{2,1,0:T(8,128)(2,1)S(1)}, u32[]{:S(2)}, u32[]{:S(2)}) collective-permute-start(bf16[64,32,128]{2,1,0:T(8,128)(2,1)S(1)} %get-tuple-element.26), channel_id=1, source_target_pairs={{0,4},{4,0},{1,5},{5,1},{2,6},{6,2},{3,7},{7,3},{8,12},{12,8},{9,1... | collective-permute-start | bytes 1572872 | tf_op jit(solution)/shard_map/ppermute | solution.py:391
  101.9 2.6 %collective-permute-start.17 = (bf16[64,32,128]{2,1,0:T(8,128)(2,1)S(1)}, bf16[64,32,128]{2,1,0:T(8,128)(2,1)S(1)}, u32[]{:S(2)}, u32[]{:S(2)}) collective-permute-start(bf16[64,32,128]{2,1,0:T(8,128)(2,1)S(1)} %get-tuple-element.28), channel_id=1, source_target_pairs={{0,4},{4,0},{1,5},{5,1},{2,6},{6,2},{3,7},{7,3},{8,12},{12,8},{9,1... | collective-permute-start | bytes 1572872 | tf_op jit(solution)/shard_map/ppermute | solution.py:391
  115.1 2.0 %collective-permute-start.18 = (bf16[64,32,128]{2,1,0:T(8,128)(2,1)S(1)}, bf16[64,32,128]{2,1,0:T(8,128)(2,1)S(1)}, u32[]{:S(2)}, u32[]{:S(2)}) collective-permute-start(bf16[64,32,128]{2,1,0:T(8,128)(2,1)S(1)} %get-tuple-element.30), channel_id=1, source_target_pairs={{0,4},{4,0},{1,5},{5,1},{2,6},{6,2},{3,7},{7,3},{8,12},{12,8},{9,1... | collective-permute-start | bytes 1572872 | tf_op jit(solution)/shard_map/ppermute | solution.py:391
  134.5 1.3 collective-permute-start.19
  135.8 4.3 %collective-permute-start.20 = (f32[128,128]{1,0:T(8,128)S(1)}, f32[128,128]{1,0:T(8,128)S(1)}, u32[]{:S(2)}, u32[]{:S(2)}) collective-permute-start(f32[128,128]{1,0:T(8,128)S(1)} %add.20), channel_id=1, source_target_pairs={{0,8},{8,0},{1,9},{9,1},{2,10},{10,2},{3,11},{11,3},{4,12},{12,4},... | collective-permute-start | bytes 196616 | tf_op jit(solution)/shard_map/ppermute | solution.py:422
  140.2 6.5 %collective-permute-start.23 = (f32[128,128]{1,0:T(8,128)S(1)}, f32[128,128]{1,0:T(8,128)S(1)}, u32[]{:S(2)}, u32[]{:S(2)}) collective-permute-start(f32[128,128]{1,0:T(8,128)S(1)} %add.21), channel_id=1, source_target_pairs={{0,3},{1,2},{2,1},{3,0},{4,7},{5,6},{6,5},{7,4},{8,11},{9,10},{10,... | collective-permute-start | bytes 196616 | tf_op jit(solution)/shard_map/ppermute | solution.py:427
  140.3 7.3 %collective-permute-start.22 = (f32[128,128]{1,0:T(8,128)S(1)}, f32[128,128]{1,0:T(8,128)S(1)}, u32[]{:S(2)}, u32[]{:S(2)}) collective-permute-start(f32[128,128]{1,0:T(8,128)S(1)} %add.21), channel_id=1, source_target_pairs={{0,2},{1,3},{2,0},{3,1},{4,6},{5,7},{6,4},{7,5},{8,10},{9,11},{10,... | collective-permute-start | bytes 196616 | tf_op jit(solution)/shard_map/ppermute | solution.py:427
  141.1 6.5 %collective-permute-start.21 = (f32[128,128]{1,0:T(8,128)S(1)}, f32[128,128]{1,0:T(8,128)S(1)}, u32[]{:S(2)}, u32[]{:S(2)}) collective-permute-start(f32[128,128]{1,0:T(8,128)S(1)} %add.21), channel_id=1, source_target_pairs={{0,1},{1,0},{2,3},{3,2},{4,5},{5,4},{6,7},{7,6},{8,9},{9,8},{10,11... | collective-permute-start | bytes 196616 | tf_op jit(solution)/shard_map/ppermute | solution.py:427
  147.5 1.3 collective-permute-start.24

commit v6 on v5

--- a/solution.py
+++ b/solution.py
@@ -184,6 +184,30 @@
     )(first, second)
 
 
+def fold(matrix):
+    half = matrix.shape[0] // 2
+    row = lax.broadcasted_iota(jnp.int32, (half, 2 * half), 0)
+    lane = lax.broadcasted_iota(jnp.int32, (half, 2 * half), 1)
+    top, bottom = rolled(matrix[:half], half), matrix[half:]
+    square = jnp.where((lane >= half) & (row >= lane - half), top, bottom)
+    diagonal = jnp.sum(jnp.where(row == lane - half, bottom, 0.0), axis=0, keepdims=True)
+    return jnp.concatenate([square, jnp.broadcast_to(diagonal, (8, 2 * half))], axis=0)
+
+
+def unfold(folded):
+    order = folded.shape[1]
+    half = order // 2
+    lane = lax.broadcasted_iota(jnp.int32, (half, order), 1)
+    bottom = folded[:half]
+    top = jnp.where(lane < half, rolled(bottom, half), bottom)
+    whole = jnp.concatenate([top, bottom], axis=0)
+    row = lax.broadcasted_iota(jnp.int32, (order, order), 0)
+    lane = lax.broadcasted_iota(jnp.int32, (order, order), 1)
+    own = ((row < half) & (row >= lane)) | ((row >= half) & ((lane < half) | (row < lane)))
+    matrix = jnp.where(own, whole, whole.T)
+    return jnp.where((row == lane) & (row >= half), folded[half : half + 1], matrix)
+
+
 def gram_kernel(core_ref, rows_ref, start_ref, keep_ref, send_ref):
     senders, groups, parts, vectors, lanes = rows_ref.shape
     total = senders * vectors
@@ -199,6 +223,7 @@
             second += lax.dot_general(
                 flat, flat, (((1,), (1,)), ((), ())), preferred_element_type=F32
             )
+    first, second = fold(0.5 * (first + first.T)), fold(second)
     is_first = core_ref[0] == 0
     keep_ref[...] = jnp.where(is_first, first, second)
     send_ref[...] = jnp.where(is_first, second, first)
@@ -208,7 +233,7 @@
     total = rows.shape[0] * rows.shape[3]
     return pl.pallas_call(
         gram_kernel,
-        out_shape=[jax.ShapeDtypeStruct((total, total), F32)] * 2,
+        out_shape=[jax.ShapeDtypeStruct((total // 2 + 8, total), F32)] * 2,
         in_specs=[pl.BlockSpec(memory_space=pltpu.SMEM)] + [pl.BlockSpec(memory_space=pltpu.VMEM)] * 2,
         out_specs=[pl.BlockSpec(memory_space=pltpu.VMEM)] * 2,
         compiler_params=pltpu.CompilerParams(vmem_limit_bytes=SMALL_BYTES),
@@ -266,9 +291,8 @@
     across = (((1,), (1,)), ((), ()))
     plain = (((1,), (0,)), ((), ()))
     is_first = core_ref[0] == 0
-    gram_first = jnp.where(is_first, kept_ref[...], given_ref[...])
-    first = inverse_factor(work_ref, 0.5 * (gram_first + gram_first.T))
-    gram_second = jnp.where(is_first, given_ref[...], kept_ref[...])
+    first = inverse_factor(work_ref, unfold(jnp.where(is_first, kept_ref[...], given_ref[...])))
+    gram_second = unfold(jnp.where(is_first, given_ref[...], kept_ref[...]))
     gram_second = exact(exact(first, gram_second, plain), first, across)
     second = inverse_factor(work_ref, gram_second)
     mixing = exact(second, first, plain) * scale
@@ -296,7 +320,9 @@
     )(core, rows, kept, given)
 
 
-def whiten_kernel(core_ref, beam_ref, noise_ref, keep_ref, send_ref):
+def whiten_kernel(core_ref, beam_ref, noise_ref, *out_refs):
+    chunks = len(out_refs) // 2
+    depth = out_refs[0].shape[2]
     parts, freqs, own, multipoles = beam_ref.shape
     half = multipoles // 2
     level = lax.rsqrt(noise_ref[...])
@@ -307,17 +333,22 @@
             low = (beam_ref[part, freq, :, :half].astype(F32) * column).astype(BF16)
             high = (beam_ref[part, freq, :, half:].astype(F32) * column).astype(BF16)
             rows = slice(part * own, (part + 1) * own)
-            keep_ref[freq, rows] = jnp.where(is_first, low, high)
-            send_ref[freq, rows] = jnp.where(is_first, high, low)
-
-
-def whiten(core, beam, noise):
+            keep = jnp.where(is_first, low, high)
+            send = jnp.where(is_first, high, low)
+            for chunk in range(chunks):
+                cut = slice(chunk * depth, (chunk + 1) * depth)
+                out_refs[chunk][freq, rows] = keep[:, cut]
+                out_refs[chunks + chunk][freq, rows] = send[:, cut]
+
+
+def whiten(core, beam, noise, chunks):
     parts, freqs, own, multipoles = beam.shape
+    depth = multipoles // (2 * chunks)
     return pl.pallas_call(
         whiten_kernel,
-        out_shape=[jax.ShapeDtypeStruct((freqs, parts * own, multipoles // 2), BF16)] * 2,
+        out_shape=[jax.ShapeDtypeStruct((freqs, parts * own, depth), BF16)] * (2 * chunks),
         in_specs=[pl.BlockSpec(memory_space=pltpu.SMEM)] + [pl.BlockSpec(memory_space=pltpu.VMEM)] * 2,
-        out_specs=[pl.BlockSpec(memory_space=pltpu.VMEM)] * 2,
+        out_specs=[pl.BlockSpec(memory_space=pltpu.VMEM)] * (2 * chunks),
         compiler_params=pltpu.CompilerParams(vmem_limit_bytes=SMALL_BYTES),
     )(core, beam, noise.T)
 
@@ -372,7 +403,7 @@
         return carry
 
     for side in range(2):
-        lax.fori_loop(0, x_count * groups, functools.partial(group, side), 0, unroll=2)
+        lax.fori_loop(0, x_count * groups, functools.partial(group, side), 0, unroll=4)
 
 
 def start_operand(sides, own):
@@ -395,7 +426,7 @@
     return lax.optimization_barrier((value, event))
 
 
-def gather_ring(blocks, late, x_count, z_count):
+def gather_ring(sets, late, x_count, z_count):
     count = x_count * z_count
     ring = [k if k < z_count else z_count + count - 1 - k for k in range(count)]
     pairs = {
@@ -404,16 +435,20 @@
     }
     x_place, z_place = lax.axis_index("x"), lax.axis_index("fc")
     place = jnp.where(x_place == 0, z_place, count - 1 - z_place).astype(jnp.int32).reshape(1)
-    moving = {(core, way): block for core, block in enumerate(blocks) for way in (1, -1)}
-    found = [(block, core, 0, 0) for core, block in enumerate(blocks)]
+    moving, found = {}, []
+    for chunk, blocks in enumerate(sets):
+        for core, block in enumerate(blocks):
+            found.append((block, core, 0, chunk))
+            moving[chunk, core, 1] = moving[chunk, core, -1] = block
     for hop in range(1, count // 2 + 1):
-        for core, way in moving:
+        for key in moving:
+            chunk, core, way = key
             if 2 * hop == count and (way == 1) != (core == 0):
                 continue
-            moving[core, way] = lax.ppermute(moving[core, way], ("x", "fc"), pairs[way])
-            if hop == 1 and core == 0 and way == 1:
-                late, moving[core, way] = after(late, moving[core, way])
-            found.append((moving[core, way], core, -way * hop, 0))
+            moving[key] = lax.ppermute(moving[key], ("x", "fc"), pairs[way])
+            if hop == 1 and key == (0, 0, 1):
+                late, moving[key] = after(late, moving[key])
+            found.append((moving[key], core, -way * hop, chunk))
     return place, found, late
 
 
@@ -442,10 +477,11 @@
     depth = multipoles // cores
 
     core_index = core.astype(jnp.int32).reshape(1)
-    kept, given = whiten(core_index, beam_transfer, noise_var)
-    given = swap_cores(given)
+    chunks = 2 if depth % 256 == 0 else 1
+    cut = whiten(core_index, beam_transfer, noise_var, chunks)
+    sets = [[cut[chunk], swap_cores(cut[chunks + chunk])] for chunk in range(chunks)]
     start = turn(start_vectors, x_count * z_count, z_count * parts * own)
-    place, beams, start = gather_ring([kept, given], start, x_count, z_count)
+    place, beams, start = gather_ring(sets, start, x_count, z_count)
 
     spec = spectra.reshape(-1, cores, depth)
     spec = lax.dynamic_index_in_dim(spec, core, 1, False)
@@ -458,9 +494,15 @@
     operand = start_operand([start, swap_cores(start)], own)
 
     apply = functools.partial(apply_covariance, place)
-    mine, theirs, mine_sent, theirs_sent = apply(
-        [[operand[0]], [operand[1]]], beams, cov, spec, own, z_count, (0, 1), (0, 1)
-    )
+    added, width = (), depth // chunks
+    for chunk in range(chunks):
+        part = [(piece, at, offset, 0) for piece, at, offset, which in beams if which == chunk]
+        part_spec = spec[:, chunk * width : (chunk + 1) * width]
+        send = (0, 1) if chunk == chunks - 1 else ()
+        added = apply(
+            [[operand[0]], [operand[1]]], part, cov, part_spec, own, z_count, (0, 1), send, added
+        )
+    mine, theirs, mine_sent, theirs_sent = added
     got_mine, got_theirs = swap_cores(theirs_sent), swap_cores(mine_sent)
     second_mine, second_sent = apply(
         [[mine, got_mine], [theirs, got_theirs]], beams, cov, spec, own, z_count, (0,), (1,)

time: 159 us -> 153 us (0.962)
  waiting for transfers between devices: 61.6 us -> 31.5 us
  starting transfers between devices: 34 us -> 56.6 us
    ppermute x14 -> x28, waiting for transfers between devices: 47.9 us -> 19.8 us  [gather_ring(): moving[key] = lax.ppermute(moving[key], ('x', 'fc'), pairs[way])]
    ppermute x14 -> x28, starting transfers between devices: 21.4 us -> 45.3 us  [gather_ring(): moving[key] = lax.ppermute(moving[key], ('x', 'fc'), pairs[way])]
    pallas_call x2 -> x3, Pallas kernels: 21.2 us -> 24.1 us  [apply_covariance(): pl.pallas_call(functools.partial(apply_kernel, n_vec, z_count, own, offse...]
    unnamed x8 -> x18, local copies, waits for them, and re-layouts: 1.94 us -> 3.34 us
    ppermute x7 -> x8, waiting for transfers between devices: 6.4 us -> 6.33 us  [swap_cores(): return lax.ppermute(value, 'core', [(0, 1), (1, 0)])]
  transfers between devices with their start and end apart: 26 -> 41, of which waited for: 15 -> 18; matrix products, arithmetic and copies ran while one was open for 4% -> 4% of each run, Pallas kernels for 3% -> 7%
where the time goes in v6:
time: 153 us; the launch traced here: 152 us
  starting transfers between devices  56.6 us (37%)
  Pallas kernels  38.9 us (25%)
  waiting for transfers between devices  31.5 us (21%)
  blocking collectives  14.9 us (10%)
  local copies, waits for them, and re-layouts  7.21 us (5%)
  other arithmetic  2.94 us (2%)
    ppermute x28, starting transfers between devices, gather_ring(): moving[key] = lax.ppermute(moving[key], ('x', 'fc'), pairs[way])  45.3 us
    pallas_call x3, Pallas kernels, apply_covariance(): pl.pallas_call(functools.partial(apply_kernel, n_vec, z_count, own, offse...  24.1 us
    ppermute x28, waiting for transfers between devices, gather_ring(): moving[key] = lax.ppermute(moving[key], ('x', 'fc'), pairs[way])  19.8 us
    all_to_all x1, blocking collectives, body_split(): received = lax.all_to_all(packed, ('x', 'fc'), 0, 0, tiled=True)  14.9 us
    pallas_call x1, Pallas kernels, finish(): pl.pallas_call(functools.partial(finish_kernel, scale), out_shape=jax.Sha...  9.66 us
    ppermute x8, waiting for transfers between devices, swap_cores(): return lax.ppermute(value, 'core', [(0, 1), (1, 0)])  6.33 us
    all_to_all x1, starting transfers between devices, body_split(): start = lax.all_to_all(start, ('x', 'fc'), 0, 0, tiled=True)  4.79 us
    ppermute x3, starting transfers between devices, sum_devices(): lax.ppermute(value, 'fc', [(j, j ^ s) for j in range(z_count)])  4.38 us
  transfers between devices with their start and end apart: 41, of which 18 were waited for; matrix products, arithmetic and copies ran while one was open for 4% of the time, Pallas kernels for 7%

profile of v6, /device:TPU:0, one launch (start us, length us, event | category | flops | bytes accessed | tf_op | source)
XLA Modules:
  0.0 152.3 jit_solution(1851306019077532426)
XLA Ops:
  0.0 0.7 copy-done.8
  0.7 1.2 copy-done.7
  2.3 0.5 collective-permute-start.2
  2.9 2.9 %collective-permute-start.18 = (bf16[32,32,128]{2,1,0:T(8,128)(2,1)S(1)}, bf16[32,32,128]{2,1,0:T(8,128)(2,1)S(1)}, u32[]{:S(2)}, u32[]{:S(2)}) collective-permute-start(bf16[32,32,128]{2,1,0:T(8,128)(2,1)S(1)} %get-tuple-element.23.refs_3_.refs_5_), channel_id=1, source_target_pairs={{1,0},{2,1},{3,2},{11,3},{10,11},{9,10},{8,9},{0,8},{5,4},{6,5},{7... | collective-permute-start | bytes 786440 | tf_op jit(solution)/shard_map/ppermute | solution.py:448
  5.9 1.9 %collective-permute-start.4 = (bf16[32,32,128]{2,1,0:T(8,128)(2,1)S(1)}, bf16[32,32,128]{2,1,0:T(8,128)(2,1)S(1)}, u32[]{:S(2)}, u32[]{:S(2)}) collective-permute-start(bf16[32,32,128]{2,1,0:T(8,128)(2,1)S(1)} %get-tuple-element.27.refs_3_.refs_7_), channel_id=1, source_target_pairs={{1,0},{2,1},{3,2},{11,3},{10,11},{9,10},{8,9},{0,8},{5,4},{6,5},{7... | collective-permute-start | bytes 786440 | tf_op jit(solution)/shard_map/ppermute | solution.py:448
  7.9 1.9 %collective-permute-start.6 = (bf16[32,32,128]{2,1,0:T(8,128)(2,1)S(1)}, bf16[32,32,128]{2,1,0:T(8,128)(2,1)S(1)}, u32[]{:S(2)}, u32[]{:S(2)}) collective-permute-start(bf16[32,32,128]{2,1,0:T(8,128)(2,1)S(1)} %collective-permute-done.2.refs_4_.refs_8_), channel_id=1, source_target_pairs={{1,0},{2,1},{3,2},{11,3},{10,11},{9,10},{8,9},{0,8},{5,4},{6,5},{7... | collective-permute-start | bytes 786440 | tf_op jit(solution)/shard_map/ppermute | solution.py:448
  9.9 3.1 %collective-permute-done.18.refs_6_.refs_10_ = bf16[32,32,128]{2,1,0:T(8,128)(2,1)S(1)} collective-permute-done((bf16[32,32,128]{2,1,0:T(8,128)(2,1)S(1)}, bf16[32,32,128]{2,1,0:T(8,128)(2,1)S(1)}, u32[]{:S(2)}, u32[]{:S(2)}) %collective-permute-start.18) | collective-permute-done | bytes 262176 | tf_op jit(solution)/shard_map/ppermute | solution.py:448
  13.0 2.1 %collective-permute-start.5 = (bf16[32,32,128]{2,1,0:T(8,128)(2,1)S(1)}, bf16[32,32,128]{2,1,0:T(8,128)(2,1)S(1)}, u32[]{:S(2)}, u32[]{:S(2)}) collective-permute-start(bf16[32,32,128]{2,1,0:T(8,128)(2,1)S(1)} %collective-permute-done.2.refs_4_.refs_8_), channel_id=1, source_target_pairs={{0,1},{1,2},{2,3},{3,11},{11,10},{10,9},{9,8},{8,0},{4,5},{5,6},{6... | collective-permute-start | bytes 786440 | tf_op jit(solution)/shard_map/ppermute | solution.py:448
  15.1 1.5 %collective-permute-start.20 = (bf16[32,32,128]{2,1,0:T(8,128)(2,1)S(1)}, bf16[32,32,128]{2,1,0:T(8,128)(2,1)S(1)}, u32[]{:S(2)}, u32[]{:S(2)}) collective-permute-start(bf16[32,32,128]{2,1,0:T(8,128)(2,1)S(1)} %collective-permute-done.17.refs_4_.refs_6_), channel_id=1, source_target_pairs={{1,0},{2,1},{3,2},{11,3},{10,11},{9,10},{8,9},{0,8},{5,4},{6,5},{7... | collective-permute-start | bytes 786440 | tf_op jit(solution)/shard_map/ppermute | solution.py:448
  16.6 2.0 %collective-permute-done.4.refs_6_.refs_14_ = bf16[32,32,128]{2,1,0:T(8,128)(2,1)S(1)} collective-permute-done((bf16[32,32,128]{2,1,0:T(8,128)(2,1)S(1)}, bf16[32,32,128]{2,1,0:T(8,128)(2,1)S(1)}, u32[]{:S(2)}, u32[]{:S(2)}) %collective-permute-start.4) | collective-permute-done | bytes 262176 | tf_op jit(solution)/shard_map/ppermute | solution.py:448
  18.6 2.1 %collective-permute-start.19 = (bf16[32,32,128]{2,1,0:T(8,128)(2,1)S(1)}, bf16[32,32,128]{2,1,0:T(8,128)(2,1)S(1)}, u32[]{:S(2)}, u32[]{:S(2)}) collective-permute-start(bf16[32,32,128]{2,1,0:T(8,128)(2,1)S(1)} %collective-permute-done.17.refs_4_.refs_6_), channel_id=1, source_target_pairs={{0,1},{1,2},{2,3},{3,11},{11,10},{10,9},{9,8},{8,0},{4,5},{5,6},{6... | collective-permute-start | bytes 786440 | tf_op jit(solution)/shard_map/ppermute | solution.py:448
  20.7 1.5 %collective-permute-start.22 = (bf16[32,32,128]{2,1,0:T(8,128)(2,1)S(1)}, bf16[32,32,128]{2,1,0:T(8,128)(2,1)S(1)}, u32[]{:S(2)}, u32[]{:S(2)}) collective-permute-start(bf16[32,32,128]{2,1,0:T(8,128)(2,1)S(1)} %collective-permute-done.18.refs_6_.refs_10_), channel_id=1, source_target_pairs={{1,0},{2,1},{3,2},{11,3},{10,11},{9,10},{8,9},{0,8},{5,4},{6,5},{7... | collective-permute-start | bytes 786440 | tf_op jit(solution)/shard_map/ppermute | solution.py:448
  22.2 0.8 shard_map.55
  23.0 0.7 copy-done.6
  23.7 0.5 collective-permute-done.6.refs_8_.refs_16_
  24.2 2.1 %collective-permute-start.21 = (bf16[32,32,128]{2,1,0:T(8,128)(2,1)S(1)}, bf16[32,32,128]{2,1,0:T(8,128)(2,1)}, u32[]{:S(2)}, u32[]{:S(2)}) collective-permute-start(bf16[32,32,128]{2,1,0:T(8,128)(2,1)S(1)} %collective-permute-done.refs_5_.refs_9_), channel_id=1, source_target_pairs={{0,1},{1,2},{2,3},{3,11},{11,10},{10,9},{9,8},{8,0},{4,5},{5,6},{6... | collective-permute-start | bytes 786440 | tf_op jit(solution)/shard_map/ppermute | solution.py:448
  26.3 1.5 %collective-permute-start.8 = (bf16[32,32,128]{2,1,0:T(8,128)(2,1)S(1)}, bf16[32,32,128]{2,1,0:T(8,128)(2,1)}, u32[]{:S(2)}, u32[]{:S(2)}) collective-permute-start(bf16[32,32,128]{2,1,0:T(8,128)(2,1)S(1)} %collective-permute-done.4.refs_6_.refs_14_), channel_id=1, source_target_pairs={{1,0},{2,1},{3,2},{11,3},{10,11},{9,10},{8,9},{0,8},{5,4},{6,5},{7... | collective-permute-start | bytes 786440 | tf_op jit(solution)/shard_map/ppermute | solution.py:448
  27.8 2.0 %collective-permute-done.20.refs_8_.refs_12_ = bf16[32,32,128]{2,1,0:T(8,128)(2,1)S(1)} collective-permute-done((bf16[32,32,128]{2,1,0:T(8,128)(2,1)S(1)}, bf16[32,32,128]{2,1,0:T(8,128)(2,1)S(1)}, u32[]{:S(2)}, u32[]{:S(2)}) %collective-permute-start.20) | collective-permute-done | bytes 262176 | tf_op jit(solution)/shard_map/ppermute | solution.py:448
  29.8 2.1 %collective-permute-start.7 = (bf16[32,32,128]{2,1,0:T(8,128)(2,1)S(1)}, bf16[32,32,128]{2,1,0:T(8,128)(2,1)}, u32[]{:S(2)}, u32[]{:S(2)}) collective-permute-start(bf16[32,32,128]{2,1,0:T(8,128)(2,1)S(1)} %collective-permute-done.3.refs_5_.refs_13_), channel_id=1, source_target_pairs={{0,1},{1,2},{2,3},{3,11},{11,10},{10,9},{9,8},{8,0},{4,5},{5,6},{6... | collective-permute-start | bytes 786440 | tf_op jit(solution)/shard_map/ppermute | solution.py:448
  31.9 1.5 %collective-permute-start.10 = (bf16[32,32,128]{2,1,0:T(8,128)(2,1)S(1)}, bf16[32,32,128]{2,1,0:T(8,128)(2,1)}, u32[]{:S(2)}, u32[]{:S(2)}) collective-permute-start(bf16[32,32,128]{2,1,0:T(8,128)(2,1)S(1)} %collective-permute-done.6.refs_8_.refs_16_), channel_id=1, source_target_pairs={{1,0},{2,1},{3,2},{11,3},{10,11},{9,10},{8,9},{0,8},{5,4},{6,5},{7... | collective-permute-start | bytes 786440 | tf_op jit(solution)/shard_map/ppermute | solution.py:448
  33.4 2.0 %collective-permute-done.22.refs_10_.refs_18_ = bf16[32,32,128]{2,1,0:T(8,128)(2,1)S(1)} collective-permute-done((bf16[32,32,128]{2,1,0:T(8,128)(2,1)S(1)}, bf16[32,32,128]{2,1,0:T(8,128)(2,1)S(1)}, u32[]{:S(2)}, u32[]{:S(2)}) %collective-permute-start.22) | collective-permute-done | bytes 262176 | tf_op jit(solution)/shard_map/ppermute | solution.py:448
  35.5 0.7 copy-done.4
  36.2 2.1 %collective-permute-start.9 = (bf16[32,32,128]{2,1,0:T(8,128)(2,1)S(1)}, bf16[32,32,128]{2,1,0:T(8,128)(2,1)}, u32[]{:S(2)}, u32[]{:S(2)}) collective-permute-start(bf16[32,32,128]{2,1,0:T(8,128)(2,1)S(1)} %collective-permute-done.5.refs_7_.refs_15_), channel_id=1, source_target_pairs={{0,1},{1,2},{2,3},{3,11},{11,10},{10,9},{9,8},{8,0},{4,5},{5,6},{6... | collective-permute-start | bytes 786440 | tf_op jit(solution)/shard_map/ppermute | solution.py:448
  38.2 4.8 %all-to-all-start = ((bf16[8,8,16,128]{3,2,1,0:T(8,128)(2,1)}), bf16[8,8,16,128]{3,2,1,0:T(8,128)(2,1)}, u32[]{:S(2)}, u32[]{:S(2)}) async-start(bf16[8,8,16,128]{3,2,1,0:T(8,128)(2,1)} %copy-done.6), calls=%async_computation | async-start | bytes 524288 | tf_op jit(solution)/shard_map/all_to_all | solution.py:492
  43.0 2.0 %collective-permute-start.24 = (bf16[32,32,128]{2,1,0:T(8,128)(2,1)S(1)}, bf16[32,32,128]{2,1,0:T(8,128)(2,1)}, u32[]{:S(2)}, u32[]{:S(2)}) collective-permute-start(bf16[32,32,128]{2,1,0:T(8,128)(2,1)S(1)} %collective-permute-done.20.refs_8_.refs_12_), channel_id=1, source_target_pairs={{1,0},{2,1},{3,2},{11,3},{10,11},{9,10},{8,9},{0,8},{5,4},{6,5},{7... | collective-permute-start | bytes 786440 | tf_op jit(solution)/shard_map/ppermute | solution.py:448
  45.1 2.0 %collective-permute-start.26 = (bf16[32,32,128]{2,1,0:T(8,128)(2,1)}, bf16[32,32,128]{2,1,0:T(8,128)(2,1)}, u32[]{:S(2)}, u32[]{:S(2)}) collective-permute-start(bf16[32,32,128]{2,1,0:T(8,128)(2,1)} %copy-done.4), channel_id=1, source_target_pairs={{1,0},{2,1},{3,2},{11,3},{10,11},{9,10},{8,9},{0,8},{5,4},{6,5},{7... | collective-permute-start | bytes 786440 | tf_op jit(solution)/shard_map/ppermute | solution.py:448
  47.1 1.8 %collective-permute-start.25 = (bf16[32,32,128]{2,1,0:T(8,128)(2,1)}, bf16[32,32,128]{2,1,0:T(8,128)(2,1)}, u32[]{:S(2)}, u32[]{:S(2)}) collective-permute-start(bf16[32,32,128]{2,1,0:T(8,128)(2,1)} %collective-permute-done.21.refs_9_.refs_17_), channel_id=1, source_target_pairs={{0,1},{1,2},{2,3},{3,11},{11,10},{10,9},{9,8},{8,0},{4,5},{5,6},{6... | collective-permute-start | bytes 786440 | tf_op jit(solution)/shard_map/ppermute | solution.py:448
  49.2 1.8 %collective-permute-start.11 = (bf16[32,32,128]{2,1,0:T(8,128)(2,1)}, bf16[32,32,128]{2,1,0:T(8,128)(2,1)}, u32[]{:S(2)}, u32[]{:S(2)}) collective-permute-start(bf16[32,32,128]{2,1,0:T(8,128)(2,1)} %collective-permute-done.7.refs_9_.refs_21_), channel_id=1, source_target_pairs={{0,1},{1,2},{2,3},{3,11},{11,10},{10,9},{9,8},{8,0},{4,5},{5,6},{6... | collective-permute-start | bytes 786440 | tf_op jit(solution)/shard_map/ppermute | solution.py:448
  51.0 5.8 %collective-permute-done.24.refs_12_.refs_20_ = bf16[32,32,128]{2,1,0:T(8,128)(2,1)} collective-permute-done((bf16[32,32,128]{2,1,0:T(8,128)(2,1)S(1)}, bf16[32,32,128]{2,1,0:T(8,128)(2,1)}, u32[]{:S(2)}, u32[]{:S(2)}) %collective-permute-start.24) | collective-permute-done | bytes 262176 | tf_op jit(solution)/shard_map/ppermute | solution.py:448
  56.8 0.9 collective-permute-start.28
  57.6 0.9 convert_element_type.6
  58.6 0.9 convert_element_type.7
  59.4 1.8 %copy.7 = bf16[2,2,2,32,2,2,32]{6,4,5,0,3,1,2:T(2,128)(2,1)} copy(bf16[2,2,2,32,2,2,32]{6,5,4,3,2,1,0:T(2,128)(2,1)} %convert_element_type.7) | data formatting | bytes 131072 | tf_op jit(solution)/shard_map/convert_element_type | solution.py:488
  61.3 1.1 collective-permute-done.26.refs_14_.refs_26_
  62.4 1.9 %collective-permute-start.14 = (bf16[32,32,128]{2,1,0:T(8,128)(2,1)}, bf16[32,32,128]{2,1,0:T(8,128)(2,1)}, u32[]{:S(2)}, u32[]{:S(2)}) collective-permute-start(bf16[32,32,128]{2,1,0:T(8,128)(2,1)} %collective-permute-done.10.refs_12_.refs_24_), channel_id=1, source_target_pairs={{1,0},{2,1},{3,2},{11,3},{10,11},{9,10},{8,9},{0,8},{5,4},{6,5},{7... | collective-permute-start | bytes 786440 | tf_op jit(solution)/shard_map/ppermute | solution.py:448
  64.3 1.5 collective-permute-start.27
  65.7 1.8 %collective-permute-done.11.refs_13_.refs_29_ = bf16[32,32,128]{2,1,0:T(8,128)(2,1)} collective-permute-done((bf16[32,32,128]{2,1,0:T(8,128)(2,1)}, bf16[32,32,128]{2,1,0:T(8,128)(2,1)}, u32[]{:S(2)}, u32[]{:S(2)}) %collective-permute-start.11) | collective-permute-done | bytes 262176 | tf_op jit(solution)/shard_map/ppermute | solution.py:448
  67.5 3.4 %collective-permute-start.29 = (bf16[32,32,128]{2,1,0:T(8,128)(2,1)}, bf16[32,32,128]{2,1,0:T(8,128)(2,1)}, u32[]{:S(2)}, u32[]{:S(2)}) collective-permute-start(bf16[32,32,128]{2,1,0:T(8,128)(2,1)} %collective-permute-done.25.refs_13_.refs_25_), channel_id=1, source_target_pairs={{0,1},{1,2},{2,3},{3,11},{11,10},{10,9},{9,8},{8,0},{4,5},{5,6},{6... | collective-permute-start | bytes 786440 | tf_op jit(solution)/shard_map/ppermute | solution.py:448
  70.9 2.0 %fusion = bf16[2,2,32,2,2,2,32]{6,5,4,3,2,1,0:T(2,128)(2,1)} fusion(bf16[2,2,2,32,2,2,32]{6,4,5,0,3,1,2:T(2,128)(2,1)} %copy.7, pred[]{:T(512)S(6)} %eq.7), kind=kLoop, calls=%fused_computation.1 | loop fusion | flops 32768 | bytes 131073 | tf_op jit(solution)/shard_map/transpose | solution.py:490
  73.0 1.2 reshape.29.refs_19_.refs_37_
  74.2 3.5 %collective-permute-start.12 = (bf16[32,32,128]{2,1,0:T(8,128)(2,1)}, bf16[32,32,128]{2,1,0:T(8,128)(2,1)S(1)}, u32[]{:S(2)}, u32[]{:S(2)}) collective-permute-start(bf16[32,32,128]{2,1,0:T(8,128)(2,1)} %collective-permute-done.8.refs_10_.refs_22_), channel_id=1, source_target_pairs={{1,0},{2,1},{3,2},{11,3},{10,11},{9,10},{8,9},{0,8},{5,4},{6,5},{7... | collective-permute-start | bytes 786440 | tf_op jit(solution)/shard_map/ppermute | solution.py:448
  77.7 1.0 collective-permute-start.15
  78.8 1.1 collective-permute-done.29.refs_17_.refs_33_
  79.9 2.1 %collective-permute-start.16 = (bf16[32,32,128]{2,1,0:T(8,128)(2,1)}, bf16[32,32,128]{2,1,0:T(8,128)(2,1)S(1)}, u32[]{:S(2)}, u32[]{:S(2)}) collective-permute-start(bf16[32,32,128]{2,1,0:T(8,128)(2,1)} %collective-permute-done.14.refs_16_.refs_32_), channel_id=1, source_target_pairs={{1,0},{2,1},{3,2},{11,3},{10,11},{9,10},{8,9},{0,8},{5,4},{6,5},{7... | collective-permute-start | bytes 786440 | tf_op jit(solution)/shard_map/ppermute | solution.py:448
  81.9 2.8 %shard_map.57 = (bf16[64,32,128]{2,1,0:T(8,128)(2,1)S(1)}, bf16[64,32,128]{2,1,0:T(8,128)(2,1)S(1)}) custom-call(bf16[2,4,8,16,128]{4,3,2,1,0:T(8,128)(2,1)} %bitcast.3.refs_0_, bf16[2,4,8,16,128]{4,3,2,1,0:T(8,128)(2,1)} %collective-permute-done.1.refs_1_), custom_call_target="tpu_custom_call" | custom-call | tf_op jit(solution)/shard_map/pallas_call | solution.py:412
  84.8 6.7 %shard_map.58 = (f32[64,32,128]{2,1,0:T(8,128)S(1)}, f32[64,32,128]{2,1,0:T(8,128)S(1)}) custom-call(s32[1]{0:T(128)} %bitcast.1.refs_0_, bf16[64,32,128]{2,1,0:T(8,128)(2,1)S(1)} %get-tuple-element.25.refs_1_, bf16[64,32,128]{2,1,0:T(8,128)(2,1)S(1)} %get-tuple-element.26.refs_2_, bf16[32,32,128]{2,1,0:T(8,128)(2,1)S(1)} %get-tuple-element.23.refs_3_.refs_5_, ...), custom_call_target="tpu_custom_call" | custom-call | flops 536870912 | bytes 4194304 | tf_op jit(solution)/shard_map/pallas_call | solution.py:130
  91.5 6.6 %shard_map.59 = (f32[64,32,128]{2,1,0:T(8,128)S(1)}, f32[64,32,128]{2,1,0:T(8,128)S(1)}, bf16[64,32,128]{2,1,0:T(8,128)(2,1)S(1)}, bf16[64,32,128]{2,1,0:T(8,128)(2,1)S(1)}) custom-call(s32[1]{0:T(128)} %bitcast.1.refs_0_, bf16[64,32,128]{2,1,0:T(8,128)(2,1)S(1)} %get-tuple-element.25.refs_1_, bf16[64,32,128]{2,1,0:T(8,128)(2,1)S(1)} %get-tuple-element.26.refs_2_, ...), custom_call_target="tpu_custom_call" | custom-call | flops 536870912 | bytes 4194304 | tf_op jit(solution)/shard_map/pallas_call | solution.py:130
  98.2 0.5 collective-permute-start.32
  98.7 1.4 collective-permute-done.31.refs_2_
  100.1 0.7 collective-permute-done.32.refs_4_
  100.8 10.8 %shard_map.60 = (f32[64,32,128]{2,1,0:T(8,128)S(1)}, bf16[64,32,128]{2,1,0:T(8,128)(2,1)S(1)}) custom-call(s32[1]{0:T(128)} %bitcast.1.refs_0_, f32[64,32,128]{2,1,0:T(8,128)S(1)} %get-tuple-element.33.refs_1_, bf16[64,32,128]{2,1,0:T(8,128)(2,1)S(1)} %collective-permute-done.31.refs_2_, f32[64,32,128]{2,1,0:T(8,128)S(1)} %get-tuple-element.35.refs_3_, ...), custom_call_target="tpu_custom_call" | custom-call | flops 1073741824 | bytes 8388608 | tf_op jit(solution)/shard_map/pallas_call | solution.py:130
  111.8 1.8 %collective-permute-done.33.second_ref = bf16[64,32,128]{2,1,0:T(8,128)(2,1)S(1)} collective-permute-done((bf16[64,32,128]{2,1,0:T(8,128)(2,1)S(1)}, bf16[64,32,128]{2,1,0:T(8,128)(2,1)S(1)}, u32[]{:S(2)}, u32[]{:S(2)}) %collective-permute-start.33) | collective-permute-done | bytes 524320 | tf_op jit(solution)/shard_map/ppermute | solution.py:422
  113.6 0.8 shard_map.61
  114.4 14.9 %all_to_all.10 = bf16[8,4,32,128]{3,2,1,0:T(8,128)(2,1)S(1)} all-to-all(bf16[8,4,32,128]{3,2,1,0:T(8,128)(2,1)S(1)} %bitcast.15), channel_id=1, replica_groups=mesh['ma'=2,'x'=2,'core'=2,'fc'=4] {'x','fc'}, dimensions={0} | all-to-all | bytes 524288 | tf_op jit(solution)/shard_map/all_to_all | solution.py:512
  129.3 0.5 shard_map.62
  129.9 1.2 collective-permute-done.34
  131.1 0.6 collective-permute-start.35
  131.6 3.4 %collective-permute-done.35 = f32[72,128]{1,0:T(8,128)S(1)} collective-permute-done((f32[72,128]{1,0:T(8,128)S(1)}, f32[72,128]{1,0:T(8,128)S(1)}, u32[]{:S(2)}, u32[]{:S(2)}) %collective-permute-start.35) | collective-permute-done | bytes 36896 | tf_op jit(solution)/shard_map/ppermute | solution.py:457
  135.0 0.8 collective-permute-start.37
  135.9 3.6 %collective-permute-start.36 = (f32[72,128]{1,0:T(8,128)S(1)}, f32[72,128]{1,0:T(8,128)S(1)}, u32[]{:S(2)}, u32[]{:S(2)}) collective-permute-start(f32[72,128]{1,0:T(8,128)S(1)} %add.21), channel_id=1, source_target_pairs={{0,1},{1,0},{2,3},{3,2},{4,5},{5,4},{6,7},{7,6},{8,9},{9,8},{10,11... | collective-permute-start | bytes 110600 | tf_op jit(solution)/shard_map/ppermute | solution.py:462
  139.4 1.4 collective-permute-done.38
  140.8 0.6 collective-permute-done.36
  141.4 1.2 collective-permute-done.39.given_ref
  142.7 9.7 %shard_map.63 = f32[2,4,128,128]{3,2,1,0:T(8,128)} custom-call(s32[1]{0:T(128)} %bitcast.core_ref, bf16[8,4,2,16,128]{4,3,2,1,0:T(8,128)(2,1)S(1)} %bitcast.14, f32[72,128]{1,0:T(8,128)S(1)} %add_add_fusion.kept_ref, f32[72,128]{1,0:T(8,128)S(1)} %collective-permute-done.39.given_ref), custom_call_target="tpu_custom_call" | custom-call | tf_op jit(solution)/shard_map/pallas_call | solution.py:313
  (56 shorter events, 1.5 us)
Async XLA Ops:
  0.0 72.9 %copy-start = (f32[2,512]{1,0:T(2,128)S(1)}, f32[2,512]{1,0:T(2,128)}, u32[]{:S(2)}) copy-start(f32[2,512]{1,0:T(2,128)} %param.7) | copy-start | bytes 12292
  0.0 0.7 copy-start.8
  0.7 1.2 copy-start.7
  1.9 20.3 %copy-start.1 = (f32[2,32,16,128]{3,2,1,0:T(8,128)S(1)}, f32[2,32,16,128]{3,2,1,0:T(8,128)}, u32[]{:S(2)}) copy-start(f32[2,32,16,128]{3,2,1,0:T(8,128)} %start_ref.3) | copy-start | bytes 1572868
  2.3 5.5 %collective-permute-start.2 = (bf16[32,32,128]{2,1,0:T(8,128)(2,1)S(1)}, bf16[32,32,128]{2,1,0:T(8,128)(2,1)S(1)}, u32[]{:S(2)}, u32[]{:S(2)}) collective-permute-start(bf16[32,32,128]{2,1,0:T(8,128)(2,1)S(1)} %get-tuple-element.28), channel_id=1, source_target_pairs={{0,4},{4,0},{1,5},{5,1},{2,6},{6,2},{3,7},{7,3},{8,12},{12,8},{9,1... | collective-permute-start | bytes 786440 | tf_op jit(solution)/shard_map/ppermute | solution.py:422
  2.8 5.1 %collective-permute-start.17 = (bf16[32,32,128]{2,1,0:T(8,128)(2,1)S(1)}, bf16[32,32,128]{2,1,0:T(8,128)(2,1)S(1)}, u32[]{:S(2)}, u32[]{:S(2)}) collective-permute-start(bf16[32,32,128]{2,1,0:T(8,128)(2,1)S(1)} %get-tuple-element.29), channel_id=1, source_target_pairs={{0,4},{4,0},{1,5},{5,1},{2,6},{6,2},{3,7},{7,3},{8,12},{12,8},{9,1... | collective-permute-start | bytes 786440 | tf_op jit(solution)/shard_map/ppermute | solution.py:422
  2.9 10.1 %collective-permute-start.18 = (bf16[32,32,128]{2,1,0:T(8,128)(2,1)S(1)}, bf16[32,32,128]{2,1,0:T(8,128)(2,1)S(1)}, u32[]{:S(2)}, u32[]{:S(2)}) collective-permute-start(bf16[32,32,128]{2,1,0:T(8,128)(2,1)S(1)} %get-tuple-element.23.refs_3_.refs_5_), channel_id=1, source_target_pairs={{1,0},{2,1},{3,2},{11,3},{10,11},{9,10},{8,9},{0,8},{5,4},{6,5},{7... | collective-permute-start | bytes 786440 | tf_op jit(solution)/shard_map/ppermute | solution.py:448
  5.8 9.2 %collective-permute-start = (bf16[32,32,128]{2,1,0:T(8,128)(2,1)S(1)}, bf16[32,32,128]{2,1,0:T(8,128)(2,1)S(1)}, u32[]{:S(2)}, u32[]{:S(2)}) collective-permute-start(bf16[32,32,128]{2,1,0:T(8,128)(2,1)S(1)} %get-tuple-element.23.refs_3_.refs_5_), channel_id=1, source_target_pairs={{0,1},{1,2},{2,3},{3,11},{11,10},{10,9},{9,8},{8,0},{4,5},{5,6},{6... | collective-permute-start | bytes 786440 | tf_op jit(solution)/shard_map/ppermute | solution.py:448
  5.9 12.7 %collective-permute-start.4 = (bf16[32,32,128]{2,1,0:T(8,128)(2,1)S(1)}, bf16[32,32,128]{2,1,0:T(8,128)(2,1)S(1)}, u32[]{:S(2)}, u32[]{:S(2)}) collective-permute-start(bf16[32,32,128]{2,1,0:T(8,128)(2,1)S(1)} %get-tuple-element.27.refs_3_.refs_7_), channel_id=1, source_target_pairs={{1,0},{2,1},{3,2},{11,3},{10,11},{9,10},{8,9},{0,8},{5,4},{6,5},{7... | collective-permute-start | bytes 786440 | tf_op jit(solution)/shard_map/ppermute | solution.py:448
  7.8 12.8 %collective-permute-start.3 = (bf16[32,32,128]{2,1,0:T(8,128)(2,1)S(1)}, bf16[32,32,128]{2,1,0:T(8,128)(2,1)S(1)}, u32[]{:S(2)}, u32[]{:S(2)}) collective-permute-start(bf16[32,32,128]{2,1,0:T(8,128)(2,1)S(1)} %get-tuple-element.27.refs_3_.refs_7_), channel_id=1, source_target_pairs={{0,1},{1,2},{2,3},{3,11},{11,10},{10,9},{9,8},{8,0},{4,5},{5,6},{6... | collective-permute-start | bytes 786440 | tf_op jit(solution)/shard_map/ppermute | solution.py:448
  7.9 16.3 %collective-permute-start.6 = (bf16[32,32,128]{2,1,0:T(8,128)(2,1)S(1)}, bf16[32,32,128]{2,1,0:T(8,128)(2,1)S(1)}, u32[]{:S(2)}, u32[]{:S(2)}) collective-permute-start(bf16[32,32,128]{2,1,0:T(8,128)(2,1)S(1)} %collective-permute-done.2.refs_4_.refs_8_), channel_id=1, source_target_pairs={{1,0},{2,1},{3,2},{11,3},{10,11},{9,10},{8,9},{0,8},{5,4},{6,5},{7... | collective-permute-start | bytes 786440 | tf_op jit(solution)/shard_map/ppermute | solution.py:448
  13.0 13.3 %collective-permute-start.5 = (bf16[32,32,128]{2,1,0:T(8,128)(2,1)S(1)}, bf16[32,32,128]{2,1,0:T(8,128)(2,1)S(1)}, u32[]{:S(2)}, u32[]{:S(2)}) collective-permute-start(bf16[32,32,128]{2,1,0:T(8,128)(2,1)S(1)} %collective-permute-done.2.refs_4_.refs_8_), channel_id=1, source_target_pairs={{0,1},{1,2},{2,3},{3,11},{11,10},{10,9},{9,8},{8,0},{4,5},{5,6},{6... | collective-permute-start | bytes 786440 | tf_op jit(solution)/shard_map/ppermute | solution.py:448
  15.1 14.8 %collective-permute-start.20 = (bf16[32,32,128]{2,1,0:T(8,128)(2,1)S(1)}, bf16[32,32,128]{2,1,0:T(8,128)(2,1)S(1)}, u32[]{:S(2)}, u32[]{:S(2)}) collective-permute-start(bf16[32,32,128]{2,1,0:T(8,128)(2,1)S(1)} %collective-permute-done.17.refs_4_.refs_6_), channel_id=1, source_target_pairs={{1,0},{2,1},{3,2},{11,3},{10,11},{9,10},{8,9},{0,8},{5,4},{6,5},{7... | collective-permute-start | bytes 786440 | tf_op jit(solution)/shard_map/ppermute | solution.py:448
  18.6 13.3 %collective-permute-start.19 = (bf16[32,32,128]{2,1,0:T(8,128)(2,1)S(1)}, bf16[32,32,128]{2,1,0:T(8,128)(2,1)S(1)}, u32[]{:S(2)}, u32[]{:S(2)}) collective-permute-start(bf16[32,32,128]{2,1,0:T(8,128)(2,1)S(1)} %collective-permute-done.17.refs_4_.refs_6_), channel_id=1, source_target_pairs={{0,1},{1,2},{2,3},{3,11},{11,10},{10,9},{9,8},{8,0},{4,5},{5,6},{6... | collective-permute-start | bytes 786440 | tf_op jit(solution)/shard_map/ppermute | solution.py:448
  20.7 14.8 %collective-permute-start.22 = (bf16[32,32,128]{2,1,0:T(8,128)(2,1)S(1)}, bf16[32,32,128]{2,1,0:T(8,128)(2,1)S(1)}, u32[]{:S(2)}, u32[]{:S(2)}) collective-permute-start(bf16[32,32,128]{2,1,0:T(8,128)(2,1)S(1)} %collective-permute-done.18.refs_6_.refs_10_), channel_id=1, source_target_pairs={{1,0},{2,1},{3,2},{11,3},{10,11},{9,10},{8,9},{0,8},{5,4},{6,5},{7... | collective-permute-start | bytes 786440 | tf_op jit(solution)/shard_map/ppermute | solution.py:448
  23.0 0.7 copy-start.6
  24.2 18.8 %collective-permute-start.21 = (bf16[32,32,128]{2,1,0:T(8,128)(2,1)S(1)}, bf16[32,32,128]{2,1,0:T(8,128)(2,1)}, u32[]{:S(2)}, u32[]{:S(2)}) collective-permute-start(bf16[32,32,128]{2,1,0:T(8,128)(2,1)S(1)} %collective-permute-done.refs_5_.refs_9_), channel_id=1, source_target_pairs={{0,1},{1,2},{2,3},{3,11},{11,10},{10,9},{9,8},{8,0},{4,5},{5,6},{6... | collective-permute-start | bytes 786440 | tf_op jit(solution)/shard_map/ppermute | solution.py:448
  26.3 18.7 %collective-permute-start.8 = (bf16[32,32,128]{2,1,0:T(8,128)(2,1)S(1)}, bf16[32,32,128]{2,1,0:T(8,128)(2,1)}, u32[]{:S(2)}, u32[]{:S(2)}) collective-permute-start(bf16[32,32,128]{2,1,0:T(8,128)(2,1)S(1)} %collective-permute-done.4.refs_6_.refs_14_), channel_id=1, source_target_pairs={{1,0},{2,1},{3,2},{11,3},{10,11},{9,10},{8,9},{0,8},{5,4},{6,5},{7... | collective-permute-start | bytes 786440 | tf_op jit(solution)/shard_map/ppermute | solution.py:448
  29.8 15.3 %collective-permute-start.7 = (bf16[32,32,128]{2,1,0:T(8,128)(2,1)S(1)}, bf16[32,32,128]{2,1,0:T(8,128)(2,1)}, u32[]{:S(2)}, u32[]{:S(2)}) collective-permute-start(bf16[32,32,128]{2,1,0:T(8,128)(2,1)S(1)} %collective-permute-done.3.refs_5_.refs_13_), channel_id=1, source_target_pairs={{0,1},{1,2},{2,3},{3,11},{11,10},{10,9},{9,8},{8,0},{4,5},{5,6},{6... | collective-permute-start | bytes 786440 | tf_op jit(solution)/shard_map/ppermute | solution.py:448
  31.9 3.6 %copy-start.2 = (bf16[32,32,128]{2,1,0:T(8,128)(2,1)}, bf16[32,32,128]{2,1,0:T(8,128)(2,1)S(1)}, u32[]{:S(2)}) copy-start(bf16[32,32,128]{2,1,0:T(8,128)(2,1)S(1)} %collective-permute-done.19.refs_7_.refs_11_) | copy-start | bytes 786436
  31.9 15.2 %collective-permute-start.10 = (bf16[32,32,128]{2,1,0:T(8,128)(2,1)S(1)}, bf16[32,32,128]{2,1,0:T(8,128)(2,1)}, u32[]{:S(2)}, u32[]{:S(2)}) collective-permute-start(bf16[32,32,128]{2,1,0:T(8,128)(2,1)S(1)} %collective-permute-done.6.refs_8_.refs_16_), channel_id=1, source_target_pairs={{1,0},{2,1},{3,2},{11,3},{10,11},{9,10},{8,9},{0,8},{5,4},{6,5},{7... | collective-permute-start | bytes 786440 | tf_op jit(solution)/shard_map/ppermute | solution.py:448
  35.5 0.7 copy-start.4
  36.2 13.0 %collective-permute-start.9 = (bf16[32,32,128]{2,1,0:T(8,128)(2,1)S(1)}, bf16[32,32,128]{2,1,0:T(8,128)(2,1)}, u32[]{:S(2)}, u32[]{:S(2)}) collective-permute-start(bf16[32,32,128]{2,1,0:T(8,128)(2,1)S(1)} %collective-permute-done.5.refs_7_.refs_15_), channel_id=1, source_target_pairs={{0,1},{1,2},{2,3},{3,11},{11,10},{10,9},{9,8},{8,0},{4,5},{5,6},{6... | collective-permute-start | bytes 786440 | tf_op jit(solution)/shard_map/ppermute | solution.py:448
  38.2 23.0 %all-to-all-start = ((bf16[8,8,16,128]{3,2,1,0:T(8,128)(2,1)}), bf16[8,8,16,128]{3,2,1,0:T(8,128)(2,1)}, u32[]{:S(2)}, u32[]{:S(2)}) async-start(bf16[8,8,16,128]{3,2,1,0:T(8,128)(2,1)} %copy-done.6), calls=%async_computation | async-start | bytes 524288 | tf_op jit(solution)/shard_map/all_to_all | solution.py:492
  43.0 13.8 %collective-permute-start.24 = (bf16[32,32,128]{2,1,0:T(8,128)(2,1)S(1)}, bf16[32,32,128]{2,1,0:T(8,128)(2,1)}, u32[]{:S(2)}, u32[]{:S(2)}) collective-permute-start(bf16[32,32,128]{2,1,0:T(8,128)(2,1)S(1)} %collective-permute-done.20.refs_8_.refs_12_), channel_id=1, source_target_pairs={{1,0},{2,1},{3,2},{11,3},{10,11},{9,10},{8,9},{0,8},{5,4},{6,5},{7... | collective-permute-start | bytes 786440 | tf_op jit(solution)/shard_map/ppermute | solution.py:448
  45.0 16.2 %collective-permute-start.23 = (bf16[32,32,128]{2,1,0:T(8,128)(2,1)}, bf16[32,32,128]{2,1,0:T(8,128)(2,1)}, u32[]{:S(2)}, u32[]{:S(2)}) collective-permute-start(bf16[32,32,128]{2,1,0:T(8,128)(2,1)} %copy-done.2), channel_id=1, source_target_pairs={{0,1},{1,2},{2,3},{3,11},{11,10},{10,9},{9,8},{8,0},{4,5},{5,6},{6... | collective-permute-start | bytes 786440 | tf_op jit(solution)/shard_map/ppermute | solution.py:448
  45.1 17.3 %collective-permute-start.26 = (bf16[32,32,128]{2,1,0:T(8,128)(2,1)}, bf16[32,32,128]{2,1,0:T(8,128)(2,1)}, u32[]{:S(2)}, u32[]{:S(2)}) collective-permute-start(bf16[32,32,128]{2,1,0:T(8,128)(2,1)} %copy-done.4), channel_id=1, source_target_pairs={{1,0},{2,1},{3,2},{11,3},{10,11},{9,10},{8,9},{0,8},{5,4},{6,5},{7... | collective-permute-start | bytes 786440 | tf_op jit(solution)/shard_map/ppermute | solution.py:448
  47.1 17.2 %collective-permute-start.25 = (bf16[32,32,128]{2,1,0:T(8,128)(2,1)}, bf16[32,32,128]{2,1,0:T(8,128)(2,1)}, u32[]{:S(2)}, u32[]{:S(2)}) collective-permute-start(bf16[32,32,128]{2,1,0:T(8,128)(2,1)} %collective-permute-done.21.refs_9_.refs_17_), channel_id=1, source_target_pairs={{0,1},{1,2},{2,3},{3,11},{11,10},{10,9},{9,8},{8,0},{4,5},{5,6},{6... | collective-permute-start | bytes 786440 | tf_op jit(solution)/shard_map/ppermute | solution.py:448
  49.2 18.3 %collective-permute-start.11 = (bf16[32,32,128]{2,1,0:T(8,128)(2,1)}, bf16[32,32,128]{2,1,0:T(8,128)(2,1)}, u32[]{:S(2)}, u32[]{:S(2)}) collective-permute-start(bf16[32,32,128]{2,1,0:T(8,128)(2,1)} %collective-permute-done.7.refs_9_.refs_21_), channel_id=1, source_target_pairs={{0,1},{1,2},{2,3},{3,11},{11,10},{10,9},{9,8},{8,0},{4,5},{5,6},{6... | collective-permute-start | bytes 786440 | tf_op jit(solution)/shard_map/ppermute | solution.py:448
  56.8 16.1 %collective-permute-start.28 = (bf16[32,32,128]{2,1,0:T(8,128)(2,1)}, bf16[32,32,128]{2,1,0:T(8,128)(2,1)}, u32[]{:S(2)}, u32[]{:S(2)}) collective-permute-start(bf16[32,32,128]{2,1,0:T(8,128)(2,1)} %collective-permute-done.24.refs_12_.refs_20_), channel_id=1, source_target_pairs={{1,0},{2,1},{3,2},{11,3},{10,11},{9,10},{8,9},{0,8},{5,4},{6,5},{7... | collective-permute-start | bytes 786440 | tf_op jit(solution)/shard_map/ppermute | solution.py:448
  61.2 12.9 %collective-permute-start.1 = (bf16[2,4,8,16,128]{4,3,2,1,0:T(8,128)(2,1)}, bf16[2,4,8,16,128]{4,3,2,1,0:T(8,128)(2,1)}, u32[]{:S(2)}, u32[]{:S(2)}) collective-permute-start(bf16[2,4,8,16,128]{4,3,2,1,0:T(8,128)(2,1)} %bitcast.3.refs_0_), channel_id=1, source_target_pairs={{0,4},{4,0},{1,5},{5,1},{2,6},{6,2},{3,7},{7,3},{8,12},{12,8},{9,1... | collective-permute-start | bytes 786440 | tf_op jit(solution)/shard_map/ppermute | solution.py:422
  62.4 15.3 %collective-permute-start.14 = (bf16[32,32,128]{2,1,0:T(8,128)(2,1)}, bf16[32,32,128]{2,1,0:T(8,128)(2,1)}, u32[]{:S(2)}, u32[]{:S(2)}) collective-permute-start(bf16[32,32,128]{2,1,0:T(8,128)(2,1)} %collective-permute-done.10.refs_12_.refs_24_), channel_id=1, source_target_pairs={{1,0},{2,1},{3,2},{11,3},{10,11},{9,10},{8,9},{0,8},{5,4},{6,5},{7... | collective-permute-start | bytes 786440 | tf_op jit(solution)/shard_map/ppermute | solution.py:448
  64.3 13.5 %collective-permute-start.27 = (bf16[32,32,128]{2,1,0:T(8,128)(2,1)}, bf16[32,32,128]{2,1,0:T(8,128)(2,1)}, u32[]{:S(2)}, u32[]{:S(2)}) collective-permute-start(bf16[32,32,128]{2,1,0:T(8,128)(2,1)} %collective-permute-done.23.refs_11_.refs_19_), channel_id=1, source_target_pairs={{0,1},{1,2},{2,3},{3,11},{11,10},{10,9},{9,8},{8,0},{4,5},{5,6},{6... | collective-permute-start | bytes 786440 | tf_op jit(solution)/shard_map/ppermute | solution.py:448
  67.5 12.4 %collective-permute-start.29 = (bf16[32,32,128]{2,1,0:T(8,128)(2,1)}, bf16[32,32,128]{2,1,0:T(8,128)(2,1)}, u32[]{:S(2)}, u32[]{:S(2)}) collective-permute-start(bf16[32,32,128]{2,1,0:T(8,128)(2,1)} %collective-permute-done.25.refs_13_.refs_25_), channel_id=1, source_target_pairs={{0,1},{1,2},{2,3},{3,11},{11,10},{10,9},{9,8},{8,0},{4,5},{5,6},{6... | collective-permute-start | bytes 786440 | tf_op jit(solution)/shard_map/ppermute | solution.py:448
  72.9 11.8 %collective-permute-start.30 = (bf16[32,32,128]{2,1,0:T(8,128)(2,1)}, bf16[32,32,128]{2,1,0:T(8,128)(2,1)}, u32[]{:S(2)}, u32[]{:S(2)}) collective-permute-start(bf16[32,32,128]{2,1,0:T(8,128)(2,1)} %collective-permute-done.28.refs_16_.refs_28_), channel_id=1, source_target_pairs={{1,0},{2,1},{3,2},{11,3},{10,11},{9,10},{8,9},{0,8},{5,4},{6,5},{7... | collective-permute-start | bytes 786440 | tf_op jit(solution)/shard_map/ppermute | solution.py:448
  74.2 17.3 %collective-permute-start.12 = (bf16[32,32,128]{2,1,0:T(8,128)(2,1)}, bf16[32,32,128]{2,1,0:T(8,128)(2,1)S(1)}, u32[]{:S(2)}, u32[]{:S(2)}) collective-permute-start(bf16[32,32,128]{2,1,0:T(8,128)(2,1)} %collective-permute-done.8.refs_10_.refs_22_), channel_id=1, source_target_pairs={{1,0},{2,1},{3,2},{11,3},{10,11},{9,10},{8,9},{0,8},{5,4},{6,5},{7... | collective-permute-start | bytes 786440 | tf_op jit(solution)/shard_map/ppermute | solution.py:448
  77.7 13.8 %collective-permute-start.13 = (bf16[32,32,128]{2,1,0:T(8,128)(2,1)}, bf16[32,32,128]{2,1,0:T(8,128)(2,1)S(1)}, u32[]{:S(2)}, u32[]{:S(2)}) collective-permute-start(bf16[32,32,128]{2,1,0:T(8,128)(2,1)} %collective-permute-done.9.refs_11_.refs_23_), channel_id=1, source_target_pairs={{0,1},{1,2},{2,3},{3,11},{11,10},{10,9},{9,8},{8,0},{4,5},{5,6},{6... | collective-permute-start | bytes 786440 | tf_op jit(solution)/shard_map/ppermute | solution.py:448
  77.7 13.8 %collective-permute-start.15 = (bf16[32,32,128]{2,1,0:T(8,128)(2,1)}, bf16[32,32,128]{2,1,0:T(8,128)(2,1)S(1)}, u32[]{:S(2)}, u32[]{:S(2)}) collective-permute-start(bf16[32,32,128]{2,1,0:T(8,128)(2,1)} %collective-permute-done.11.refs_13_.refs_29_), channel_id=1, source_target_pairs={{0,1},{1,2},{2,3},{3,11},{11,10},{10,9},{9,8},{8,0},{4,5},{5,6},{6... | collective-permute-start | bytes 786440 | tf_op jit(solution)/shard_map/ppermute | solution.py:448
  79.9 11.7 %collective-permute-start.16 = (bf16[32,32,128]{2,1,0:T(8,128)(2,1)}, bf16[32,32,128]{2,1,0:T(8,128)(2,1)S(1)}, u32[]{:S(2)}, u32[]{:S(2)}) collective-permute-start(bf16[32,32,128]{2,1,0:T(8,128)(2,1)} %collective-permute-done.14.refs_16_.refs_32_), channel_id=1, source_target_pairs={{1,0},{2,1},{3,2},{11,3},{10,11},{9,10},{8,9},{0,8},{5,4},{6,5},{7... | collective-permute-start | bytes 786440 | tf_op jit(solution)/shard_map/ppermute | solution.py:448
  81.9 2.8 %copy-start.3 = (bf16[32,32,128]{2,1,0:T(8,128)(2,1)S(1)}, bf16[32,32,128]{2,1,0:T(8,128)(2,1)}, u32[]{:S(2)}) copy-start(bf16[32,32,128]{2,1,0:T(8,128)(2,1)} %copy-done.2) | copy-start | bytes 786436
  81.9 2.8 %copy-start.5 = (bf16[32,32,128]{2,1,0:T(8,128)(2,1)S(1)}, bf16[32,32,128]{2,1,0:T(8,128)(2,1)}, u32[]{:S(2)}) copy-start(bf16[32,32,128]{2,1,0:T(8,128)(2,1)} %copy-done.4) | copy-start | bytes 786436
  98.1 2.0 %collective-permute-start.31 = (bf16[64,32,128]{2,1,0:T(8,128)(2,1)S(1)}, bf16[64,32,128]{2,1,0:T(8,128)(2,1)S(1)}, u32[]{:S(2)}, u32[]{:S(2)}) collective-permute-start(bf16[64,32,128]{2,1,0:T(8,128)(2,1)S(1)} %get-tuple-element.34), channel_id=1, source_target_pairs={{0,4},{4,0},{1,5},{5,1},{2,6},{6,2},{3,7},{7,3},{8,12},{12,8},{9,1... | collective-permute-start | bytes 1572872 | tf_op jit(solution)/shard_map/ppermute | solution.py:422
  98.2 2.6 %collective-permute-start.32 = (bf16[64,32,128]{2,1,0:T(8,128)(2,1)S(1)}, bf16[64,32,128]{2,1,0:T(8,128)(2,1)S(1)}, u32[]{:S(2)}, u32[]{:S(2)}) collective-permute-start(bf16[64,32,128]{2,1,0:T(8,128)(2,1)S(1)} %get-tuple-element.36), channel_id=1, source_target_pairs={{0,4},{4,0},{1,5},{5,1},{2,6},{6,2},{3,7},{7,3},{8,12},{12,8},{9,1... | collective-permute-start | bytes 1572872 | tf_op jit(solution)/shard_map/ppermute | solution.py:422
  111.6 2.0 %collective-permute-start.33 = (bf16[64,32,128]{2,1,0:T(8,128)(2,1)S(1)}, bf16[64,32,128]{2,1,0:T(8,128)(2,1)S(1)}, u32[]{:S(2)}, u32[]{:S(2)}) collective-permute-start(bf16[64,32,128]{2,1,0:T(8,128)(2,1)S(1)} %get-tuple-element.38), channel_id=1, source_target_pairs={{0,4},{4,0},{1,5},{5,1},{2,6},{6,2},{3,7},{7,3},{8,12},{12,8},{9,1... | collective-permute-start | bytes 1572872 | tf_op jit(solution)/shard_map/ppermute | solution.py:422
  129.8 1.3 collective-permute-start.34
  131.1 4.0 %collective-permute-start.35 = (f32[72,128]{1,0:T(8,128)S(1)}, f32[72,128]{1,0:T(8,128)S(1)}, u32[]{:S(2)}, u32[]{:S(2)}) collective-permute-start(f32[72,128]{1,0:T(8,128)S(1)} %add.20), channel_id=1, source_target_pairs={{0,8},{8,0},{1,9},{9,1},{2,10},{10,2},{3,11},{11,3},{4,12},{12,4},... | collective-permute-start | bytes 110600 | tf_op jit(solution)/shard_map/ppermute | solution.py:457
  135.0 5.8 %collective-permute-start.38 = (f32[72,128]{1,0:T(8,128)S(1)}, f32[72,128]{1,0:T(8,128)S(1)}, u32[]{:S(2)}, u32[]{:S(2)}) collective-permute-start(f32[72,128]{1,0:T(8,128)S(1)} %add.21), channel_id=1, source_target_pairs={{0,3},{1,2},{2,1},{3,0},{4,7},{5,6},{6,5},{7,4},{8,11},{9,10},{10,... | collective-permute-start | bytes 110600 | tf_op jit(solution)/shard_map/ppermute | solution.py:462
  135.0 5.8 %collective-permute-start.37 = (f32[72,128]{1,0:T(8,128)S(1)}, f32[72,128]{1,0:T(8,128)S(1)}, u32[]{:S(2)}, u32[]{:S(2)}) collective-permute-start(f32[72,128]{1,0:T(8,128)S(1)} %add.21), channel_id=1, source_target_pairs={{0,2},{1,3},{2,0},{3,1},{4,6},{5,7},{6,4},{7,5},{8,10},{9,11},{10,... | collective-permute-start | bytes 110600 | tf_op jit(solution)/shard_map/ppermute | solution.py:462
  135.9 5.5 %collective-permute-start.36 = (f32[72,128]{1,0:T(8,128)S(1)}, f32[72,128]{1,0:T(8,128)S(1)}, u32[]{:S(2)}, u32[]{:S(2)}) collective-permute-start(f32[72,128]{1,0:T(8,128)S(1)} %add.21), channel_id=1, source_target_pairs={{0,1},{1,0},{2,3},{3,2},{4,5},{5,4},{6,7},{7,6},{8,9},{9,8},{10,11... | collective-permute-start | bytes 110600 | tf_op jit(solution)/shard_map/ppermute | solution.py:462
  141.4 1.3 collective-permute-start.39

commit v7 on v6

--- a/solution.py
+++ b/solution.py
@@ -22,11 +22,12 @@
     return pltpu.roll(value, shift % value.shape[-1], 1)
 
 
-def apply_kernel(n_vec, z_count, own, offsets, keep, send, *refs):
+def apply_kernel(n_vec, n_whole, z_count, own, offsets, keep, send, *refs):
     place_ref, *refs = refs
     vec_refs = (refs[:n_vec], refs[n_vec : 2 * n_vec])
-    piece_refs = refs[2 * n_vec : 2 * n_vec + len(offsets)]
-    cov_ref, spec_ref, *refs = refs[2 * n_vec + len(offsets) :]
+    n_beam = len(offsets) + n_whole
+    beam_refs = refs[2 * n_vec : 2 * n_vec + n_beam]
+    cov_ref, spec_ref, *refs = refs[2 * n_vec + n_beam :]
     *refs, beam_ref, vec_ref, z_ref, y_ref, sems = refs
     n_out = len(keep) + len(send)
     added, out_refs = refs[: len(refs) - n_out], refs[len(refs) - n_out :]
@@ -34,26 +35,28 @@
     freqs = 2 * count
     half = rows // 2
     components = spec_ref.shape[0]
-    size, width, part_depth = piece_refs[0].shape
-    chips = count // size * z_count
     tiles, _, step = z_ref.shape
     lane = lax.broadcasted_iota(jnp.int32, (half, lanes), 1)
     is_real = (lane // own) % 2 == 0
     sign = jnp.where(is_real, -1.0, 1.0).astype(F32)
 
     copies = []
-    for index, (core, offset, part) in enumerate(offsets):
+    for index, (core, offset) in enumerate(offsets):
+        size, width, _ = beam_refs[index].shape
+        chips = count // size * z_count
         at = lax.rem(place_ref[0] + (offset % chips), chips)
         x_at = at // z_count
         z_at = jnp.where(x_at == 0, at, chips - 1 - at)
         target = beam_ref.at[
-            pl.ds(core * count + x_at * size, size),
-            pl.ds(pl.multiple_of(z_at * width, width), width),
-            pl.ds(part * part_depth, part_depth),
+            pl.ds(core * count + x_at * size, size), pl.ds(pl.multiple_of(z_at * width, width), width)
         ]
-        copies.append(pltpu.make_async_copy(piece_refs[index], target, sems.at[index]))
+        copies.append(pltpu.make_async_copy(beam_refs[index], target, sems.at[index]))
     for copy in copies:
         copy.start()
+
+    def beam_of(freq):
+        side_by_side = [beam_ref, *beam_refs[len(offsets) :]]
+        return jnp.concatenate([beam[freq] for beam in side_by_side], axis=1)
 
     def gather(side, place, carry):
         vec = vec_refs[side][0][place]
@@ -68,7 +71,7 @@
         copy.wait()
 
     def project(freq, carry):
-        z = jnp.dot(vec_ref[freq], beam_ref[freq], preferred_element_type=F32)
+        z = jnp.dot(vec_ref[freq], beam_of(freq), preferred_element_type=F32)
         for tile in range(tiles):
             z_ref[tile, pl.ds(freq, rows, stride=freqs), :] = z[:, tile * step : (tile + 1) * step]
         return carry
@@ -93,7 +96,7 @@
         ]
         product = lax.dot_general(
             jnp.concatenate(y, axis=1),
-            beam_ref[freq],
+            beam_of(freq),
             (((1,), (1,)), ((), ())),
             preferred_element_type=F32,
         )
@@ -117,7 +120,7 @@
         lax.fori_loop(0, count, functools.partial(expand, side), 0, unroll=64)
 
 
-def apply_covariance(place, vecs, beams, cov, spec, own, z_count, keep, send, added=()):
+def apply_covariance(place, vecs, beams, wholes, cov, spec, own, z_count, keep, send, give, added=()):
     count, rows, lanes = vecs[0][0].shape
     freqs = 2 * count
     depth = spec.shape[1]
@@ -126,28 +129,30 @@
     vmem = pl.BlockSpec(memory_space=pltpu.VMEM)
     n_vec = len(vecs[0])
     offsets = tuple(beam[1:] for beam in beams)
+    arrays = [beam[0] for beam in beams] + wholes
+    whole = (freqs, lanes, beams[0][0].shape[2])
+    out_shape = [jax.ShapeDtypeStruct((count, rows, lanes), F32)] * len(keep)
+    out_shape += [jax.ShapeDtypeStruct((count, rows, lanes), BF16)] * len(send)
+    out_shape += [jax.ShapeDtypeStruct(whole, BF16)] * give
     tiles = pltpu.VMEM((depth // step, rows * freqs, step), F32)
-    return pl.pallas_call(
-        functools.partial(apply_kernel, n_vec, z_count, own, offsets, keep, send),
-        out_shape=[jax.ShapeDtypeStruct((count, rows, lanes), F32)] * len(keep)
-        + [jax.ShapeDtypeStruct((count, rows, lanes), BF16)] * len(send),
+    kernel = functools.partial(
+        apply_kernel, n_vec, len(wholes), z_count, own, offsets, keep, send
+    )
+    return pl.pallas_call(
+        kernel,
+        out_shape=out_shape,
         in_specs=[pl.BlockSpec(memory_space=pltpu.SMEM)]
         + [vmem] * (2 * n_vec)
         + [pl.BlockSpec(memory_space=pl.ANY)] * len(beams)
-        + [vmem] * (2 + len(added)),
-        out_specs=[vmem] * (len(keep) + len(send)),
-        scratch_shapes=[
-            pltpu.VMEM((freqs, lanes, depth), BF16),
-            pltpu.VMEM((freqs, rows, lanes), BF16),
-            tiles,
-            tiles,
-            pltpu.SemaphoreType.DMA((len(beams),)),
-        ],
+        + [vmem] * (len(wholes) + 2 + len(added)),
+        out_specs=[vmem] * len(out_shape),
+        scratch_shapes=[pltpu.VMEM(whole, BF16)] * (not give)
+        + [pltpu.VMEM((freqs, rows, lanes), BF16), tiles, tiles, pltpu.SemaphoreType.DMA((len(beams),))],
         compiler_params=pltpu.CompilerParams(vmem_limit_bytes=APPLY_BYTES),
         cost_estimate=pl.CostEstimate(
             flops=flops, bytes_accessed=freqs * lanes * depth * 2, transcendentals=0
         ),
-    )(place, *vecs[0], *vecs[1], *[beam[0] for beam in beams], cov, spec, *added)
+    )(place, *vecs[0], *vecs[1], *arrays, cov, spec, *added)
 
 
 def pack_kernel(own, first_ref, second_ref, out_ref):
@@ -351,6 +356,33 @@
         out_specs=[pl.BlockSpec(memory_space=pltpu.VMEM)] * (2 * chunks),
         compiler_params=pltpu.CompilerParams(vmem_limit_bytes=SMALL_BYTES),
     )(core, beam, noise.T)
+
+
+def order_kernel(size, core_ref, cov_ref, out_ref):
+    components, order, _ = cov_ref.shape
+    places = range(order // (2 * size))
+    is_first = core_ref[0] == 0
+
+    def ordered(value):
+        found = []
+        for core in range(2):
+            starts = [(2 * x + (side ^ core)) * size for side in range(2) for x in places]
+            found.append(jnp.concatenate([value[start : start + size] for start in starts], axis=0))
+        return jnp.where(is_first, found[0], found[1])
+
+    for k in range(components):
+        out_ref[:, k * order : (k + 1) * order] = ordered(ordered(cov_ref[k]).T).T.astype(BF16)
+
+
+def order_covariance(core, cov, size):
+    components, order, _ = cov.shape
+    return pl.pallas_call(
+        functools.partial(order_kernel, size),
+        out_shape=jax.ShapeDtypeStruct((order, components * order), BF16),
+        in_specs=[pl.BlockSpec(memory_space=pltpu.SMEM), pl.BlockSpec(memory_space=pltpu.VMEM)],
+        out_specs=pl.BlockSpec(memory_space=pltpu.VMEM),
+        compiler_params=pltpu.CompilerParams(vmem_limit_bytes=SMALL_BYTES),
+    )(core, cov)
 
 
 def turn_kernel(start_ref, out_ref):
@@ -485,27 +517,40 @@
 
     spec = spectra.reshape(-1, cores, depth)
     spec = lax.dynamic_index_in_dim(spec, core, 1, False)
-    cov = freq_covariance.reshape(-1, x_count, cores, freqs, x_count, cores, freqs).astype(BF16)
-    cov = jnp.where(core == 0, cov, jnp.flip(cov, (2, 5)))
-    cov = cov.transpose(2, 1, 3, 0, 5, 4, 6).reshape(all_freqs, -1)
+    cov = order_covariance(core_index, freq_covariance, freqs)
 
     start = lax.all_to_all(start, ("x", "fc"), 0, 0, tiled=True)
     start = start.reshape(x_count, z_count, *start.shape[1:])
     operand = start_operand([start, swap_cores(start)], own)
 
     apply = functools.partial(apply_covariance, place)
-    added, width = (), depth // chunks
+    added, wholes, width = [], [], depth // chunks
+    cut_beams = [
+        [(piece, at, offset) for piece, at, offset, which in beams if which == chunk]
+        for chunk in range(chunks)
+    ]
     for chunk in range(chunks):
-        part = [(piece, at, offset, 0) for piece, at, offset, which in beams if which == chunk]
         part_spec = spec[:, chunk * width : (chunk + 1) * width]
         send = (0, 1) if chunk == chunks - 1 else ()
-        added = apply(
-            [[operand[0]], [operand[1]]], part, cov, part_spec, own, z_count, (0, 1), send, added
+        found = apply(
+            [[operand[0]], [operand[1]]],
+            cut_beams[chunk],
+            [],
+            cov,
+            part_spec,
+            own,
+            z_count,
+            (0, 1),
+            send,
+            chunk > 0,
+            added,
         )
+        added, whole = found[: 2 + len(send)], found[2 + len(send) :]
+        wholes += whole
     mine, theirs, mine_sent, theirs_sent = added
     got_mine, got_theirs = swap_cores(theirs_sent), swap_cores(mine_sent)
     second_mine, second_sent = apply(
-        [[mine, got_mine], [theirs, got_theirs]], beams, cov, spec, own, z_count, (0,), (1,)
+        [[mine, got_mine], [theirs, got_theirs]], cut_beams[0], wholes, cov, spec, own, z_count, (0,), (1,), False
     )
     packed = pack(second_mine, swap_cores(second_sent), x_count, z_count, own)
     packed = packed.reshape(x_count * z_count, *packed.shape[2:])

time: 153 us -> 151 us (0.987)
  waiting for transfers between devices: 31.5 us -> 39.1 us
  other arithmetic: 2.94 us -> 0.02 us
  starting transfers between devices: 56.6 us -> 54.7 us
  local copies, waits for them, and re-layouts: 7.21 us -> 5.39 us
  blocking collectives: 14.9 us -> 13.2 us
    ppermute x28, waiting for transfers between devices: 19.8 us -> 27.4 us  [gather_ring(): moving[key] = lax.ppermute(moving[key], ('x', 'fc'), pairs[way])]
    convert_element_type x2 -> x0, local copies, waits for them, and re-layouts: 2.67 us -> none  [body_split(): freq_covariance.reshape(-1, x_count, cores, freqs, x_count, cores, freqs)]
    unnamed x18 -> x44, local copies, waits for them, and re-layouts: 3.34 us -> 5.39 us
    transpose x1 -> x0, other arithmetic: 2 us -> none  [body_split(): cov = cov.transpose(2, 1, 3, 0, 5, 4, 6).reshape(all_freqs, -1)]
    ppermute x28, starting transfers between devices: 45.3 us -> 43.4 us  [gather_ring(): moving[key] = lax.ppermute(moving[key], ('x', 'fc'), pairs[way])]
    pallas_call x3 -> x4, Pallas kernels: 24.1 us -> 22.3 us  [the longest x3 22.2 us: apply_covariance(): pl.pallas_call(kernel, out_shape=out_shape, in_specs=[pl.BlockSpec(memory...]
    all_to_all x1, blocking collectives: 14.9 us -> 13.2 us  [body_split(): received = lax.all_to_all(packed, ('x', 'fc'), 0, 0, tiled=True)]
  transfers between devices with their start and end apart: 41 -> 41, of which waited for: 18 -> 18; matrix products, arithmetic and copies ran while one was open for 4% -> 0% of each run, Pallas kernels for 7% -> 7%
where the time goes in v7:
time: 151 us
  starting transfers between devices  54.7 us (36%)
  waiting for transfers between devices  39.1 us (26%)
  Pallas kernels  37.9 us (25%)
  blocking collectives  13.2 us (9%)
  local copies, waits for them, and re-layouts  5.39 us (4%)
    ppermute x28, starting transfers between devices, gather_ring(): moving[key] = lax.ppermute(moving[key], ('x', 'fc'), pairs[way])  43.4 us
    ppermute x28, waiting for transfers between devices, gather_ring(): moving[key] = lax.ppermute(moving[key], ('x', 'fc'), pairs[way])  27.4 us
    pallas_call x3, Pallas kernels, apply_covariance(): pl.pallas_call(kernel, out_shape=out_shape, in_specs=[pl.BlockSpec(memory...  22.2 us
    all_to_all x1, blocking collectives, body_split(): received = lax.all_to_all(packed, ('x', 'fc'), 0, 0, tiled=True)  13.2 us
    pallas_call x1, Pallas kernels, finish(): pl.pallas_call(functools.partial(finish_kernel, scale), out_shape=jax.Sha...  9.66 us
    ppermute x8, waiting for transfers between devices, swap_cores(): return lax.ppermute(value, 'core', [(0, 1), (1, 0)])  6.34 us
    unnamed x44, local copies, waits for them, and re-layouts  5.39 us
    all_to_all x1, starting transfers between devices, body_split(): start = lax.all_to_all(start, ('x', 'fc'), 0, 0, tiled=True)  4.79 us
  transfers between devices with their start and end apart: 41, of which 18 were waited for; matrix products, arithmetic and copies ran while one was open for 0% of the time, Pallas kernels for 7%

profile of v7, /device:TPU:0, one launch (start us, length us, event | category | flops | bytes accessed | tf_op | source)
XLA Modules:
  0.0 150.6 jit_solution(374249509094024861)
XLA Ops:
  0.0 1.2 copy-done.3
  1.2 0.7 copy-done.21
  1.9 0.3 shard_map.56
  2.3 0.5 collective-permute-start.2
  2.9 2.9 %collective-permute-start.4 = (bf16[32,32,128]{2,1,0:T(8,128)(2,1)S(1)}, bf16[32,32,128]{2,1,0:T(8,128)(2,1)S(1)}, u32[]{:S(2)}, u32[]{:S(2)}) collective-permute-start(bf16[32,32,128]{2,1,0:T(8,128)(2,1)S(1)} %get-tuple-element.28.refs_3_), channel_id=1, source_target_pairs={{1,0},{2,1},{3,2},{11,3},{10,11},{9,10},{8,9},{0,8},{5,4},{6,5},{7... | collective-permute-start | bytes 786440 | tf_op jit(solution)/shard_map/ppermute | solution.py:480
  5.9 1.9 %collective-permute-start.18 = (bf16[32,32,128]{2,1,0:T(8,128)(2,1)S(1)}, bf16[32,32,128]{2,1,0:T(8,128)(2,1)S(1)}, u32[]{:S(2)}, u32[]{:S(2)}) collective-permute-start(bf16[32,32,128]{2,1,0:T(8,128)(2,1)S(1)} %get-tuple-element.24.refs_3_.refs_5_), channel_id=1, source_target_pairs={{1,0},{2,1},{3,2},{11,3},{10,11},{9,10},{8,9},{0,8},{5,4},{6,5},{7... | collective-permute-start | bytes 786440 | tf_op jit(solution)/shard_map/ppermute | solution.py:480
  7.8 0.1 collective-permute-start
  8.0 1.9 %collective-permute-start.6 = (bf16[32,32,128]{2,1,0:T(8,128)(2,1)S(1)}, bf16[32,32,128]{2,1,0:T(8,128)(2,1)S(1)}, u32[]{:S(2)}, u32[]{:S(2)}) collective-permute-start(bf16[32,32,128]{2,1,0:T(8,128)(2,1)S(1)} %collective-permute-done.2.refs_4_), channel_id=1, source_target_pairs={{1,0},{2,1},{3,2},{11,3},{10,11},{9,10},{8,9},{0,8},{5,4},{6,5},{7... | collective-permute-start | bytes 786440 | tf_op jit(solution)/shard_map/ppermute | solution.py:480
  9.9 3.1 %collective-permute-done.4.refs_6_ = bf16[32,32,128]{2,1,0:T(8,128)(2,1)S(1)} collective-permute-done((bf16[32,32,128]{2,1,0:T(8,128)(2,1)S(1)}, bf16[32,32,128]{2,1,0:T(8,128)(2,1)S(1)}, u32[]{:S(2)}, u32[]{:S(2)}) %collective-permute-start.4) | collective-permute-done | bytes 262176 | tf_op jit(solution)/shard_map/ppermute | solution.py:480
  13.0 2.1 %collective-permute-start.5 = (bf16[32,32,128]{2,1,0:T(8,128)(2,1)S(1)}, bf16[32,32,128]{2,1,0:T(8,128)(2,1)S(1)}, u32[]{:S(2)}, u32[]{:S(2)}) collective-permute-start(bf16[32,32,128]{2,1,0:T(8,128)(2,1)S(1)} %collective-permute-done.2.refs_4_), channel_id=1, source_target_pairs={{0,1},{1,2},{2,3},{3,11},{11,10},{10,9},{9,8},{8,0},{4,5},{5,6},{6... | collective-permute-start | bytes 786440 | tf_op jit(solution)/shard_map/ppermute | solution.py:480
  15.1 1.5 %collective-permute-start.20 = (bf16[32,32,128]{2,1,0:T(8,128)(2,1)S(1)}, bf16[32,32,128]{2,1,0:T(8,128)(2,1)S(1)}, u32[]{:S(2)}, u32[]{:S(2)}) collective-permute-start(bf16[32,32,128]{2,1,0:T(8,128)(2,1)S(1)} %collective-permute-done.17.refs_4_.refs_6_), channel_id=1, source_target_pairs={{1,0},{2,1},{3,2},{11,3},{10,11},{9,10},{8,9},{0,8},{5,4},{6,5},{7... | collective-permute-start | bytes 786440 | tf_op jit(solution)/shard_map/ppermute | solution.py:480
  16.6 2.0 %collective-permute-done.18.refs_6_.refs_8_ = bf16[32,32,128]{2,1,0:T(8,128)(2,1)S(1)} collective-permute-done((bf16[32,32,128]{2,1,0:T(8,128)(2,1)S(1)}, bf16[32,32,128]{2,1,0:T(8,128)(2,1)S(1)}, u32[]{:S(2)}, u32[]{:S(2)}) %collective-permute-start.18) | collective-permute-done | bytes 262176 | tf_op jit(solution)/shard_map/ppermute | solution.py:480
  18.6 2.1 %collective-permute-start.19 = (bf16[32,32,128]{2,1,0:T(8,128)(2,1)S(1)}, bf16[32,32,128]{2,1,0:T(8,128)(2,1)S(1)}, u32[]{:S(2)}, u32[]{:S(2)}) collective-permute-start(bf16[32,32,128]{2,1,0:T(8,128)(2,1)S(1)} %collective-permute-done.17.refs_4_.refs_6_), channel_id=1, source_target_pairs={{0,1},{1,2},{2,3},{3,11},{11,10},{10,9},{9,8},{8,0},{4,5},{5,6},{6... | collective-permute-start | bytes 786440 | tf_op jit(solution)/shard_map/ppermute | solution.py:480
  20.7 1.5 %collective-permute-start.8 = (bf16[32,32,128]{2,1,0:T(8,128)(2,1)S(1)}, bf16[32,32,128]{2,1,0:T(8,128)(2,1)S(1)}, u32[]{:S(2)}, u32[]{:S(2)}) collective-permute-start(bf16[32,32,128]{2,1,0:T(8,128)(2,1)S(1)} %collective-permute-done.4.refs_6_), channel_id=1, source_target_pairs={{1,0},{2,1},{3,2},{11,3},{10,11},{9,10},{8,9},{0,8},{5,4},{6,5},{7... | collective-permute-start | bytes 786440 | tf_op jit(solution)/shard_map/ppermute | solution.py:480
  22.2 2.0 %collective-permute-done.6.refs_8_ = bf16[32,32,128]{2,1,0:T(8,128)(2,1)S(1)} collective-permute-done((bf16[32,32,128]{2,1,0:T(8,128)(2,1)S(1)}, bf16[32,32,128]{2,1,0:T(8,128)(2,1)S(1)}, u32[]{:S(2)}, u32[]{:S(2)}) %collective-permute-start.6) | collective-permute-done | bytes 262176 | tf_op jit(solution)/shard_map/ppermute | solution.py:480
  24.2 2.1 %collective-permute-start.7 = (bf16[32,32,128]{2,1,0:T(8,128)(2,1)S(1)}, bf16[32,32,128]{2,1,0:T(8,128)(2,1)}, u32[]{:S(2)}, u32[]{:S(2)}) collective-permute-start(bf16[32,32,128]{2,1,0:T(8,128)(2,1)S(1)} %collective-permute-done.3.refs_5_), channel_id=1, source_target_pairs={{0,1},{1,2},{2,3},{3,11},{11,10},{10,9},{9,8},{8,0},{4,5},{5,6},{6... | collective-permute-start | bytes 786440 | tf_op jit(solution)/shard_map/ppermute | solution.py:480
  26.3 1.0 copy-done.1
  27.3 1.5 %shard_map.55 = bf16[8,8,16,128]{3,2,1,0:T(8,128)(2,1)} custom-call(f32[2,32,16,128]{3,2,1,0:T(8,128)S(1)} %copy-done.1), custom_call_target="tpu_custom_call" | custom-call | tf_op jit(solution)/shard_map/pallas_call | solution.py:409
  28.9 1.0 collective-permute-done.20.refs_8_.refs_10_
  29.9 2.1 %collective-permute-start.21 = (bf16[32,32,128]{2,1,0:T(8,128)(2,1)S(1)}, bf16[32,32,128]{2,1,0:T(8,128)(2,1)S(1)}, u32[]{:S(2)}, u32[]{:S(2)}) collective-permute-start(bf16[32,32,128]{2,1,0:T(8,128)(2,1)S(1)} %collective-permute-done.refs_5_.refs_7_), channel_id=1, source_target_pairs={{0,1},{1,2},{2,3},{3,11},{11,10},{10,9},{9,8},{8,0},{4,5},{5,6},{6... | collective-permute-start | bytes 786440 | tf_op jit(solution)/shard_map/ppermute | solution.py:480
  31.9 1.5 %collective-permute-start.10 = (bf16[32,32,128]{2,1,0:T(8,128)(2,1)S(1)}, bf16[32,32,128]{2,1,0:T(8,128)(2,1)S(1)}, u32[]{:S(2)}, u32[]{:S(2)}) collective-permute-start(bf16[32,32,128]{2,1,0:T(8,128)(2,1)S(1)} %collective-permute-done.6.refs_8_), channel_id=1, source_target_pairs={{1,0},{2,1},{3,2},{11,3},{10,11},{9,10},{8,9},{0,8},{5,4},{6,5},{7... | collective-permute-start | bytes 786440 | tf_op jit(solution)/shard_map/ppermute | solution.py:480
  33.5 2.0 %collective-permute-done.8.refs_10_ = bf16[32,32,128]{2,1,0:T(8,128)(2,1)S(1)} collective-permute-done((bf16[32,32,128]{2,1,0:T(8,128)(2,1)S(1)}, bf16[32,32,128]{2,1,0:T(8,128)(2,1)S(1)}, u32[]{:S(2)}, u32[]{:S(2)}) %collective-permute-start.8) | collective-permute-done | bytes 262176 | tf_op jit(solution)/shard_map/ppermute | solution.py:480
  35.5 0.7 copy-done.16
  36.2 2.1 %collective-permute-start.9 = (bf16[32,32,128]{2,1,0:T(8,128)(2,1)S(1)}, bf16[32,32,128]{2,1,0:T(8,128)(2,1)}, u32[]{:S(2)}, u32[]{:S(2)}) collective-permute-start(bf16[32,32,128]{2,1,0:T(8,128)(2,1)S(1)} %collective-permute-done.5.refs_7_), channel_id=1, source_target_pairs={{0,1},{1,2},{2,3},{3,11},{11,10},{10,9},{9,8},{8,0},{4,5},{5,6},{6... | collective-permute-start | bytes 786440 | tf_op jit(solution)/shard_map/ppermute | solution.py:480
  38.3 0.7 copy-done.14
  39.0 4.8 %all-to-all-start = ((bf16[8,8,16,128]{3,2,1,0:T(8,128)(2,1)}), bf16[8,8,16,128]{3,2,1,0:T(8,128)(2,1)}, u32[]{:S(2)}, u32[]{:S(2)}) async-start(bf16[8,8,16,128]{3,2,1,0:T(8,128)(2,1)} %shard_map.55), calls=%async_computation | async-start | bytes 524288 | tf_op jit(solution)/shard_map/all_to_all | solution.py:522
  43.8 2.1 %collective-permute-start.24 = (bf16[32,32,128]{2,1,0:T(8,128)(2,1)S(1)}, bf16[32,32,128]{2,1,0:T(8,128)(2,1)S(1)}, u32[]{:S(2)}, u32[]{:S(2)}) collective-permute-start(bf16[32,32,128]{2,1,0:T(8,128)(2,1)S(1)} %collective-permute-done.20.refs_8_.refs_10_), channel_id=1, source_target_pairs={{1,0},{2,1},{3,2},{11,3},{10,11},{9,10},{8,9},{0,8},{5,4},{6,5},{7... | collective-permute-start | bytes 786440 | tf_op jit(solution)/shard_map/ppermute | solution.py:480
  45.9 2.0 %collective-permute-start.11 = (bf16[32,32,128]{2,1,0:T(8,128)(2,1)}, bf16[32,32,128]{2,1,0:T(8,128)(2,1)}, u32[]{:S(2)}, u32[]{:S(2)}) collective-permute-start(bf16[32,32,128]{2,1,0:T(8,128)(2,1)} %collective-permute-done.7.refs_9_), channel_id=1, source_target_pairs={{0,1},{1,2},{2,3},{3,11},{11,10},{10,9},{9,8},{8,0},{4,5},{5,6},{6... | collective-permute-start | bytes 786440 | tf_op jit(solution)/shard_map/ppermute | solution.py:480
  47.9 1.1 collective-permute-start.26
  49.2 1.8 %collective-permute-start.25 = (bf16[32,32,128]{2,1,0:T(8,128)(2,1)S(1)}, bf16[32,32,128]{2,1,0:T(8,128)(2,1)S(1)}, u32[]{:S(2)}, u32[]{:S(2)}) collective-permute-start(bf16[32,32,128]{2,1,0:T(8,128)(2,1)S(1)} %collective-permute-done.21.refs_9_.refs_11_), channel_id=1, source_target_pairs={{0,1},{1,2},{2,3},{3,11},{11,10},{10,9},{9,8},{8,0},{4,5},{5,6},{6... | collective-permute-start | bytes 786440 | tf_op jit(solution)/shard_map/ppermute | solution.py:480
  51.0 6.4 %collective-permute-done.24.refs_12_.refs_14_ = bf16[32,32,128]{2,1,0:T(8,128)(2,1)S(1)} collective-permute-done((bf16[32,32,128]{2,1,0:T(8,128)(2,1)S(1)}, bf16[32,32,128]{2,1,0:T(8,128)(2,1)S(1)}, u32[]{:S(2)}, u32[]{:S(2)}) %collective-permute-start.24) | collective-permute-done | bytes 262176 | tf_op jit(solution)/shard_map/ppermute | solution.py:480
  57.4 0.2 collective-permute-start.28
  57.7 5.2 %collective-permute-done.11.refs_13_ = bf16[32,32,128]{2,1,0:T(8,128)(2,1)} collective-permute-done((bf16[32,32,128]{2,1,0:T(8,128)(2,1)}, bf16[32,32,128]{2,1,0:T(8,128)(2,1)}, u32[]{:S(2)}, u32[]{:S(2)}) %collective-permute-start.11) | collective-permute-done | bytes 262176 | tf_op jit(solution)/shard_map/ppermute | solution.py:480
  62.9 3.0 %collective-permute-start.14 = (bf16[32,32,128]{2,1,0:T(8,128)(2,1)}, bf16[32,32,128]{2,1,0:T(8,128)(2,1)}, u32[]{:S(2)}, u32[]{:S(2)}) collective-permute-start(bf16[32,32,128]{2,1,0:T(8,128)(2,1)} %copy-done.18), channel_id=1, source_target_pairs={{1,0},{2,1},{3,2},{11,3},{10,11},{9,10},{8,9},{0,8},{5,4},{6,5},{7... | collective-permute-start | bytes 786440 | tf_op jit(solution)/shard_map/ppermute | solution.py:480
  65.9 1.5 collective-permute-done.25.refs_13_.refs_15_
  67.4 3.4 %collective-permute-start.29 = (bf16[32,32,128]{2,1,0:T(8,128)(2,1)S(1)}, bf16[32,32,128]{2,1,0:T(8,128)(2,1)}, u32[]{:S(2)}, u32[]{:S(2)}) collective-permute-start(bf16[32,32,128]{2,1,0:T(8,128)(2,1)S(1)} %collective-permute-done.25.refs_13_.refs_15_), channel_id=1, source_target_pairs={{0,1},{1,2},{2,3},{3,11},{11,10},{10,9},{9,8},{8,0},{4,5},{5,6},{6... | collective-permute-start | bytes 786440 | tf_op jit(solution)/shard_map/ppermute | solution.py:480
  70.8 0.5 collective-permute-start.30
  71.4 0.9 copy-done.20
  72.3 0.2 shard_map.58.refs_19_.refs_22_
  72.6 3.0 %collective-permute-start.12 = (bf16[32,32,128]{2,1,0:T(8,128)(2,1)}, bf16[32,32,128]{2,1,0:T(8,128)(2,1)S(1)}, u32[]{:S(2)}, u32[]{:S(2)}) collective-permute-start(bf16[32,32,128]{2,1,0:T(8,128)(2,1)} %copy-done.16), channel_id=1, source_target_pairs={{1,0},{2,1},{3,2},{11,3},{10,11},{9,10},{8,9},{0,8},{5,4},{6,5},{7... | collective-permute-start | bytes 786440 | tf_op jit(solution)/shard_map/ppermute | solution.py:480
  75.6 1.6 %collective-permute-start.13 = (bf16[32,32,128]{2,1,0:T(8,128)(2,1)}, bf16[32,32,128]{2,1,0:T(8,128)(2,1)S(1)}, u32[]{:S(2)}, u32[]{:S(2)}) collective-permute-start(bf16[32,32,128]{2,1,0:T(8,128)(2,1)} %collective-permute-done.9.refs_11_), channel_id=1, source_target_pairs={{0,1},{1,2},{2,3},{3,11},{11,10},{10,9},{9,8},{8,0},{4,5},{5,6},{6... | collective-permute-start | bytes 786440 | tf_op jit(solution)/shard_map/ppermute | solution.py:480
  77.3 4.0 %collective-permute-done.29.refs_17_.refs_19_ = bf16[32,32,128]{2,1,0:T(8,128)(2,1)} collective-permute-done((bf16[32,32,128]{2,1,0:T(8,128)(2,1)S(1)}, bf16[32,32,128]{2,1,0:T(8,128)(2,1)}, u32[]{:S(2)}, u32[]{:S(2)}) %collective-permute-start.29) | collective-permute-done | bytes 262176 | tf_op jit(solution)/shard_map/ppermute | solution.py:480
  81.3 2.5 %collective-permute-start.16 = (bf16[32,32,128]{2,1,0:T(8,128)(2,1)}, bf16[32,32,128]{2,1,0:T(8,128)(2,1)S(1)}, u32[]{:S(2)}, u32[]{:S(2)}) collective-permute-start(bf16[32,32,128]{2,1,0:T(8,128)(2,1)} %collective-permute-done.14.refs_16_), channel_id=1, source_target_pairs={{1,0},{2,1},{3,2},{11,3},{10,11},{9,10},{8,9},{0,8},{5,4},{6,5},{7... | collective-permute-start | bytes 786440 | tf_op jit(solution)/shard_map/ppermute | solution.py:480
  83.8 2.7 %shard_map.57 = (bf16[64,32,128]{2,1,0:T(8,128)(2,1)S(1)}, bf16[64,32,128]{2,1,0:T(8,128)(2,1)S(1)}) custom-call(bf16[2,4,8,16,128]{4,3,2,1,0:T(8,128)(2,1)} %bitcast.3.refs_0_, bf16[2,4,8,16,128]{4,3,2,1,0:T(8,128)(2,1)} %collective-permute-done.1.refs_1_), custom_call_target="tpu_custom_call" | custom-call | tf_op jit(solution)/shard_map/pallas_call | solution.py:444
  86.6 6.4 %shard_map.59 = (f32[64,32,128]{2,1,0:T(8,128)S(1)}, f32[64,32,128]{2,1,0:T(8,128)S(1)}) custom-call(s32[1]{0:T(128)} %bitcast.1.refs_0_, bf16[64,32,128]{2,1,0:T(8,128)(2,1)S(1)} %get-tuple-element.26.refs_1_, bf16[64,32,128]{2,1,0:T(8,128)(2,1)S(1)} %get-tuple-element.27.refs_2_, bf16[32,32,128]{2,1,0:T(8,128)(2,1)S(1)} %get-tuple-element.24.refs_3_.refs_5_, ...), custom_call_target="tpu_custom_call" | custom-call | flops 536870912 | bytes 4194304 | tf_op jit(solution)/shard_map/pallas_call | solution.py:141
  93.1 6.5 %shard_map.60 = (f32[64,32,128]{2,1,0:T(8,128)S(1)}, f32[64,32,128]{2,1,0:T(8,128)S(1)}, bf16[64,32,128]{2,1,0:T(8,128)(2,1)S(1)}, bf16[64,32,128]{2,1,0:T(8,128)(2,1)S(1)}, bf16[128,128,128]{2,1,0:T(8,128)(2,1)S(1)}) custom-call(s32[1]{0:T(128)} %bitcast.1.refs_0_, bf16[64,32,128]{2,1,0:T(8,128)(2,1)S(1)} %get-tuple-element.26.refs_1_, ...), custom_call_target="tpu_custom_call" | custom-call | flops 536870912 | bytes 4194304 | tf_op jit(solution)/shard_map/pallas_call | solution.py:141
  99.6 0.5 collective-permute-start.32
  100.1 1.4 collective-permute-done.31.refs_2_
  101.5 0.7 collective-permute-done.32.refs_4_
  102.3 9.3 %shard_map.61 = (f32[64,32,128]{2,1,0:T(8,128)S(1)}, bf16[64,32,128]{2,1,0:T(8,128)(2,1)S(1)}) custom-call(s32[1]{0:T(128)} %bitcast.1.refs_0_, f32[64,32,128]{2,1,0:T(8,128)S(1)} %get-tuple-element.34.refs_1_, bf16[64,32,128]{2,1,0:T(8,128)(2,1)S(1)} %collective-permute-done.31.refs_2_, f32[64,32,128]{2,1,0:T(8,128)S(1)} %get-tuple-element.36.refs_3_, ...), custom_call_target="tpu_custom_call" | custom-call | flops 1073741824 | bytes 8388608 | tf_op jit(solution)/shard_map/pallas_call | solution.py:141
  111.6 0.2 collective-permute-start.33
  111.8 1.8 %collective-permute-done.33.second_ref = bf16[64,32,128]{2,1,0:T(8,128)(2,1)S(1)} collective-permute-done((bf16[64,32,128]{2,1,0:T(8,128)(2,1)S(1)}, bf16[64,32,128]{2,1,0:T(8,128)(2,1)S(1)}, u32[]{:S(2)}, u32[]{:S(2)}) %collective-permute-start.33) | collective-permute-done | bytes 524320 | tf_op jit(solution)/shard_map/ppermute | solution.py:454
  113.6 0.8 shard_map.62
  114.3 13.2 %all_to_all.10 = bf16[8,4,32,128]{3,2,1,0:T(8,128)(2,1)S(1)} all-to-all(bf16[8,4,32,128]{3,2,1,0:T(8,128)(2,1)S(1)} %bitcast.13), channel_id=1, replica_groups=mesh['ma'=2,'x'=2,'core'=2,'fc'=4] {'x','fc'}, dimensions={0} | all-to-all | bytes 524288 | tf_op jit(solution)/shard_map/all_to_all | solution.py:557
  127.6 0.5 shard_map.63
  128.2 1.2 collective-permute-done.34
  129.4 0.6 collective-permute-start.35
  129.9 3.4 %collective-permute-done.35 = f32[72,128]{1,0:T(8,128)S(1)} collective-permute-done((f32[72,128]{1,0:T(8,128)S(1)}, f32[72,128]{1,0:T(8,128)S(1)}, u32[]{:S(2)}, u32[]{:S(2)}) %collective-permute-start.35) | collective-permute-done | bytes 36896 | tf_op jit(solution)/shard_map/ppermute | solution.py:489
  133.3 0.8 collective-permute-start.37
  134.2 3.6 %collective-permute-start.36 = (f32[72,128]{1,0:T(8,128)S(1)}, f32[72,128]{1,0:T(8,128)S(1)}, u32[]{:S(2)}, u32[]{:S(2)}) collective-permute-start(f32[72,128]{1,0:T(8,128)S(1)} %add.21), channel_id=1, source_target_pairs={{0,1},{1,0},{2,3},{3,2},{4,5},{5,4},{6,7},{7,6},{8,9},{9,8},{10,11... | collective-permute-start | bytes 110600 | tf_op jit(solution)/shard_map/ppermute | solution.py:494
  137.7 1.4 collective-permute-done.38
  139.1 0.6 collective-permute-done.36
  139.8 1.2 collective-permute-done.39.given_ref
  141.0 9.7 %shard_map.64 = f32[2,4,128,128]{3,2,1,0:T(8,128)} custom-call(s32[1]{0:T(128)} %bitcast.core_ref, bf16[8,4,2,16,128]{4,3,2,1,0:T(8,128)(2,1)S(1)} %bitcast.12, f32[72,128]{1,0:T(8,128)S(1)} %add_add_fusion.kept_ref, f32[72,128]{1,0:T(8,128)S(1)} %collective-permute-done.39.given_ref), custom_call_target="tpu_custom_call" | custom-call | tf_op jit(solution)/shard_map/pallas_call | solution.py:318
  (78 shorter events, 0.9 us)
Async XLA Ops:
  0.0 71.4 %copy-start = (f32[2,512]{1,0:T(2,128)S(1)}, f32[2,512]{1,0:T(2,128)}, u32[]{:S(2)}) copy-start(f32[2,512]{1,0:T(2,128)} %param.7) | copy-start | bytes 12292
  0.0 1.2 copy-start.3
  1.2 0.7 copy-start.21
  2.3 29.6 %copy-start.4 = (bf16[32,32,128]{2,1,0:T(8,128)(2,1)}, bf16[32,32,128]{2,1,0:T(8,128)(2,1)S(1)}, u32[]{:S(2)}) copy-start(bf16[32,32,128]{2,1,0:T(8,128)(2,1)S(1)} %get-tuple-element.28.refs_3_) | copy-start | bytes 786436
  2.3 5.5 %collective-permute-start.2 = (bf16[32,32,128]{2,1,0:T(8,128)(2,1)S(1)}, bf16[32,32,128]{2,1,0:T(8,128)(2,1)S(1)}, u32[]{:S(2)}, u32[]{:S(2)}) collective-permute-start(bf16[32,32,128]{2,1,0:T(8,128)(2,1)S(1)} %get-tuple-element.29), channel_id=1, source_target_pairs={{0,4},{4,0},{1,5},{5,1},{2,6},{6,2},{3,7},{7,3},{8,12},{12,8},{9,1... | collective-permute-start | bytes 786440 | tf_op jit(solution)/shard_map/ppermute | solution.py:454
  2.8 5.2 %collective-permute-start.17 = (bf16[32,32,128]{2,1,0:T(8,128)(2,1)S(1)}, bf16[32,32,128]{2,1,0:T(8,128)(2,1)S(1)}, u32[]{:S(2)}, u32[]{:S(2)}) collective-permute-start(bf16[32,32,128]{2,1,0:T(8,128)(2,1)S(1)} %get-tuple-element.30), channel_id=1, source_target_pairs={{0,4},{4,0},{1,5},{5,1},{2,6},{6,2},{3,7},{7,3},{8,12},{12,8},{9,1... | collective-permute-start | bytes 786440 | tf_op jit(solution)/shard_map/ppermute | solution.py:454
  2.9 10.1 %collective-permute-start.4 = (bf16[32,32,128]{2,1,0:T(8,128)(2,1)S(1)}, bf16[32,32,128]{2,1,0:T(8,128)(2,1)S(1)}, u32[]{:S(2)}, u32[]{:S(2)}) collective-permute-start(bf16[32,32,128]{2,1,0:T(8,128)(2,1)S(1)} %get-tuple-element.28.refs_3_), channel_id=1, source_target_pairs={{1,0},{2,1},{3,2},{11,3},{10,11},{9,10},{8,9},{0,8},{5,4},{6,5},{7... | collective-permute-start | bytes 786440 | tf_op jit(solution)/shard_map/ppermute | solution.py:480
  5.8 9.3 %collective-permute-start.3 = (bf16[32,32,128]{2,1,0:T(8,128)(2,1)S(1)}, bf16[32,32,128]{2,1,0:T(8,128)(2,1)S(1)}, u32[]{:S(2)}, u32[]{:S(2)}) collective-permute-start(bf16[32,32,128]{2,1,0:T(8,128)(2,1)S(1)} %get-tuple-element.28.refs_3_), channel_id=1, source_target_pairs={{0,1},{1,2},{2,3},{3,11},{11,10},{10,9},{9,8},{8,0},{4,5},{5,6},{6... | collective-permute-start | bytes 786440 | tf_op jit(solution)/shard_map/ppermute | solution.py:480
  5.9 12.7 %collective-permute-start.18 = (bf16[32,32,128]{2,1,0:T(8,128)(2,1)S(1)}, bf16[32,32,128]{2,1,0:T(8,128)(2,1)S(1)}, u32[]{:S(2)}, u32[]{:S(2)}) collective-permute-start(bf16[32,32,128]{2,1,0:T(8,128)(2,1)S(1)} %get-tuple-element.24.refs_3_.refs_5_), channel_id=1, source_target_pairs={{1,0},{2,1},{3,2},{11,3},{10,11},{9,10},{8,9},{0,8},{5,4},{6,5},{7... | collective-permute-start | bytes 786440 | tf_op jit(solution)/shard_map/ppermute | solution.py:480
  7.8 25.6 %copy-start.6 = (bf16[32,32,128]{2,1,0:T(8,128)(2,1)}, bf16[32,32,128]{2,1,0:T(8,128)(2,1)S(1)}, u32[]{:S(2)}) copy-start(bf16[32,32,128]{2,1,0:T(8,128)(2,1)S(1)} %collective-permute-done.2.refs_4_) | copy-start | bytes 786436
  7.8 12.8 %collective-permute-start = (bf16[32,32,128]{2,1,0:T(8,128)(2,1)S(1)}, bf16[32,32,128]{2,1,0:T(8,128)(2,1)S(1)}, u32[]{:S(2)}, u32[]{:S(2)}) collective-permute-start(bf16[32,32,128]{2,1,0:T(8,128)(2,1)S(1)} %get-tuple-element.24.refs_3_.refs_5_), channel_id=1, source_target_pairs={{0,1},{1,2},{2,3},{3,11},{11,10},{10,9},{9,8},{8,0},{4,5},{5,6},{6... | collective-permute-start | bytes 786440 | tf_op jit(solution)/shard_map/ppermute | solution.py:480
  8.0 16.2 %collective-permute-start.6 = (bf16[32,32,128]{2,1,0:T(8,128)(2,1)S(1)}, bf16[32,32,128]{2,1,0:T(8,128)(2,1)S(1)}, u32[]{:S(2)}, u32[]{:S(2)}) collective-permute-start(bf16[32,32,128]{2,1,0:T(8,128)(2,1)S(1)} %collective-permute-done.2.refs_4_), channel_id=1, source_target_pairs={{1,0},{2,1},{3,2},{11,3},{10,11},{9,10},{8,9},{0,8},{5,4},{6,5},{7... | collective-permute-start | bytes 786440 | tf_op jit(solution)/shard_map/ppermute | solution.py:480
  13.0 22.5 %copy-start.8 = (bf16[32,32,128]{2,1,0:T(8,128)(2,1)}, bf16[32,32,128]{2,1,0:T(8,128)(2,1)S(1)}, u32[]{:S(2)}) copy-start(bf16[32,32,128]{2,1,0:T(8,128)(2,1)S(1)} %collective-permute-done.4.refs_6_) | copy-start | bytes 786436
  13.0 15.9 %collective-permute-start.5 = (bf16[32,32,128]{2,1,0:T(8,128)(2,1)S(1)}, bf16[32,32,128]{2,1,0:T(8,128)(2,1)S(1)}, u32[]{:S(2)}, u32[]{:S(2)}) collective-permute-start(bf16[32,32,128]{2,1,0:T(8,128)(2,1)S(1)} %collective-permute-done.2.refs_4_), channel_id=1, source_target_pairs={{0,1},{1,2},{2,3},{3,11},{11,10},{10,9},{9,8},{8,0},{4,5},{5,6},{6... | collective-permute-start | bytes 786440 | tf_op jit(solution)/shard_map/ppermute | solution.py:480
  15.1 28.7 %copy-start.10 = (bf16[32,32,128]{2,1,0:T(8,128)(2,1)}, bf16[32,32,128]{2,1,0:T(8,128)(2,1)S(1)}, u32[]{:S(2)}) copy-start(bf16[32,32,128]{2,1,0:T(8,128)(2,1)S(1)} %collective-permute-done.3.refs_5_) | copy-start | bytes 786436
  15.1 14.8 %collective-permute-start.20 = (bf16[32,32,128]{2,1,0:T(8,128)(2,1)S(1)}, bf16[32,32,128]{2,1,0:T(8,128)(2,1)S(1)}, u32[]{:S(2)}, u32[]{:S(2)}) collective-permute-start(bf16[32,32,128]{2,1,0:T(8,128)(2,1)S(1)} %collective-permute-done.17.refs_4_.refs_6_), channel_id=1, source_target_pairs={{1,0},{2,1},{3,2},{11,3},{10,11},{9,10},{8,9},{0,8},{5,4},{6,5},{7... | collective-permute-start | bytes 786440 | tf_op jit(solution)/shard_map/ppermute | solution.py:480
  18.6 13.3 %collective-permute-start.19 = (bf16[32,32,128]{2,1,0:T(8,128)(2,1)S(1)}, bf16[32,32,128]{2,1,0:T(8,128)(2,1)S(1)}, u32[]{:S(2)}, u32[]{:S(2)}) collective-permute-start(bf16[32,32,128]{2,1,0:T(8,128)(2,1)S(1)} %collective-permute-done.17.refs_4_.refs_6_), channel_id=1, source_target_pairs={{0,1},{1,2},{2,3},{3,11},{11,10},{10,9},{9,8},{8,0},{4,5},{5,6},{6... | collective-permute-start | bytes 786440 | tf_op jit(solution)/shard_map/ppermute | solution.py:480
  20.7 14.8 %collective-permute-start.8 = (bf16[32,32,128]{2,1,0:T(8,128)(2,1)S(1)}, bf16[32,32,128]{2,1,0:T(8,128)(2,1)S(1)}, u32[]{:S(2)}, u32[]{:S(2)}) collective-permute-start(bf16[32,32,128]{2,1,0:T(8,128)(2,1)S(1)} %collective-permute-done.4.refs_6_), channel_id=1, source_target_pairs={{1,0},{2,1},{3,2},{11,3},{10,11},{9,10},{8,9},{0,8},{5,4},{6,5},{7... | collective-permute-start | bytes 786440 | tf_op jit(solution)/shard_map/ppermute | solution.py:480
  24.2 23.7 %copy-start.12 = (bf16[32,32,128]{2,1,0:T(8,128)(2,1)}, bf16[32,32,128]{2,1,0:T(8,128)(2,1)S(1)}, u32[]{:S(2)}) copy-start(bf16[32,32,128]{2,1,0:T(8,128)(2,1)S(1)} %collective-permute-done.6.refs_8_) | copy-start | bytes 786436
  24.2 19.5 %collective-permute-start.7 = (bf16[32,32,128]{2,1,0:T(8,128)(2,1)S(1)}, bf16[32,32,128]{2,1,0:T(8,128)(2,1)}, u32[]{:S(2)}, u32[]{:S(2)}) collective-permute-start(bf16[32,32,128]{2,1,0:T(8,128)(2,1)S(1)} %collective-permute-done.3.refs_5_), channel_id=1, source_target_pairs={{0,1},{1,2},{2,3},{3,11},{11,10},{10,9},{9,8},{8,0},{4,5},{5,6},{6... | collective-permute-start | bytes 786440 | tf_op jit(solution)/shard_map/ppermute | solution.py:480
  26.3 1.0 copy-start.1
  28.9 17.0 %collective-permute-start.22 = (bf16[32,32,128]{2,1,0:T(8,128)(2,1)S(1)}, bf16[32,32,128]{2,1,0:T(8,128)(2,1)S(1)}, u32[]{:S(2)}, u32[]{:S(2)}) collective-permute-start(bf16[32,32,128]{2,1,0:T(8,128)(2,1)S(1)} %collective-permute-done.18.refs_6_.refs_8_), channel_id=1, source_target_pairs={{1,0},{2,1},{3,2},{11,3},{10,11},{9,10},{8,9},{0,8},{5,4},{6,5},{7... | collective-permute-start | bytes 786440 | tf_op jit(solution)/shard_map/ppermute | solution.py:480
  29.9 16.1 %collective-permute-start.21 = (bf16[32,32,128]{2,1,0:T(8,128)(2,1)S(1)}, bf16[32,32,128]{2,1,0:T(8,128)(2,1)S(1)}, u32[]{:S(2)}, u32[]{:S(2)}) collective-permute-start(bf16[32,32,128]{2,1,0:T(8,128)(2,1)S(1)} %collective-permute-done.refs_5_.refs_7_), channel_id=1, source_target_pairs={{0,1},{1,2},{2,3},{3,11},{11,10},{10,9},{9,8},{8,0},{4,5},{5,6},{6... | collective-permute-start | bytes 786440 | tf_op jit(solution)/shard_map/ppermute | solution.py:480
  31.9 16.0 %collective-permute-start.10 = (bf16[32,32,128]{2,1,0:T(8,128)(2,1)S(1)}, bf16[32,32,128]{2,1,0:T(8,128)(2,1)S(1)}, u32[]{:S(2)}, u32[]{:S(2)}) collective-permute-start(bf16[32,32,128]{2,1,0:T(8,128)(2,1)S(1)} %collective-permute-done.6.refs_8_), channel_id=1, source_target_pairs={{1,0},{2,1},{3,2},{11,3},{10,11},{9,10},{8,9},{0,8},{5,4},{6,5},{7... | collective-permute-start | bytes 786440 | tf_op jit(solution)/shard_map/ppermute | solution.py:480
  35.5 0.7 copy-start.16
  36.2 13.0 %collective-permute-start.9 = (bf16[32,32,128]{2,1,0:T(8,128)(2,1)S(1)}, bf16[32,32,128]{2,1,0:T(8,128)(2,1)}, u32[]{:S(2)}, u32[]{:S(2)}) collective-permute-start(bf16[32,32,128]{2,1,0:T(8,128)(2,1)S(1)} %collective-permute-done.5.refs_7_), channel_id=1, source_target_pairs={{0,1},{1,2},{2,3},{3,11},{11,10},{10,9},{9,8},{8,0},{4,5},{5,6},{6... | collective-permute-start | bytes 786440 | tf_op jit(solution)/shard_map/ppermute | solution.py:480
  38.3 0.7 copy-start.14
  39.0 18.7 %all-to-all-start = ((bf16[8,8,16,128]{3,2,1,0:T(8,128)(2,1)}), bf16[8,8,16,128]{3,2,1,0:T(8,128)(2,1)}, u32[]{:S(2)}, u32[]{:S(2)}) async-start(bf16[8,8,16,128]{3,2,1,0:T(8,128)(2,1)} %shard_map.55), calls=%async_computation | async-start | bytes 524288 | tf_op jit(solution)/shard_map/all_to_all | solution.py:522
  43.8 13.6 %collective-permute-start.24 = (bf16[32,32,128]{2,1,0:T(8,128)(2,1)S(1)}, bf16[32,32,128]{2,1,0:T(8,128)(2,1)S(1)}, u32[]{:S(2)}, u32[]{:S(2)}) collective-permute-start(bf16[32,32,128]{2,1,0:T(8,128)(2,1)S(1)} %collective-permute-done.20.refs_8_.refs_10_), channel_id=1, source_target_pairs={{1,0},{2,1},{3,2},{11,3},{10,11},{9,10},{8,9},{0,8},{5,4},{6,5},{7... | collective-permute-start | bytes 786440 | tf_op jit(solution)/shard_map/ppermute | solution.py:480
  45.9 11.8 %collective-permute-start.23 = (bf16[32,32,128]{2,1,0:T(8,128)(2,1)S(1)}, bf16[32,32,128]{2,1,0:T(8,128)(2,1)S(1)}, u32[]{:S(2)}, u32[]{:S(2)}) collective-permute-start(bf16[32,32,128]{2,1,0:T(8,128)(2,1)S(1)} %collective-permute-done.19.refs_7_.refs_9_), channel_id=1, source_target_pairs={{0,1},{1,2},{2,3},{3,11},{11,10},{10,9},{9,8},{8,0},{4,5},{5,6},{6... | collective-permute-start | bytes 786440 | tf_op jit(solution)/shard_map/ppermute | solution.py:480
  45.9 16.9 %collective-permute-start.11 = (bf16[32,32,128]{2,1,0:T(8,128)(2,1)}, bf16[32,32,128]{2,1,0:T(8,128)(2,1)}, u32[]{:S(2)}, u32[]{:S(2)}) collective-permute-start(bf16[32,32,128]{2,1,0:T(8,128)(2,1)} %collective-permute-done.7.refs_9_), channel_id=1, source_target_pairs={{0,1},{1,2},{2,3},{3,11},{11,10},{10,9},{9,8},{8,0},{4,5},{5,6},{6... | collective-permute-start | bytes 786440 | tf_op jit(solution)/shard_map/ppermute | solution.py:480
  47.9 3.1 %copy-start.18 = (bf16[32,32,128]{2,1,0:T(8,128)(2,1)}, bf16[32,32,128]{2,1,0:T(8,128)(2,1)S(1)}, u32[]{:S(2)}) copy-start(bf16[32,32,128]{2,1,0:T(8,128)(2,1)S(1)} %collective-permute-done.10.refs_12_) | copy-start | bytes 786436
  47.9 18.0 %collective-permute-start.26 = (bf16[32,32,128]{2,1,0:T(8,128)(2,1)S(1)}, bf16[32,32,128]{2,1,0:T(8,128)(2,1)S(1)}, u32[]{:S(2)}, u32[]{:S(2)}) collective-permute-start(bf16[32,32,128]{2,1,0:T(8,128)(2,1)S(1)} %collective-permute-done.22.refs_10_.refs_12_), channel_id=1, source_target_pairs={{1,0},{2,1},{3,2},{11,3},{10,11},{9,10},{8,9},{0,8},{5,4},{6,5},{7... | collective-permute-start | bytes 786440 | tf_op jit(solution)/shard_map/ppermute | solution.py:480
  49.2 18.2 %collective-permute-start.25 = (bf16[32,32,128]{2,1,0:T(8,128)(2,1)S(1)}, bf16[32,32,128]{2,1,0:T(8,128)(2,1)S(1)}, u32[]{:S(2)}, u32[]{:S(2)}) collective-permute-start(bf16[32,32,128]{2,1,0:T(8,128)(2,1)S(1)} %collective-permute-done.21.refs_9_.refs_11_), channel_id=1, source_target_pairs={{0,1},{1,2},{2,3},{3,11},{11,10},{10,9},{9,8},{8,0},{4,5},{5,6},{6... | collective-permute-start | bytes 786440 | tf_op jit(solution)/shard_map/ppermute | solution.py:480
  57.4 13.4 %collective-permute-start.28 = (bf16[32,32,128]{2,1,0:T(8,128)(2,1)S(1)}, bf16[32,32,128]{2,1,0:T(8,128)(2,1)S(1)}, u32[]{:S(2)}, u32[]{:S(2)}) collective-permute-start(bf16[32,32,128]{2,1,0:T(8,128)(2,1)S(1)} %collective-permute-done.24.refs_12_.refs_14_), channel_id=1, source_target_pairs={{1,0},{2,1},{3,2},{11,3},{10,11},{9,10},{8,9},{0,8},{5,4},{6,5},{7... | collective-permute-start | bytes 786440 | tf_op jit(solution)/shard_map/ppermute | solution.py:480
  57.7 14.9 %collective-permute-start.1 = (bf16[2,4,8,16,128]{4,3,2,1,0:T(8,128)(2,1)}, bf16[2,4,8,16,128]{4,3,2,1,0:T(8,128)(2,1)}, u32[]{:S(2)}, u32[]{:S(2)}) collective-permute-start(bf16[2,4,8,16,128]{4,3,2,1,0:T(8,128)(2,1)} %bitcast.3.refs_0_), channel_id=1, source_target_pairs={{0,4},{4,0},{1,5},{5,1},{2,6},{6,2},{3,7},{7,3},{8,12},{12,8},{9,1... | collective-permute-start | bytes 786440 | tf_op jit(solution)/shard_map/ppermute | solution.py:454
  62.9 12.7 %collective-permute-start.14 = (bf16[32,32,128]{2,1,0:T(8,128)(2,1)}, bf16[32,32,128]{2,1,0:T(8,128)(2,1)}, u32[]{:S(2)}, u32[]{:S(2)}) collective-permute-start(bf16[32,32,128]{2,1,0:T(8,128)(2,1)} %copy-done.18), channel_id=1, source_target_pairs={{1,0},{2,1},{3,2},{11,3},{10,11},{9,10},{8,9},{0,8},{5,4},{6,5},{7... | collective-permute-start | bytes 786440 | tf_op jit(solution)/shard_map/ppermute | solution.py:480
  65.9 11.4 %collective-permute-start.27 = (bf16[32,32,128]{2,1,0:T(8,128)(2,1)S(1)}, bf16[32,32,128]{2,1,0:T(8,128)(2,1)}, u32[]{:S(2)}, u32[]{:S(2)}) collective-permute-start(bf16[32,32,128]{2,1,0:T(8,128)(2,1)S(1)} %collective-permute-done.23.refs_11_.refs_13_), channel_id=1, source_target_pairs={{0,1},{1,2},{2,3},{3,11},{11,10},{10,9},{9,8},{8,0},{4,5},{5,6},{6... | collective-permute-start | bytes 786440 | tf_op jit(solution)/shard_map/ppermute | solution.py:480
  67.4 13.9 %collective-permute-start.29 = (bf16[32,32,128]{2,1,0:T(8,128)(2,1)S(1)}, bf16[32,32,128]{2,1,0:T(8,128)(2,1)}, u32[]{:S(2)}, u32[]{:S(2)}) collective-permute-start(bf16[32,32,128]{2,1,0:T(8,128)(2,1)S(1)} %collective-permute-done.25.refs_13_.refs_15_), channel_id=1, source_target_pairs={{0,1},{1,2},{2,3},{3,11},{11,10},{10,9},{9,8},{8,0},{4,5},{5,6},{6... | collective-permute-start | bytes 786440 | tf_op jit(solution)/shard_map/ppermute | solution.py:480
  70.8 15.7 %collective-permute-start.30 = (bf16[32,32,128]{2,1,0:T(8,128)(2,1)S(1)}, bf16[32,32,128]{2,1,0:T(8,128)(2,1)}, u32[]{:S(2)}, u32[]{:S(2)}) collective-permute-start(bf16[32,32,128]{2,1,0:T(8,128)(2,1)S(1)} %collective-permute-done.28.refs_16_.refs_18_), channel_id=1, source_target_pairs={{1,0},{2,1},{3,2},{11,3},{10,11},{9,10},{8,9},{0,8},{5,4},{6,5},{7... | collective-permute-start | bytes 786440 | tf_op jit(solution)/shard_map/ppermute | solution.py:480
  71.4 0.9 copy-start.20
  72.5 20.5 %copy-start.5 = (bf16[32,32,128]{2,1,0:T(8,128)(2,1)S(1)}, bf16[32,32,128]{2,1,0:T(8,128)(2,1)}, u32[]{:S(2)}) copy-start(bf16[32,32,128]{2,1,0:T(8,128)(2,1)} %copy-done.4) | copy-start | bytes 786436
  72.5 20.5 %copy-start.7 = (bf16[32,32,128]{2,1,0:T(8,128)(2,1)S(1)}, bf16[32,32,128]{2,1,0:T(8,128)(2,1)}, u32[]{:S(2)}) copy-start(bf16[32,32,128]{2,1,0:T(8,128)(2,1)} %copy-done.6) | copy-start | bytes 786436
  72.5 20.5 %copy-start.9 = (bf16[32,32,128]{2,1,0:T(8,128)(2,1)S(1)}, bf16[32,32,128]{2,1,0:T(8,128)(2,1)}, u32[]{:S(2)}) copy-start(bf16[32,32,128]{2,1,0:T(8,128)(2,1)} %copy-done.8) | copy-start | bytes 786436
  72.5 20.5 %copy-start.11 = (bf16[32,32,128]{2,1,0:T(8,128)(2,1)S(1)}, bf16[32,32,128]{2,1,0:T(8,128)(2,1)}, u32[]{:S(2)}) copy-start(bf16[32,32,128]{2,1,0:T(8,128)(2,1)} %copy-done.10) | copy-start | bytes 786436
  72.5 20.5 %copy-start.13 = (bf16[32,32,128]{2,1,0:T(8,128)(2,1)S(1)}, bf16[32,32,128]{2,1,0:T(8,128)(2,1)}, u32[]{:S(2)}) copy-start(bf16[32,32,128]{2,1,0:T(8,128)(2,1)} %copy-done.12) | copy-start | bytes 786436
  72.5 20.5 %copy-start.15 = (bf16[32,32,128]{2,1,0:T(8,128)(2,1)S(1)}, bf16[32,32,128]{2,1,0:T(8,128)(2,1)}, u32[]{:S(2)}) copy-start(bf16[32,32,128]{2,1,0:T(8,128)(2,1)} %copy-done.14) | copy-start | bytes 786436
  72.5 20.5 %copy-start.17 = (bf16[32,32,128]{2,1,0:T(8,128)(2,1)S(1)}, bf16[32,32,128]{2,1,0:T(8,128)(2,1)}, u32[]{:S(2)}) copy-start(bf16[32,32,128]{2,1,0:T(8,128)(2,1)} %copy-done.16) | copy-start | bytes 786436
  72.6 20.5 %copy-start.19 = (bf16[32,32,128]{2,1,0:T(8,128)(2,1)S(1)}, bf16[32,32,128]{2,1,0:T(8,128)(2,1)}, u32[]{:S(2)}) copy-start(bf16[32,32,128]{2,1,0:T(8,128)(2,1)} %copy-done.18) | copy-start | bytes 786436
  72.6 20.4 %collective-permute-start.12 = (bf16[32,32,128]{2,1,0:T(8,128)(2,1)}, bf16[32,32,128]{2,1,0:T(8,128)(2,1)S(1)}, u32[]{:S(2)}, u32[]{:S(2)}) collective-permute-start(bf16[32,32,128]{2,1,0:T(8,128)(2,1)} %copy-done.16), channel_id=1, source_target_pairs={{1,0},{2,1},{3,2},{11,3},{10,11},{9,10},{8,9},{0,8},{5,4},{6,5},{7... | collective-permute-start | bytes 786440 | tf_op jit(solution)/shard_map/ppermute | solution.py:480
  75.6 17.3 %collective-permute-start.13 = (bf16[32,32,128]{2,1,0:T(8,128)(2,1)}, bf16[32,32,128]{2,1,0:T(8,128)(2,1)S(1)}, u32[]{:S(2)}, u32[]{:S(2)}) collective-permute-start(bf16[32,32,128]{2,1,0:T(8,128)(2,1)} %collective-permute-done.9.refs_11_), channel_id=1, source_target_pairs={{0,1},{1,2},{2,3},{3,11},{11,10},{10,9},{9,8},{8,0},{4,5},{5,6},{6... | collective-permute-start | bytes 786440 | tf_op jit(solution)/shard_map/ppermute | solution.py:480
  77.3 15.7 %collective-permute-start.15 = (bf16[32,32,128]{2,1,0:T(8,128)(2,1)}, bf16[32,32,128]{2,1,0:T(8,128)(2,1)S(1)}, u32[]{:S(2)}, u32[]{:S(2)}) collective-permute-start(bf16[32,32,128]{2,1,0:T(8,128)(2,1)} %collective-permute-done.11.refs_13_), channel_id=1, source_target_pairs={{0,1},{1,2},{2,3},{3,11},{11,10},{10,9},{9,8},{8,0},{4,5},{5,6},{6... | collective-permute-start | bytes 786440 | tf_op jit(solution)/shard_map/ppermute | solution.py:480
  81.3 11.7 %collective-permute-start.16 = (bf16[32,32,128]{2,1,0:T(8,128)(2,1)}, bf16[32,32,128]{2,1,0:T(8,128)(2,1)S(1)}, u32[]{:S(2)}, u32[]{:S(2)}) collective-permute-start(bf16[32,32,128]{2,1,0:T(8,128)(2,1)} %collective-permute-done.14.refs_16_), channel_id=1, source_target_pairs={{1,0},{2,1},{3,2},{11,3},{10,11},{9,10},{8,9},{0,8},{5,4},{6,5},{7... | collective-permute-start | bytes 786440 | tf_op jit(solution)/shard_map/ppermute | solution.py:480
  99.5 2.0 %collective-permute-start.31 = (bf16[64,32,128]{2,1,0:T(8,128)(2,1)S(1)}, bf16[64,32,128]{2,1,0:T(8,128)(2,1)S(1)}, u32[]{:S(2)}, u32[]{:S(2)}) collective-permute-start(bf16[64,32,128]{2,1,0:T(8,128)(2,1)S(1)} %get-tuple-element.35), channel_id=1, source_target_pairs={{0,4},{4,0},{1,5},{5,1},{2,6},{6,2},{3,7},{7,3},{8,12},{12,8},{9,1... | collective-permute-start | bytes 1572872 | tf_op jit(solution)/shard_map/ppermute | solution.py:454
  99.6 2.6 %collective-permute-start.32 = (bf16[64,32,128]{2,1,0:T(8,128)(2,1)S(1)}, bf16[64,32,128]{2,1,0:T(8,128)(2,1)S(1)}, u32[]{:S(2)}, u32[]{:S(2)}) collective-permute-start(bf16[64,32,128]{2,1,0:T(8,128)(2,1)S(1)} %get-tuple-element.37), channel_id=1, source_target_pairs={{0,4},{4,0},{1,5},{5,1},{2,6},{6,2},{3,7},{7,3},{8,12},{12,8},{9,1... | collective-permute-start | bytes 1572872 | tf_op jit(solution)/shard_map/ppermute | solution.py:454
  102.3 25.3 %copy-start.2 = (f32[2,32,16,128]{3,2,1,0:T(8,128)S(1)}, f32[2,32,16,128]{3,2,1,0:T(8,128)}, u32[]{:S(2)}) copy-start(f32[2,32,16,128]{3,2,1,0:T(8,128)} %start_ref.3) | copy-start | bytes 1572868
  111.6 2.0 %collective-permute-start.33 = (bf16[64,32,128]{2,1,0:T(8,128)(2,1)S(1)}, bf16[64,32,128]{2,1,0:T(8,128)(2,1)S(1)}, u32[]{:S(2)}, u32[]{:S(2)}) collective-permute-start(bf16[64,32,128]{2,1,0:T(8,128)(2,1)S(1)} %get-tuple-element.40), channel_id=1, source_target_pairs={{0,4},{4,0},{1,5},{5,1},{2,6},{6,2},{3,7},{7,3},{8,12},{12,8},{9,1... | collective-permute-start | bytes 1572872 | tf_op jit(solution)/shard_map/ppermute | solution.py:454
  128.1 1.3 collective-permute-start.34
  129.4 4.0 %collective-permute-start.35 = (f32[72,128]{1,0:T(8,128)S(1)}, f32[72,128]{1,0:T(8,128)S(1)}, u32[]{:S(2)}, u32[]{:S(2)}) collective-permute-start(f32[72,128]{1,0:T(8,128)S(1)} %add.20), channel_id=1, source_target_pairs={{0,8},{8,0},{1,9},{9,1},{2,10},{10,2},{3,11},{11,3},{4,12},{12,4},... | collective-permute-start | bytes 110600 | tf_op jit(solution)/shard_map/ppermute | solution.py:489
  133.3 5.8 %collective-permute-start.38 = (f32[72,128]{1,0:T(8,128)S(1)}, f32[72,128]{1,0:T(8,128)S(1)}, u32[]{:S(2)}, u32[]{:S(2)}) collective-permute-start(f32[72,128]{1,0:T(8,128)S(1)} %add.21), channel_id=1, source_target_pairs={{0,3},{1,2},{2,1},{3,0},{4,7},{5,6},{6,5},{7,4},{8,11},{9,10},{10,... | collective-permute-start | bytes 110600 | tf_op jit(solution)/shard_map/ppermute | solution.py:494
  133.3 5.8 %collective-permute-start.37 = (f32[72,128]{1,0:T(8,128)S(1)}, f32[72,128]{1,0:T(8,128)S(1)}, u32[]{:S(2)}, u32[]{:S(2)}) collective-permute-start(f32[72,128]{1,0:T(8,128)S(1)} %add.21), channel_id=1, source_target_pairs={{0,2},{1,3},{2,0},{3,1},{4,6},{5,7},{6,4},{7,5},{8,10},{9,11},{10,... | collective-permute-start | bytes 110600 | tf_op jit(solution)/shard_map/ppermute | solution.py:494
  134.2 5.5 %collective-permute-start.36 = (f32[72,128]{1,0:T(8,128)S(1)}, f32[72,128]{1,0:T(8,128)S(1)}, u32[]{:S(2)}, u32[]{:S(2)}) collective-permute-start(f32[72,128]{1,0:T(8,128)S(1)} %add.21), channel_id=1, source_target_pairs={{0,1},{1,0},{2,3},{3,2},{4,5},{5,4},{6,7},{7,6},{8,9},{9,8},{10,11... | collective-permute-start | bytes 110600 | tf_op jit(solution)/shard_map/ppermute | solution.py:494
  139.7 1.3 collective-permute-start.39

commit v8 on v7

--- a/solution.py
+++ b/solution.py
@@ -485,8 +485,9 @@
 
 
 def sum_devices(keep, send, z_count):
-    value = keep + swap_cores(send)
-    value = value + lax.ppermute(value, "x", [(0, 1), (1, 0)])
+    far = lax.ppermute(send, ("x", "core"), [(0, 3), (1, 2), (2, 1), (3, 0)])
+    across = lax.ppermute(keep, "x", [(0, 1), (1, 0)])
+    value = (keep + swap_cores(send)) + (across + far)
     if z_count & (z_count - 1):
         value = lax.psum(value, "fc")
     else:

time: 151 us -> 151 us (level)
  waiting for transfers between devices: 39.1 us -> 36.9 us
  starting transfers between devices: 54.7 us -> 56.3 us
    ppermute x1 -> x2, waiting for transfers between devices: 3.39 us -> 2.2 us  [the longest x1 2.2 us: sum_devices(): across = lax.ppermute(keep, 'x', [(0, 1), (1, 0)])]
  transfers between devices with their start and end apart: 41 -> 42, of which waited for: 18 -> 17; matrix products, arithmetic and copies ran while one was open for 0% -> 0% of each run, Pallas kernels for 7% -> 7%
where the time goes in v8:
time: 151 us; the launch traced here: 150 us
  starting transfers between devices  56.3 us (37%)
  Pallas kernels  37.9 us (25%)
  waiting for transfers between devices  36.9 us (24%)
  blocking collectives  13.2 us (9%)
  local copies, waits for them, and re-layouts  5.37 us (4%)
    ppermute x28, starting transfers between devices, gather_ring(): moving[key] = lax.ppermute(moving[key], ('x', 'fc'), pairs[way])  43.4 us
    ppermute x28, waiting for transfers between devices, gather_ring(): moving[key] = lax.ppermute(moving[key], ('x', 'fc'), pairs[way])  27.4 us
    pallas_call x3, Pallas kernels, apply_covariance(): pl.pallas_call(kernel, out_shape=out_shape, in_specs=[pl.BlockSpec(memory...  22.2 us
    all_to_all x1, blocking collectives, body_split(): received = lax.all_to_all(packed, ('x', 'fc'), 0, 0, tiled=True)  13.2 us
    pallas_call x1, Pallas kernels, finish(): pl.pallas_call(functools.partial(finish_kernel, scale), out_shape=jax.Sha...  9.66 us
    unnamed x44, local copies, waits for them, and re-layouts  5.37 us
    ppermute x8, waiting for transfers between devices, swap_cores(): return lax.ppermute(value, 'core', [(0, 1), (1, 0)])  5.14 us
    all_to_all x1, starting transfers between devices, body_split(): start = lax.all_to_all(start, ('x', 'fc'), 0, 0, tiled=True)  4.79 us
  transfers between devices with their start and end apart: 42, of which 17 were waited for; matrix products, arithmetic and copies ran while one was open for 0% of the time, Pallas kernels for 7%

profile of v8, /device:TPU:0, one launch (start us, length us, event | category | flops | bytes accessed | tf_op | source)
XLA Modules:
  0.0 150.1 jit_solution(13464771078337536224)
XLA Ops:
  0.0 1.2 copy-done.3
  1.2 0.7 copy-done.21
  1.9 0.3 shard_map.56
  2.3 0.5 collective-permute-start.2
  2.9 2.9 %collective-permute-start.4 = (bf16[32,32,128]{2,1,0:T(8,128)(2,1)S(1)}, bf16[32,32,128]{2,1,0:T(8,128)(2,1)S(1)}, u32[]{:S(2)}, u32[]{:S(2)}) collective-permute-start(bf16[32,32,128]{2,1,0:T(8,128)(2,1)S(1)} %get-tuple-element.28.refs_3_), channel_id=1, source_target_pairs={{1,0},{2,1},{3,2},{11,3},{10,11},{9,10},{8,9},{0,8},{5,4},{6,5},{7... | collective-permute-start | bytes 786440 | tf_op jit(solution)/shard_map/ppermute | solution.py:480
  5.9 1.9 %collective-permute-start.18 = (bf16[32,32,128]{2,1,0:T(8,128)(2,1)S(1)}, bf16[32,32,128]{2,1,0:T(8,128)(2,1)S(1)}, u32[]{:S(2)}, u32[]{:S(2)}) collective-permute-start(bf16[32,32,128]{2,1,0:T(8,128)(2,1)S(1)} %get-tuple-element.24.refs_3_.refs_5_), channel_id=1, source_target_pairs={{1,0},{2,1},{3,2},{11,3},{10,11},{9,10},{8,9},{0,8},{5,4},{6,5},{7... | collective-permute-start | bytes 786440 | tf_op jit(solution)/shard_map/ppermute | solution.py:480
  7.8 0.1 collective-permute-start
  8.0 1.9 %collective-permute-start.6 = (bf16[32,32,128]{2,1,0:T(8,128)(2,1)S(1)}, bf16[32,32,128]{2,1,0:T(8,128)(2,1)S(1)}, u32[]{:S(2)}, u32[]{:S(2)}) collective-permute-start(bf16[32,32,128]{2,1,0:T(8,128)(2,1)S(1)} %collective-permute-done.2.refs_4_), channel_id=1, source_target_pairs={{1,0},{2,1},{3,2},{11,3},{10,11},{9,10},{8,9},{0,8},{5,4},{6,5},{7... | collective-permute-start | bytes 786440 | tf_op jit(solution)/shard_map/ppermute | solution.py:480
  9.9 3.1 %collective-permute-done.4.refs_6_ = bf16[32,32,128]{2,1,0:T(8,128)(2,1)S(1)} collective-permute-done((bf16[32,32,128]{2,1,0:T(8,128)(2,1)S(1)}, bf16[32,32,128]{2,1,0:T(8,128)(2,1)S(1)}, u32[]{:S(2)}, u32[]{:S(2)}) %collective-permute-start.4) | collective-permute-done | bytes 262176 | tf_op jit(solution)/shard_map/ppermute | solution.py:480
  13.0 2.1 %collective-permute-start.5 = (bf16[32,32,128]{2,1,0:T(8,128)(2,1)S(1)}, bf16[32,32,128]{2,1,0:T(8,128)(2,1)S(1)}, u32[]{:S(2)}, u32[]{:S(2)}) collective-permute-start(bf16[32,32,128]{2,1,0:T(8,128)(2,1)S(1)} %collective-permute-done.2.refs_4_), channel_id=1, source_target_pairs={{0,1},{1,2},{2,3},{3,11},{11,10},{10,9},{9,8},{8,0},{4,5},{5,6},{6... | collective-permute-start | bytes 786440 | tf_op jit(solution)/shard_map/ppermute | solution.py:480
  15.1 1.5 %collective-permute-start.20 = (bf16[32,32,128]{2,1,0:T(8,128)(2,1)S(1)}, bf16[32,32,128]{2,1,0:T(8,128)(2,1)S(1)}, u32[]{:S(2)}, u32[]{:S(2)}) collective-permute-start(bf16[32,32,128]{2,1,0:T(8,128)(2,1)S(1)} %collective-permute-done.17.refs_4_.refs_6_), channel_id=1, source_target_pairs={{1,0},{2,1},{3,2},{11,3},{10,11},{9,10},{8,9},{0,8},{5,4},{6,5},{7... | collective-permute-start | bytes 786440 | tf_op jit(solution)/shard_map/ppermute | solution.py:480
  16.6 2.0 %collective-permute-done.18.refs_6_.refs_8_ = bf16[32,32,128]{2,1,0:T(8,128)(2,1)S(1)} collective-permute-done((bf16[32,32,128]{2,1,0:T(8,128)(2,1)S(1)}, bf16[32,32,128]{2,1,0:T(8,128)(2,1)S(1)}, u32[]{:S(2)}, u32[]{:S(2)}) %collective-permute-start.18) | collective-permute-done | bytes 262176 | tf_op jit(solution)/shard_map/ppermute | solution.py:480
  18.6 2.1 %collective-permute-start.19 = (bf16[32,32,128]{2,1,0:T(8,128)(2,1)S(1)}, bf16[32,32,128]{2,1,0:T(8,128)(2,1)S(1)}, u32[]{:S(2)}, u32[]{:S(2)}) collective-permute-start(bf16[32,32,128]{2,1,0:T(8,128)(2,1)S(1)} %collective-permute-done.17.refs_4_.refs_6_), channel_id=1, source_target_pairs={{0,1},{1,2},{2,3},{3,11},{11,10},{10,9},{9,8},{8,0},{4,5},{5,6},{6... | collective-permute-start | bytes 786440 | tf_op jit(solution)/shard_map/ppermute | solution.py:480
  20.7 1.5 %collective-permute-start.8 = (bf16[32,32,128]{2,1,0:T(8,128)(2,1)S(1)}, bf16[32,32,128]{2,1,0:T(8,128)(2,1)S(1)}, u32[]{:S(2)}, u32[]{:S(2)}) collective-permute-start(bf16[32,32,128]{2,1,0:T(8,128)(2,1)S(1)} %collective-permute-done.4.refs_6_), channel_id=1, source_target_pairs={{1,0},{2,1},{3,2},{11,3},{10,11},{9,10},{8,9},{0,8},{5,4},{6,5},{7... | collective-permute-start | bytes 786440 | tf_op jit(solution)/shard_map/ppermute | solution.py:480
  22.2 2.0 %collective-permute-done.6.refs_8_ = bf16[32,32,128]{2,1,0:T(8,128)(2,1)S(1)} collective-permute-done((bf16[32,32,128]{2,1,0:T(8,128)(2,1)S(1)}, bf16[32,32,128]{2,1,0:T(8,128)(2,1)S(1)}, u32[]{:S(2)}, u32[]{:S(2)}) %collective-permute-start.6) | collective-permute-done | bytes 262176 | tf_op jit(solution)/shard_map/ppermute | solution.py:480
  24.2 2.1 %collective-permute-start.7 = (bf16[32,32,128]{2,1,0:T(8,128)(2,1)S(1)}, bf16[32,32,128]{2,1,0:T(8,128)(2,1)}, u32[]{:S(2)}, u32[]{:S(2)}) collective-permute-start(bf16[32,32,128]{2,1,0:T(8,128)(2,1)S(1)} %collective-permute-done.3.refs_5_), channel_id=1, source_target_pairs={{0,1},{1,2},{2,3},{3,11},{11,10},{10,9},{9,8},{8,0},{4,5},{5,6},{6... | collective-permute-start | bytes 786440 | tf_op jit(solution)/shard_map/ppermute | solution.py:480
  26.3 1.0 copy-done.1
  27.3 1.5 %shard_map.55 = bf16[8,8,16,128]{3,2,1,0:T(8,128)(2,1)} custom-call(f32[2,32,16,128]{3,2,1,0:T(8,128)S(1)} %copy-done.1), custom_call_target="tpu_custom_call" | custom-call | tf_op jit(solution)/shard_map/pallas_call | solution.py:409
  28.9 1.0 collective-permute-done.20.refs_8_.refs_10_
  29.9 2.1 %collective-permute-start.21 = (bf16[32,32,128]{2,1,0:T(8,128)(2,1)S(1)}, bf16[32,32,128]{2,1,0:T(8,128)(2,1)S(1)}, u32[]{:S(2)}, u32[]{:S(2)}) collective-permute-start(bf16[32,32,128]{2,1,0:T(8,128)(2,1)S(1)} %collective-permute-done.refs_5_.refs_7_), channel_id=1, source_target_pairs={{0,1},{1,2},{2,3},{3,11},{11,10},{10,9},{9,8},{8,0},{4,5},{5,6},{6... | collective-permute-start | bytes 786440 | tf_op jit(solution)/shard_map/ppermute | solution.py:480
  31.9 1.5 %collective-permute-start.10 = (bf16[32,32,128]{2,1,0:T(8,128)(2,1)S(1)}, bf16[32,32,128]{2,1,0:T(8,128)(2,1)S(1)}, u32[]{:S(2)}, u32[]{:S(2)}) collective-permute-start(bf16[32,32,128]{2,1,0:T(8,128)(2,1)S(1)} %collective-permute-done.6.refs_8_), channel_id=1, source_target_pairs={{1,0},{2,1},{3,2},{11,3},{10,11},{9,10},{8,9},{0,8},{5,4},{6,5},{7... | collective-permute-start | bytes 786440 | tf_op jit(solution)/shard_map/ppermute | solution.py:480
  33.5 2.0 %collective-permute-done.8.refs_10_ = bf16[32,32,128]{2,1,0:T(8,128)(2,1)S(1)} collective-permute-done((bf16[32,32,128]{2,1,0:T(8,128)(2,1)S(1)}, bf16[32,32,128]{2,1,0:T(8,128)(2,1)S(1)}, u32[]{:S(2)}, u32[]{:S(2)}) %collective-permute-start.8) | collective-permute-done | bytes 262176 | tf_op jit(solution)/shard_map/ppermute | solution.py:480
  35.5 0.7 copy-done.16
  36.2 2.1 %collective-permute-start.9 = (bf16[32,32,128]{2,1,0:T(8,128)(2,1)S(1)}, bf16[32,32,128]{2,1,0:T(8,128)(2,1)}, u32[]{:S(2)}, u32[]{:S(2)}) collective-permute-start(bf16[32,32,128]{2,1,0:T(8,128)(2,1)S(1)} %collective-permute-done.5.refs_7_), channel_id=1, source_target_pairs={{0,1},{1,2},{2,3},{3,11},{11,10},{10,9},{9,8},{8,0},{4,5},{5,6},{6... | collective-permute-start | bytes 786440 | tf_op jit(solution)/shard_map/ppermute | solution.py:480
  38.3 0.7 copy-done.14
  39.0 4.8 %all-to-all-start = ((bf16[8,8,16,128]{3,2,1,0:T(8,128)(2,1)}), bf16[8,8,16,128]{3,2,1,0:T(8,128)(2,1)}, u32[]{:S(2)}, u32[]{:S(2)}) async-start(bf16[8,8,16,128]{3,2,1,0:T(8,128)(2,1)} %shard_map.55), calls=%async_computation | async-start | bytes 524288 | tf_op jit(solution)/shard_map/all_to_all | solution.py:523
  43.8 2.1 %collective-permute-start.24 = (bf16[32,32,128]{2,1,0:T(8,128)(2,1)S(1)}, bf16[32,32,128]{2,1,0:T(8,128)(2,1)S(1)}, u32[]{:S(2)}, u32[]{:S(2)}) collective-permute-start(bf16[32,32,128]{2,1,0:T(8,128)(2,1)S(1)} %collective-permute-done.20.refs_8_.refs_10_), channel_id=1, source_target_pairs={{1,0},{2,1},{3,2},{11,3},{10,11},{9,10},{8,9},{0,8},{5,4},{6,5},{7... | collective-permute-start | bytes 786440 | tf_op jit(solution)/shard_map/ppermute | solution.py:480
  45.9 2.0 %collective-permute-start.11 = (bf16[32,32,128]{2,1,0:T(8,128)(2,1)}, bf16[32,32,128]{2,1,0:T(8,128)(2,1)}, u32[]{:S(2)}, u32[]{:S(2)}) collective-permute-start(bf16[32,32,128]{2,1,0:T(8,128)(2,1)} %collective-permute-done.7.refs_9_), channel_id=1, source_target_pairs={{0,1},{1,2},{2,3},{3,11},{11,10},{10,9},{9,8},{8,0},{4,5},{5,6},{6... | collective-permute-start | bytes 786440 | tf_op jit(solution)/shard_map/ppermute | solution.py:480
  47.9 1.2 collective-permute-start.26
  49.2 1.8 %collective-permute-start.25 = (bf16[32,32,128]{2,1,0:T(8,128)(2,1)S(1)}, bf16[32,32,128]{2,1,0:T(8,128)(2,1)S(1)}, u32[]{:S(2)}, u32[]{:S(2)}) collective-permute-start(bf16[32,32,128]{2,1,0:T(8,128)(2,1)S(1)} %collective-permute-done.21.refs_9_.refs_11_), channel_id=1, source_target_pairs={{0,1},{1,2},{2,3},{3,11},{11,10},{10,9},{9,8},{8,0},{4,5},{5,6},{6... | collective-permute-start | bytes 786440 | tf_op jit(solution)/shard_map/ppermute | solution.py:480
  51.0 6.4 %collective-permute-done.24.refs_12_.refs_14_ = bf16[32,32,128]{2,1,0:T(8,128)(2,1)S(1)} collective-permute-done((bf16[32,32,128]{2,1,0:T(8,128)(2,1)S(1)}, bf16[32,32,128]{2,1,0:T(8,128)(2,1)S(1)}, u32[]{:S(2)}, u32[]{:S(2)}) %collective-permute-start.24) | collective-permute-done | bytes 262176 | tf_op jit(solution)/shard_map/ppermute | solution.py:480
  57.4 0.2 collective-permute-start.28
  57.7 5.2 %collective-permute-done.11.refs_13_ = bf16[32,32,128]{2,1,0:T(8,128)(2,1)} collective-permute-done((bf16[32,32,128]{2,1,0:T(8,128)(2,1)}, bf16[32,32,128]{2,1,0:T(8,128)(2,1)}, u32[]{:S(2)}, u32[]{:S(2)}) %collective-permute-start.11) | collective-permute-done | bytes 262176 | tf_op jit(solution)/shard_map/ppermute | solution.py:480
  62.9 3.0 %collective-permute-start.14 = (bf16[32,32,128]{2,1,0:T(8,128)(2,1)}, bf16[32,32,128]{2,1,0:T(8,128)(2,1)}, u32[]{:S(2)}, u32[]{:S(2)}) collective-permute-start(bf16[32,32,128]{2,1,0:T(8,128)(2,1)} %copy-done.18), channel_id=1, source_target_pairs={{1,0},{2,1},{3,2},{11,3},{10,11},{9,10},{8,9},{0,8},{5,4},{6,5},{7... | collective-permute-start | bytes 786440 | tf_op jit(solution)/shard_map/ppermute | solution.py:480
  65.9 1.5 collective-permute-done.25.refs_13_.refs_15_
  67.4 3.4 %collective-permute-start.29 = (bf16[32,32,128]{2,1,0:T(8,128)(2,1)S(1)}, bf16[32,32,128]{2,1,0:T(8,128)(2,1)}, u32[]{:S(2)}, u32[]{:S(2)}) collective-permute-start(bf16[32,32,128]{2,1,0:T(8,128)(2,1)S(1)} %collective-permute-done.25.refs_13_.refs_15_), channel_id=1, source_target_pairs={{0,1},{1,2},{2,3},{3,11},{11,10},{10,9},{9,8},{8,0},{4,5},{5,6},{6... | collective-permute-start | bytes 786440 | tf_op jit(solution)/shard_map/ppermute | solution.py:480
  70.8 0.5 collective-permute-start.30
  71.4 0.9 copy-done.20
  72.3 0.2 shard_map.58.refs_19_.refs_22_
  72.6 3.0 %collective-permute-start.12 = (bf16[32,32,128]{2,1,0:T(8,128)(2,1)}, bf16[32,32,128]{2,1,0:T(8,128)(2,1)S(1)}, u32[]{:S(2)}, u32[]{:S(2)}) collective-permute-start(bf16[32,32,128]{2,1,0:T(8,128)(2,1)} %copy-done.16), channel_id=1, source_target_pairs={{1,0},{2,1},{3,2},{11,3},{10,11},{9,10},{8,9},{0,8},{5,4},{6,5},{7... | collective-permute-start | bytes 786440 | tf_op jit(solution)/shard_map/ppermute | solution.py:480
  75.6 1.6 %collective-permute-start.13 = (bf16[32,32,128]{2,1,0:T(8,128)(2,1)}, bf16[32,32,128]{2,1,0:T(8,128)(2,1)S(1)}, u32[]{:S(2)}, u32[]{:S(2)}) collective-permute-start(bf16[32,32,128]{2,1,0:T(8,128)(2,1)} %collective-permute-done.9.refs_11_), channel_id=1, source_target_pairs={{0,1},{1,2},{2,3},{3,11},{11,10},{10,9},{9,8},{8,0},{4,5},{5,6},{6... | collective-permute-start | bytes 786440 | tf_op jit(solution)/shard_map/ppermute | solution.py:480
  77.3 4.0 %collective-permute-done.29.refs_17_.refs_19_ = bf16[32,32,128]{2,1,0:T(8,128)(2,1)} collective-permute-done((bf16[32,32,128]{2,1,0:T(8,128)(2,1)S(1)}, bf16[32,32,128]{2,1,0:T(8,128)(2,1)}, u32[]{:S(2)}, u32[]{:S(2)}) %collective-permute-start.29) | collective-permute-done | bytes 262176 | tf_op jit(solution)/shard_map/ppermute | solution.py:480
  81.3 2.5 %collective-permute-start.16 = (bf16[32,32,128]{2,1,0:T(8,128)(2,1)}, bf16[32,32,128]{2,1,0:T(8,128)(2,1)S(1)}, u32[]{:S(2)}, u32[]{:S(2)}) collective-permute-start(bf16[32,32,128]{2,1,0:T(8,128)(2,1)} %collective-permute-done.14.refs_16_), channel_id=1, source_target_pairs={{1,0},{2,1},{3,2},{11,3},{10,11},{9,10},{8,9},{0,8},{5,4},{6,5},{7... | collective-permute-start | bytes 786440 | tf_op jit(solution)/shard_map/ppermute | solution.py:480
  83.8 2.7 %shard_map.57 = (bf16[64,32,128]{2,1,0:T(8,128)(2,1)S(1)}, bf16[64,32,128]{2,1,0:T(8,128)(2,1)S(1)}) custom-call(bf16[2,4,8,16,128]{4,3,2,1,0:T(8,128)(2,1)} %bitcast.3.refs_0_, bf16[2,4,8,16,128]{4,3,2,1,0:T(8,128)(2,1)} %collective-permute-done.1.refs_1_), custom_call_target="tpu_custom_call" | custom-call | tf_op jit(solution)/shard_map/pallas_call | solution.py:444
  86.6 6.4 %shard_map.59 = (f32[64,32,128]{2,1,0:T(8,128)S(1)}, f32[64,32,128]{2,1,0:T(8,128)S(1)}) custom-call(s32[1]{0:T(128)} %bitcast.1.refs_0_, bf16[64,32,128]{2,1,0:T(8,128)(2,1)S(1)} %get-tuple-element.26.refs_1_, bf16[64,32,128]{2,1,0:T(8,128)(2,1)S(1)} %get-tuple-element.27.refs_2_, bf16[32,32,128]{2,1,0:T(8,128)(2,1)S(1)} %get-tuple-element.24.refs_3_.refs_5_, ...), custom_call_target="tpu_custom_call" | custom-call | flops 536870912 | bytes 4194304 | tf_op jit(solution)/shard_map/pallas_call | solution.py:141
  93.1 6.5 %shard_map.60 = (f32[64,32,128]{2,1,0:T(8,128)S(1)}, f32[64,32,128]{2,1,0:T(8,128)S(1)}, bf16[64,32,128]{2,1,0:T(8,128)(2,1)S(1)}, bf16[64,32,128]{2,1,0:T(8,128)(2,1)S(1)}, bf16[128,128,128]{2,1,0:T(8,128)(2,1)S(1)}) custom-call(s32[1]{0:T(128)} %bitcast.1.refs_0_, bf16[64,32,128]{2,1,0:T(8,128)(2,1)S(1)} %get-tuple-element.26.refs_1_, ...), custom_call_target="tpu_custom_call" | custom-call | flops 536870912 | bytes 4194304 | tf_op jit(solution)/shard_map/pallas_call | solution.py:141
  99.6 0.5 collective-permute-start.32
  100.1 1.4 collective-permute-done.31.refs_2_
  101.5 0.7 collective-permute-done.32.refs_4_
  102.3 9.3 %shard_map.61 = (f32[64,32,128]{2,1,0:T(8,128)S(1)}, bf16[64,32,128]{2,1,0:T(8,128)(2,1)S(1)}) custom-call(s32[1]{0:T(128)} %bitcast.1.refs_0_, f32[64,32,128]{2,1,0:T(8,128)S(1)} %get-tuple-element.34.refs_1_, bf16[64,32,128]{2,1,0:T(8,128)(2,1)S(1)} %collective-permute-done.31.refs_2_, f32[64,32,128]{2,1,0:T(8,128)S(1)} %get-tuple-element.36.refs_3_, ...), custom_call_target="tpu_custom_call" | custom-call | flops 1073741824 | bytes 8388608 | tf_op jit(solution)/shard_map/pallas_call | solution.py:141
  111.6 0.2 collective-permute-start.33
  111.8 1.8 %collective-permute-done.33.second_ref = bf16[64,32,128]{2,1,0:T(8,128)(2,1)S(1)} collective-permute-done((bf16[64,32,128]{2,1,0:T(8,128)(2,1)S(1)}, bf16[64,32,128]{2,1,0:T(8,128)(2,1)S(1)}, u32[]{:S(2)}, u32[]{:S(2)}) %collective-permute-start.33) | collective-permute-done | bytes 524320 | tf_op jit(solution)/shard_map/ppermute | solution.py:454
  113.6 0.8 shard_map.62
  114.3 13.2 %all_to_all.10 = bf16[8,4,32,128]{3,2,1,0:T(8,128)(2,1)S(1)} all-to-all(bf16[8,4,32,128]{3,2,1,0:T(8,128)(2,1)S(1)} %bitcast.13), channel_id=1, replica_groups=mesh['ma'=2,'x'=2,'core'=2,'fc'=4] {'x','fc'}, dimensions={0} | all-to-all | bytes 524288 | tf_op jit(solution)/shard_map/all_to_all | solution.py:558
  127.6 0.5 shard_map.63
  128.1 0.6 collective-permute-start.35
  128.7 1.6 %collective-permute-start.34 = (f32[72,128]{1,0:T(8,128)S(1)}, f32[72,128]{1,0:T(8,128)S(1)}, u32[]{:S(2)}, u32[]{:S(2)}) collective-permute-start(f32[72,128]{1,0:T(8,128)S(1)} %get-tuple-element.42), channel_id=1, source_target_pairs={{0,4},{4,0},{1,5},{5,1},{2,6},{6,2},{3,7},{7,3},{8,12},{12,8},{9,1... | collective-permute-start | bytes 110600 | tf_op jit(solution)/shard_map/ppermute | solution.py:454
  130.3 2.2 %collective-permute-done.35 = f32[72,128]{1,0:T(8,128)S(1)} collective-permute-done((f32[72,128]{1,0:T(8,128)S(1)}, f32[72,128]{1,0:T(8,128)S(1)}, u32[]{:S(2)}, u32[]{:S(2)}) %collective-permute-start.35) | collective-permute-done | bytes 36896 | tf_op jit(solution)/shard_map/ppermute | solution.py:489
  132.6 0.8 collective-permute-start.38
  133.4 3.6 %collective-permute-start.37 = (f32[72,128]{1,0:T(8,128)S(1)}, f32[72,128]{1,0:T(8,128)S(1)}, u32[]{:S(2)}, u32[]{:S(2)}) collective-permute-start(f32[72,128]{1,0:T(8,128)S(1)} %add_add_fusion.1), channel_id=1, source_target_pairs={{0,1},{1,0},{2,3},{3,2},{4,5},{5,4},{6,7},{7,6},{8,9},{9,8},{10,11... | collective-permute-start | bytes 110600 | tf_op jit(solution)/shard_map/ppermute | solution.py:495
  137.0 1.7 %collective-permute-done.39 = f32[72,128]{1,0:T(8,128)S(1)} collective-permute-done((f32[72,128]{1,0:T(8,128)S(1)}, f32[72,128]{1,0:T(8,128)S(1)}, u32[]{:S(2)}, u32[]{:S(2)}) %collective-permute-start.39) | collective-permute-done | bytes 36896 | tf_op jit(solution)/shard_map/ppermute | solution.py:495
  138.7 0.4 collective-permute-done.37
  139.2 1.2 collective-permute-done.40.given_ref
  140.4 9.7 %shard_map.64 = f32[2,4,128,128]{3,2,1,0:T(8,128)} custom-call(s32[1]{0:T(128)} %bitcast.core_ref, bf16[8,4,2,16,128]{4,3,2,1,0:T(8,128)(2,1)S(1)} %bitcast.12, f32[72,128]{1,0:T(8,128)S(1)} %add_add_fusion.kept_ref, f32[72,128]{1,0:T(8,128)S(1)} %collective-permute-done.40.given_ref), custom_call_target="tpu_custom_call" | custom-call | tf_op jit(solution)/shard_map/pallas_call | solution.py:318
  (79 shorter events, 0.9 us)
Async XLA Ops:
  0.0 71.4 %copy-start = (f32[2,512]{1,0:T(2,128)S(1)}, f32[2,512]{1,0:T(2,128)}, u32[]{:S(2)}) copy-start(f32[2,512]{1,0:T(2,128)} %param.7) | copy-start | bytes 12292
  0.0 1.2 copy-start.3
  1.2 0.7 copy-start.21
  2.3 29.6 %copy-start.4 = (bf16[32,32,128]{2,1,0:T(8,128)(2,1)}, bf16[32,32,128]{2,1,0:T(8,128)(2,1)S(1)}, u32[]{:S(2)}) copy-start(bf16[32,32,128]{2,1,0:T(8,128)(2,1)S(1)} %get-tuple-element.28.refs_3_) | copy-start | bytes 786436
  2.3 5.5 %collective-permute-start.2 = (bf16[32,32,128]{2,1,0:T(8,128)(2,1)S(1)}, bf16[32,32,128]{2,1,0:T(8,128)(2,1)S(1)}, u32[]{:S(2)}, u32[]{:S(2)}) collective-permute-start(bf16[32,32,128]{2,1,0:T(8,128)(2,1)S(1)} %get-tuple-element.29), channel_id=1, source_target_pairs={{0,4},{4,0},{1,5},{5,1},{2,6},{6,2},{3,7},{7,3},{8,12},{12,8},{9,1... | collective-permute-start | bytes 786440 | tf_op jit(solution)/shard_map/ppermute | solution.py:454
  2.8 5.2 %collective-permute-start.17 = (bf16[32,32,128]{2,1,0:T(8,128)(2,1)S(1)}, bf16[32,32,128]{2,1,0:T(8,128)(2,1)S(1)}, u32[]{:S(2)}, u32[]{:S(2)}) collective-permute-start(bf16[32,32,128]{2,1,0:T(8,128)(2,1)S(1)} %get-tuple-element.30), channel_id=1, source_target_pairs={{0,4},{4,0},{1,5},{5,1},{2,6},{6,2},{3,7},{7,3},{8,12},{12,8},{9,1... | collective-permute-start | bytes 786440 | tf_op jit(solution)/shard_map/ppermute | solution.py:454
  2.9 10.1 %collective-permute-start.4 = (bf16[32,32,128]{2,1,0:T(8,128)(2,1)S(1)}, bf16[32,32,128]{2,1,0:T(8,128)(2,1)S(1)}, u32[]{:S(2)}, u32[]{:S(2)}) collective-permute-start(bf16[32,32,128]{2,1,0:T(8,128)(2,1)S(1)} %get-tuple-element.28.refs_3_), channel_id=1, source_target_pairs={{1,0},{2,1},{3,2},{11,3},{10,11},{9,10},{8,9},{0,8},{5,4},{6,5},{7... | collective-permute-start | bytes 786440 | tf_op jit(solution)/shard_map/ppermute | solution.py:480
  5.8 9.3 %collective-permute-start.3 = (bf16[32,32,128]{2,1,0:T(8,128)(2,1)S(1)}, bf16[32,32,128]{2,1,0:T(8,128)(2,1)S(1)}, u32[]{:S(2)}, u32[]{:S(2)}) collective-permute-start(bf16[32,32,128]{2,1,0:T(8,128)(2,1)S(1)} %get-tuple-element.28.refs_3_), channel_id=1, source_target_pairs={{0,1},{1,2},{2,3},{3,11},{11,10},{10,9},{9,8},{8,0},{4,5},{5,6},{6... | collective-permute-start | bytes 786440 | tf_op jit(solution)/shard_map/ppermute | solution.py:480
  5.9 12.7 %collective-permute-start.18 = (bf16[32,32,128]{2,1,0:T(8,128)(2,1)S(1)}, bf16[32,32,128]{2,1,0:T(8,128)(2,1)S(1)}, u32[]{:S(2)}, u32[]{:S(2)}) collective-permute-start(bf16[32,32,128]{2,1,0:T(8,128)(2,1)S(1)} %get-tuple-element.24.refs_3_.refs_5_), channel_id=1, source_target_pairs={{1,0},{2,1},{3,2},{11,3},{10,11},{9,10},{8,9},{0,8},{5,4},{6,5},{7... | collective-permute-start | bytes 786440 | tf_op jit(solution)/shard_map/ppermute | solution.py:480
  7.8 25.6 %copy-start.6 = (bf16[32,32,128]{2,1,0:T(8,128)(2,1)}, bf16[32,32,128]{2,1,0:T(8,128)(2,1)S(1)}, u32[]{:S(2)}) copy-start(bf16[32,32,128]{2,1,0:T(8,128)(2,1)S(1)} %collective-permute-done.2.refs_4_) | copy-start | bytes 786436
  7.8 12.8 %collective-permute-start = (bf16[32,32,128]{2,1,0:T(8,128)(2,1)S(1)}, bf16[32,32,128]{2,1,0:T(8,128)(2,1)S(1)}, u32[]{:S(2)}, u32[]{:S(2)}) collective-permute-start(bf16[32,32,128]{2,1,0:T(8,128)(2,1)S(1)} %get-tuple-element.24.refs_3_.refs_5_), channel_id=1, source_target_pairs={{0,1},{1,2},{2,3},{3,11},{11,10},{10,9},{9,8},{8,0},{4,5},{5,6},{6... | collective-permute-start | bytes 786440 | tf_op jit(solution)/shard_map/ppermute | solution.py:480
  8.0 16.2 %collective-permute-start.6 = (bf16[32,32,128]{2,1,0:T(8,128)(2,1)S(1)}, bf16[32,32,128]{2,1,0:T(8,128)(2,1)S(1)}, u32[]{:S(2)}, u32[]{:S(2)}) collective-permute-start(bf16[32,32,128]{2,1,0:T(8,128)(2,1)S(1)} %collective-permute-done.2.refs_4_), channel_id=1, source_target_pairs={{1,0},{2,1},{3,2},{11,3},{10,11},{9,10},{8,9},{0,8},{5,4},{6,5},{7... | collective-permute-start | bytes 786440 | tf_op jit(solution)/shard_map/ppermute | solution.py:480
  13.0 22.5 %copy-start.8 = (bf16[32,32,128]{2,1,0:T(8,128)(2,1)}, bf16[32,32,128]{2,1,0:T(8,128)(2,1)S(1)}, u32[]{:S(2)}) copy-start(bf16[32,32,128]{2,1,0:T(8,128)(2,1)S(1)} %collective-permute-done.4.refs_6_) | copy-start | bytes 786436
  13.0 15.9 %collective-permute-start.5 = (bf16[32,32,128]{2,1,0:T(8,128)(2,1)S(1)}, bf16[32,32,128]{2,1,0:T(8,128)(2,1)S(1)}, u32[]{:S(2)}, u32[]{:S(2)}) collective-permute-start(bf16[32,32,128]{2,1,0:T(8,128)(2,1)S(1)} %collective-permute-done.2.refs_4_), channel_id=1, source_target_pairs={{0,1},{1,2},{2,3},{3,11},{11,10},{10,9},{9,8},{8,0},{4,5},{5,6},{6... | collective-permute-start | bytes 786440 | tf_op jit(solution)/shard_map/ppermute | solution.py:480
  15.1 28.7 %copy-start.10 = (bf16[32,32,128]{2,1,0:T(8,128)(2,1)}, bf16[32,32,128]{2,1,0:T(8,128)(2,1)S(1)}, u32[]{:S(2)}) copy-start(bf16[32,32,128]{2,1,0:T(8,128)(2,1)S(1)} %collective-permute-done.3.refs_5_) | copy-start | bytes 786436
  15.1 14.8 %collective-permute-start.20 = (bf16[32,32,128]{2,1,0:T(8,128)(2,1)S(1)}, bf16[32,32,128]{2,1,0:T(8,128)(2,1)S(1)}, u32[]{:S(2)}, u32[]{:S(2)}) collective-permute-start(bf16[32,32,128]{2,1,0:T(8,128)(2,1)S(1)} %collective-permute-done.17.refs_4_.refs_6_), channel_id=1, source_target_pairs={{1,0},{2,1},{3,2},{11,3},{10,11},{9,10},{8,9},{0,8},{5,4},{6,5},{7... | collective-permute-start | bytes 786440 | tf_op jit(solution)/shard_map/ppermute | solution.py:480
  18.6 13.3 %collective-permute-start.19 = (bf16[32,32,128]{2,1,0:T(8,128)(2,1)S(1)}, bf16[32,32,128]{2,1,0:T(8,128)(2,1)S(1)}, u32[]{:S(2)}, u32[]{:S(2)}) collective-permute-start(bf16[32,32,128]{2,1,0:T(8,128)(2,1)S(1)} %collective-permute-done.17.refs_4_.refs_6_), channel_id=1, source_target_pairs={{0,1},{1,2},{2,3},{3,11},{11,10},{10,9},{9,8},{8,0},{4,5},{5,6},{6... | collective-permute-start | bytes 786440 | tf_op jit(solution)/shard_map/ppermute | solution.py:480
  20.7 14.8 %collective-permute-start.8 = (bf16[32,32,128]{2,1,0:T(8,128)(2,1)S(1)}, bf16[32,32,128]{2,1,0:T(8,128)(2,1)S(1)}, u32[]{:S(2)}, u32[]{:S(2)}) collective-permute-start(bf16[32,32,128]{2,1,0:T(8,128)(2,1)S(1)} %collective-permute-done.4.refs_6_), channel_id=1, source_target_pairs={{1,0},{2,1},{3,2},{11,3},{10,11},{9,10},{8,9},{0,8},{5,4},{6,5},{7... | collective-permute-start | bytes 786440 | tf_op jit(solution)/shard_map/ppermute | solution.py:480
  24.2 23.6 %copy-start.12 = (bf16[32,32,128]{2,1,0:T(8,128)(2,1)}, bf16[32,32,128]{2,1,0:T(8,128)(2,1)S(1)}, u32[]{:S(2)}) copy-start(bf16[32,32,128]{2,1,0:T(8,128)(2,1)S(1)} %collective-permute-done.6.refs_8_) | copy-start | bytes 786436
  24.2 19.5 %collective-permute-start.7 = (bf16[32,32,128]{2,1,0:T(8,128)(2,1)S(1)}, bf16[32,32,128]{2,1,0:T(8,128)(2,1)}, u32[]{:S(2)}, u32[]{:S(2)}) collective-permute-start(bf16[32,32,128]{2,1,0:T(8,128)(2,1)S(1)} %collective-permute-done.3.refs_5_), channel_id=1, source_target_pairs={{0,1},{1,2},{2,3},{3,11},{11,10},{10,9},{9,8},{8,0},{4,5},{5,6},{6... | collective-permute-start | bytes 786440 | tf_op jit(solution)/shard_map/ppermute | solution.py:480
  26.3 1.0 copy-start.1
  28.9 17.0 %collective-permute-start.22 = (bf16[32,32,128]{2,1,0:T(8,128)(2,1)S(1)}, bf16[32,32,128]{2,1,0:T(8,128)(2,1)S(1)}, u32[]{:S(2)}, u32[]{:S(2)}) collective-permute-start(bf16[32,32,128]{2,1,0:T(8,128)(2,1)S(1)} %collective-permute-done.18.refs_6_.refs_8_), channel_id=1, source_target_pairs={{1,0},{2,1},{3,2},{11,3},{10,11},{9,10},{8,9},{0,8},{5,4},{6,5},{7... | collective-permute-start | bytes 786440 | tf_op jit(solution)/shard_map/ppermute | solution.py:480
  29.9 16.1 %collective-permute-start.21 = (bf16[32,32,128]{2,1,0:T(8,128)(2,1)S(1)}, bf16[32,32,128]{2,1,0:T(8,128)(2,1)S(1)}, u32[]{:S(2)}, u32[]{:S(2)}) collective-permute-start(bf16[32,32,128]{2,1,0:T(8,128)(2,1)S(1)} %collective-permute-done.refs_5_.refs_7_), channel_id=1, source_target_pairs={{0,1},{1,2},{2,3},{3,11},{11,10},{10,9},{9,8},{8,0},{4,5},{5,6},{6... | collective-permute-start | bytes 786440 | tf_op jit(solution)/shard_map/ppermute | solution.py:480
  31.9 16.0 %collective-permute-start.10 = (bf16[32,32,128]{2,1,0:T(8,128)(2,1)S(1)}, bf16[32,32,128]{2,1,0:T(8,128)(2,1)S(1)}, u32[]{:S(2)}, u32[]{:S(2)}) collective-permute-start(bf16[32,32,128]{2,1,0:T(8,128)(2,1)S(1)} %collective-permute-done.6.refs_8_), channel_id=1, source_target_pairs={{1,0},{2,1},{3,2},{11,3},{10,11},{9,10},{8,9},{0,8},{5,4},{6,5},{7... | collective-permute-start | bytes 786440 | tf_op jit(solution)/shard_map/ppermute | solution.py:480
  35.5 0.7 copy-start.16
  36.2 13.0 %collective-permute-start.9 = (bf16[32,32,128]{2,1,0:T(8,128)(2,1)S(1)}, bf16[32,32,128]{2,1,0:T(8,128)(2,1)}, u32[]{:S(2)}, u32[]{:S(2)}) collective-permute-start(bf16[32,32,128]{2,1,0:T(8,128)(2,1)S(1)} %collective-permute-done.5.refs_7_), channel_id=1, source_target_pairs={{0,1},{1,2},{2,3},{3,11},{11,10},{10,9},{9,8},{8,0},{4,5},{5,6},{6... | collective-permute-start | bytes 786440 | tf_op jit(solution)/shard_map/ppermute | solution.py:480
  38.3 0.7 copy-start.14
  39.0 18.7 %all-to-all-start = ((bf16[8,8,16,128]{3,2,1,0:T(8,128)(2,1)}), bf16[8,8,16,128]{3,2,1,0:T(8,128)(2,1)}, u32[]{:S(2)}, u32[]{:S(2)}) async-start(bf16[8,8,16,128]{3,2,1,0:T(8,128)(2,1)} %shard_map.55), calls=%async_computation | async-start | bytes 524288 | tf_op jit(solution)/shard_map/all_to_all | solution.py:523
  43.8 13.6 %collective-permute-start.24 = (bf16[32,32,128]{2,1,0:T(8,128)(2,1)S(1)}, bf16[32,32,128]{2,1,0:T(8,128)(2,1)S(1)}, u32[]{:S(2)}, u32[]{:S(2)}) collective-permute-start(bf16[32,32,128]{2,1,0:T(8,128)(2,1)S(1)} %collective-permute-done.20.refs_8_.refs_10_), channel_id=1, source_target_pairs={{1,0},{2,1},{3,2},{11,3},{10,11},{9,10},{8,9},{0,8},{5,4},{6,5},{7... | collective-permute-start | bytes 786440 | tf_op jit(solution)/shard_map/ppermute | solution.py:480
  45.8 11.8 %collective-permute-start.23 = (bf16[32,32,128]{2,1,0:T(8,128)(2,1)S(1)}, bf16[32,32,128]{2,1,0:T(8,128)(2,1)S(1)}, u32[]{:S(2)}, u32[]{:S(2)}) collective-permute-start(bf16[32,32,128]{2,1,0:T(8,128)(2,1)S(1)} %collective-permute-done.19.refs_7_.refs_9_), channel_id=1, source_target_pairs={{0,1},{1,2},{2,3},{3,11},{11,10},{10,9},{9,8},{8,0},{4,5},{5,6},{6... | collective-permute-start | bytes 786440 | tf_op jit(solution)/shard_map/ppermute | solution.py:480
  45.9 17.0 %collective-permute-start.11 = (bf16[32,32,128]{2,1,0:T(8,128)(2,1)}, bf16[32,32,128]{2,1,0:T(8,128)(2,1)}, u32[]{:S(2)}, u32[]{:S(2)}) collective-permute-start(bf16[32,32,128]{2,1,0:T(8,128)(2,1)} %collective-permute-done.7.refs_9_), channel_id=1, source_target_pairs={{0,1},{1,2},{2,3},{3,11},{11,10},{10,9},{9,8},{8,0},{4,5},{5,6},{6... | collective-permute-start | bytes 786440 | tf_op jit(solution)/shard_map/ppermute | solution.py:480
  47.9 3.1 %copy-start.18 = (bf16[32,32,128]{2,1,0:T(8,128)(2,1)}, bf16[32,32,128]{2,1,0:T(8,128)(2,1)S(1)}, u32[]{:S(2)}) copy-start(bf16[32,32,128]{2,1,0:T(8,128)(2,1)S(1)} %collective-permute-done.10.refs_12_) | copy-start | bytes 786436
  47.9 18.0 %collective-permute-start.26 = (bf16[32,32,128]{2,1,0:T(8,128)(2,1)S(1)}, bf16[32,32,128]{2,1,0:T(8,128)(2,1)S(1)}, u32[]{:S(2)}, u32[]{:S(2)}) collective-permute-start(bf16[32,32,128]{2,1,0:T(8,128)(2,1)S(1)} %collective-permute-done.22.refs_10_.refs_12_), channel_id=1, source_target_pairs={{1,0},{2,1},{3,2},{11,3},{10,11},{9,10},{8,9},{0,8},{5,4},{6,5},{7... | collective-permute-start | bytes 786440 | tf_op jit(solution)/shard_map/ppermute | solution.py:480
  49.2 18.2 %collective-permute-start.25 = (bf16[32,32,128]{2,1,0:T(8,128)(2,1)S(1)}, bf16[32,32,128]{2,1,0:T(8,128)(2,1)S(1)}, u32[]{:S(2)}, u32[]{:S(2)}) collective-permute-start(bf16[32,32,128]{2,1,0:T(8,128)(2,1)S(1)} %collective-permute-done.21.refs_9_.refs_11_), channel_id=1, source_target_pairs={{0,1},{1,2},{2,3},{3,11},{11,10},{10,9},{9,8},{8,0},{4,5},{5,6},{6... | collective-permute-start | bytes 786440 | tf_op jit(solution)/shard_map/ppermute | solution.py:480
  57.4 13.4 %collective-permute-start.28 = (bf16[32,32,128]{2,1,0:T(8,128)(2,1)S(1)}, bf16[32,32,128]{2,1,0:T(8,128)(2,1)S(1)}, u32[]{:S(2)}, u32[]{:S(2)}) collective-permute-start(bf16[32,32,128]{2,1,0:T(8,128)(2,1)S(1)} %collective-permute-done.24.refs_12_.refs_14_), channel_id=1, source_target_pairs={{1,0},{2,1},{3,2},{11,3},{10,11},{9,10},{8,9},{0,8},{5,4},{6,5},{7... | collective-permute-start | bytes 786440 | tf_op jit(solution)/shard_map/ppermute | solution.py:480
  57.7 14.9 %collective-permute-start.1 = (bf16[2,4,8,16,128]{4,3,2,1,0:T(8,128)(2,1)}, bf16[2,4,8,16,128]{4,3,2,1,0:T(8,128)(2,1)}, u32[]{:S(2)}, u32[]{:S(2)}) collective-permute-start(bf16[2,4,8,16,128]{4,3,2,1,0:T(8,128)(2,1)} %bitcast.3.refs_0_), channel_id=1, source_target_pairs={{0,4},{4,0},{1,5},{5,1},{2,6},{6,2},{3,7},{7,3},{8,12},{12,8},{9,1... | collective-permute-start | bytes 786440 | tf_op jit(solution)/shard_map/ppermute | solution.py:454
  62.9 12.7 %collective-permute-start.14 = (bf16[32,32,128]{2,1,0:T(8,128)(2,1)}, bf16[32,32,128]{2,1,0:T(8,128)(2,1)}, u32[]{:S(2)}, u32[]{:S(2)}) collective-permute-start(bf16[32,32,128]{2,1,0:T(8,128)(2,1)} %copy-done.18), channel_id=1, source_target_pairs={{1,0},{2,1},{3,2},{11,3},{10,11},{9,10},{8,9},{0,8},{5,4},{6,5},{7... | collective-permute-start | bytes 786440 | tf_op jit(solution)/shard_map/ppermute | solution.py:480
  65.9 11.4 %collective-permute-start.27 = (bf16[32,32,128]{2,1,0:T(8,128)(2,1)S(1)}, bf16[32,32,128]{2,1,0:T(8,128)(2,1)}, u32[]{:S(2)}, u32[]{:S(2)}) collective-permute-start(bf16[32,32,128]{2,1,0:T(8,128)(2,1)S(1)} %collective-permute-done.23.refs_11_.refs_13_), channel_id=1, source_target_pairs={{0,1},{1,2},{2,3},{3,11},{11,10},{10,9},{9,8},{8,0},{4,5},{5,6},{6... | collective-permute-start | bytes 786440 | tf_op jit(solution)/shard_map/ppermute | solution.py:480
  67.4 13.9 %collective-permute-start.29 = (bf16[32,32,128]{2,1,0:T(8,128)(2,1)S(1)}, bf16[32,32,128]{2,1,0:T(8,128)(2,1)}, u32[]{:S(2)}, u32[]{:S(2)}) collective-permute-start(bf16[32,32,128]{2,1,0:T(8,128)(2,1)S(1)} %collective-permute-done.25.refs_13_.refs_15_), channel_id=1, source_target_pairs={{0,1},{1,2},{2,3},{3,11},{11,10},{10,9},{9,8},{8,0},{4,5},{5,6},{6... | collective-permute-start | bytes 786440 | tf_op jit(solution)/shard_map/ppermute | solution.py:480
  70.8 15.7 %collective-permute-start.30 = (bf16[32,32,128]{2,1,0:T(8,128)(2,1)S(1)}, bf16[32,32,128]{2,1,0:T(8,128)(2,1)}, u32[]{:S(2)}, u32[]{:S(2)}) collective-permute-start(bf16[32,32,128]{2,1,0:T(8,128)(2,1)S(1)} %collective-permute-done.28.refs_16_.refs_18_), channel_id=1, source_target_pairs={{1,0},{2,1},{3,2},{11,3},{10,11},{9,10},{8,9},{0,8},{5,4},{6,5},{7... | collective-permute-start | bytes 786440 | tf_op jit(solution)/shard_map/ppermute | solution.py:480
  71.4 0.9 copy-start.20
  72.5 20.5 %copy-start.5 = (bf16[32,32,128]{2,1,0:T(8,128)(2,1)S(1)}, bf16[32,32,128]{2,1,0:T(8,128)(2,1)}, u32[]{:S(2)}) copy-start(bf16[32,32,128]{2,1,0:T(8,128)(2,1)} %copy-done.4) | copy-start | bytes 786436
  72.5 20.5 %copy-start.7 = (bf16[32,32,128]{2,1,0:T(8,128)(2,1)S(1)}, bf16[32,32,128]{2,1,0:T(8,128)(2,1)}, u32[]{:S(2)}) copy-start(bf16[32,32,128]{2,1,0:T(8,128)(2,1)} %copy-done.6) | copy-start | bytes 786436
  72.5 20.5 %copy-start.9 = (bf16[32,32,128]{2,1,0:T(8,128)(2,1)S(1)}, bf16[32,32,128]{2,1,0:T(8,128)(2,1)}, u32[]{:S(2)}) copy-start(bf16[32,32,128]{2,1,0:T(8,128)(2,1)} %copy-done.8) | copy-start | bytes 786436
  72.5 20.5 %copy-start.11 = (bf16[32,32,128]{2,1,0:T(8,128)(2,1)S(1)}, bf16[32,32,128]{2,1,0:T(8,128)(2,1)}, u32[]{:S(2)}) copy-start(bf16[32,32,128]{2,1,0:T(8,128)(2,1)} %copy-done.10) | copy-start | bytes 786436
  72.5 20.5 %copy-start.13 = (bf16[32,32,128]{2,1,0:T(8,128)(2,1)S(1)}, bf16[32,32,128]{2,1,0:T(8,128)(2,1)}, u32[]{:S(2)}) copy-start(bf16[32,32,128]{2,1,0:T(8,128)(2,1)} %copy-done.12) | copy-start | bytes 786436
  72.5 20.5 %copy-start.15 = (bf16[32,32,128]{2,1,0:T(8,128)(2,1)S(1)}, bf16[32,32,128]{2,1,0:T(8,128)(2,1)}, u32[]{:S(2)}) copy-start(bf16[32,32,128]{2,1,0:T(8,128)(2,1)} %copy-done.14) | copy-start | bytes 786436
  72.5 20.5 %copy-start.17 = (bf16[32,32,128]{2,1,0:T(8,128)(2,1)S(1)}, bf16[32,32,128]{2,1,0:T(8,128)(2,1)}, u32[]{:S(2)}) copy-start(bf16[32,32,128]{2,1,0:T(8,128)(2,1)} %copy-done.16) | copy-start | bytes 786436
  72.6 20.5 %copy-start.19 = (bf16[32,32,128]{2,1,0:T(8,128)(2,1)S(1)}, bf16[32,32,128]{2,1,0:T(8,128)(2,1)}, u32[]{:S(2)}) copy-start(bf16[32,32,128]{2,1,0:T(8,128)(2,1)} %copy-done.18) | copy-start | bytes 786436
  72.6 20.4 %collective-permute-start.12 = (bf16[32,32,128]{2,1,0:T(8,128)(2,1)}, bf16[32,32,128]{2,1,0:T(8,128)(2,1)S(1)}, u32[]{:S(2)}, u32[]{:S(2)}) collective-permute-start(bf16[32,32,128]{2,1,0:T(8,128)(2,1)} %copy-done.16), channel_id=1, source_target_pairs={{1,0},{2,1},{3,2},{11,3},{10,11},{9,10},{8,9},{0,8},{5,4},{6,5},{7... | collective-permute-start | bytes 786440 | tf_op jit(solution)/shard_map/ppermute | solution.py:480
  75.6 17.3 %collective-permute-start.13 = (bf16[32,32,128]{2,1,0:T(8,128)(2,1)}, bf16[32,32,128]{2,1,0:T(8,128)(2,1)S(1)}, u32[]{:S(2)}, u32[]{:S(2)}) collective-permute-start(bf16[32,32,128]{2,1,0:T(8,128)(2,1)} %collective-permute-done.9.refs_11_), channel_id=1, source_target_pairs={{0,1},{1,2},{2,3},{3,11},{11,10},{10,9},{9,8},{8,0},{4,5},{5,6},{6... | collective-permute-start | bytes 786440 | tf_op jit(solution)/shard_map/ppermute | solution.py:480
  77.2 15.7 %collective-permute-start.15 = (bf16[32,32,128]{2,1,0:T(8,128)(2,1)}, bf16[32,32,128]{2,1,0:T(8,128)(2,1)S(1)}, u32[]{:S(2)}, u32[]{:S(2)}) collective-permute-start(bf16[32,32,128]{2,1,0:T(8,128)(2,1)} %collective-permute-done.11.refs_13_), channel_id=1, source_target_pairs={{0,1},{1,2},{2,3},{3,11},{11,10},{10,9},{9,8},{8,0},{4,5},{5,6},{6... | collective-permute-start | bytes 786440 | tf_op jit(solution)/shard_map/ppermute | solution.py:480
  81.3 11.7 %collective-permute-start.16 = (bf16[32,32,128]{2,1,0:T(8,128)(2,1)}, bf16[32,32,128]{2,1,0:T(8,128)(2,1)S(1)}, u32[]{:S(2)}, u32[]{:S(2)}) collective-permute-start(bf16[32,32,128]{2,1,0:T(8,128)(2,1)} %collective-permute-done.14.refs_16_), channel_id=1, source_target_pairs={{1,0},{2,1},{3,2},{11,3},{10,11},{9,10},{8,9},{0,8},{5,4},{6,5},{7... | collective-permute-start | bytes 786440 | tf_op jit(solution)/shard_map/ppermute | solution.py:480
  99.5 2.0 %collective-permute-start.31 = (bf16[64,32,128]{2,1,0:T(8,128)(2,1)S(1)}, bf16[64,32,128]{2,1,0:T(8,128)(2,1)S(1)}, u32[]{:S(2)}, u32[]{:S(2)}) collective-permute-start(bf16[64,32,128]{2,1,0:T(8,128)(2,1)S(1)} %get-tuple-element.35), channel_id=1, source_target_pairs={{0,4},{4,0},{1,5},{5,1},{2,6},{6,2},{3,7},{7,3},{8,12},{12,8},{9,1... | collective-permute-start | bytes 1572872 | tf_op jit(solution)/shard_map/ppermute | solution.py:454
  99.6 2.6 %collective-permute-start.32 = (bf16[64,32,128]{2,1,0:T(8,128)(2,1)S(1)}, bf16[64,32,128]{2,1,0:T(8,128)(2,1)S(1)}, u32[]{:S(2)}, u32[]{:S(2)}) collective-permute-start(bf16[64,32,128]{2,1,0:T(8,128)(2,1)S(1)} %get-tuple-element.37), channel_id=1, source_target_pairs={{0,4},{4,0},{1,5},{5,1},{2,6},{6,2},{3,7},{7,3},{8,12},{12,8},{9,1... | collective-permute-start | bytes 1572872 | tf_op jit(solution)/shard_map/ppermute | solution.py:454
  102.3 25.3 %copy-start.2 = (f32[2,32,16,128]{3,2,1,0:T(8,128)S(1)}, f32[2,32,16,128]{3,2,1,0:T(8,128)}, u32[]{:S(2)}) copy-start(f32[2,32,16,128]{3,2,1,0:T(8,128)} %start_ref.3) | copy-start | bytes 1572868
  111.6 2.0 %collective-permute-start.33 = (bf16[64,32,128]{2,1,0:T(8,128)(2,1)S(1)}, bf16[64,32,128]{2,1,0:T(8,128)(2,1)S(1)}, u32[]{:S(2)}, u32[]{:S(2)}) collective-permute-start(bf16[64,32,128]{2,1,0:T(8,128)(2,1)S(1)} %get-tuple-element.40), channel_id=1, source_target_pairs={{0,4},{4,0},{1,5},{5,1},{2,6},{6,2},{3,7},{7,3},{8,12},{12,8},{9,1... | collective-permute-start | bytes 1572872 | tf_op jit(solution)/shard_map/ppermute | solution.py:454
  128.1 4.4 %collective-permute-start.35 = (f32[72,128]{1,0:T(8,128)S(1)}, f32[72,128]{1,0:T(8,128)S(1)}, u32[]{:S(2)}, u32[]{:S(2)}) collective-permute-start(f32[72,128]{1,0:T(8,128)S(1)} %get-tuple-element.41), channel_id=1, source_target_pairs={{0,8},{8,0},{1,9},{9,1},{2,10},{10,2},{3,11},{11,3},{4,12},{12,4},... | collective-permute-start | bytes 110600 | tf_op jit(solution)/shard_map/ppermute | solution.py:489
  128.7 3.8 %collective-permute-start.36 = (f32[72,128]{1,0:T(8,128)S(1)}, f32[72,128]{1,0:T(8,128)S(1)}, u32[]{:S(2)}, u32[]{:S(2)}) collective-permute-start(f32[72,128]{1,0:T(8,128)S(1)} %get-tuple-element.42), channel_id=1, source_target_pairs={{0,12},{4,8},{8,4},{12,0},{1,13},{5,9},{9,5},{13,1},{2,14},{6,10},... | collective-permute-start | bytes 110600 | tf_op jit(solution)/shard_map/ppermute | solution.py:488
  128.7 3.8 %collective-permute-start.34 = (f32[72,128]{1,0:T(8,128)S(1)}, f32[72,128]{1,0:T(8,128)S(1)}, u32[]{:S(2)}, u32[]{:S(2)}) collective-permute-start(f32[72,128]{1,0:T(8,128)S(1)} %get-tuple-element.42), channel_id=1, source_target_pairs={{0,4},{4,0},{1,5},{5,1},{2,6},{6,2},{3,7},{7,3},{8,12},{12,8},{9,1... | collective-permute-start | bytes 110600 | tf_op jit(solution)/shard_map/ppermute | solution.py:454
  132.5 6.2 %collective-permute-start.39 = (f32[72,128]{1,0:T(8,128)S(1)}, f32[72,128]{1,0:T(8,128)S(1)}, u32[]{:S(2)}, u32[]{:S(2)}) collective-permute-start(f32[72,128]{1,0:T(8,128)S(1)} %add_add_fusion.1), channel_id=1, source_target_pairs={{0,3},{1,2},{2,1},{3,0},{4,7},{5,6},{6,5},{7,4},{8,11},{9,10},{10,... | collective-permute-start | bytes 110600 | tf_op jit(solution)/shard_map/ppermute | solution.py:495
  132.6 6.1 %collective-permute-start.38 = (f32[72,128]{1,0:T(8,128)S(1)}, f32[72,128]{1,0:T(8,128)S(1)}, u32[]{:S(2)}, u32[]{:S(2)}) collective-permute-start(f32[72,128]{1,0:T(8,128)S(1)} %add_add_fusion.1), channel_id=1, source_target_pairs={{0,2},{1,3},{2,0},{3,1},{4,6},{5,7},{6,4},{7,5},{8,10},{9,11},{10,... | collective-permute-start | bytes 110600 | tf_op jit(solution)/shard_map/ppermute | solution.py:495
  133.4 5.7 %collective-permute-start.37 = (f32[72,128]{1,0:T(8,128)S(1)}, f32[72,128]{1,0:T(8,128)S(1)}, u32[]{:S(2)}, u32[]{:S(2)}) collective-permute-start(f32[72,128]{1,0:T(8,128)S(1)} %add_add_fusion.1), channel_id=1, source_target_pairs={{0,1},{1,0},{2,3},{3,2},{4,5},{5,4},{6,7},{7,6},{8,9},{9,8},{10,11... | collective-permute-start | bytes 110600 | tf_op jit(solution)/shard_map/ppermute | solution.py:495
  139.1 1.3 collective-permute-start.40
